TPU v7x, 32 devices: a whole 2x2x4 slice. The times are simulated.
32 devices in a mesh: stars: 8 (over z, x), seg: 4 (over y, core).
Axes of the slice: x: 2, y: 2, z: 4, core: 2. Of those that a mesh axis runs over, the one named last changes fastest.
Arguments:
- obs_star: int32 [4096, 128], P(('stars', 'seg')), may hold values from 0 to 8191
- obs_knot: int32 [4096, 128], P(('stars', 'seg')), may hold values from 0 to 8191
- obs_frac: float32 [4096, 128], P(('stars', 'seg')), may hold values from 0 to 1
- star_coef: float32 [5, 4096, 128], P(None, ('stars', 'seg')), may hold values from -6 to 6
- att_coef: float32 [4, 4096, 128], P(None, ('stars', 'seg')), may hold values from -3 to 3
- cal_coef: float32 [4096, 128], P(('stars', 'seg')), may hold values from -6 to 6
- tile_cal: int32 [4096], P(('stars', 'seg')), may hold values from 0 to 255
- live_tiles: int32 [32], P(('stars', 'seg')), may hold values from 1 to 128, as said below
- obs_value: float32 [4096, 128], P(('stars', 'seg')), may hold values from -8 to 8
Outputs:
- star_solution: float32 [5, 65536], P(None, 'stars')
- attitude_solution: float32 [4, 32768], P(None, 'seg')
- calibration_solution: float32 [1024, 128], P('seg')
- residual: float32 [4096, 128], P(('stars', 'seg'))
Inputs may be any that keep to these rules, and one draw needn't show every extreme that they name: Entry d belongs to device d in the order of the stars axis, then seg; that device's first live_tiles[d] tile slots are live and the rest are padding; some device has all 128 slots live. `obs_knot`: knots past a segment's last knot are the next segment's first knots.
All inputs are finite; a program needn't handle non-finite values.
Results may differ from a plain program's by a relative error of at most 0.00017.
Values sent between devices are 32-bit elements; how exact they have to be, the bound alone decides.
No kernel may reach another device: no remote copies, remote signals or barrier semaphores. Data moves between devices by JAX's collectives and lax.ppermute only.
A program may use at most 128 MiB of HBM per device.

v0:
```python
import math

import jax
import jax.numpy as jnp
from jax import lax
from jax.sharding import PartitionSpec as P

STAR_DEV = 8192
KNOT_DEV = 8192
CALB_DEV = 256
ITERS = 2


def shifted(block, axis, distance):
    devices = range(lax.axis_size(axis))
    route = [(i - distance, i) for i in devices if i - distance in devices]
    return lax.ppermute(block, axis, route)


def spline_weights(fraction):
    remain = 1.0 - fraction
    square = fraction * fraction
    cubed = square * fraction
    return (
        remain * remain * remain / 6.0,
        (3.0 * cubed - 6.0 * square + 4.0) / 6.0,
        (-3.0 * cubed + 3.0 * square + 3.0 * fraction + 1.0) / 6.0,
        cubed / 6.0,
    )


def on_device(
    obs_star, obs_knot, obs_frac, star_coef, att_coef, cal_coef, tile_cal, live_tiles, obs_value
):
    tile_count, tile_width = obs_star.shape
    per_turn = math.gcd(64, tile_count)
    live_count = live_tiles[0]
    turn_count = (live_count + per_turn - 1) // per_turn
    tile_rows = jnp.arange(tile_count, dtype=jnp.int32)
    full_mask = (tile_rows < live_count).astype(jnp.float32)[:, None]

    def block_slices(start):

        def cut(array, axis_pos):
            return lax.dynamic_slice_in_dim(array, start, per_turn, axis_pos)

        local_rows = start + jnp.arange(per_turn, dtype=jnp.int32)
        block_mask = (local_rows < live_count).astype(jnp.float32)[:, None]
        return (
            cut(obs_star, 0),
            cut(obs_knot, 0),
            spline_weights(cut(obs_frac, 0)),
            cut(star_coef, 1),
            cut(att_coef, 1),
            cut(cal_coef, 0),
            cut(tile_cal, 0),
            block_mask,
        )

    def gradient(values):

        def gradient_one_turn(turn_index, carry):
            star_grad, att_grad, cal_grad = carry
            start = turn_index * per_turn
            star_ids, knot_ids, weights, star_rows, att_rows, cal_rows, cal_ids, block_mask = (
                block_slices(start)
            )
            masked = lax.dynamic_slice_in_dim(values, start, per_turn, 0) * block_mask
            star_grad = star_grad.at[:, star_ids].add(star_rows * masked)
            for offset in range(4):
                att_grad = att_grad.at[:, knot_ids + offset].add(
                    att_rows * (weights[offset] * masked)
                )
            cal_grad = cal_grad.at[cal_ids].add(cal_rows * masked)
            return (star_grad, att_grad, cal_grad)

        start_carry = (
            jnp.zeros((5, STAR_DEV), jnp.float32),
            jnp.zeros((4, KNOT_DEV + 3), jnp.float32),
            jnp.zeros((CALB_DEV, tile_width), jnp.float32),
        )
        star_grad, att_grad, cal_grad = lax.fori_loop(0, turn_count, gradient_one_turn, start_carry)
        behind_knots = shifted(att_grad[:, KNOT_DEV:], "seg", 1)
        att_grad = att_grad[:, :KNOT_DEV].at[:, :3].add(behind_knots)
        att_sum, cal_sum = lax.psum((att_grad, cal_grad), "stars")
        star_sum = lax.psum(star_grad, "seg")
        return (star_sum, att_sum, cal_sum)

    def total(local_value):
        return lax.psum(local_value, ("stars", "seg"))

    def square_term(parts):
        star_part = jnp.sum(parts[0] * parts[0]) / lax.axis_size("seg")
        time_part = (jnp.sum(parts[1] * parts[1]) + jnp.sum(parts[2] * parts[2])) / lax.axis_size(
            "stars"
        )
        return star_part + time_part

    residual = obs_value * full_mask
    grad_parts = gradient(residual)
    grad_norm = total(square_term(grad_parts))
    direction = grad_parts
    solution = tuple((jnp.zeros_like(current) for current in grad_parts))
    for iteration in range(ITERS):
        star_x = direction[0]
        att_x = direction[1]
        cal_x = direction[2]
        ahead_knots = shifted(att_x[:, :3], "seg", -1)
        extended = jnp.concatenate([att_x, ahead_knots], axis=1)

        def forward_one_turn(turn_index, result):
            start = turn_index * per_turn
            star_ids, knot_ids, weights, star_rows, att_rows, cal_rows, cal_ids, block_mask = (
                block_slices(start)
            )
            row_values = jnp.sum(star_rows * star_x[:, star_ids], axis=0)
            for offset in range(4):
                row_values = row_values + weights[offset] * jnp.sum(
                    att_rows * extended[:, knot_ids + offset], axis=0
                )
            row_values = row_values + cal_rows * cal_x[cal_ids]
            return lax.dynamic_update_slice_in_dim(result, row_values * block_mask, start, 0)

        image = lax.fori_loop(
            0, turn_count, forward_one_turn, jnp.zeros((tile_count, tile_width), jnp.float32)
        )
        curvature = total(jnp.sum(image * image))
        back_image = gradient(image)
        step_size = grad_norm / curvature
        grad_parts = tuple(
            (current - step_size * change for current, change in zip(grad_parts, back_image))
        )
        residual = residual - step_size * image
        solution = tuple(
            (current + step_size * moving for current, moving in zip(solution, direction))
        )
        new_norm = total(square_term(grad_parts))
        direction = tuple(
            (fresh + new_norm / grad_norm * moving for fresh, moving in zip(grad_parts, direction))
        )
        grad_norm = new_norm
    return (solution[0], solution[1], solution[2], residual)


def solution(mesh):
    placed = (
        P(("stars", "seg"), None),
        P(("stars", "seg"), None),
        P(("stars", "seg"), None),
        P(None, ("stars", "seg"), None),
        P(None, ("stars", "seg"), None),
        P(("stars", "seg"), None),
        P(("stars", "seg")),
        P(("stars", "seg")),
        P(("stars", "seg"), None),
    )
    return jax.shard_map(
        on_device,
        mesh=mesh,
        in_specs=placed,
        out_specs=(P(None, "stars"), P(None, "seg"), P("seg", None), P(("stars", "seg"), None)),
        check_vma=False,
    )
```

profile of v0, /device:TPU:0, one launch (start us, length us, event | category | flops | bytes accessed | tf_op | source)
XLA Modules:
  0.0 1977.3 jit_solution(5470035122241427912)
XLA Ops:
  23.0 233.9 %while.58 = (s32[]{:T(128)}, f32[5,8192]{0,1:T(8,128)}, f32[4,8195]{0,1:T(8,128)}, f32[256,128]{1,0:T(8,128)S(1)}, s32[]{:T(128)}, /*index=5*/s32[128,128]{1,0:T...) while((s32[]{:T(128)}, f32[5,8192]{0,1:T(8,128)}, ...), condition=%wide.region_7.8_spmd, body=%wide.region_0.7_spmd.sunk | while | flops 721286 | bytes 4097275 | solution.py:82
  31.7 44.0 %scatter_fusion.1 = f32[4,8195]{0,1:T(8,128)} fusion(f32[4,8195]{0,1:T(8,128)} %get-tuple-element.1428, s32[8192]{0:T(1024)S(1)} %get-tuple-element.1322, f32[8192,4]{1,0:T(8,128)} %bitcast.181), kind=kCustom, calls=%fused_computation.13.clone.1 | custom fusion | flops 32768 | bytes 425984 | tf_op jit(solution)/shard_map/while/body/scatter-add | solution.py:71
  75.7 44.0 %scatter_fusion.2 = f32[4,8195]{0,1:T(8,128)} fusion(f32[4,8195]{0,1:T(8,128)} %scatter_fusion.1, s32[8192]{0:T(1024)S(1)} %get-tuple-element.1328, f32[8192,4]{1,0:T(8,128)} %bitcast.179), kind=kCustom, calls=%fused_computation.14.clone.1 | custom fusion | flops 32768 | bytes 425984 | tf_op jit(solution)/shard_map/while/body/scatter-add | solution.py:71
  119.6 44.0 %scatter_fusion.3 = f32[4,8195]{0,1:T(8,128)} fusion(f32[4,8195]{0,1:T(8,128)} %scatter_fusion.2, s32[8192]{0:T(1024)S(1)} %get-tuple-element.1330, f32[8192,4]{1,0:T(8,128)} %bitcast.177), kind=kCustom, calls=%fused_computation.15.clone.1 | custom fusion | flops 32768 | bytes 425984 | tf_op jit(solution)/shard_map/while/body/scatter-add | solution.py:71
  163.6 44.0 %scatter_fusion.4 = f32[4,8195]{0,1:T(8,128)} fusion(f32[4,8195]{0,1:T(8,128)} %scatter_fusion.3, s32[8192]{0:T(1024)S(1)} %get-tuple-element.1332, f32[8192,4]{1,0:T(8,128)} %bitcast.175), kind=kCustom, calls=%fused_computation.16.clone.1 | custom fusion | flops 32768 | bytes 425984 | tf_op jit(solution)/shard_map/while/body/scatter-add | solution.py:71
  211.7 44.0 %scatter_fusion = f32[5,8192]{0,1:T(8,128)} fusion(f32[5,8192]{0,1:T(8,128)} %get-tuple-element.1427, s32[8192]{0:T(1024)S(1)} %get-tuple-element.1320, f32[8192,5]{1,0:T(8,128)} %bitcast.171), kind=kCustom, calls=%fused_computation.12.clone.1 | custom fusion | flops 40960 | bytes 524288 | tf_op jit(solution)/shard_map/while/body/scatter-add | solution.py:69
  268.4 266.1 %all-reduce.8.cloned.1.call-done = f32[5,8192]{1,0:T(8,128)} async-done(((f32[5,8192]{1,0:T(8,128)}), f32[5,8192]{1,0:T(8,128)}) %all-reduce.8.cloned.1.call-update) | async-done | bytes 163856 | tf_op jit(solution)/shard_map/psum | solution.py:86
  540.2 69.5 %all-reduce.14.cloned.1.call-done = (f32[4,8192]{1,0:T(4,128)}, f32[256,128]{1,0:T(8,128)}) async-done(((f32[4,8192]{1,0:T(4,128)}, f32[256,128]{1,0:T(8,128)}), (f32[4,8192]{1,0:T(4,128)}, f32[256,128]{1,0:T(8,128)})) %all-reduce.14.cloned.1.call-update) | async-done | bytes 262160 | tf_op jit(solution)/shard_map/psum | solution.py:85
  618.8 165.7 %while.59 = (s32[]{:T(128)}, f32[128,128]{1,0:T(8,128)S(1)}, s32[]{:T(128)}, f32[5,128,128]{0,2,1:T(8,128)}, s32[128,128]{1,0:T(8,128)S(1)}, /*index=5*/f32[5,81...) while((s32[]{:T(128)}, f32[128,128]{1,0:T(8,128)S(1)}, ...), condition=%wide.region_22.23_spmd, body=%wide.region_16.22_spmd.sunk | while | flops 738694 | bytes 3282927 | solution.py:124
  649.0 30.1 %gather_fusion.1 = f32[8192,4]{1,0:T(8,128)} fusion(f32[4,8195]{0,1:T(8,128)} %get-tuple-element.1507, s32[8192]{0:T(1024)S(1)} %get-tuple-element.1349), kind=kCustom, calls=%fused_computation.2.clone.1 | custom fusion | bytes 294912 | tf_op jit(solution)/shard_map/while/body/gather | solution.py:119
  709.1 30.0 %gather_fusion.3 = f32[8192,4]{1,0:T(8,128)} fusion(f32[4,8195]{0,1:T(8,128)} %get-tuple-element.1507, s32[8192]{0:T(1024)S(1)} %get-tuple-element.1351), kind=kCustom, calls=%fused_computation.1.clone.1 | custom fusion | bytes 294912 | tf_op jit(solution)/shard_map/while/body/gather | solution.py:119
  788.9 234.2 %while.60 = (s32[]{:T(128)}, f32[5,8192]{0,1:T(8,128)}, f32[4,8195]{0,1:T(8,128)}, f32[256,128]{1,0:T(8,128)S(1)}, s32[]{:T(128)}, /*index=5*/s32[128,128]{1,0:T...) while((s32[]{:T(128)}, f32[5,8192]{0,1:T(8,128)}, ...), condition=%wide.region_32.33_spmd, body=%wide.region_25.32_spmd.sunk | while | flops 721286 | bytes 4097275 | solution.py:82
  797.7 44.0 %scatter_fusion.6 = f32[4,8195]{0,1:T(8,128)} fusion(f32[4,8195]{0,1:T(8,128)} %get-tuple-element.1536, s32[8192]{0:T(1024)S(1)} %get-tuple-element.1373, f32[8192,4]{1,0:T(8,128)} %bitcast.182), kind=kCustom, calls=%fused_computation.19.clone.1 | custom fusion | flops 32768 | bytes 425984 | tf_op jit(solution)/shard_map/while/body/scatter-add | solution.py:71
  841.7 44.0 %scatter_fusion.7 = f32[4,8195]{0,1:T(8,128)} fusion(f32[4,8195]{0,1:T(8,128)} %scatter_fusion.6, s32[8192]{0:T(1024)S(1)} %get-tuple-element.1379, f32[8192,4]{1,0:T(8,128)} %bitcast.180), kind=kCustom, calls=%fused_computation.20.clone.1 | custom fusion | flops 32768 | bytes 425984 | tf_op jit(solution)/shard_map/while/body/scatter-add | solution.py:71
  885.7 44.0 %scatter_fusion.8 = f32[4,8195]{0,1:T(8,128)} fusion(f32[4,8195]{0,1:T(8,128)} %scatter_fusion.7, s32[8192]{0:T(1024)S(1)} %get-tuple-element.1381, f32[8192,4]{1,0:T(8,128)} %bitcast.178), kind=kCustom, calls=%fused_computation.21.clone.1 | custom fusion | flops 32768 | bytes 425984 | tf_op jit(solution)/shard_map/while/body/scatter-add | solution.py:71
  929.6 44.0 %scatter_fusion.9 = f32[4,8195]{0,1:T(8,128)} fusion(f32[4,8195]{0,1:T(8,128)} %scatter_fusion.8, s32[8192]{0:T(1024)S(1)} %get-tuple-element.1383, f32[8192,4]{1,0:T(8,128)} %bitcast.176), kind=kCustom, calls=%fused_computation.22.clone.1 | custom fusion | flops 32768 | bytes 425984 | tf_op jit(solution)/shard_map/while/body/scatter-add | solution.py:71
  977.8 44.0 %scatter_fusion.5 = f32[5,8192]{0,1:T(8,128)} fusion(f32[5,8192]{0,1:T(8,128)} %get-tuple-element.1535, s32[8192]{0:T(1024)S(1)} %get-tuple-element.1371, f32[8192,5]{1,0:T(8,128)} %bitcast.172), kind=kCustom, calls=%fused_computation.18.clone.1 | custom fusion | flops 40960 | bytes 524288 | tf_op jit(solution)/shard_map/while/body/scatter-add | solution.py:69
  1037.6 437.8 %all-reduce = (f32[]{:T(128)}, f32[]{:T(128)}) all-reduce(f32[]{:T(128)S(6)} %add.667, f32[]{:T(128)} %multiply_reduce_fusion.17), channel_id=1, replica_groups=mesh['stars'=8,'seg'=4] {'stars','seg'}, use_global_device_ids=true, to_apply=%region_15.16 | all-reduce | flops 2 | bytes 16 | tf_op jit(solution)/shard_map/psum | solution.py:90
  1479.0 59.4 %all-reduce.12.cloned.1.call-done = (f32[4,8192]{1,0:T(4,128)}, f32[256,128]{1,0:T(8,128)}) async-done(((f32[4,8192]{1,0:T(4,128)}, f32[256,128]{1,0:T(8,128)}), (f32[4,8192]{1,0:T(4,128)}, f32[256,128]{1,0:T(8,128)})) %all-reduce.12.cloned.1.call-update) | async-done | bytes 262160 | tf_op jit(solution)/shard_map/psum | solution.py:85
  1542.8 39.6 %psum.78 = f32[]{:T(128)} all-reduce(f32[]{:T(128)S(6)} %add.670), channel_id=1, replica_groups=mesh['stars'=8,'seg'=4] {'stars','seg'}, use_global_device_ids=true, to_apply=%region_39.40 | all-reduce | flops 1 | bytes 8 | tf_op jit(solution)/shard_map/psum | solution.py:90
  1593.5 165.7 %while.61 = (s32[]{:T(128)}, f32[128,128]{1,0:T(8,128)S(1)}, s32[]{:T(128)}, f32[5,128,128]{0,2,1:T(8,128)}, s32[128,128]{1,0:T(8,128)S(1)}, /*index=5*/f32[5,81...) while((s32[]{:T(128)}, f32[128,128]{1,0:T(8,128)S(1)}, ...), condition=%wide.region_46.47_spmd, body=%wide.region_40.46_spmd.sunk | while | flops 738694 | bytes 3282927 | solution.py:124
  1623.6 30.1 %gather_fusion.7 = f32[8192,4]{1,0:T(8,128)} fusion(f32[4,8195]{0,1:T(8,128)} %get-tuple-element.1615, s32[8192]{0:T(1024)S(1)} %get-tuple-element.1400), kind=kCustom, calls=%fused_computation.8.clone.1 | custom fusion | bytes 294912 | tf_op jit(solution)/shard_map/while/body/gather | solution.py:119
  1683.8 30.0 %gather_fusion.9 = f32[8192,4]{1,0:T(8,128)} fusion(f32[4,8195]{0,1:T(8,128)} %get-tuple-element.1615, s32[8192]{0:T(1024)S(1)} %get-tuple-element.1402), kind=kCustom, calls=%fused_computation.7.clone.1 | custom fusion | bytes 294912 | tf_op jit(solution)/shard_map/while/body/gather | solution.py:119
  1759.8 206.3 %psum.79 = f32[]{:T(128)} all-reduce(f32[]{:T(128)} %multiply_reduce_fusion.16), channel_id=1, replica_groups=mesh['stars'=8,'seg'=4] {'stars','seg'}, use_global_device_ids=true, to_apply=%region_48.49 | all-reduce | flops 1 | bytes 8 | tf_op jit(solution)/shard_map/psum | solution.py:90
  (137 shorter events, 314.9 us)
Async XLA Ops:
  7.2 527.3 %all-reduce.8.cloned.1.call-start = ((), (), s32[]{:S(2)}) async-start(), calls=%async_computation | async-start | bytes 524288 | tf_op jit(solution)/shard_map/psum | solution.py:86
  7.9 5.9 copy-start.11
  13.8 4.7 copy-start.12
  18.5 4.5 copy-start.14
  18.6 4.4 copy-start.1
  18.6 4.4 copy-start.2
  18.6 4.4 copy-start.3
  18.6 4.4 copy-start.5
  18.6 4.4 copy-start.16
  256.9 9.0 copy-start.8
  260.1 6.7 collective-permute-start
  266.0 343.7 %all-reduce.14.cloned.1.call-start = ((), (), s32[]{:S(2)}) async-start(), calls=%async_computation.3 | async-start | bytes 524288 | tf_op jit(solution)/shard_map/psum | solution.py:85
  267.6 0.7 copy-start.10
  268.3 1208.4 %all-reduce.10.cloned.1.call-start = ((), (), s32[]{:S(2)}) async-start(), calls=%async_computation.1 | async-start | bytes 524288 | tf_op jit(solution)/shard_map/psum | solution.py:86
  609.7 9.1 copy-start
  612.0 3.0 collective-permute-start.1
  1023.1 10.5 copy-start.9
  1023.1 453.7 %copy-start.4 = (f32[5,8192]{1,0:T(8,128)S(1)}, f32[5,8192]{1,0:T(8,128)}, u32[]{:S(2)}) copy-start(f32[5,8192]{1,0:T(8,128)} %all-reduce.8.cloned.1.call-done) | copy-start | bytes 491524
  1026.2 513.7 %copy-start.6 = (f32[4,8192]{1,0:T(4,128)S(1)}, f32[4,8192]{1,0:T(4,128)}, u32[]{:S(2)}) copy-start(f32[4,8192]{1,0:T(4,128)} %get-tuple-element.932) | copy-start | bytes 393220
  1026.3 7.3 collective-permute-start.2
  1033.6 504.8 %all-reduce.12.cloned.1.call-start = ((), (), s32[]{:S(2)}) async-start(), calls=%async_computation.2 | async-start | bytes 524288 | tf_op jit(solution)/shard_map/psum | solution.py:85
  1585.6 5.0 collective-permute-start.3
  1593.5 374.0 %copy-start.13 = (f32[128,128]{1,0:T(8,128)S(1)}, f32[128,128]{1,0:T(8,128)}, u32[]{:S(2)}) copy-start(f32[128,128]{1,0:T(8,128)} %param.29) | copy-start | bytes 196612
  1593.5 374.0 %copy-start.15 = (f32[128]{0:T(128)S(1)}, f32[128]{0:T(128)}, u32[]{:S(2)}) copy-start(f32[128]{0:T(128)} %copy-done.14) | copy-start | bytes 1540
  (1 other events, 0.7 us)
Sparse Core Ops, SparseCore 0:
  266.1 268.2 all-reduce.7
  538.9 70.7 all-reduce.13
  1033.7 429.6 all-reduce.9
  1467.7 70.6 all-reduce.11
where the time goes:
time: 1990 us; the launch traced here: 1980 us
  blocking collectives  684 us (34%)
  other arithmetic  516 us (26%)
  waiting for transfers between devices  397 us (20%)
  local copies, waits for them, and re-layouts  349 us (18%)
  between operations  22.9 us (1%)
    psum x3, blocking collectives, total(): return lax.psum(local_value, ('stars', 'seg'))  684 us
    scatter-add x8, other arithmetic, gradient_one_turn(): att_grad.at[:, knot_ids + offset].add(att_rows * (weights[offset] * masked))  352 us
    psum x2, waiting for transfers between devices, gradient(): star_sum = lax.psum(star_grad, 'seg')  266 us
    gather x8, local copies, waits for them, and re-layouts, forward_one_turn(): extended[:, knot_ids + offset]  240 us
    psum x2, waiting for transfers between devices, gradient(): att_sum, cal_sum = lax.psum((att_grad, cal_grad), 'stars')  129 us
    scatter-add x2, other arithmetic, gradient_one_turn(): star_grad = star_grad.at[:, star_ids].add(star_rows * masked)  88 us
    gather x2, local copies, waits for them, and re-layouts, forward_one_turn(): row_values = jnp.sum(star_rows * star_x[:, star_ids], axis=0)  60.1 us
  transfers between devices with their start and end apart: 8, of which 4 were waited for; matrix products, arithmetic and copies ran while one was open for 1% of the time, Pallas kernels for 0%

commit v1 on v0

v1 whole, which is shorter than its diff:
```python
import functools

import jax
import jax.numpy as jnp
from jax import lax
from jax.experimental import pallas as pl
from jax.experimental.pallas import tpu as pltpu
from jax.sharding import PartitionSpec as P

STAR_DEV = 8192
KNOT_DEV = 8192
CALB_DEV = 256
FINE = 32
COARSE = 256
GROUP = 8
STAR_ROWS = 5 * FINE
KNOT_ROWS = 4 * FINE
TABLE_ROWS = KNOT_ROWS + CALB_DEV // 2
BF16 = jnp.bfloat16
F32 = jnp.float32
SCALAR_LANE = 64


def two_parts(values):
    high = values.astype(BF16)
    return high, (values - high.astype(F32)).astype(BF16)


def rows_and_columns(shape):
    return lax.broadcasted_iota(jnp.int32, shape, 0), lax.broadcasted_iota(jnp.int32, shape, 1)


def one_hot(index_row, size):
    rows, _ = rows_and_columns((size, index_row.shape[1]))
    return jnp.where(rows == index_row, 1.0, 0.0).astype(BF16)


def spline_weights(fraction):
    remain = 1.0 - fraction
    square = fraction * fraction
    cubed = square * fraction
    return (
        remain * remain * remain / 6.0,
        (3.0 * cubed - 6.0 * square + 4.0) / 6.0,
        (-3.0 * cubed + 3.0 * square + 3.0 * fraction + 1.0) / 6.0,
        cubed / 6.0,
    )


def weight_columns(weights, fine, tile):
    rows, _ = rows_and_columns((FINE + 8, weights[0].shape[1]))
    behind = rows - fine[tile : tile + 1]
    result = jnp.zeros(behind.shape, F32)
    for offset in range(4):
        result = jnp.where(behind == offset, weights[offset][tile : tile + 1], result)
    return result


def product(left, right, contract):
    return lax.dot_general(left, right, (contract, ((), ())), preferred_element_type=F32)


def live_mask(live_ref, first, shape):
    rows, _ = rows_and_columns(shape)
    return (rows + first < live_ref[0]).astype(F32)


def backward_kernel(
    live_ref, star_ref, knot_ref, frac_ref, star_coef_ref, att_coef_ref, cal_coef_ref, tile_cal_ref,
    value_ref, scalar_ref, star_out, table_out, edge_out, star_acc, knot_acc,
):
    star_acc[...] = jnp.zeros_like(star_acc)
    knot_acc[...] = jnp.zeros_like(knot_acc)

    @pl.loop(0, star_ref.shape[0] // GROUP)
    def _(group):
        first = pl.multiple_of(group * GROUP, GROUP)
        rows = pl.ds(first, GROUP)
        star, knot = star_ref[rows, :], knot_ref[rows, :]
        values = value_ref[rows, :]
        values = values * live_mask(live_ref, first, values.shape)
        star_coarse, star_fine = star & (COARSE - 1), star >> 8
        knot_coarse, knot_fine = knot >> 5, knot & (FINE - 1)
        weights = spline_weights(frac_ref[rows, :])
        star_terms = [star_coef_ref[comp, rows, :] * values for comp in range(5)]
        knot_terms = [att_coef_ref[comp, rows, :] * values for comp in range(4)]
        star_parts = [two_parts(term) for term in star_terms]
        star_parts = [parts[half].astype(F32) for half in range(2) for parts in star_parts]
        star_left, star_right, knot_left, knot_right = [], [], [], []
        fine_rows, _ = rows_and_columns((FINE, star.shape[1]))
        for tile in range(GROUP):
            here = slice(tile, tile + 1)
            star_right.append(one_hot(star_coarse[here], COARSE))
            knot_right.append(one_hot(knot_coarse[here], COARSE))
            chosen = fine_rows == star_fine[here]
            star_left.append(
                jnp.concatenate(
                    [jnp.where(chosen, part[here], 0.0) for part in star_parts], axis=0
                ).astype(BF16)
            )
            columns = weight_columns(weights, knot_fine, tile)
            spread = jnp.concatenate(
                [term[here] * columns[:FINE] for term in knot_terms]
                + [term[here] * columns[FINE:] for term in knot_terms],
                axis=0,
            )
            knot_left.append(jnp.concatenate(two_parts(spread), axis=0))
        star_acc[...] += product(
            jnp.concatenate(star_left, axis=1), jnp.concatenate(star_right, axis=1), ((1,), (1,))
        )
        knot_acc[...] += product(
            jnp.concatenate(knot_left, axis=1), jnp.concatenate(knot_right, axis=1), ((1,), (1,))
        )

    star_out[...] = star_acc[:STAR_ROWS] + star_acc[STAR_ROWS:]

    half = KNOT_ROWS + 32
    lane = lax.broadcasted_iota(jnp.int32, (8, 128), 1)
    row = lax.broadcasted_iota(jnp.int32, (8, 128), 0)
    wide_lane = lax.broadcasted_iota(jnp.int32, (8, COARSE), 1)
    edges = scalar_ref[...]
    for comp in range(4):
        main = knot_acc[comp * FINE : (comp + 1) * FINE] + knot_acc[half + comp * FINE : half + (comp + 1) * FINE]
        past = KNOT_ROWS + comp * 8
        beyond = knot_acc[past : past + 8] + knot_acc[half + past : half + past + 8]
        moved = pltpu.roll(beyond, 1, 1)
        top = main[:8] + jnp.where(wide_lane > 0, moved, 0.0)
        table_out[comp * FINE : comp * FINE + 8, :] = top
        table_out[comp * FINE + 8 : (comp + 1) * FINE, :] = main[8:]
        tail, head = moved[:, :128], top[:, :128]
        if comp:
            tail = pltpu.roll(tail, 2 * comp, 1)
        head = pltpu.roll(head, 2 * comp + 1, 1)
        edges = jnp.where((lane == 2 * comp) & (row < 3), tail, edges)
        edges = jnp.where((lane == 2 * comp + 1) & (row < 3), head, edges)
    edge_out[...] = edges

    values = value_ref[...]
    values = values * live_mask(live_ref, 0, values.shape) * cal_coef_ref[...]
    blocks = product(
        one_hot(tile_cal_ref[...], CALB_DEV), jnp.concatenate(two_parts(values), axis=1), ((1,), (0,))
    )
    width = values.shape[1]
    blocks = blocks[:, :width] + blocks[:, width:]
    table_out[KNOT_ROWS:, :] = jnp.concatenate(
        [blocks[: CALB_DEV // 2], blocks[CALB_DEV // 2 :]], axis=1
    )


def forward_kernel(
    n_stars, n_seg, later, live_ref, place_ref, star_ref, knot_ref, frac_ref, star_coef_ref,
    att_coef_ref, cal_coef_ref, tile_cal_ref, other_ref, star_x_ref, table_x_ref, edges_ref, *refs,
):
    if later:
        star_0_ref, table_0_ref, ahead_0_ref, image_ref, star_out, table_out, scalar_out = refs[:7]
    else:
        image_ref, table_out, ahead_out, scalar_out = refs[:4]
    star_parts_ref, knot_parts_ref, cal_ref = refs[-3:]
    segment = place_ref[0]
    lane = lax.broadcasted_iota(jnp.int32, (8, 128), 1)
    row = lax.broadcasted_iota(jnp.int32, (8, 128), 0)
    wide_lane = lax.broadcasted_iota(jnp.int32, (8, COARSE), 1)

    before, own, after, everyone = [jnp.zeros((8, 128), F32) for _ in range(4)]
    for block in range(n_stars):
        start = block * n_seg
        before += edges_ref[start + jnp.maximum(segment - 1, 0)]
        own += edges_ref[start + segment]
        after += edges_ref[start + jnp.minimum(segment + 1, n_seg - 1)]
        if later:
            for other in range(n_seg):
                everyone += edges_ref[start + other]
    before = jnp.where(segment > 0, before, 0.0)
    ahead = jnp.where(lane % 2 == 0, own, 0.0) + pltpu.roll(jnp.where(lane % 2 == 1, after, 0.0), 127, 1)
    ahead = jnp.where((segment < n_seg - 1) & (lane < 8) & (row < 3), ahead, 0.0)

    table = table_x_ref[...]
    for comp in range(4):
        shifted = pltpu.roll(before, 128 - 2 * comp, 1) if comp else before
        shifted = jnp.where((lane == 0) & (row < 3), shifted, 0.0)
        top = table[comp * FINE : comp * FINE + 8]
        top = top + jnp.concatenate([shifted, jnp.zeros_like(shifted)], axis=1)
        table_out[comp * FINE : comp * FINE + 8, :] = top
        table_out[comp * FINE + 8 : (comp + 1) * FINE, :] = table[comp * FINE + 8 : (comp + 1) * FINE]
    table_out[KNOT_ROWS:, :] = table[KNOT_ROWS:]
    star_x = star_x_ref[...]
    if later:
        def total(which):
            return jnp.sum(jnp.where((row == 0) & (lane == SCALAR_LANE + which), everyone, 0.0), keepdims=True)

        step = total(0) / total(1)
        star_x = star_0_ref[...] - step * star_x
        star_out[...] = star_x
        table_out[...] = table_0_ref[...] - step * table_out[...]
        ahead = ahead_0_ref[...] - step * ahead
    else:
        ahead_out[...] = ahead
    table = table_out[...]
    norm = jnp.sum(star_x * star_x, keepdims=True) / n_seg + jnp.sum(table * table, keepdims=True) / n_stars

    star_high, star_low = two_parts(star_x)
    star_parts_ref[:STAR_ROWS] = star_high
    star_parts_ref[STAR_ROWS:] = star_low
    beyond = []
    for comp in range(4):
        moved = pltpu.roll(table[comp * FINE : comp * FINE + 8], COARSE - 1, 1)
        last = pltpu.roll(ahead, 127 - 2 * comp, 1)
        beyond.append(jnp.where(wide_lane == COARSE - 1, jnp.concatenate([last, last], axis=1), moved))
    knot_high, knot_low = two_parts(jnp.concatenate([table[:KNOT_ROWS]] + beyond, axis=0))
    half = KNOT_ROWS + 32
    knot_parts_ref[:half] = knot_high
    knot_parts_ref[half:] = knot_low

    blocks = jnp.concatenate([table[KNOT_ROWS:, :128], table[KNOT_ROWS:, 128:]], axis=0)
    rows = product(
        one_hot(tile_cal_ref[...], CALB_DEV), jnp.concatenate(two_parts(blocks), axis=1), ((0,), (0,))
    )
    cal_ref[...] = (rows[:, :128] + rows[:, 128:]) * cal_coef_ref[...]

    def one_group(group, sums):
        first = pl.multiple_of(group * GROUP, GROUP)
        rows = pl.ds(first, GROUP)
        star, knot = star_ref[rows, :], knot_ref[rows, :]
        star_coarse, star_fine = star & (COARSE - 1), star >> 8
        knot_coarse, knot_fine = knot >> 5, knot & (FINE - 1)
        weights = spline_weights(frac_ref[rows, :])
        star_coef = [star_coef_ref[comp, rows, :] for comp in range(5)]
        att_coef = [att_coef_ref[comp, rows, :] for comp in range(4)]
        tiles = [slice(tile, tile + 1) for tile in range(GROUP)]
        star_hot = jnp.concatenate([one_hot(star_coarse[here], COARSE) for here in tiles], axis=1)
        knot_hot = jnp.concatenate([one_hot(knot_coarse[here], COARSE) for here in tiles], axis=1)
        star_found = product(star_parts_ref[...], star_hot, ((1,), (0,)))
        knot_found = product(knot_parts_ref[...], knot_hot, ((1,), (0,)))
        width = star.shape[1]
        fine_rows, _ = rows_and_columns((FINE, width))
        image_rows = []
        for tile, here in enumerate(tiles):
            across = slice(tile * width, (tile + 1) * width)

            def star_part(comp):
                begin = comp * FINE
                return (
                    star_found[begin : begin + FINE, across]
                    + star_found[STAR_ROWS + begin : STAR_ROWS + begin + FINE, across]
                )

            def knot_part(begin, size):
                return (
                    knot_found[begin : begin + size, across]
                    + knot_found[half + begin : half + begin + size, across]
                )

            star_sum = sum(star_coef[comp][here] * star_part(comp) for comp in range(5))
            star_sum = jnp.where(fine_rows == star_fine[here], star_sum, 0.0)
            columns = weight_columns(weights, knot_fine, tile)
            main = sum(att_coef[comp][here] * knot_part(comp * FINE, FINE) for comp in range(4))
            past = sum(att_coef[comp][here] * knot_part(KNOT_ROWS + comp * 8, 8) for comp in range(4))
            both = star_sum + main * columns[:FINE]
            both = both[:8] + both[8:16] + both[16:24] + both[24:] + past * columns[FINE:]
            image_rows.append(jnp.sum(both, axis=0, keepdims=True))
        image = jnp.concatenate(image_rows, axis=0) + cal_ref[rows, :]
        image = image * live_mask(live_ref, first, image.shape)
        image_ref[rows, :] = image
        if later:
            return sums[0] + image * image, sums[1] + image * other_ref[rows, :]
        return (sums[0] + image * image,)

    zero = jnp.zeros((GROUP, star_ref.shape[1]), F32)
    sums = lax.fori_loop(0, star_ref.shape[0] // GROUP, one_group, (zero, zero) if later else (zero,))
    result = jnp.where((row == 0) & (lane == SCALAR_LANE), norm, 0.0)
    for which, part in enumerate(sums):
        result = jnp.where(
            (row == 0) & (lane == SCALAR_LANE + 1 + which), jnp.sum(part, keepdims=True), result
        )
    scalar_out[...] = result


def in_vmem(count):
    return [pl.BlockSpec(memory_space=pltpu.VMEM)] * count


def in_smem(count):
    return [pl.BlockSpec(memory_space=pltpu.SMEM)] * count


def table_shape(*shape, kind=F32):
    return jax.ShapeDtypeStruct(shape, kind)


PARAMS = pltpu.CompilerParams(vmem_limit_bytes=48 * 1024 * 1024)


def on_device(
    obs_star, obs_knot, obs_frac, star_coef, att_coef, cal_coef, tile_cal, live_tiles, obs_value
):
    n_stars, n_seg = lax.axis_size("stars"), lax.axis_size("seg")
    tile_count, width = obs_star.shape
    tile_row = tile_cal[None, :]
    place = lax.axis_index("seg").astype(jnp.int32)[None]
    observed = (obs_star, obs_knot, obs_frac, star_coef, att_coef, cal_coef, tile_row)
    half = KNOT_ROWS + 32

    def backward(values, scalars):
        return pl.pallas_call(
            backward_kernel,
            out_shape=(
                table_shape(STAR_ROWS, COARSE),
                table_shape(TABLE_ROWS, COARSE),
                table_shape(8, 128),
            ),
            in_specs=in_smem(1) + in_vmem(9),
            out_specs=tuple(in_vmem(3)),
            scratch_shapes=[
                pltpu.VMEM((2 * STAR_ROWS, COARSE), F32),
                pltpu.VMEM((2 * half, COARSE), F32),
            ],
            compiler_params=PARAMS,
            name="backward",
        )(live_tiles, *observed, values, scalars)

    def forward(later, other, *tables):
        image = table_shape(tile_count, width)
        if later:
            outs = (image, table_shape(STAR_ROWS, COARSE), table_shape(TABLE_ROWS, COARSE), table_shape(8, 128))
        else:
            outs = (image, table_shape(TABLE_ROWS, COARSE), table_shape(8, 128), table_shape(8, 128))
        return pl.pallas_call(
            functools.partial(forward_kernel, n_stars, n_seg, later),
            out_shape=outs,
            in_specs=in_smem(2) + in_vmem(8 + len(tables)),
            out_specs=tuple(in_vmem(len(outs))),
            scratch_shapes=[
                pltpu.VMEM((2 * STAR_ROWS, COARSE), BF16),
                pltpu.VMEM((2 * half, COARSE), BF16),
                pltpu.VMEM((tile_count, width), F32),
            ],
            compiler_params=PARAMS,
            name="forward",
        )(live_tiles, place, *observed, other, *tables)

    def swap(blocks, axes):
        return lax.all_to_all(blocks, axes, 0, 0)

    def all_sum(array, axis, count):
        rows, columns = array.shape
        blocks = swap(array.reshape(count, rows // count, columns), axis)
        part = jnp.sum(blocks, axis=0)
        return swap(jnp.broadcast_to(part[None], blocks.shape), axis).reshape(rows, columns)

    def everyones(array):
        count = n_stars * n_seg
        return swap(jnp.broadcast_to(array[None], (count, *array.shape)), ("stars", "seg"))

    def reduced(parts):
        star, table, edges = parts
        return all_sum(star, "seg", n_seg), all_sum(table, "stars", n_stars), everyones(edges)

    mask = (jnp.arange(tile_count, dtype=jnp.int32) < live_tiles[0]).astype(F32)[:, None]
    residual = obs_value * mask
    star_0, table_0, edges_0 = reduced(backward(obs_value, jnp.zeros((8, 128), F32)))
    image_0, table_0, ahead_0, scalars_0 = forward(False, obs_value, star_0, table_0, edges_0)
    star_h, table_h, edges_h = reduced(backward(image_0, scalars_0))
    image_1, star_1, table_1, scalars_1 = forward(
        True, image_0, star_h, table_h, edges_h, star_0, table_0, ahead_0
    )
    first = jnp.sum(edges_h[:, 0, SCALAR_LANE : SCALAR_LANE + 2], axis=0)
    second = jnp.sum(everyones(scalars_1)[:, 0, SCALAR_LANE : SCALAR_LANE + 3], axis=0)
    norm_0, square_0 = first[0], first[1]
    norm_1, square_1, cross = second[0], second[1], second[2]
    step_0 = norm_0 / square_0
    ratio = norm_1 / norm_0
    step_1 = norm_1 / (square_1 + 2.0 * ratio * cross + ratio * ratio * square_0)

    def combined(old, new):
        return (step_0 + step_1 * ratio) * old + step_1 * new

    star = combined(star_0, star_1).reshape(5, STAR_DEV)
    att = combined(table_0[:KNOT_ROWS], table_1[:KNOT_ROWS])
    att = att.reshape(4, FINE, COARSE).transpose(0, 2, 1).reshape(4, KNOT_DEV)
    cal = combined(table_0[KNOT_ROWS:], table_1[KNOT_ROWS:])
    cal = cal.reshape(CALB_DEV // 2, 2, width).transpose(1, 0, 2).reshape(CALB_DEV, width)
    return (star, att, cal, residual - combined(image_0, image_1))


def solution(mesh):
    placed = (
        P(("stars", "seg"), None),
        P(("stars", "seg"), None),
        P(("stars", "seg"), None),
        P(None, ("stars", "seg"), None),
        P(None, ("stars", "seg"), None),
        P(("stars", "seg"), None),
        P(("stars", "seg")),
        P(("stars", "seg")),
        P(("stars", "seg"), None),
    )
    return jax.shard_map(
        on_device,
        mesh=mesh,
        in_specs=placed,
        out_specs=(P(None, "stars"), P(None, "seg"), P("seg", None), P(("stars", "seg"), None)),
        check_vma=False,
    )
```

time: 1990 us -> 174 us (0.09)
  blocking collectives: 684 us -> 70 us
  other arithmetic: 516 us -> 1.08 us
  waiting for transfers between devices: 397 us -> 32.1 us
  local copies, waits for them, and re-layouts: 349 us -> 13.3 us
  Pallas kernels: 0 us -> 38.2 us
    psum x3 -> x0, blocking collectives: 684 us -> none  [total(): return lax.psum(local_value, ('stars', 'seg'))]
    scatter-add x12 -> x0, other arithmetic: 442 us -> none  [the longest x8 352 us: gradient_one_turn(): att_grad.at[:, knot_ids + offset].add(att_rows * (weights[offset] * masked))]
    psum x4 -> x0, waiting for transfers between devices: 395 us -> none  [the longest x2 266 us: gradient(): star_sum = lax.psum(star_grad, 'seg')]
    gather x12 -> x0, local copies, waits for them, and re-layouts: 302 us -> none  [the longest x8 240 us: forward_one_turn(): extended[:, knot_ids + offset]]
    all_to_all x0 -> x7, blocking collectives: none -> 70 us  [swap(): return lax.all_to_all(blocks, axes, 0, 0)]
    pallas_call x0 -> x4, Pallas kernels: none -> 38.2 us  [the longest x2 19.4 us: forward(): pl.pallas_call(functools.partial(forward_kernel, n_stars, n_seg, later),...]
    reduce_sum x12 -> x6, other arithmetic: 37.7 us -> 0.3 us  [the longest x1 0.12 us: on_device(): first = jnp.sum(edges_h[:, 0, SCALAR_LANE:SCALAR_LANE + 2], axis=0)]
    while x10 -> x0, local copies, waits for them, and re-layouts: 35.8 us -> none  [the longest x6 23.9 us: gradient(): lax.fori_loop(0, turn_count, gradient_one_turn, start_carry)]
  transfers between devices with their start and end apart: 8 -> 4, of which waited for: 4 -> 4; matrix products, arithmetic and copies ran while one was open for 1% -> 0% of each run, Pallas kernels for 0% -> 0%
where the time goes in v1:
time: 174 us; the launch traced here: 173 us
  blocking collectives  70 us (40%)
  Pallas kernels  38.2 us (22%)
  waiting for transfers between devices  32.1 us (18%)
  local copies, waits for them, and re-layouts  13.3 us (8%)
  starting transfers between devices  11.6 us (7%)
  between operations  6.76 us (4%)
    all_to_all x7, blocking collectives, swap(): return lax.all_to_all(blocks, axes, 0, 0)  70 us
    all_to_all x4, waiting for transfers between devices, swap(): return lax.all_to_all(blocks, axes, 0, 0)  32.1 us
    pallas_call x2, Pallas kernels, forward(): pl.pallas_call(functools.partial(forward_kernel, n_stars, n_seg, later),...  19.4 us
    pallas_call x2, Pallas kernels, backward(): pl.pallas_call(backward_kernel, out_shape=(table_shape(STAR_ROWS, COARSE)...  18.8 us
    all_to_all x4, starting transfers between devices, swap(): return lax.all_to_all(blocks, axes, 0, 0)  11.6 us
    unnamed x30, local copies, waits for them, and re-layouts  6.79 us
  transfers between devices with their start and end apart: 4, of which 4 were waited for; matrix products, arithmetic and copies ran while one was open for 0% of the time, Pallas kernels for 0%

profile of v1, /device:TPU:0, one launch (start us, length us, event | category | flops | bytes accessed | tf_op | source)
XLA Modules:
  0.0 173.0 jit_solution(9107571570417310780)
XLA Ops:
  1.9 1.0 copy-done
  2.9 0.9 copy-done.2
  3.9 0.8 copy-done.4
  4.7 0.8 copy-done.6
  8.1 9.4 %backward.2 = (f32[160,256]{1,0:T(8,128)S(1)}, f32[256,256]{1,0:T(8,128)S(1)}, f32[8,128]{1,0:T(8,128)S(1)}) custom-call(s32[1]{0:T(128)} %copy.27.live_ref, s32[128,128]{1,0:T(8,128)S(1)} %copy-done.4, s32[128,128]{1,0:T(8,128)S(1)} %copy-done.6, f32[128,128]{1,0:T(8,128)S(1)} %copy-done.8, f32[5,128,128]{2,1,0:T(8,128)S(1)} %copy-done, ...), custom_call_target="tpu_custom_call" | custom-call | tf_op jit(solution)/shard_map/backward/pallas_call | solution.py:304
  17.5 9.0 %all_to_all.55 = f32[4,40,256]{2,1,0:T(8,128)S(1)} all-to-all(f32[4,40,256]{2,1,0:T(8,128)S(1)} %bitcast.29), channel_id=1, replica_groups=mesh['stars'=8,'seg'=4] {'seg'}, dimensions={0} | all-to-all | bytes 327680 | tf_op jit(solution)/shard_map/all_to_all | solution.py:342
  26.5 7.3 %all_to_all.56 = f32[4,40,256]{2,1,0:T(8,128)S(1)} all-to-all(f32[4,40,256]{2,1,0:T(8,128)S(1)} %broadcast_in_dim.23), channel_id=1, replica_groups=mesh['stars'=8,'seg'=4] {'seg'}, dimensions={0} | all-to-all | bytes 327680 | tf_op jit(solution)/shard_map/all_to_all | solution.py:342
  33.9 14.6 %all_to_all.57 = f32[8,32,256]{2,1,0:T(8,128)S(1)} all-to-all(f32[8,32,256]{2,1,0:T(8,128)S(1)} %bitcast.27), channel_id=1, replica_groups=mesh['stars'=8,'seg'=4] {'stars'}, dimensions={0} | all-to-all | bytes 524288 | tf_op jit(solution)/shard_map/all_to_all | solution.py:342
  49.1 2.7 %all-to-all-start.4 = ((f32[32,8,128]{2,1,0:T(8,128)}), f32[32,8,128]{2,1,0:T(8,128)S(1)}, u32[]{:S(2)}, u32[]{:S(2)}) async-start(f32[32,8,128]{2,1,0:T(8,128)} %broadcast_in_dim.25), calls=%async_computation.4 | async-start | bytes 262144 | tf_op jit(solution)/shard_map/all_to_all | solution.py:342
  51.9 8.2 %all-to-all-done.4.edges_ref = f32[32,8,128]{2,1,0:T(8,128)S(1)} async-done(((f32[32,8,128]{2,1,0:T(8,128)}), f32[32,8,128]{2,1,0:T(8,128)S(1)}, u32[]{:S(2)}, u32[]{:S(2)}) %all-to-all-start.4) | async-done | bytes 131104 | tf_op jit(solution)/shard_map/all_to_all | solution.py:342
  60.8 3.6 %all-to-all-start.3 = ((f32[8,32,256]{2,1,0:T(8,128)}), f32[8,32,256]{2,1,0:T(8,128)S(1)}, u32[]{:S(2)}, u32[]{:S(2)}) async-start(f32[8,32,256]{2,1,0:T(8,128)} %broadcast_in_dim.24), calls=%async_computation.3 | async-start | bytes 524288 | tf_op jit(solution)/shard_map/all_to_all | solution.py:342
  64.3 9.5 %all-to-all-done.3 = f32[8,32,256]{2,1,0:T(8,128)S(1)} async-done(((f32[8,32,256]{2,1,0:T(8,128)}), f32[8,32,256]{2,1,0:T(8,128)S(1)}, u32[]{:S(2)}, u32[]{:S(2)}) %all-to-all-start.3) | async-done | bytes 262176 | tf_op jit(solution)/shard_map/all_to_all | solution.py:342
  73.9 9.7 %forward.2 = (f32[128,128]{1,0:T(8,128)S(1)}, f32[256,256]{1,0:T(8,128)S(1)}, f32[8,128]{1,0:T(8,128)S(1)}, f32[8,128]{1,0:T(8,128)S(1)}) custom-call(s32[1]{0:T(128)} %copy.27.live_ref, s32[1]{0:T(128)} %bitcast.1.place_ref, s32[128,128]{1,0:T(8,128)S(1)} %copy-done.5, s32[128,128]{1,0:T(8,128)S(1)} %copy-done.7, f32[128,128]{1,0:T(8,128)S(1)} %copy-done.9, ...), custom_call_target="tpu_custom_call" | custom-call | tf_op jit(solution)/shard_map/forward/pallas_call | solution.py:327
  83.6 9.4 %backward.3 = (f32[160,256]{1,0:T(8,128)S(1)}, f32[256,256]{1,0:T(8,128)S(1)}, f32[8,128]{1,0:T(8,128)S(1)}) custom-call(s32[1]{0:T(128)} %copy.27.live_ref, s32[128,128]{1,0:T(8,128)S(1)} %copy-done.5, s32[128,128]{1,0:T(8,128)S(1)} %copy-done.7, f32[128,128]{1,0:T(8,128)S(1)} %copy-done.9, f32[5,128,128]{2,1,0:T(8,128)S(1)} %copy-done.1, ...), custom_call_target="tpu_custom_call" | custom-call | tf_op jit(solution)/shard_map/backward/pallas_call | solution.py:304
  93.0 7.3 %all_to_all.58 = f32[4,40,256]{2,1,0:T(8,128)S(1)} all-to-all(f32[4,40,256]{2,1,0:T(8,128)S(1)} %bitcast.30), channel_id=1, replica_groups=mesh['stars'=8,'seg'=4] {'seg'}, dimensions={0} | all-to-all | bytes 327680 | tf_op jit(solution)/shard_map/all_to_all | solution.py:342
  100.4 7.3 %all_to_all.59 = f32[4,40,256]{2,1,0:T(8,128)S(1)} all-to-all(f32[4,40,256]{2,1,0:T(8,128)S(1)} %broadcast_in_dim.27), channel_id=1, replica_groups=mesh['stars'=8,'seg'=4] {'seg'}, dimensions={0} | all-to-all | bytes 327680 | tf_op jit(solution)/shard_map/all_to_all | solution.py:342
  107.7 12.4 %all_to_all.60 = f32[8,32,256]{2,1,0:T(8,128)S(1)} all-to-all(f32[8,32,256]{2,1,0:T(8,128)S(1)} %bitcast.28), channel_id=1, replica_groups=mesh['stars'=8,'seg'=4] {'stars'}, dimensions={0} | all-to-all | bytes 524288 | tf_op jit(solution)/shard_map/all_to_all | solution.py:342
  120.7 2.7 %all-to-all-start.5 = ((f32[32,8,128]{2,1,0:T(8,128)}), f32[32,8,128]{2,1,0:T(8,128)S(1)}, u32[]{:S(2)}, u32[]{:S(2)}) async-start(f32[32,8,128]{2,1,0:T(8,128)} %broadcast_in_dim.26), calls=%async_computation.5 | async-start | bytes 262144 | tf_op jit(solution)/shard_map/all_to_all | solution.py:342
  123.4 8.2 %all-to-all-done.5.edges_ref = f32[32,8,128]{2,1,0:T(8,128)S(1)} async-done(((f32[32,8,128]{2,1,0:T(8,128)}), f32[32,8,128]{2,1,0:T(8,128)S(1)}, u32[]{:S(2)}, u32[]{:S(2)}) %all-to-all-start.5) | async-done | bytes 131104 | tf_op jit(solution)/shard_map/all_to_all | solution.py:342
  131.7 12.0 %all_to_all.61 = f32[8,32,256]{2,1,0:T(8,128)S(1)} all-to-all(f32[8,32,256]{2,1,0:T(8,128)S(1)} %broadcast_in_dim.28), channel_id=1, replica_groups=mesh['stars'=8,'seg'=4] {'stars'}, dimensions={0} | all-to-all | bytes 524288 | tf_op jit(solution)/shard_map/all_to_all | solution.py:342
  143.7 9.7 %forward.3 = (f32[128,128]{1,0:T(8,128)S(1)}, f32[160,256]{1,0:T(8,128)S(1)}, f32[256,256]{1,0:T(8,128)S(1)}, f32[8,128]{1,0:T(8,128)S(1)}) custom-call(s32[1]{0:T(128)} %copy.27.live_ref, s32[1]{0:T(128)} %bitcast.1.place_ref, s32[128,128]{1,0:T(8,128)S(1)} %copy-done.5, s32[128,128]{1,0:T(8,128)S(1)} %copy-done.7, f32[128,128]{1,0:T(8,128)S(1)} %copy-done.9, ...), custom_call_target="tpu_custom_call" | custom-call | tf_op jit(solution)/shard_map/forward/pallas_call | solution.py:327
  154.0 2.7 %all-to-all-start.10 = ((f32[32,8,128]{2,1,0:T(8,128)}), f32[32,8,128]{2,1,0:T(8,128)S(1)}, u32[]{:S(2)}, u32[]{:S(2)}) async-start(f32[32,8,128]{2,1,0:T(8,128)} %broadcast_in_dim.29), calls=%async_computation.10 | async-start | bytes 262144 | tf_op jit(solution)/shard_map/all_to_all | solution.py:342
  158.7 6.2 %all-to-all-done.10 = f32[32,8,128]{2,1,0:T(8,128)S(1)} async-done(((f32[32,8,128]{2,1,0:T(8,128)}), f32[32,8,128]{2,1,0:T(8,128)S(1)}, u32[]{:S(2)}, u32[]{:S(2)}) %all-to-all-start.10) | async-done | bytes 131104 | tf_op jit(solution)/shard_map/all_to_all | solution.py:342
  169.8 0.9 reshape.69
  (50 shorter events, 9.9 us)
Async XLA Ops:
  1.3 0.7 copy-start.14
  1.9 1.0 copy-start
  2.9 0.9 copy-start.2
  3.9 0.8 copy-start.4
  4.7 0.8 copy-start.6
  5.5 0.8 copy-start.8
  6.4 0.8 copy-start.10
  7.2 0.8 copy-start.12
  49.1 10.9 %all-to-all-start.4 = ((f32[32,8,128]{2,1,0:T(8,128)}), f32[32,8,128]{2,1,0:T(8,128)S(1)}, u32[]{:S(2)}, u32[]{:S(2)}) async-start(f32[32,8,128]{2,1,0:T(8,128)} %broadcast_in_dim.25), calls=%async_computation.4 | async-start | bytes 262144 | tf_op jit(solution)/shard_map/all_to_all | solution.py:342
  51.8 22.0 %copy-start.11 = (f32[128,128]{1,0:T(8,128)S(1)}, f32[128,128]{1,0:T(8,128)}, u32[]{:S(2)}) copy-start(f32[128,128]{1,0:T(8,128)} %cal_coef_ref.7) | copy-start | bytes 196612
  51.8 22.0 %copy-start.13 = (f32[128,128]{1,0:T(8,128)S(1)}, f32[128,128]{1,0:T(8,128)}, u32[]{:S(2)}) copy-start(f32[128,128]{1,0:T(8,128)} %other_ref.1) | copy-start | bytes 196612
  60.0 13.8 %copy-start.3 = (f32[4,128,128]{2,1,0:T(8,128)S(1)}, f32[4,128,128]{2,1,0:T(8,128)}, u32[]{:S(2)}) copy-start(f32[4,128,128]{2,1,0:T(8,128)} %att_coef_ref.7) | copy-start | bytes 786436
  60.8 13.1 %copy-start.1 = (f32[5,128,128]{2,1,0:T(8,128)S(1)}, f32[5,128,128]{2,1,0:T(8,128)}, u32[]{:S(2)}) copy-start(f32[5,128,128]{2,1,0:T(8,128)} %star_coef_ref.7) | copy-start | bytes 983044
  60.8 13.1 %copy-start.5 = (s32[128,128]{1,0:T(8,128)S(1)}, s32[128,128]{1,0:T(8,128)}, u32[]{:S(2)}) copy-start(s32[128,128]{1,0:T(8,128)} %star_ref.7) | copy-start | bytes 196612
  60.8 13.1 %copy-start.7 = (s32[128,128]{1,0:T(8,128)S(1)}, s32[128,128]{1,0:T(8,128)}, u32[]{:S(2)}) copy-start(s32[128,128]{1,0:T(8,128)} %knot_ref.7) | copy-start | bytes 196612
  60.8 13.1 %copy-start.9 = (f32[128,128]{1,0:T(8,128)S(1)}, f32[128,128]{1,0:T(8,128)}, u32[]{:S(2)}) copy-start(f32[128,128]{1,0:T(8,128)} %frac_ref.7) | copy-start | bytes 196612
  60.8 13.1 %all-to-all-start.3 = ((f32[8,32,256]{2,1,0:T(8,128)}), f32[8,32,256]{2,1,0:T(8,128)S(1)}, u32[]{:S(2)}, u32[]{:S(2)}) async-start(f32[8,32,256]{2,1,0:T(8,128)} %broadcast_in_dim.24), calls=%async_computation.3 | async-start | bytes 524288 | tf_op jit(solution)/shard_map/all_to_all | solution.py:342
  120.7 10.9 %all-to-all-start.5 = ((f32[32,8,128]{2,1,0:T(8,128)}), f32[32,8,128]{2,1,0:T(8,128)S(1)}, u32[]{:S(2)}, u32[]{:S(2)}) async-start(f32[32,8,128]{2,1,0:T(8,128)} %broadcast_in_dim.26), calls=%async_computation.5 | async-start | bytes 262144 | tf_op jit(solution)/shard_map/all_to_all | solution.py:342
  154.0 10.9 %all-to-all-start.10 = ((f32[32,8,128]{2,1,0:T(8,128)}), f32[32,8,128]{2,1,0:T(8,128)S(1)}, u32[]{:S(2)}, u32[]{:S(2)}) async-start(f32[32,8,128]{2,1,0:T(8,128)} %broadcast_in_dim.29), calls=%async_computation.10 | async-start | bytes 262144 | tf_op jit(solution)/shard_map/all_to_all | solution.py:342

commit v2 on v1

v2 whole, which is shorter than its diff:
```python
import functools

import jax
import jax.numpy as jnp
from jax import lax
from jax.experimental import pallas as pl
from jax.experimental.pallas import tpu as pltpu
from jax.sharding import PartitionSpec as P

STAR_DEV = 8192
KNOT_DEV = 8192
CALB_DEV = 256
FINE = 32
COARSE = 256
GROUP = 8
STAR_ROWS = 5 * FINE
KNOT_ROWS = 4 * FINE
TABLE_ROWS = KNOT_ROWS + CALB_DEV // 2
BF16 = jnp.bfloat16
F32 = jnp.float32
SCALAR_LANE = 64
KNOT_HALF = KNOT_ROWS + 32


def two_parts(values):
    high = values.astype(BF16)
    return high, (values - high.astype(F32)).astype(BF16)


def rows_and_columns(shape):
    return lax.broadcasted_iota(jnp.int32, shape, 0), lax.broadcasted_iota(jnp.int32, shape, 1)


def one_hot(index_row, size):
    rows, _ = rows_and_columns((size, index_row.shape[1]))
    return jnp.where(rows == index_row, 1.0, 0.0).astype(BF16)


def spline_weights(fraction):
    remain = 1.0 - fraction
    square = fraction * fraction
    cubed = square * fraction
    return (
        remain * remain * remain / 6.0,
        (3.0 * cubed - 6.0 * square + 4.0) / 6.0,
        (-3.0 * cubed + 3.0 * square + 3.0 * fraction + 1.0) / 6.0,
        cubed / 6.0,
    )


def weight_columns(weights, fine, tile):
    rows, _ = rows_and_columns((FINE + 8, weights[0].shape[1]))
    behind = rows - fine[tile : tile + 1]
    result = jnp.zeros(behind.shape, F32)
    for offset in range(4):
        result = jnp.where(behind == offset, weights[offset][tile : tile + 1], result)
    return result


def product(left, right, contract):
    return lax.dot_general(left, right, (contract, ((), ())), preferred_element_type=F32)


def live_mask(live_ref, first, shape):
    rows, _ = rows_and_columns(shape)
    return (rows + first < live_ref[0]).astype(F32)


def knot_backward_kernel(arrive, live_ref, *refs):
    observed, (scalar_ref, table_out, edge_out, knot_acc) = refs[:6], refs[6:10]
    if arrive:
        buffers, sems = refs[10:16], refs[16]
        copies = [
            pltpu.make_async_copy(source, target, sems.at[which])
            for which, (source, target) in enumerate(zip(observed, buffers))
        ]
        for copy in copies:
            copy.start()
        observed = buffers
    knot_ref, frac_ref, att_coef_ref, value_ref, cal_coef_ref, tile_cal_ref = observed
    knot_acc[...] = jnp.zeros_like(knot_acc)
    if arrive:
        for copy in copies:
            copy.wait()

    @pl.loop(0, knot_ref.shape[0] // GROUP)
    def _(group):
        first = pl.multiple_of(group * GROUP, GROUP)
        rows = pl.ds(first, GROUP)
        knot = knot_ref[rows, :]
        values = value_ref[rows, :]
        values = values * live_mask(live_ref, first, values.shape)
        coarse, fine = knot >> 5, knot & (FINE - 1)
        weights = spline_weights(frac_ref[rows, :])
        terms = [att_coef_ref[comp, rows, :] * values for comp in range(4)]
        left, right = [], []
        for tile in range(GROUP):
            here = slice(tile, tile + 1)
            right.append(one_hot(coarse[here], COARSE))
            columns = weight_columns(weights, fine, tile)
            spread = jnp.concatenate(
                [term[here] * columns[:FINE] for term in terms]
                + [term[here] * columns[FINE:] for term in terms],
                axis=0,
            )
            left.append(jnp.concatenate(two_parts(spread), axis=0))
        knot_acc[...] += product(
            jnp.concatenate(left, axis=1), jnp.concatenate(right, axis=1), ((1,), (1,))
        )

    lane = lax.broadcasted_iota(jnp.int32, (8, 128), 1)
    row = lax.broadcasted_iota(jnp.int32, (8, 128), 0)
    wide_lane = lax.broadcasted_iota(jnp.int32, (8, COARSE), 1)
    edges = scalar_ref[...]
    for comp in range(4):
        begin, past = comp * FINE, KNOT_ROWS + comp * 8
        main = knot_acc[begin : begin + FINE] + knot_acc[KNOT_HALF + begin : KNOT_HALF + begin + FINE]
        beyond = knot_acc[past : past + 8] + knot_acc[KNOT_HALF + past : KNOT_HALF + past + 8]
        moved = pltpu.roll(beyond, 1, 1)
        top = main[:8] + jnp.where(wide_lane > 0, moved, 0.0)
        table_out[begin : begin + 8, :] = top
        table_out[begin + 8 : begin + FINE, :] = main[8:]
        tail, head = moved[:, :128], top[:, :128]
        if comp:
            tail = pltpu.roll(tail, 2 * comp, 1)
        head = pltpu.roll(head, 2 * comp + 1, 1)
        edges = jnp.where((lane == 2 * comp) & (row < 3), tail, edges)
        edges = jnp.where((lane == 2 * comp + 1) & (row < 3), head, edges)
    for device in range(edge_out.shape[0]):
        edge_out[device] = edges

    values = value_ref[...]
    values = values * live_mask(live_ref, 0, values.shape) * cal_coef_ref[...]
    blocks = product(
        one_hot(tile_cal_ref[...], CALB_DEV), jnp.concatenate(two_parts(values), axis=1), ((1,), (0,))
    )
    width = values.shape[1]
    blocks = blocks[:, :width] + blocks[:, width:]
    table_out[KNOT_ROWS:, :] = jnp.concatenate(
        [blocks[: CALB_DEV // 2], blocks[CALB_DEV // 2 :]], axis=1
    )


def star_backward_kernel(live_ref, star_ref, star_coef_ref, value_ref, after_ref, star_out, star_acc):
    star_acc[...] = jnp.zeros_like(star_acc)

    @pl.loop(0, star_ref.shape[0] // GROUP)
    def _(group):
        first = pl.multiple_of(group * GROUP, GROUP)
        rows = pl.ds(first, GROUP)
        star = star_ref[rows, :]
        values = value_ref[rows, :]
        values = values * live_mask(live_ref, first, values.shape)
        coarse, fine = star & (COARSE - 1), star >> 8
        parts = [two_parts(star_coef_ref[comp, rows, :] * values) for comp in range(5)]
        parts = [pair[half].astype(F32) for half in range(2) for pair in parts]
        left, right = [], []
        fine_rows, _ = rows_and_columns((FINE, star.shape[1]))
        for tile in range(GROUP):
            here = slice(tile, tile + 1)
            right.append(one_hot(coarse[here], COARSE))
            chosen = fine_rows == fine[here]
            left.append(
                jnp.concatenate([jnp.where(chosen, part[here], 0.0) for part in parts], axis=0).astype(BF16)
            )
        star_acc[...] += product(
            jnp.concatenate(left, axis=1), jnp.concatenate(right, axis=1), ((1,), (1,))
        )

    star_out[...] = star_acc[:STAR_ROWS] + star_acc[STAR_ROWS:]


def sum_kernel(block_ref, out_ref):
    total = block_ref[0]
    for device in range(1, block_ref.shape[0]):
        total = total + block_ref[device]
    for device in range(block_ref.shape[0]):
        out_ref[device] = total


def picked(array, which):
    row = lax.broadcasted_iota(jnp.int32, array.shape, 0)
    lane = lax.broadcasted_iota(jnp.int32, array.shape, 1)
    chosen = (row == 0) & (lane == SCALAR_LANE + which)
    return jnp.sum(jnp.where(chosen, array, 0.0), keepdims=True)


def with_scalars(array, scalars):
    row = lax.broadcasted_iota(jnp.int32, array.shape, 0)
    lane = lax.broadcasted_iota(jnp.int32, array.shape, 1)
    for which, value in scalars:
        array = jnp.where((row == 0) & (lane == SCALAR_LANE + which), value, array)
    return array


def over_devices(ref):
    total = ref[0]
    for device in range(1, ref.shape[0]):
        total = total + ref[device]
    return total


def first_step(edges_ref):
    everyone = over_devices(edges_ref)
    return picked(everyone, 0), picked(everyone, 1)


def star_forward_kernel(n_seg, later, star_ref, star_coef_ref, own_ref, other_ref, *refs):
    if later:
        edges_ref, star_0_ref = refs[:2]
    image_ref, star_out, scalar_out, star_parts_ref = refs[-4:]
    star_x = own_ref[...] + other_ref[...]
    if later:
        norm_0, square_0 = first_step(edges_ref)
        star_x = star_0_ref[...] - norm_0 / square_0 * star_x
    star_out[...] = star_x
    norm = jnp.sum(star_x * star_x, keepdims=True) / n_seg
    scalar_out[...] = with_scalars(jnp.zeros((8, 128), F32), [(0, norm)])
    star_high, star_low = two_parts(star_x)
    star_parts_ref[:STAR_ROWS] = star_high
    star_parts_ref[STAR_ROWS:] = star_low

    @pl.loop(0, star_ref.shape[0] // GROUP)
    def _(group):
        rows = pl.ds(pl.multiple_of(group * GROUP, GROUP), GROUP)
        star = star_ref[rows, :]
        coarse, fine = star & (COARSE - 1), star >> 8
        coef = [star_coef_ref[comp, rows, :] for comp in range(5)]
        tiles = [slice(tile, tile + 1) for tile in range(GROUP)]
        hot = jnp.concatenate([one_hot(coarse[here], COARSE) for here in tiles], axis=1)
        found = product(star_parts_ref[...], hot, ((1,), (0,)))
        width = star.shape[1]
        fine_rows, _ = rows_and_columns((FINE, width))
        image_rows = []
        for tile, here in enumerate(tiles):
            across = slice(tile * width, (tile + 1) * width)

            def part(comp):
                begin = comp * FINE
                return (
                    found[begin : begin + FINE, across]
                    + found[STAR_ROWS + begin : STAR_ROWS + begin + FINE, across]
                )

            both = sum(coef[comp][here] * part(comp) for comp in range(5))
            both = jnp.where(fine_rows == fine[here], both, 0.0)
            both = both[:8] + both[8:16] + both[16:24] + both[24:]
            image_rows.append(jnp.sum(both, axis=0, keepdims=True))
        image_ref[rows, :] = jnp.concatenate(image_rows, axis=0)


def knot_forward_kernel(
    n_stars, n_seg, later, live_ref, place_ref, knot_ref, frac_ref, att_coef_ref, cal_coef_ref,
    tile_cal_ref, star_image_ref, star_scalar_ref, table_x_ref, edges_ref, *refs,
):
    if later:
        table_0_ref, ahead_0_ref, image_0_ref, image_ref, table_out, scalar_out = refs[:6]
    else:
        image_ref, table_out, scalar_out, ahead_out = refs[:4]
    knot_parts_ref, cal_ref = refs[-2:]
    segment = place_ref[0]
    lane = lax.broadcasted_iota(jnp.int32, (8, 128), 1)
    row = lax.broadcasted_iota(jnp.int32, (8, 128), 0)
    wide_lane = lax.broadcasted_iota(jnp.int32, (8, COARSE), 1)

    before, own, after = [jnp.zeros((8, 128), F32) for _ in range(3)]
    for block in range(n_stars):
        start = block * n_seg
        before += edges_ref[start + jnp.maximum(segment - 1, 0)]
        own += edges_ref[start + segment]
        after += edges_ref[start + jnp.minimum(segment + 1, n_seg - 1)]
    before = jnp.where(segment > 0, before, 0.0)
    ahead = jnp.where(lane % 2 == 0, own, 0.0) + pltpu.roll(jnp.where(lane % 2 == 1, after, 0.0), 127, 1)
    ahead = jnp.where((segment < n_seg - 1) & (lane < 8) & (row < 3), ahead, 0.0)

    table = table_x_ref[...]
    pieces = []
    for comp in range(4):
        shifted = pltpu.roll(before, 128 - 2 * comp, 1) if comp else before
        shifted = jnp.where((lane == 0) & (row < 3), shifted, 0.0)
        top = table[comp * FINE : comp * FINE + 8]
        pieces.append(top + jnp.concatenate([shifted, jnp.zeros_like(shifted)], axis=1))
        pieces.append(table[comp * FINE + 8 : (comp + 1) * FINE])
    table = jnp.concatenate(pieces + [table[KNOT_ROWS:]], axis=0)
    if later:
        norm_0, square_0 = first_step(edges_ref)
        step = norm_0 / square_0
        table = table_0_ref[...] - step * table
        ahead = ahead_0_ref[...] - step * ahead
    else:
        ahead_out[...] = ahead
    table_out[...] = table
    norm = picked(star_scalar_ref[...], 0) + jnp.sum(table * table, keepdims=True) / n_stars

    beyond = []
    for comp in range(4):
        moved = pltpu.roll(table[comp * FINE : comp * FINE + 8], COARSE - 1, 1)
        last = pltpu.roll(ahead, 127 - 2 * comp, 1)
        beyond.append(jnp.where(wide_lane == COARSE - 1, jnp.concatenate([last, last], axis=1), moved))
    knot_high, knot_low = two_parts(jnp.concatenate([table[:KNOT_ROWS]] + beyond, axis=0))
    knot_parts_ref[:KNOT_HALF] = knot_high
    knot_parts_ref[KNOT_HALF:] = knot_low

    blocks = jnp.concatenate([table[KNOT_ROWS:, :128], table[KNOT_ROWS:, 128:]], axis=0)
    rows = product(
        one_hot(tile_cal_ref[...], CALB_DEV), jnp.concatenate(two_parts(blocks), axis=1), ((0,), (0,))
    )
    cal_ref[...] = (rows[:, :128] + rows[:, 128:]) * cal_coef_ref[...] + star_image_ref[...]

    def one_group(group, sums):
        first = pl.multiple_of(group * GROUP, GROUP)
        rows = pl.ds(first, GROUP)
        knot = knot_ref[rows, :]
        coarse, fine = knot >> 5, knot & (FINE - 1)
        weights = spline_weights(frac_ref[rows, :])
        coef = [att_coef_ref[comp, rows, :] for comp in range(4)]
        tiles = [slice(tile, tile + 1) for tile in range(GROUP)]
        hot = jnp.concatenate([one_hot(coarse[here], COARSE) for here in tiles], axis=1)
        found = product(knot_parts_ref[...], hot, ((1,), (0,)))
        width = knot.shape[1]
        image_rows = []
        for tile, here in enumerate(tiles):
            across = slice(tile * width, (tile + 1) * width)

            def part(begin, size):
                return (
                    found[begin : begin + size, across]
                    + found[KNOT_HALF + begin : KNOT_HALF + begin + size, across]
                )

            columns = weight_columns(weights, fine, tile)
            main = sum(coef[comp][here] * part(comp * FINE, FINE) for comp in range(4))
            past = sum(coef[comp][here] * part(KNOT_ROWS + comp * 8, 8) for comp in range(4))
            both = main * columns[:FINE]
            both = both[:8] + both[8:16] + both[16:24] + both[24:] + past * columns[FINE:]
            image_rows.append(jnp.sum(both, axis=0, keepdims=True))
        image = jnp.concatenate(image_rows, axis=0) + cal_ref[rows, :]
        image = image * live_mask(live_ref, first, image.shape)
        image_ref[rows, :] = image
        if later:
            return sums[0] + image * image, sums[1] + image * image_0_ref[rows, :]
        return (sums[0] + image * image,)

    zero = jnp.zeros((GROUP, knot_ref.shape[1]), F32)
    sums = lax.fori_loop(0, knot_ref.shape[0] // GROUP, one_group, (zero, zero) if later else (zero,))
    scalars = [(0, norm)] + [(1 + which, jnp.sum(part, keepdims=True)) for which, part in enumerate(sums)]
    result = with_scalars(jnp.zeros((8, 128), F32), scalars)
    for device in range(scalar_out.shape[0]):
        scalar_out[device] = result


def output_kernel(
    live_ref, edges_ref, scalar_ref, star_0_ref, star_1_ref, att_0_ref, att_1_ref, table_0_ref,
    table_1_ref, value_ref, image_0_ref, image_1_ref, star_out, att_out, cal_out, residual_out,
):
    norm_0, square_0 = first_step(edges_ref)
    everyone = over_devices(scalar_ref)
    norm_1, square_1, cross = [picked(everyone, which) for which in range(3)]
    ratio = norm_1 / norm_0
    step_1 = norm_1 / (square_1 + 2.0 * ratio * cross + ratio * ratio * square_0)
    scale = norm_0 / square_0 + step_1 * ratio

    def combined(old, new):
        return scale * old + step_1 * new

    star_out[...] = combined(star_0_ref[...], star_1_ref[...])
    att_out[...] = combined(att_0_ref[...], att_1_ref[...])
    cal = combined(table_0_ref[KNOT_ROWS:, :], table_1_ref[KNOT_ROWS:, :])
    cal_out[...] = jnp.concatenate([cal[:, :128], cal[:, 128:]], axis=0)
    values = value_ref[...] * live_mask(live_ref, 0, value_ref.shape)
    residual_out[...] = values - combined(image_0_ref[...], image_1_ref[...])


def in_vmem(count):
    return [pl.BlockSpec(memory_space=pltpu.VMEM)] * count


def in_smem(count):
    return [pl.BlockSpec(memory_space=pltpu.SMEM)] * count


def in_hbm(count):
    return [pl.BlockSpec(memory_space=pltpu.HBM)] * count


def shaped(*shape):
    return jax.ShapeDtypeStruct(shape, F32)


PARAMS = pltpu.CompilerParams(vmem_limit_bytes=40 * 1024 * 1024)
PASS_COST = pl.CostEstimate(flops=3_000_000_000, bytes_accessed=1_000_000, transcendentals=0)
SMALL_COST = pl.CostEstimate(flops=1_000_000, bytes_accessed=600_000, transcendentals=0)


def on_device(
    obs_star, obs_knot, obs_frac, star_coef, att_coef, cal_coef, tile_cal, live_tiles, obs_value
):
    n_stars, n_seg = lax.axis_size("stars"), lax.axis_size("seg")
    count = n_stars * n_seg
    tile_count, width = obs_star.shape
    tile_row = tile_cal[None, :]
    place = lax.axis_index("seg").astype(jnp.int32)[None]
    image_shape = shaped(tile_count, width)
    table_shape = shaped(TABLE_ROWS, COARSE)
    star_shape = shaped(STAR_ROWS, COARSE)
    scalar_shape, scalar_copies = shaped(8, 128), shaped(count, 8, 128)

    def knot_backward(values, scalars, arrive):
        observed = (obs_knot, obs_frac, att_coef, values, cal_coef, tile_row)
        scratch = [pltpu.VMEM((2 * KNOT_HALF, COARSE), F32)]
        if arrive:
            scratch += [pltpu.VMEM(array.shape, array.dtype) for array in observed]
            scratch += [pltpu.SemaphoreType.DMA((len(observed),))]
        return pl.pallas_call(
            functools.partial(knot_backward_kernel, arrive),
            out_shape=(table_shape, scalar_copies),
            in_specs=in_smem(1) + (in_hbm if arrive else in_vmem)(len(observed)) + in_vmem(1),
            out_specs=tuple(in_vmem(2)),
            scratch_shapes=scratch,
            compiler_params=PARAMS,
            cost_estimate=PASS_COST,
            name="knot_backward",
        )(live_tiles, *observed, scalars)

    def star_backward(values, after):
        return pl.pallas_call(
            star_backward_kernel,
            out_shape=star_shape,
            in_specs=in_smem(1) + in_vmem(3) + [pl.BlockSpec(memory_space=pl.ANY)],
            out_specs=in_vmem(1)[0],
            scratch_shapes=[pltpu.VMEM((2 * STAR_ROWS, COARSE), F32)],
            compiler_params=PARAMS,
            cost_estimate=PASS_COST,
            name="star_backward",
        )(live_tiles, obs_star, star_coef, values, after)

    def star_forward(own, other, *first):
        return pl.pallas_call(
            functools.partial(star_forward_kernel, n_seg, bool(first)),
            out_shape=(image_shape, star_shape, scalar_shape),
            in_specs=in_vmem(4 + len(first)),
            out_specs=tuple(in_vmem(3)),
            scratch_shapes=[pltpu.VMEM((2 * STAR_ROWS, COARSE), BF16)],
            compiler_params=PARAMS,
            cost_estimate=PASS_COST,
            name="star_forward",
        )(obs_star, star_coef, own, other, *first)

    def knot_forward(star_image, star_scalars, table, edges, *first):
        outs = (image_shape, table_shape) + ((scalar_copies,) if first else (shaped(1, 8, 128), scalar_shape))
        return pl.pallas_call(
            functools.partial(knot_forward_kernel, n_stars, n_seg, bool(first)),
            out_shape=outs,
            in_specs=in_smem(2) + in_vmem(9 + len(first)),
            out_specs=tuple(in_vmem(len(outs))),
            scratch_shapes=[
                pltpu.VMEM((2 * KNOT_HALF, COARSE), BF16),
                pltpu.VMEM((tile_count, width), F32),
            ],
            compiler_params=PARAMS,
            cost_estimate=PASS_COST,
            name="knot_forward",
        )(
            live_tiles, place, obs_knot, obs_frac, att_coef, cal_coef, tile_row, star_image,
            star_scalars, table, edges, *first,
        )

    def swap(blocks, axes):
        return lax.all_to_all(blocks, axes, 0, 0)

    def table_sum(table):
        blocks = swap(table.reshape(n_stars, TABLE_ROWS // n_stars, COARSE), "stars")
        copies = pl.pallas_call(
            sum_kernel,
            out_shape=shaped(*blocks.shape),
            in_specs=in_vmem(1),
            out_specs=in_vmem(1)[0],
            compiler_params=PARAMS,
            cost_estimate=SMALL_COST,
            name="table_sum",
        )(blocks)
        return swap(copies, "stars").reshape(TABLE_ROWS, COARSE)

    def star_terms(star):
        distance = 1
        while True:
            other = lax.ppermute(star, "seg", [(i, i ^ distance) for i in range(n_seg)])
            distance *= 2
            if distance >= n_seg:
                return star, other
            star = star + other

    def half(values, scalars, arrive):
        table, edges = knot_backward(values, scalars, arrive)
        star = star_backward(values, edges)
        return (*star_terms(star), table_sum(table), swap(edges, ("stars", "seg")))

    own, other, table, edges = half(obs_value, jnp.zeros((8, 128), F32), True)
    star_image, star_0, star_scalars = star_forward(own, other)
    image_0, table_0, scalars, ahead_0 = knot_forward(star_image, star_scalars, table, edges)
    own, other, table, edges = half(image_0, scalars[0], False)
    star_image, star_1, star_scalars = star_forward(own, other, edges, star_0)
    image_1, table_1, scalars = knot_forward(
        star_image, star_scalars, table, edges, table_0, ahead_0, image_0
    )

    def star_order(star):
        return star.reshape(5, STAR_DEV)

    def att_order(table):
        att = table[:KNOT_ROWS].reshape(4, FINE, COARSE)
        return att.transpose(0, 2, 1).reshape(4, KNOT_DEV)

    return pl.pallas_call(
        output_kernel,
        out_shape=(shaped(5, STAR_DEV), shaped(4, KNOT_DEV), shaped(CALB_DEV, width), image_shape),
        in_specs=in_smem(1) + in_vmem(11),
        out_specs=tuple(in_vmem(4)),
        compiler_params=PARAMS,
        cost_estimate=SMALL_COST,
        name="outputs",
    )(
        live_tiles, edges, swap(scalars, ("stars", "seg")), star_order(star_0), star_order(star_1),
        att_order(table_0), att_order(table_1), table_0, table_1, obs_value, image_0, image_1,
    )


def solution(mesh):
    placed = (
        P(("stars", "seg"), None),
        P(("stars", "seg"), None),
        P(("stars", "seg"), None),
        P(None, ("stars", "seg"), None),
        P(None, ("stars", "seg"), None),
        P(("stars", "seg"), None),
        P(("stars", "seg")),
        P(("stars", "seg")),
        P(("stars", "seg"), None),
    )
    return jax.shard_map(
        on_device,
        mesh=mesh,
        in_specs=placed,
        out_specs=(P(None, "stars"), P(None, "seg"), P("seg", None), P(("stars", "seg"), None)),
        check_vma=False,
    )
```

time: 174 us -> 140 us (0.80)
  blocking collectives: 70 us -> 29.8 us
  Pallas kernels: 38.2 us -> 57.5 us
  starting transfers between devices: 11.6 us -> 26.1 us
  waiting for transfers between devices: 32.1 us -> 18.4 us
  local copies, waits for them, and re-layouts: 13.3 us -> 6.01 us
  between operations: 6.76 us -> 1.54 us
    all_to_all x7 -> x2, blocking collectives: 70 us -> 29.8 us  [swap(): return lax.all_to_all(blocks, axes, 0, 0)]
    all_to_all x4 -> x5, waiting for transfers between devices: 32.1 us -> 9.01 us  [swap(): return lax.all_to_all(blocks, axes, 0, 0)]
    pallas_call x4 -> x11, Pallas kernels: 38.2 us -> 57.5 us  [the longest x2 16.3 us: knot_backward(): pl.pallas_call(functools.partial(knot_backward_kernel, arrive), out_shape...]
    all_to_all x4 -> x5, starting transfers between devices: 11.6 us -> 22.3 us  [swap(): return lax.all_to_all(blocks, axes, 0, 0)]
    ppermute x0 -> x4, waiting for transfers between devices: none -> 9.35 us  [star_terms(): other = lax.ppermute(star, 'seg', [(i, i ^ distance) for i in range(n_seg)])]
    ppermute x0 -> x4, starting transfers between devices: none -> 3.76 us  [star_terms(): other = lax.ppermute(star, 'seg', [(i, i ^ distance) for i in range(n_seg)])]
    broadcast_in_dim x8 -> x1, local copies, waits for them, and re-layouts: 2.76 us -> 0.01 us  [on_device(): own, other, table, edges = half(obs_value, jnp.zeros((8, 128), F32), True)]
    unnamed x30 -> x26, local copies, waits for them, and re-layouts: 6.79 us -> 4.97 us
  transfers between devices with their start and end apart: 4 -> 9, of which waited for: 4 -> 5; matrix products, arithmetic and copies ran while one was open for 0% -> 1% of each run, Pallas kernels for 0% -> 20%
where the time goes in v2:
time: 140 us; the launch traced here: 139 us
  Pallas kernels  57.5 us (41%)
  blocking collectives  29.8 us (21%)
  starting transfers between devices  26.1 us (19%)
  waiting for transfers between devices  18.4 us (13%)
  local copies, waits for them, and re-layouts  6.01 us (4%)
  between operations  1.54 us (1%)
    all_to_all x2, blocking collectives, swap(): return lax.all_to_all(blocks, axes, 0, 0)  29.8 us
    all_to_all x5, starting transfers between devices, swap(): return lax.all_to_all(blocks, axes, 0, 0)  22.3 us
    pallas_call x2, Pallas kernels, knot_backward(): pl.pallas_call(functools.partial(knot_backward_kernel, arrive), out_shape...  16.3 us
    pallas_call x2, Pallas kernels, star_forward(): pl.pallas_call(functools.partial(star_forward_kernel, n_seg, bool(first))...  13.3 us
    pallas_call x2, Pallas kernels, knot_forward(): pl.pallas_call(functools.partial(knot_forward_kernel, n_stars, n_seg, boo...  13 us
    pallas_call x2, Pallas kernels, star_backward(): pl.pallas_call(star_backward_kernel, out_shape=star_shape, in_specs=in_sm...  12.5 us
    ppermute x4, waiting for transfers between devices, star_terms(): other = lax.ppermute(star, 'seg', [(i, i ^ distance) for i in range(n_seg)])  9.35 us
    all_to_all x5, waiting for transfers between devices, swap(): return lax.all_to_all(blocks, axes, 0, 0)  9.01 us
  transfers between devices with their start and end apart: 9, of which 5 were waited for; matrix products, arithmetic and copies ran while one was open for 1% of the time, Pallas kernels for 20%

profile of v2, /device:TPU:0, one launch (start us, length us, event | category | flops | bytes accessed | tf_op | source)
XLA Modules:
  0.0 139.3 jit_solution(14180007698062773506)
XLA Ops:
  2.8 0.9 copy-done.3
  6.2 8.3 %knot_backward.2 = (f32[256,256]{1,0:T(8,128)S(1)}, f32[32,8,128]{2,1,0:T(8,128)}) custom-call(s32[1]{0:T(128)S(6)} %copy.17.live_ref, s32[128,128]{1,0:T(8,128)S(1)} %copy-done.6, f32[128,128]{1,0:T(8,128)S(1)} %copy-done.8, f32[4,128,128]{2,1,0:T(8,128)S(1)} %copy-done.3, f32[128,128]{1,0:T(8,128)S(1)} %copy-done, f32[128,128]{1,0:T(8,128)S(1)} %copy-done.10, ...), custom_call_target="tpu_custom_call" | custom-call | flops 3000000000 | bytes 1000000 | tf_op jit(solution)/shard_map/knot_backward/pallas_call | solution.py:414
  14.6 16.1 %all_to_all.35.block_ref = f32[8,32,256]{2,1,0:T(8,128)S(1)} all-to-all(f32[8,32,256]{2,1,0:T(8,128)S(1)} %bitcast.13), channel_id=1, replica_groups=mesh['stars'=8,'seg'=4] {'stars'}, dimensions={0} | all-to-all | bytes 524288 | tf_op jit(solution)/shard_map/all_to_all | solution.py:469
  30.7 3.6 %all-to-all-start.2 = ((f32[32,8,128]{2,1,0:T(8,128)}), f32[32,8,128]{2,1,0:T(8,128)S(1)}, u32[]{:S(2)}, u32[]{:S(2)}) async-start(f32[32,8,128]{2,1,0:T(8,128)} %get-tuple-element.21.after_ref), calls=%async_computation.2 | async-start | bytes 262144 | tf_op jit(solution)/shard_map/all_to_all | solution.py:469
  34.4 6.2 %star_backward.2 = f32[160,256]{1,0:T(8,128)S(1)} custom-call(s32[1]{0:T(128)S(6)} %copy.17.live_ref, s32[128,128]{1,0:T(8,128)S(1)} %copy-done.5, f32[5,128,128]{2,1,0:T(8,128)S(1)} %copy-done.2, f32[128,128]{1,0:T(8,128)S(1)} %copy-done.1, f32[32,8,128]{2,1,0:T(8,128)} %get-tuple-element.21.after_ref), custom_call_target="tpu_custom_call" | custom-call | flops 3000000000 | bytes 1000000 | tf_op jit(solution)/shard_map/star_backward/pallas_call | solution.py:426
  41.6 0.9 all-to-all-done.2.edges_ref
  42.6 4.8 %all-to-all-start.1 = ((f32[8,32,256]{2,1,0:T(8,128)}), f32[8,32,256]{2,1,0:T(8,128)S(1)}, u32[]{:S(2)}, u32[]{:S(2)}) async-start(f32[8,32,256]{2,1,0:T(8,128)} %table_sum.2), calls=%async_computation.1 | async-start | bytes 524288 | tf_op jit(solution)/shard_map/all_to_all | solution.py:469
  47.4 1.6 %collective-permute-start.1 = (f32[160,256]{1,0:T(8,128)S(1)}, f32[160,256]{1,0:T(8,128)S(1)}, u32[]{:S(2)}, u32[]{:S(2)}) collective-permute-start(f32[160,256]{1,0:T(8,128)S(1)} %add.6.own_ref), channel_id=1, source_target_pairs={{0,2},{1,3},{2,0},{3,1},{4,6},{5,7},{6,4},{7,5},{8,10},{9,11},{10,... | collective-permute-start | bytes 491528 | tf_op jit(solution)/shard_map/ppermute | solution.py:487
  49.0 4.7 %collective-permute-done.1.other_ref = f32[160,256]{1,0:T(8,128)S(1)} collective-permute-done((f32[160,256]{1,0:T(8,128)S(1)}, f32[160,256]{1,0:T(8,128)S(1)}, u32[]{:S(2)}, u32[]{:S(2)}) %collective-permute-start.1) | collective-permute-done | bytes 163872 | tf_op jit(solution)/shard_map/ppermute | solution.py:487
  53.6 6.6 %star_forward.2 = (f32[128,128]{1,0:T(8,128)S(1)}, f32[160,256]{1,0:T(8,128)S(1)}, f32[8,128]{1,0:T(8,128)S(1)}) custom-call(s32[128,128]{1,0:T(8,128)S(1)} %copy-done.5, f32[5,128,128]{2,1,0:T(8,128)S(1)} %copy-done.2, f32[160,256]{1,0:T(8,128)S(1)} %add.6.own_ref, f32[160,256]{1,0:T(8,128)S(1)} %collective-permute-done.1.other_ref), custom_call_target="tpu_custom_call" | custom-call | flops 3000000000 | bytes 1000000 | tf_op jit(solution)/shard_map/star_forward/pallas_call | solution.py:438
  60.3 6.1 %knot_forward.2 = (f32[128,128]{1,0:T(8,128)S(1)}, f32[256,256]{1,0:T(8,128)S(1)}, f32[1,8,128]{2,1,0:T(8,128)S(1)}, f32[8,128]{1,0:T(8,128)S(1)}) custom-call(s32[1]{0:T(128)S(6)} %copy.17.live_ref, s32[1]{0:T(128)} %bitcast.place_ref, s32[128,128]{1,0:T(8,128)S(1)} %copy-done.7, f32[128,128]{1,0:T(8,128)S(1)} %copy-done.9, f32[4,128,128]{2,1,0:T(8,128)S(1)} %copy-done.4, ...), custom_call_target="tpu_custom_call" | custom-call | flops 3000000000 | bytes 1000000 | tf_op jit(solution)/shard_map/knot_forward/pallas_call | solution.py:451
  66.5 7.9 %knot_backward.3 = (f32[256,256]{1,0:T(8,128)S(1)}, f32[32,8,128]{2,1,0:T(8,128)}) custom-call(s32[1]{0:T(128)S(6)} %copy.17.live_ref, s32[128,128]{1,0:T(8,128)S(1)} %copy-done.7, f32[128,128]{1,0:T(8,128)S(1)} %copy-done.9, f32[4,128,128]{2,1,0:T(8,128)S(1)} %copy-done.4, f32[128,128]{1,0:T(8,128)S(1)} %get-tuple-element.25.refs_3_.value_ref.refs_2_.image_0_ref, ...), custom_call_target="tpu_custom_call" | custom-call | flops 3000000000 | bytes 1000000 | tf_op jit(solution)/shard_map/knot_backward/pallas_call | solution.py:414
  74.4 13.7 %all_to_all.36.block_ref = f32[8,32,256]{2,1,0:T(8,128)S(1)} all-to-all(f32[8,32,256]{2,1,0:T(8,128)S(1)} %bitcast.14), channel_id=1, replica_groups=mesh['stars'=8,'seg'=4] {'stars'}, dimensions={0} | all-to-all | bytes 524288 | tf_op jit(solution)/shard_map/all_to_all | solution.py:469
  88.1 3.4 %all-to-all-start.3 = ((f32[32,8,128]{2,1,0:T(8,128)}), f32[32,8,128]{2,1,0:T(8,128)S(1)}, u32[]{:S(2)}, u32[]{:S(2)}) async-start(f32[32,8,128]{2,1,0:T(8,128)} %get-tuple-element.27.after_ref), calls=%async_computation.3 | async-start | bytes 262144 | tf_op jit(solution)/shard_map/all_to_all | solution.py:469
  91.5 6.2 %star_backward.3 = f32[160,256]{1,0:T(8,128)S(1)} custom-call(s32[1]{0:T(128)S(6)} %copy.17.live_ref, s32[128,128]{1,0:T(8,128)S(1)} %copy-done.5, f32[5,128,128]{2,1,0:T(8,128)S(1)} %copy-done.2, f32[128,128]{1,0:T(8,128)S(1)} %get-tuple-element.25.refs_3_.value_ref.refs_2_.image_0_ref, f32[32,8,128]{2,1,0:T(8,128)} %get-tuple-element.27.after_ref), custom_call_target="tpu_custom_call" | custom-call | flops 3000000000 | bytes 1000000 | tf_op jit(solution)/shard_map/star_backward/pallas_call | solution.py:426
  98.8 0.9 all-to-all-done.3.refs_0_.edges_ref
  99.7 4.8 %all-to-all-start.5 = ((f32[8,32,256]{2,1,0:T(8,128)}), f32[8,32,256]{2,1,0:T(8,128)S(1)}, u32[]{:S(2)}, u32[]{:S(2)}) async-start(f32[8,32,256]{2,1,0:T(8,128)} %table_sum.3), calls=%async_computation.5 | async-start | bytes 524288 | tf_op jit(solution)/shard_map/all_to_all | solution.py:469
  104.5 1.6 %collective-permute-start.3 = (f32[160,256]{1,0:T(8,128)S(1)}, f32[160,256]{1,0:T(8,128)S(1)}, u32[]{:S(2)}, u32[]{:S(2)}) collective-permute-start(f32[160,256]{1,0:T(8,128)S(1)} %add.7.own_ref), channel_id=1, source_target_pairs={{0,2},{1,3},{2,0},{3,1},{4,6},{5,7},{6,4},{7,5},{8,10},{9,11},{10,... | collective-permute-start | bytes 491528 | tf_op jit(solution)/shard_map/ppermute | solution.py:487
  106.1 4.7 %collective-permute-done.3.other_ref = f32[160,256]{1,0:T(8,128)S(1)} collective-permute-done((f32[160,256]{1,0:T(8,128)S(1)}, f32[160,256]{1,0:T(8,128)S(1)}, u32[]{:S(2)}, u32[]{:S(2)}) %collective-permute-start.3) | collective-permute-done | bytes 163872 | tf_op jit(solution)/shard_map/ppermute | solution.py:487
  110.8 6.7 %star_forward.3 = (f32[128,128]{1,0:T(8,128)S(1)}, f32[160,256]{1,0:T(8,128)S(1)}, f32[8,128]{1,0:T(8,128)S(1)}) custom-call(s32[128,128]{1,0:T(8,128)S(1)} %copy-done.5, f32[5,128,128]{2,1,0:T(8,128)S(1)} %copy-done.2, f32[160,256]{1,0:T(8,128)S(1)} %add.7.own_ref, f32[160,256]{1,0:T(8,128)S(1)} %collective-permute-done.3.other_ref, ...), custom_call_target="tpu_custom_call" | custom-call | flops 3000000000 | bytes 1000000 | tf_op jit(solution)/shard_map/star_forward/pallas_call | solution.py:438
  117.5 6.9 %knot_forward.3 = (f32[128,128]{1,0:T(8,128)S(1)}, f32[256,256]{1,0:T(8,128)S(1)}, f32[32,8,128]{2,1,0:T(8,128)}) custom-call(s32[1]{0:T(128)S(6)} %copy.17.live_ref, s32[1]{0:T(128)} %bitcast.place_ref, s32[128,128]{1,0:T(8,128)S(1)} %copy-done.7, f32[128,128]{1,0:T(8,128)S(1)} %copy-done.9, f32[4,128,128]{2,1,0:T(8,128)S(1)} %copy-done.4, ...), custom_call_target="tpu_custom_call" | custom-call | flops 3000000000 | bytes 1000000 | tf_op jit(solution)/shard_map/knot_forward/pallas_call | solution.py:451
  124.4 5.7 %all-to-all-start.6 = ((f32[32,8,128]{2,1,0:T(8,128)}), f32[32,8,128]{2,1,0:T(8,128)S(1)}, u32[]{:S(2)}, u32[]{:S(2)}) async-start(f32[32,8,128]{2,1,0:T(8,128)} %get-tuple-element.34), calls=%async_computation.6 | async-start | bytes 262144 | tf_op jit(solution)/shard_map/all_to_all | solution.py:469
  131.2 7.1 %all-to-all-done.6.scalar_ref = f32[32,8,128]{2,1,0:T(8,128)S(1)} async-done(((f32[32,8,128]{2,1,0:T(8,128)}), f32[32,8,128]{2,1,0:T(8,128)S(1)}, u32[]{:S(2)}, u32[]{:S(2)}) %all-to-all-start.6) | async-done | bytes 131104 | tf_op jit(solution)/shard_map/all_to_all | solution.py:469
  138.4 1.0 outputs.1
  (44 shorter events, 7.2 us)
Async XLA Ops:
  1.3 0.7 copy-start.12
  1.9 0.8 copy-start
  2.8 0.9 copy-start.3
  3.7 0.8 copy-start.6
  4.6 0.8 copy-start.8
  5.4 0.8 copy-start.10
  14.6 19.8 %copy-start.2 = (f32[5,128,128]{2,1,0:T(8,128)S(1)}, f32[5,128,128]{2,1,0:T(8,128)}, u32[]{:S(2)}) copy-start(f32[5,128,128]{2,1,0:T(8,128)} %star_coef_ref.7) | copy-start | bytes 983044
  30.7 3.7 %copy-start.1 = (f32[128,128]{1,0:T(8,128)S(1)}, f32[128,128]{1,0:T(8,128)}, u32[]{:S(2)}) copy-start(f32[128,128]{1,0:T(8,128)} %value_ref.3) | copy-start | bytes 196612
  30.7 3.7 %copy-start.5 = (s32[128,128]{1,0:T(8,128)S(1)}, s32[128,128]{1,0:T(8,128)}, u32[]{:S(2)}) copy-start(s32[128,128]{1,0:T(8,128)} %star_ref.7) | copy-start | bytes 196612
  30.7 11.9 %all-to-all-start.2 = ((f32[32,8,128]{2,1,0:T(8,128)}), f32[32,8,128]{2,1,0:T(8,128)S(1)}, u32[]{:S(2)}, u32[]{:S(2)}) async-start(f32[32,8,128]{2,1,0:T(8,128)} %get-tuple-element.21.after_ref), calls=%async_computation.2 | async-start | bytes 262144 | tf_op jit(solution)/shard_map/all_to_all | solution.py:469
  40.6 6.8 %collective-permute-start = (f32[160,256]{1,0:T(8,128)S(1)}, f32[160,256]{1,0:T(8,128)S(1)}, u32[]{:S(2)}, u32[]{:S(2)}) collective-permute-start(f32[160,256]{1,0:T(8,128)S(1)} %star_backward.2), channel_id=1, source_target_pairs={{0,1},{1,0},{2,3},{3,2},{4,5},{5,4},{6,7},{7,6},{8,9},{9,8},{10,11... | collective-permute-start | bytes 491528 | tf_op jit(solution)/shard_map/ppermute | solution.py:487
  42.6 17.7 %all-to-all-start.1 = ((f32[8,32,256]{2,1,0:T(8,128)}), f32[8,32,256]{2,1,0:T(8,128)S(1)}, u32[]{:S(2)}, u32[]{:S(2)}) async-start(f32[8,32,256]{2,1,0:T(8,128)} %table_sum.2), calls=%async_computation.1 | async-start | bytes 524288 | tf_op jit(solution)/shard_map/all_to_all | solution.py:469
  47.4 6.2 %collective-permute-start.1 = (f32[160,256]{1,0:T(8,128)S(1)}, f32[160,256]{1,0:T(8,128)S(1)}, u32[]{:S(2)}, u32[]{:S(2)}) collective-permute-start(f32[160,256]{1,0:T(8,128)S(1)} %add.6.own_ref), channel_id=1, source_target_pairs={{0,2},{1,3},{2,0},{3,1},{4,6},{5,7},{6,4},{7,5},{8,10},{9,11},{10,... | collective-permute-start | bytes 491528 | tf_op jit(solution)/shard_map/ppermute | solution.py:487
  49.0 11.3 %copy-start.4 = (f32[4,128,128]{2,1,0:T(8,128)S(1)}, f32[4,128,128]{2,1,0:T(8,128)}, u32[]{:S(2)}) copy-start(f32[4,128,128]{2,1,0:T(8,128)} %att_coef_ref.3) | copy-start | bytes 786436
  49.0 11.3 %copy-start.7 = (s32[128,128]{1,0:T(8,128)S(1)}, s32[128,128]{1,0:T(8,128)}, u32[]{:S(2)}) copy-start(s32[128,128]{1,0:T(8,128)} %knot_ref.3) | copy-start | bytes 196612
  49.0 11.3 %copy-start.9 = (f32[128,128]{1,0:T(8,128)S(1)}, f32[128,128]{1,0:T(8,128)}, u32[]{:S(2)}) copy-start(f32[128,128]{1,0:T(8,128)} %frac_ref.3) | copy-start | bytes 196612
  49.0 11.3 %copy-start.11 = (f32[128,128]{1,0:T(8,128)S(1)}, f32[128,128]{1,0:T(8,128)}, u32[]{:S(2)}) copy-start(f32[128,128]{1,0:T(8,128)} %cal_coef_ref.3) | copy-start | bytes 196612
  88.1 11.6 %all-to-all-start.3 = ((f32[32,8,128]{2,1,0:T(8,128)}), f32[32,8,128]{2,1,0:T(8,128)S(1)}, u32[]{:S(2)}, u32[]{:S(2)}) async-start(f32[32,8,128]{2,1,0:T(8,128)} %get-tuple-element.27.after_ref), calls=%async_computation.3 | async-start | bytes 262144 | tf_op jit(solution)/shard_map/all_to_all | solution.py:469
  97.7 6.8 %collective-permute-start.2 = (f32[160,256]{1,0:T(8,128)S(1)}, f32[160,256]{1,0:T(8,128)S(1)}, u32[]{:S(2)}, u32[]{:S(2)}) collective-permute-start(f32[160,256]{1,0:T(8,128)S(1)} %star_backward.3), channel_id=1, source_target_pairs={{0,1},{1,0},{2,3},{3,2},{4,5},{5,4},{6,7},{7,6},{8,9},{9,8},{10,11... | collective-permute-start | bytes 491528 | tf_op jit(solution)/shard_map/ppermute | solution.py:487
  99.7 17.8 %all-to-all-start.5 = ((f32[8,32,256]{2,1,0:T(8,128)}), f32[8,32,256]{2,1,0:T(8,128)S(1)}, u32[]{:S(2)}, u32[]{:S(2)}) async-start(f32[8,32,256]{2,1,0:T(8,128)} %table_sum.3), calls=%async_computation.5 | async-start | bytes 524288 | tf_op jit(solution)/shard_map/all_to_all | solution.py:469
  104.5 6.2 %collective-permute-start.3 = (f32[160,256]{1,0:T(8,128)S(1)}, f32[160,256]{1,0:T(8,128)S(1)}, u32[]{:S(2)}, u32[]{:S(2)}) collective-permute-start(f32[160,256]{1,0:T(8,128)S(1)} %add.7.own_ref), channel_id=1, source_target_pairs={{0,2},{1,3},{2,0},{3,1},{4,6},{5,7},{6,4},{7,5},{8,10},{9,11},{10,... | collective-permute-start | bytes 491528 | tf_op jit(solution)/shard_map/ppermute | solution.py:487
  124.4 14.0 %all-to-all-start.6 = ((f32[32,8,128]{2,1,0:T(8,128)}), f32[32,8,128]{2,1,0:T(8,128)S(1)}, u32[]{:S(2)}, u32[]{:S(2)}) async-start(f32[32,8,128]{2,1,0:T(8,128)} %get-tuple-element.34), calls=%async_computation.6 | async-start | bytes 262144 | tf_op jit(solution)/shard_map/all_to_all | solution.py:469

commit v3 on v2

--- a/solution.py
+++ b/solution.py
@@ -13,6 +13,8 @@
 FINE = 32
 COARSE = 256
 GROUP = 8
+WIDE_GROUP = 16
+SLOT = 8
 STAR_ROWS = 5 * FINE
 KNOT_ROWS = 4 * FINE
 TABLE_ROWS = KNOT_ROWS + CALB_DEV // 2
@@ -66,10 +68,17 @@
     return (rows + first < live_ref[0]).astype(F32)
 
 
-def knot_backward_kernel(arrive, live_ref, *refs):
-    observed, (scalar_ref, table_out, edge_out, knot_acc) = refs[:6], refs[6:10]
+def store_rows(out_ref, begin, rows):
+    block = out_ref.shape[1] - 8
+    for offset in range(0, rows.shape[0], 8):
+        where = begin + offset
+        out_ref[where // block, where % block : where % block + 8, :] = rows[offset : offset + 8]
+
+
+def knot_backward_kernel(arrive, live_ref, place_ref, *refs):
+    observed, (scalar_ref, table_out, knot_acc) = refs[:6], refs[6:9]
     if arrive:
-        buffers, sems = refs[10:16], refs[16]
+        buffers, sems = refs[9:15], refs[15]
         copies = [
             pltpu.make_async_copy(source, target, sems.at[which])
             for which, (source, target) in enumerate(zip(observed, buffers))
@@ -83,10 +92,10 @@
         for copy in copies:
             copy.wait()
 
-    @pl.loop(0, knot_ref.shape[0] // GROUP)
+    @pl.loop(0, knot_ref.shape[0] // WIDE_GROUP)
     def _(group):
-        first = pl.multiple_of(group * GROUP, GROUP)
-        rows = pl.ds(first, GROUP)
+        first = pl.multiple_of(group * WIDE_GROUP, WIDE_GROUP)
+        rows = pl.ds(first, WIDE_GROUP)
         knot = knot_ref[rows, :]
         values = value_ref[rows, :]
         values = values * live_mask(live_ref, first, values.shape)
@@ -94,7 +103,7 @@
         weights = spline_weights(frac_ref[rows, :])
         terms = [att_coef_ref[comp, rows, :] * values for comp in range(4)]
         left, right = [], []
-        for tile in range(GROUP):
+        for tile in range(WIDE_GROUP):
             here = slice(tile, tile + 1)
             right.append(one_hot(coarse[here], COARSE))
             columns = weight_columns(weights, fine, tile)
@@ -111,23 +120,25 @@
     lane = lax.broadcasted_iota(jnp.int32, (8, 128), 1)
     row = lax.broadcasted_iota(jnp.int32, (8, 128), 0)
     wide_lane = lax.broadcasted_iota(jnp.int32, (8, COARSE), 1)
-    edges = scalar_ref[...]
+    edges = jnp.zeros((8, 128), F32)
     for comp in range(4):
         begin, past = comp * FINE, KNOT_ROWS + comp * 8
         main = knot_acc[begin : begin + FINE] + knot_acc[KNOT_HALF + begin : KNOT_HALF + begin + FINE]
         beyond = knot_acc[past : past + 8] + knot_acc[KNOT_HALF + past : KNOT_HALF + past + 8]
         moved = pltpu.roll(beyond, 1, 1)
         top = main[:8] + jnp.where(wide_lane > 0, moved, 0.0)
-        table_out[begin : begin + 8, :] = top
-        table_out[begin + 8 : begin + FINE, :] = main[8:]
+        store_rows(table_out, begin, top)
+        store_rows(table_out, begin + 8, main[8:])
         tail, head = moved[:, :128], top[:, :128]
         if comp:
             tail = pltpu.roll(tail, 2 * comp, 1)
         head = pltpu.roll(head, 2 * comp + 1, 1)
         edges = jnp.where((lane == 2 * comp) & (row < 3), tail, edges)
         edges = jnp.where((lane == 2 * comp + 1) & (row < 3), head, edges)
-    for device in range(edge_out.shape[0]):
-        edge_out[device] = edges
+    edges = scalar_ref[...] + pltpu.roll(edges, SLOT * place_ref[0], 1)
+    edges = jnp.concatenate([edges, jnp.zeros_like(edges)], axis=1)
+    for device in range(table_out.shape[0]):
+        table_out[device, table_out.shape[1] - 8 :, :] = edges
 
     values = value_ref[...]
     values = values * live_mask(live_ref, 0, values.shape) * cal_coef_ref[...]
@@ -136,18 +147,17 @@
     )
     width = values.shape[1]
     blocks = blocks[:, :width] + blocks[:, width:]
-    table_out[KNOT_ROWS:, :] = jnp.concatenate(
-        [blocks[: CALB_DEV // 2], blocks[CALB_DEV // 2 :]], axis=1
-    )
+    blocks = jnp.concatenate([blocks[: CALB_DEV // 2], blocks[CALB_DEV // 2 :]], axis=1)
+    store_rows(table_out, KNOT_ROWS, blocks)
 
 
 def star_backward_kernel(live_ref, star_ref, star_coef_ref, value_ref, after_ref, star_out, star_acc):
     star_acc[...] = jnp.zeros_like(star_acc)
 
-    @pl.loop(0, star_ref.shape[0] // GROUP)
+    @pl.loop(0, star_ref.shape[0] // WIDE_GROUP)
     def _(group):
-        first = pl.multiple_of(group * GROUP, GROUP)
-        rows = pl.ds(first, GROUP)
+        first = pl.multiple_of(group * WIDE_GROUP, WIDE_GROUP)
+        rows = pl.ds(first, WIDE_GROUP)
         star = star_ref[rows, :]
         values = value_ref[rows, :]
         values = values * live_mask(live_ref, first, values.shape)
@@ -156,7 +166,7 @@
         parts = [pair[half].astype(F32) for half in range(2) for pair in parts]
         left, right = [], []
         fine_rows, _ = rows_and_columns((FINE, star.shape[1]))
-        for tile in range(GROUP):
+        for tile in range(WIDE_GROUP):
             here = slice(tile, tile + 1)
             right.append(one_hot(coarse[here], COARSE))
             chosen = fine_rows == fine[here]
@@ -170,12 +180,14 @@
     star_out[...] = star_acc[:STAR_ROWS] + star_acc[STAR_ROWS:]
 
 
-def sum_kernel(block_ref, out_ref):
+def sum_kernel(block_ref, out_ref, edge_out):
     total = block_ref[0]
     for device in range(1, block_ref.shape[0]):
         total = total + block_ref[device]
+    rows = out_ref.shape[1]
     for device in range(block_ref.shape[0]):
-        out_ref[device] = total
+        out_ref[device] = total[:rows]
+    edge_out[...] = total[rows:, :128]
 
 
 def picked(array, which):
@@ -200,18 +212,17 @@
     return total
 
 
-def first_step(edges_ref):
-    everyone = over_devices(edges_ref)
-    return picked(everyone, 0), picked(everyone, 1)
+def first_step(edges):
+    return picked(edges, 0), picked(edges, 1)
 
 
 def star_forward_kernel(n_seg, later, star_ref, star_coef_ref, own_ref, other_ref, *refs):
     if later:
-        edges_ref, star_0_ref = refs[:2]
+        edge_ref, other_edge_ref, star_0_ref = refs[:3]
     image_ref, star_out, scalar_out, star_parts_ref = refs[-4:]
     star_x = own_ref[...] + other_ref[...]
     if later:
-        norm_0, square_0 = first_step(edges_ref)
+        norm_0, square_0 = first_step(edge_ref[...] + other_edge_ref[...])
         star_x = star_0_ref[...] - norm_0 / square_0 * star_x
     star_out[...] = star_x
     norm = jnp.sum(star_x * star_x, keepdims=True) / n_seg
@@ -220,7 +231,7 @@
     star_parts_ref[:STAR_ROWS] = star_high
     star_parts_ref[STAR_ROWS:] = star_low
 
-    @pl.loop(0, star_ref.shape[0] // GROUP)
+    @pl.loop(0, star_ref.shape[0] // GROUP, unroll=2)
     def _(group):
         rows = pl.ds(pl.multiple_of(group * GROUP, GROUP), GROUP)
         star = star_ref[rows, :]
@@ -251,7 +262,7 @@
 
 def knot_forward_kernel(
     n_stars, n_seg, later, live_ref, place_ref, knot_ref, frac_ref, att_coef_ref, cal_coef_ref,
-    tile_cal_ref, star_image_ref, star_scalar_ref, table_x_ref, edges_ref, *refs,
+    tile_cal_ref, star_image_ref, star_scalar_ref, table_x_ref, edge_ref, other_edge_ref, *refs,
 ):
     if later:
         table_0_ref, ahead_0_ref, image_0_ref, image_ref, table_out, scalar_out = refs[:6]
@@ -263,12 +274,12 @@
     row = lax.broadcasted_iota(jnp.int32, (8, 128), 0)
     wide_lane = lax.broadcasted_iota(jnp.int32, (8, COARSE), 1)
 
-    before, own, after = [jnp.zeros((8, 128), F32) for _ in range(3)]
-    for block in range(n_stars):
-        start = block * n_seg
-        before += edges_ref[start + jnp.maximum(segment - 1, 0)]
-        own += edges_ref[start + segment]
-        after += edges_ref[start + jnp.minimum(segment + 1, n_seg - 1)]
+    edges = edge_ref[...] + other_edge_ref[...]
+
+    def slot(which):
+        return pltpu.roll(edges, 128 - SLOT * jnp.clip(which, 0, n_seg - 1), 1)
+
+    before, own, after = slot(segment - 1), slot(segment), slot(segment + 1)
     before = jnp.where(segment > 0, before, 0.0)
     ahead = jnp.where(lane % 2 == 0, own, 0.0) + pltpu.roll(jnp.where(lane % 2 == 1, after, 0.0), 127, 1)
     ahead = jnp.where((segment < n_seg - 1) & (lane < 8) & (row < 3), ahead, 0.0)
@@ -283,7 +294,7 @@
         pieces.append(table[comp * FINE + 8 : (comp + 1) * FINE])
     table = jnp.concatenate(pieces + [table[KNOT_ROWS:]], axis=0)
     if later:
-        norm_0, square_0 = first_step(edges_ref)
+        norm_0, square_0 = first_step(edges)
         step = norm_0 / square_0
         table = table_0_ref[...] - step * table
         ahead = ahead_0_ref[...] - step * ahead
@@ -342,7 +353,8 @@
         return (sums[0] + image * image,)
 
     zero = jnp.zeros((GROUP, knot_ref.shape[1]), F32)
-    sums = lax.fori_loop(0, knot_ref.shape[0] // GROUP, one_group, (zero, zero) if later else (zero,))
+    start = (zero, zero) if later else (zero,)
+    sums = lax.fori_loop(0, knot_ref.shape[0] // GROUP, one_group, start, unroll=2)
     scalars = [(0, norm)] + [(1 + which, jnp.sum(part, keepdims=True)) for which, part in enumerate(sums)]
     result = with_scalars(jnp.zeros((8, 128), F32), scalars)
     for device in range(scalar_out.shape[0]):
@@ -350,10 +362,10 @@
 
 
 def output_kernel(
-    live_ref, edges_ref, scalar_ref, star_0_ref, star_1_ref, att_0_ref, att_1_ref, table_0_ref,
+    live_ref, edge_ref, other_edge_ref, scalar_ref, star_0_ref, star_1_ref, att_0_ref, att_1_ref, table_0_ref,
     table_1_ref, value_ref, image_0_ref, image_1_ref, star_out, att_out, cal_out, residual_out,
 ):
-    norm_0, square_0 = first_step(edges_ref)
+    norm_0, square_0 = first_step(edge_ref[...] + other_edge_ref[...])
     everyone = over_devices(scalar_ref)
     norm_1, square_1, cross = [picked(everyone, which) for which in range(3)]
     ratio = norm_1 / norm_0
@@ -387,6 +399,7 @@
     return jax.ShapeDtypeStruct(shape, F32)
 
 
+ARRIVE_PARAMS = pltpu.CompilerParams(vmem_limit_bytes=60 * 1024 * 1024)
 PARAMS = pltpu.CompilerParams(vmem_limit_bytes=40 * 1024 * 1024)
 PASS_COST = pl.CostEstimate(flops=3_000_000_000, bytes_accessed=1_000_000, transcendentals=0)
 SMALL_COST = pl.CostEstimate(flops=1_000_000, bytes_accessed=600_000, transcendentals=0)
@@ -413,14 +426,14 @@
             scratch += [pltpu.SemaphoreType.DMA((len(observed),))]
         return pl.pallas_call(
             functools.partial(knot_backward_kernel, arrive),
-            out_shape=(table_shape, scalar_copies),
-            in_specs=in_smem(1) + (in_hbm if arrive else in_vmem)(len(observed)) + in_vmem(1),
-            out_specs=tuple(in_vmem(2)),
+            out_shape=shaped(n_stars, TABLE_ROWS // n_stars + 8, COARSE),
+            in_specs=in_smem(2) + (in_hbm if arrive else in_vmem)(len(observed)) + in_vmem(1),
+            out_specs=in_vmem(1)[0],
             scratch_shapes=scratch,
-            compiler_params=PARAMS,
+            compiler_params=ARRIVE_PARAMS if arrive else PARAMS,
             cost_estimate=PASS_COST,
             name="knot_backward",
-        )(live_tiles, *observed, scalars)
+        )(live_tiles, place, *observed, scalars)
 
     def star_backward(values, after):
         return pl.pallas_call(
@@ -446,12 +459,12 @@
             name="star_forward",
         )(obs_star, star_coef, own, other, *first)
 
-    def knot_forward(star_image, star_scalars, table, edges, *first):
+    def knot_forward(star_image, star_scalars, table, edge, other_edge, *first):
         outs = (image_shape, table_shape) + ((scalar_copies,) if first else (shaped(1, 8, 128), scalar_shape))
         return pl.pallas_call(
             functools.partial(knot_forward_kernel, n_stars, n_seg, bool(first)),
             out_shape=outs,
-            in_specs=in_smem(2) + in_vmem(9 + len(first)),
+            in_specs=in_smem(2) + in_vmem(10 + len(first)),
             out_specs=tuple(in_vmem(len(outs))),
             scratch_shapes=[
                 pltpu.VMEM((2 * KNOT_HALF, COARSE), BF16),
@@ -462,46 +475,46 @@
             name="knot_forward",
         )(
             live_tiles, place, obs_knot, obs_frac, att_coef, cal_coef, tile_row, star_image,
-            star_scalars, table, edges, *first,
+            star_scalars, table, edge, other_edge, *first,
         )
 
     def swap(blocks, axes):
         return lax.all_to_all(blocks, axes, 0, 0)
 
+    def seg_terms(array):
+        distance = 1
+        while True:
+            other = lax.ppermute(array, "seg", [(i, i ^ distance) for i in range(n_seg)])
+            distance *= 2
+            if distance >= n_seg:
+                return array, other
+            array = array + other
+
     def table_sum(table):
-        blocks = swap(table.reshape(n_stars, TABLE_ROWS // n_stars, COARSE), "stars")
-        copies = pl.pallas_call(
+        blocks = swap(table, "stars")
+        copies, edge = pl.pallas_call(
             sum_kernel,
-            out_shape=shaped(*blocks.shape),
+            out_shape=(shaped(n_stars, TABLE_ROWS // n_stars, COARSE), scalar_shape),
             in_specs=in_vmem(1),
-            out_specs=in_vmem(1)[0],
+            out_specs=tuple(in_vmem(2)),
             compiler_params=PARAMS,
             cost_estimate=SMALL_COST,
             name="table_sum",
         )(blocks)
-        return swap(copies, "stars").reshape(TABLE_ROWS, COARSE)
-
-    def star_terms(star):
-        distance = 1
-        while True:
-            other = lax.ppermute(star, "seg", [(i, i ^ distance) for i in range(n_seg)])
-            distance *= 2
-            if distance >= n_seg:
-                return star, other
-            star = star + other
+        return (swap(copies, "stars").reshape(TABLE_ROWS, COARSE), *seg_terms(edge))
 
     def half(values, scalars, arrive):
-        table, edges = knot_backward(values, scalars, arrive)
-        star = star_backward(values, edges)
-        return (*star_terms(star), table_sum(table), swap(edges, ("stars", "seg")))
-
-    own, other, table, edges = half(obs_value, jnp.zeros((8, 128), F32), True)
+        table = knot_backward(values, scalars, arrive)
+        star = star_backward(values, table)
+        return (*seg_terms(star), *table_sum(table))
+
+    own, other, table, edge, other_edge = half(obs_value, jnp.zeros((8, 128), F32), True)
     star_image, star_0, star_scalars = star_forward(own, other)
-    image_0, table_0, scalars, ahead_0 = knot_forward(star_image, star_scalars, table, edges)
-    own, other, table, edges = half(image_0, scalars[0], False)
-    star_image, star_1, star_scalars = star_forward(own, other, edges, star_0)
+    image_0, table_0, scalars, ahead_0 = knot_forward(star_image, star_scalars, table, edge, other_edge)
+    own, other, table, edge, other_edge = half(image_0, scalars[0], False)
+    star_image, star_1, star_scalars = star_forward(own, other, edge, other_edge, star_0)
     image_1, table_1, scalars = knot_forward(
-        star_image, star_scalars, table, edges, table_0, ahead_0, image_0
+        star_image, star_scalars, table, edge, other_edge, table_0, ahead_0, image_0
     )
 
     def star_order(star):
@@ -514,14 +527,15 @@
     return pl.pallas_call(
         output_kernel,
         out_shape=(shaped(5, STAR_DEV), shaped(4, KNOT_DEV), shaped(CALB_DEV, width), image_shape),
-        in_specs=in_smem(1) + in_vmem(11),
+        in_specs=in_smem(1) + in_vmem(12),
         out_specs=tuple(in_vmem(4)),
         compiler_params=PARAMS,
         cost_estimate=SMALL_COST,
         name="outputs",
     )(
-        live_tiles, edges, swap(scalars, ("stars", "seg")), star_order(star_0), star_order(star_1),
-        att_order(table_0), att_order(table_1), table_0, table_1, obs_value, image_0, image_1,
+        live_tiles, edge, other_edge, swap(scalars, ("stars", "seg")), star_order(star_0),
+        star_order(star_1), att_order(table_0), att_order(table_1), table_0, table_1, obs_value,
+        image_0, image_1,
     )
 
 

time: 140 us -> 105 us (0.75)
  blocking collectives: 29.8 us -> 0 us
  Pallas kernels: 57.5 us -> 46.3 us
  waiting for transfers between devices: 18.4 us -> 24.6 us
  local copies, waits for them, and re-layouts: 6.01 us -> 2.28 us
  starting transfers between devices: 26.1 us -> 29.8 us
    all_to_all x2 -> x0, blocking collectives: 29.8 us -> none  [swap(): return lax.all_to_all(blocks, axes, 0, 0)]
    all_to_all x5, waiting for transfers between devices: 9.01 us -> 17.1 us  [swap(): return lax.all_to_all(blocks, axes, 0, 0)]
    unnamed x26 -> x18, local copies, waits for them, and re-layouts: 4.97 us -> 0.65 us
    pallas_call x2, Pallas kernels: 12.5 us -> 8.82 us  [star_backward(): pl.pallas_call(star_backward_kernel, out_shape=star_shape, in_specs=in_sm...]
    pallas_call x2, Pallas kernels: 13.3 us -> 9.91 us  [star_forward(): pl.pallas_call(functools.partial(star_forward_kernel, n_seg, bool(first))...]
    all_to_all x5, starting transfers between devices: 22.3 us -> 25.5 us  [swap(): return lax.all_to_all(blocks, axes, 0, 0)]
    pallas_call x2, Pallas kernels: 13 us -> 10.6 us  [knot_forward(): pl.pallas_call(functools.partial(knot_forward_kernel, n_stars, n_seg, boo...]
    ppermute x4 -> x8, waiting for transfers between devices: 9.35 us -> 7.52 us  [seg_terms(): lax.ppermute(array, 'seg', [(i, i ^ distance) for i in range(n_seg)])]
  transfers between devices with their start and end apart: 9 -> 13, of which waited for: 5 -> 8; matrix products, arithmetic and copies ran while one was open for 1% -> 1% of each run, Pallas kernels for 20% -> 19%
where the time goes in v3:
time: 105 us
  Pallas kernels  46.3 us (44%)
  starting transfers between devices  29.8 us (28%)
  waiting for transfers between devices  24.6 us (23%)
  local copies, waits for them, and re-layouts  2.28 us (2%)
  between operations  1.58 us (2%)
    all_to_all x5, starting transfers between devices, swap(): return lax.all_to_all(blocks, axes, 0, 0)  25.5 us
    all_to_all x5, waiting for transfers between devices, swap(): return lax.all_to_all(blocks, axes, 0, 0)  17.1 us
    pallas_call x2, Pallas kernels, knot_backward(): pl.pallas_call(functools.partial(knot_backward_kernel, arrive), out_shape...  14.5 us
    pallas_call x2, Pallas kernels, knot_forward(): pl.pallas_call(functools.partial(knot_forward_kernel, n_stars, n_seg, boo...  10.6 us
    pallas_call x2, Pallas kernels, star_forward(): pl.pallas_call(functools.partial(star_forward_kernel, n_seg, bool(first))...  9.91 us
    pallas_call x2, Pallas kernels, star_backward(): pl.pallas_call(star_backward_kernel, out_shape=star_shape, in_specs=in_sm...  8.82 us
    ppermute x8, waiting for transfers between devices, seg_terms(): lax.ppermute(array, 'seg', [(i, i ^ distance) for i in range(n_seg)])  7.52 us
    ppermute x8, starting transfers between devices, seg_terms(): lax.ppermute(array, 'seg', [(i, i ^ distance) for i in range(n_seg)])  4.39 us
  transfers between devices with their start and end apart: 13, of which 8 were waited for; matrix products, arithmetic and copies ran while one was open for 1% of the time, Pallas kernels for 19%

profile of v3, /device:TPU:0, one launch (start us, length us, event | category | flops | bytes accessed | tf_op | source)
XLA Modules:
  0.0 104.7 jit_solution(4154884711389099635)
XLA Ops:
  1.9 8.2 %knot_backward.2.after_ref = f32[8,40,256]{2,1,0:T(8,128)} custom-call(s32[1]{0:T(128)S(6)} %copy.17.live_ref, s32[1]{0:T(128)} %bitcast.place_ref, s32[128,128]{1,0:T(8,128)} %knot_ref.3, f32[128,128]{1,0:T(8,128)} %frac_ref.3, f32[4,128,128]{2,1,0:T(8,128)} %att_coef_ref.3, f32[128,128]{1,0:T(8,128)} %value_ref.3, f32[128,128]{1,0:T(8,128)} %cal_coef_ref.3, ...), custom_call_target="tpu_custom_call" | custom-call | flops 3000000000 | bytes 1000000 | tf_op jit(solution)/shard_map/knot_backward/pallas_call | solution.py:427
  10.1 7.4 %all-to-all-start = ((f32[8,40,256]{2,1,0:T(8,128)}), f32[8,40,256]{2,1,0:T(8,128)S(1)}, u32[]{:S(2)}, u32[]{:S(2)}) async-start(f32[8,40,256]{2,1,0:T(8,128)} %knot_backward.2.after_ref), calls=%async_computation | async-start | bytes 655360 | tf_op jit(solution)/shard_map/all_to_all | solution.py:482
  17.5 4.4 %star_backward.2 = f32[160,256]{1,0:T(8,128)S(1)} custom-call(s32[1]{0:T(128)S(6)} %copy.17.live_ref, s32[128,128]{1,0:T(8,128)S(1)} %copy-done.4, f32[5,128,128]{2,1,0:T(8,128)S(1)} %copy-done.2, f32[128,128]{1,0:T(8,128)S(1)} %copy-done.1, f32[8,40,256]{2,1,0:T(8,128)S(1)} %copy-done), custom_call_target="tpu_custom_call" | custom-call | flops 3000000000 | bytes 1000000 | tf_op jit(solution)/shard_map/star_backward/pallas_call | solution.py:439
  22.0 5.8 %all-to-all-done.block_ref = f32[8,40,256]{2,1,0:T(8,128)S(1)} async-done(((f32[8,40,256]{2,1,0:T(8,128)}), f32[8,40,256]{2,1,0:T(8,128)S(1)}, u32[]{:S(2)}, u32[]{:S(2)}) %all-to-all-start) | async-done | bytes 327712 | tf_op jit(solution)/shard_map/all_to_all | solution.py:482
  28.5 3.6 %all-to-all-start.1 = ((f32[8,32,256]{2,1,0:T(8,128)}), f32[8,32,256]{2,1,0:T(8,128)S(1)}, u32[]{:S(2)}, u32[]{:S(2)}) async-start(f32[8,32,256]{2,1,0:T(8,128)} %get-tuple-element.23), calls=%async_computation.1 | async-start | bytes 524288 | tf_op jit(solution)/shard_map/all_to_all | solution.py:482
  32.1 1.6 %collective-permute-start.1 = (f32[160,256]{1,0:T(8,128)S(1)}, f32[160,256]{1,0:T(8,128)S(1)}, u32[]{:S(2)}, u32[]{:S(2)}) collective-permute-start(f32[160,256]{1,0:T(8,128)S(1)} %add.12.own_ref), channel_id=1, source_target_pairs={{0,2},{1,3},{2,0},{3,1},{4,6},{5,7},{6,4},{7,5},{8,10},{9,11},{10,... | collective-permute-start | bytes 491528 | tf_op jit(solution)/shard_map/ppermute | solution.py:487
  33.7 1.2 %collective-permute-done.2 = f32[8,128]{1,0:T(8,128)S(1)} collective-permute-done((f32[8,128]{1,0:T(8,128)S(1)}, f32[8,128]{1,0:T(8,128)S(1)}, u32[]{:S(2)}, u32[]{:S(2)}) %collective-permute-start.2) | collective-permute-done | bytes 4128 | tf_op jit(solution)/shard_map/ppermute | solution.py:487
  35.5 2.0 %collective-permute-done.1.other_ref = f32[160,256]{1,0:T(8,128)S(1)} collective-permute-done((f32[160,256]{1,0:T(8,128)S(1)}, f32[160,256]{1,0:T(8,128)S(1)}, u32[]{:S(2)}, u32[]{:S(2)}) %collective-permute-start.1) | collective-permute-done | bytes 163872 | tf_op jit(solution)/shard_map/ppermute | solution.py:487
  37.5 4.9 %star_forward.2 = (f32[128,128]{1,0:T(8,128)S(1)}, f32[160,256]{1,0:T(8,128)S(1)}, f32[8,128]{1,0:T(8,128)S(1)}) custom-call(s32[128,128]{1,0:T(8,128)S(1)} %copy-done.4, f32[5,128,128]{2,1,0:T(8,128)S(1)} %copy-done.2, f32[160,256]{1,0:T(8,128)S(1)} %add.12.own_ref, f32[160,256]{1,0:T(8,128)S(1)} %collective-permute-done.1.other_ref), custom_call_target="tpu_custom_call" | custom-call | flops 3000000000 | bytes 1000000 | tf_op jit(solution)/shard_map/star_forward/pallas_call | solution.py:451
  43.1 5.0 %knot_forward.2 = (f32[128,128]{1,0:T(8,128)S(1)}, f32[256,256]{1,0:T(8,128)S(1)}, f32[1,8,128]{2,1,0:T(8,128)S(1)}, f32[8,128]{1,0:T(8,128)S(1)}) custom-call(s32[1]{0:T(128)S(6)} %copy.17.live_ref, s32[1]{0:T(128)} %bitcast.place_ref, s32[128,128]{1,0:T(8,128)S(1)} %copy-done.5, f32[128,128]{1,0:T(8,128)S(1)} %copy-done.6, f32[4,128,128]{2,1,0:T(8,128)S(1)} %copy-done.3, ...), custom_call_target="tpu_custom_call" | custom-call | flops 3000000000 | bytes 1000000 | tf_op jit(solution)/shard_map/knot_forward/pallas_call | solution.py:464
  48.1 6.4 %knot_backward.3.after_ref = f32[8,40,256]{2,1,0:T(8,128)} custom-call(s32[1]{0:T(128)S(6)} %copy.17.live_ref, s32[1]{0:T(128)} %bitcast.place_ref, s32[128,128]{1,0:T(8,128)S(1)} %copy-done.5, f32[128,128]{1,0:T(8,128)S(1)} %copy-done.6, f32[4,128,128]{2,1,0:T(8,128)S(1)} %copy-done.3, ...), custom_call_target="tpu_custom_call" | custom-call | flops 3000000000 | bytes 1000000 | tf_op jit(solution)/shard_map/knot_backward/pallas_call | solution.py:427
  54.4 6.0 %all-to-all-start.2 = ((f32[8,40,256]{2,1,0:T(8,128)}), f32[8,40,256]{2,1,0:T(8,128)S(1)}, u32[]{:S(2)}, u32[]{:S(2)}) async-start(f32[8,40,256]{2,1,0:T(8,128)} %knot_backward.3.after_ref), calls=%async_computation.2 | async-start | bytes 655360 | tf_op jit(solution)/shard_map/all_to_all | solution.py:482
  60.4 4.4 %star_backward.3 = f32[160,256]{1,0:T(8,128)S(1)} custom-call(s32[1]{0:T(128)S(6)} %copy.17.live_ref, s32[128,128]{1,0:T(8,128)S(1)} %copy-done.4, f32[5,128,128]{2,1,0:T(8,128)S(1)} %copy-done.2, f32[128,128]{1,0:T(8,128)S(1)} %get-tuple-element.25.refs_3_.value_ref.refs_2_.image_0_ref, f32[8,40,256]{2,1,0:T(8,128)} %knot_backward.3.after_ref), custom_call_target="tpu_custom_call" | custom-call | flops 3000000000 | bytes 1000000 | tf_op jit(solution)/shard_map/star_backward/pallas_call | solution.py:439
  64.9 4.2 %all-to-all-done.2.block_ref = f32[8,40,256]{2,1,0:T(8,128)S(1)} async-done(((f32[8,40,256]{2,1,0:T(8,128)}), f32[8,40,256]{2,1,0:T(8,128)S(1)}, u32[]{:S(2)}, u32[]{:S(2)}) %all-to-all-start.2) | async-done | bytes 327712 | tf_op jit(solution)/shard_map/all_to_all | solution.py:482
  69.8 3.4 %all-to-all-start.3 = ((f32[8,32,256]{2,1,0:T(8,128)}), f32[8,32,256]{2,1,0:T(8,128)S(1)}, u32[]{:S(2)}, u32[]{:S(2)}) async-start(f32[8,32,256]{2,1,0:T(8,128)} %get-tuple-element.31), calls=%async_computation.3 | async-start | bytes 524288 | tf_op jit(solution)/shard_map/all_to_all | solution.py:482
  73.3 1.6 %collective-permute-start.7 = (f32[160,256]{1,0:T(8,128)S(1)}, f32[160,256]{1,0:T(8,128)S(1)}, u32[]{:S(2)}, u32[]{:S(2)}) collective-permute-start(f32[160,256]{1,0:T(8,128)S(1)} %add.15.own_ref), channel_id=1, source_target_pairs={{0,2},{1,3},{2,0},{3,1},{4,6},{5,7},{6,4},{7,5},{8,10},{9,11},{10,... | collective-permute-start | bytes 491528 | tf_op jit(solution)/shard_map/ppermute | solution.py:487
  74.9 1.2 %collective-permute-done.4 = f32[8,128]{1,0:T(8,128)S(1)} collective-permute-done((f32[8,128]{1,0:T(8,128)S(1)}, f32[8,128]{1,0:T(8,128)S(1)}, u32[]{:S(2)}, u32[]{:S(2)}) %collective-permute-start.4) | collective-permute-done | bytes 4128 | tf_op jit(solution)/shard_map/ppermute | solution.py:487
  76.5 2.1 %collective-permute-done.7.other_ref = f32[160,256]{1,0:T(8,128)S(1)} collective-permute-done((f32[160,256]{1,0:T(8,128)S(1)}, f32[160,256]{1,0:T(8,128)S(1)}, u32[]{:S(2)}, u32[]{:S(2)}) %collective-permute-start.7) | collective-permute-done | bytes 163872 | tf_op jit(solution)/shard_map/ppermute | solution.py:487
  78.7 1.0 collective-permute-done.5.refs_1_.other_edge_ref
  79.7 5.0 %star_forward.3 = (f32[128,128]{1,0:T(8,128)S(1)}, f32[160,256]{1,0:T(8,128)S(1)}, f32[8,128]{1,0:T(8,128)S(1)}) custom-call(s32[128,128]{1,0:T(8,128)S(1)} %copy-done.4, f32[5,128,128]{2,1,0:T(8,128)S(1)} %copy-done.2, f32[160,256]{1,0:T(8,128)S(1)} %add.15.own_ref, f32[160,256]{1,0:T(8,128)S(1)} %collective-permute-done.7.other_ref, ...), custom_call_target="tpu_custom_call" | custom-call | flops 3000000000 | bytes 1000000 | tf_op jit(solution)/shard_map/star_forward/pallas_call | solution.py:451
  84.7 5.6 %knot_forward.3 = (f32[128,128]{1,0:T(8,128)S(1)}, f32[256,256]{1,0:T(8,128)S(1)}, f32[32,8,128]{2,1,0:T(8,128)}) custom-call(s32[1]{0:T(128)S(6)} %copy.17.live_ref, s32[1]{0:T(128)} %bitcast.place_ref, s32[128,128]{1,0:T(8,128)S(1)} %copy-done.5, f32[128,128]{1,0:T(8,128)S(1)} %copy-done.6, f32[4,128,128]{2,1,0:T(8,128)S(1)} %copy-done.3, ...), custom_call_target="tpu_custom_call" | custom-call | flops 3000000000 | bytes 1000000 | tf_op jit(solution)/shard_map/knot_forward/pallas_call | solution.py:464
  90.4 5.1 %all-to-all-start.4 = ((f32[32,8,128]{2,1,0:T(8,128)}), f32[32,8,128]{2,1,0:T(8,128)S(1)}, u32[]{:S(2)}, u32[]{:S(2)}) async-start(f32[32,8,128]{2,1,0:T(8,128)} %get-tuple-element.34), calls=%async_computation.4 | async-start | bytes 262144 | tf_op jit(solution)/shard_map/all_to_all | solution.py:482
  96.6 7.1 %all-to-all-done.4.scalar_ref = f32[32,8,128]{2,1,0:T(8,128)S(1)} async-done(((f32[32,8,128]{2,1,0:T(8,128)}), f32[32,8,128]{2,1,0:T(8,128)S(1)}, u32[]{:S(2)}, u32[]{:S(2)}) %all-to-all-start.4) | async-done | bytes 131104 | tf_op jit(solution)/shard_map/all_to_all | solution.py:482
  103.7 1.0 outputs.1
  (44 shorter events, 5.0 us)
Async XLA Ops:
  1.9 15.6 %copy-start.2 = (f32[5,128,128]{2,1,0:T(8,128)S(1)}, f32[5,128,128]{2,1,0:T(8,128)}, u32[]{:S(2)}) copy-start(f32[5,128,128]{2,1,0:T(8,128)} %star_coef_ref.7) | copy-start | bytes 983044
  10.0 7.4 %copy-start = (f32[8,40,256]{2,1,0:T(8,128)S(1)}, f32[8,40,256]{2,1,0:T(8,128)}, u32[]{:S(2)}) copy-start(f32[8,40,256]{2,1,0:T(8,128)} %knot_backward.2.after_ref) | copy-start | bytes 983044
  10.1 7.4 %copy-start.1 = (f32[128,128]{1,0:T(8,128)S(1)}, f32[128,128]{1,0:T(8,128)}, u32[]{:S(2)}) copy-start(f32[128,128]{1,0:T(8,128)} %value_ref.3) | copy-start | bytes 196612
  10.1 7.4 %copy-start.4 = (s32[128,128]{1,0:T(8,128)S(1)}, s32[128,128]{1,0:T(8,128)}, u32[]{:S(2)}) copy-start(s32[128,128]{1,0:T(8,128)} %star_ref.7) | copy-start | bytes 196612
  10.1 17.7 %all-to-all-start = ((f32[8,40,256]{2,1,0:T(8,128)}), f32[8,40,256]{2,1,0:T(8,128)S(1)}, u32[]{:S(2)}, u32[]{:S(2)}) async-start(f32[8,40,256]{2,1,0:T(8,128)} %knot_backward.2.after_ref), calls=%async_computation | async-start | bytes 655360 | tf_op jit(solution)/shard_map/all_to_all | solution.py:482
  21.9 10.2 %collective-permute-start = (f32[160,256]{1,0:T(8,128)S(1)}, f32[160,256]{1,0:T(8,128)S(1)}, u32[]{:S(2)}, u32[]{:S(2)}) collective-permute-start(f32[160,256]{1,0:T(8,128)S(1)} %star_backward.2), channel_id=1, source_target_pairs={{0,1},{1,0},{2,3},{3,2},{4,5},{5,4},{6,7},{7,6},{8,9},{9,8},{10,11... | collective-permute-start | bytes 491528 | tf_op jit(solution)/shard_map/ppermute | solution.py:487
  28.5 13.9 %all-to-all-start.1 = ((f32[8,32,256]{2,1,0:T(8,128)}), f32[8,32,256]{2,1,0:T(8,128)S(1)}, u32[]{:S(2)}, u32[]{:S(2)}) async-start(f32[8,32,256]{2,1,0:T(8,128)} %get-tuple-element.23), calls=%async_computation.1 | async-start | bytes 524288 | tf_op jit(solution)/shard_map/all_to_all | solution.py:482
  32.1 5.4 %collective-permute-start.1 = (f32[160,256]{1,0:T(8,128)S(1)}, f32[160,256]{1,0:T(8,128)S(1)}, u32[]{:S(2)}, u32[]{:S(2)}) collective-permute-start(f32[160,256]{1,0:T(8,128)S(1)} %add.12.own_ref), channel_id=1, source_target_pairs={{0,2},{1,3},{2,0},{3,1},{4,6},{5,7},{6,4},{7,5},{8,10},{9,11},{10,... | collective-permute-start | bytes 491528 | tf_op jit(solution)/shard_map/ppermute | solution.py:487
  33.7 1.2 %collective-permute-start.2 = (f32[8,128]{1,0:T(8,128)S(1)}, f32[8,128]{1,0:T(8,128)S(1)}, u32[]{:S(2)}, u32[]{:S(2)}) collective-permute-start(f32[8,128]{1,0:T(8,128)S(1)} %get-tuple-element.24), channel_id=1, source_target_pairs={{0,1},{1,0},{2,3},{3,2},{4,5},{5,4},{6,7},{7,6},{8,9},{9,8},{10,11... | collective-permute-start | bytes 12296 | tf_op jit(solution)/shard_map/ppermute | solution.py:487
  34.9 7.6 %copy-start.3 = (f32[4,128,128]{2,1,0:T(8,128)S(1)}, f32[4,128,128]{2,1,0:T(8,128)}, u32[]{:S(2)}) copy-start(f32[4,128,128]{2,1,0:T(8,128)} %att_coef_ref.3) | copy-start | bytes 786436
  34.9 7.6 %copy-start.5 = (s32[128,128]{1,0:T(8,128)S(1)}, s32[128,128]{1,0:T(8,128)}, u32[]{:S(2)}) copy-start(s32[128,128]{1,0:T(8,128)} %knot_ref.3) | copy-start | bytes 196612
  34.9 7.6 %copy-start.6 = (f32[128,128]{1,0:T(8,128)S(1)}, f32[128,128]{1,0:T(8,128)}, u32[]{:S(2)}) copy-start(f32[128,128]{1,0:T(8,128)} %frac_ref.3) | copy-start | bytes 196612
  34.9 7.6 %copy-start.7 = (f32[128,128]{1,0:T(8,128)S(1)}, f32[128,128]{1,0:T(8,128)}, u32[]{:S(2)}) copy-start(f32[128,128]{1,0:T(8,128)} %cal_coef_ref.3) | copy-start | bytes 196612
  34.9 7.5 %collective-permute-start.3 = (f32[8,128]{1,0:T(8,128)S(1)}, f32[8,128]{1,0:T(8,128)S(1)}, u32[]{:S(2)}, u32[]{:S(2)}) collective-permute-start(f32[8,128]{1,0:T(8,128)S(1)} %add.13.edge_ref), channel_id=1, source_target_pairs={{0,2},{1,3},{2,0},{3,1},{4,6},{5,7},{6,4},{7,5},{8,10},{9,11},{10,... | collective-permute-start | bytes 12296 | tf_op jit(solution)/shard_map/ppermute | solution.py:487
  42.4 0.7 copy-start.8
  54.4 14.6 %all-to-all-start.2 = ((f32[8,40,256]{2,1,0:T(8,128)}), f32[8,40,256]{2,1,0:T(8,128)S(1)}, u32[]{:S(2)}, u32[]{:S(2)}) async-start(f32[8,40,256]{2,1,0:T(8,128)} %knot_backward.3.after_ref), calls=%async_computation.2 | async-start | bytes 655360 | tf_op jit(solution)/shard_map/all_to_all | solution.py:482
  64.8 8.4 %collective-permute-start.6 = (f32[160,256]{1,0:T(8,128)S(1)}, f32[160,256]{1,0:T(8,128)S(1)}, u32[]{:S(2)}, u32[]{:S(2)}) collective-permute-start(f32[160,256]{1,0:T(8,128)S(1)} %star_backward.3), channel_id=1, source_target_pairs={{0,1},{1,0},{2,3},{3,2},{4,5},{5,4},{6,7},{7,6},{8,9},{9,8},{10,11... | collective-permute-start | bytes 491528 | tf_op jit(solution)/shard_map/ppermute | solution.py:487
  69.8 14.9 %all-to-all-start.3 = ((f32[8,32,256]{2,1,0:T(8,128)}), f32[8,32,256]{2,1,0:T(8,128)S(1)}, u32[]{:S(2)}, u32[]{:S(2)}) async-start(f32[8,32,256]{2,1,0:T(8,128)} %get-tuple-element.31), calls=%async_computation.3 | async-start | bytes 524288 | tf_op jit(solution)/shard_map/all_to_all | solution.py:482
  73.3 5.4 %collective-permute-start.7 = (f32[160,256]{1,0:T(8,128)S(1)}, f32[160,256]{1,0:T(8,128)S(1)}, u32[]{:S(2)}, u32[]{:S(2)}) collective-permute-start(f32[160,256]{1,0:T(8,128)S(1)} %add.15.own_ref), channel_id=1, source_target_pairs={{0,2},{1,3},{2,0},{3,1},{4,6},{5,7},{6,4},{7,5},{8,10},{9,11},{10,... | collective-permute-start | bytes 491528 | tf_op jit(solution)/shard_map/ppermute | solution.py:487
  74.9 1.2 %collective-permute-start.4 = (f32[8,128]{1,0:T(8,128)S(1)}, f32[8,128]{1,0:T(8,128)S(1)}, u32[]{:S(2)}, u32[]{:S(2)}) collective-permute-start(f32[8,128]{1,0:T(8,128)S(1)} %get-tuple-element.27), channel_id=1, source_target_pairs={{0,1},{1,0},{2,3},{3,2},{4,5},{5,4},{6,7},{7,6},{8,9},{9,8},{10,11... | collective-permute-start | bytes 12296 | tf_op jit(solution)/shard_map/ppermute | solution.py:487
  76.1 3.6 %collective-permute-start.5 = (f32[8,128]{1,0:T(8,128)S(1)}, f32[8,128]{1,0:T(8,128)S(1)}, u32[]{:S(2)}, u32[]{:S(2)}) collective-permute-start(f32[8,128]{1,0:T(8,128)S(1)} %add.14.refs_0_.edge_ref), channel_id=1, source_target_pairs={{0,2},{1,3},{2,0},{3,1},{4,6},{5,7},{6,4},{7,5},{8,10},{9,11},{10,... | collective-permute-start | bytes 12296 | tf_op jit(solution)/shard_map/ppermute | solution.py:487
  90.4 13.3 %all-to-all-start.4 = ((f32[32,8,128]{2,1,0:T(8,128)}), f32[32,8,128]{2,1,0:T(8,128)S(1)}, u32[]{:S(2)}, u32[]{:S(2)}) async-start(f32[32,8,128]{2,1,0:T(8,128)} %get-tuple-element.34), calls=%async_computation.4 | async-start | bytes 262144 | tf_op jit(solution)/shard_map/all_to_all | solution.py:482

commit v4 on v3

--- a/solution.py
+++ b/solution.py
@@ -76,9 +76,9 @@
 
 
 def knot_backward_kernel(arrive, live_ref, place_ref, *refs):
-    observed, (scalar_ref, table_out, knot_acc) = refs[:6], refs[6:9]
+    observed, refs = refs[:6], refs[6:]
     if arrive:
-        buffers, sems = refs[9:15], refs[15]
+        table_out, knot_acc, *buffers, sems = refs
         copies = [
             pltpu.make_async_copy(source, target, sems.at[which])
             for which, (source, target) in enumerate(zip(observed, buffers))
@@ -86,10 +86,25 @@
         for copy in copies:
             copy.start()
         observed = buffers
-    knot_ref, frac_ref, att_coef_ref, value_ref, cal_coef_ref, tile_cal_ref = observed
+    else:
+        scalar_ref, table_out, knot_acc = refs
+    value_ref, cal_coef_ref, tile_cal_ref, knot_ref, frac_ref, att_coef_ref = observed
     knot_acc[...] = jnp.zeros_like(knot_acc)
     if arrive:
-        for copy in copies:
+        for copy in copies[:3]:
+            copy.wait()
+
+    values = value_ref[...]
+    values = values * live_mask(live_ref, 0, values.shape) * cal_coef_ref[...]
+    blocks = product(
+        one_hot(tile_cal_ref[...], CALB_DEV), jnp.concatenate(two_parts(values), axis=1), ((1,), (0,))
+    )
+    width = values.shape[1]
+    blocks = blocks[:, :width] + blocks[:, width:]
+    blocks = jnp.concatenate([blocks[: CALB_DEV // 2], blocks[CALB_DEV // 2 :]], axis=1)
+    store_rows(table_out, KNOT_ROWS, blocks)
+    if arrive:
+        for copy in copies[3:]:
             copy.wait()
 
     @pl.loop(0, knot_ref.shape[0] // WIDE_GROUP)
@@ -135,20 +150,12 @@
         head = pltpu.roll(head, 2 * comp + 1, 1)
         edges = jnp.where((lane == 2 * comp) & (row < 3), tail, edges)
         edges = jnp.where((lane == 2 * comp + 1) & (row < 3), head, edges)
-    edges = scalar_ref[...] + pltpu.roll(edges, SLOT * place_ref[0], 1)
+    edges = pltpu.roll(edges, SLOT * place_ref[0], 1)
+    if not arrive:
+        edges = edges + scalar_ref[...]
     edges = jnp.concatenate([edges, jnp.zeros_like(edges)], axis=1)
     for device in range(table_out.shape[0]):
         table_out[device, table_out.shape[1] - 8 :, :] = edges
-
-    values = value_ref[...]
-    values = values * live_mask(live_ref, 0, values.shape) * cal_coef_ref[...]
-    blocks = product(
-        one_hot(tile_cal_ref[...], CALB_DEV), jnp.concatenate(two_parts(values), axis=1), ((1,), (0,))
-    )
-    width = values.shape[1]
-    blocks = blocks[:, :width] + blocks[:, width:]
-    blocks = jnp.concatenate([blocks[: CALB_DEV // 2], blocks[CALB_DEV // 2 :]], axis=1)
-    store_rows(table_out, KNOT_ROWS, blocks)
 
 
 def star_backward_kernel(live_ref, star_ref, star_coef_ref, value_ref, after_ref, star_out, star_acc):
@@ -205,28 +212,16 @@
     return array
 
 
-def over_devices(ref):
-    total = ref[0]
-    for device in range(1, ref.shape[0]):
-        total = total + ref[device]
-    return total
-
-
 def first_step(edges):
     return picked(edges, 0), picked(edges, 1)
 
 
-def star_forward_kernel(n_seg, later, star_ref, star_coef_ref, own_ref, other_ref, *refs):
-    if later:
-        edge_ref, other_edge_ref, star_0_ref = refs[:3]
-    image_ref, star_out, scalar_out, star_parts_ref = refs[-4:]
-    star_x = own_ref[...] + other_ref[...]
-    if later:
-        norm_0, square_0 = first_step(edge_ref[...] + other_edge_ref[...])
-        star_x = star_0_ref[...] - norm_0 / square_0 * star_x
+def star_forward_kernel(n_seg, star_ref, star_coef_ref, *refs):
+    term_refs, (image_ref, star_out, star_parts_ref) = refs[:n_seg], refs[n_seg:]
+    star_x = term_refs[0][...]
+    for term_ref in term_refs[1:]:
+        star_x = star_x + term_ref[...]
     star_out[...] = star_x
-    norm = jnp.sum(star_x * star_x, keepdims=True) / n_seg
-    scalar_out[...] = with_scalars(jnp.zeros((8, 128), F32), [(0, norm)])
     star_high, star_low = two_parts(star_x)
     star_parts_ref[:STAR_ROWS] = star_high
     star_parts_ref[STAR_ROWS:] = star_low
@@ -262,12 +257,12 @@
 
 def knot_forward_kernel(
     n_stars, n_seg, later, live_ref, place_ref, knot_ref, frac_ref, att_coef_ref, cal_coef_ref,
-    tile_cal_ref, star_image_ref, star_scalar_ref, table_x_ref, edge_ref, other_edge_ref, *refs,
+    tile_cal_ref, star_image_ref, star_x_ref, table_x_ref, edge_ref, other_edge_ref, *refs,
 ):
     if later:
-        table_0_ref, ahead_0_ref, image_0_ref, image_ref, table_out, scalar_out = refs[:6]
+        star_0_ref, table_0_ref, image_0_ref, image_ref, table_out, scalar_out = refs[:6]
     else:
-        image_ref, table_out, scalar_out, ahead_out = refs[:4]
+        image_ref, table_out, scalar_out = refs[:3]
     knot_parts_ref, cal_ref = refs[-2:]
     segment = place_ref[0]
     lane = lax.broadcasted_iota(jnp.int32, (8, 128), 1)
@@ -293,15 +288,18 @@
         pieces.append(top + jnp.concatenate([shifted, jnp.zeros_like(shifted)], axis=1))
         pieces.append(table[comp * FINE + 8 : (comp + 1) * FINE])
     table = jnp.concatenate(pieces + [table[KNOT_ROWS:]], axis=0)
+    table_out[...] = table
     if later:
         norm_0, square_0 = first_step(edges)
         step = norm_0 / square_0
-        table = table_0_ref[...] - step * table
-        ahead = ahead_0_ref[...] - step * ahead
+        star_change = star_0_ref[...] - step * star_x_ref[...]
+        table_change = table_0_ref[...] - step * table
     else:
-        ahead_out[...] = ahead
-    table_out[...] = table
-    norm = picked(star_scalar_ref[...], 0) + jnp.sum(table * table, keepdims=True) / n_stars
+        star_change, table_change = star_x_ref[...], table
+    norm = (
+        jnp.sum(star_change * star_change, keepdims=True) / n_seg
+        + jnp.sum(table_change * table_change, keepdims=True) / n_stars
+    )
 
     beyond = []
     for comp in range(4):
@@ -347,40 +345,43 @@
             image_rows.append(jnp.sum(both, axis=0, keepdims=True))
         image = jnp.concatenate(image_rows, axis=0) + cal_ref[rows, :]
         image = image * live_mask(live_ref, first, image.shape)
+        if later:
+            image_0 = image_0_ref[rows, :]
+            image = image_0 - step * image
+            image_ref[rows, :] = image
+            return sums[0] + image * image, sums[1] + image * image_0
         image_ref[rows, :] = image
-        if later:
-            return sums[0] + image * image, sums[1] + image * image_0_ref[rows, :]
         return (sums[0] + image * image,)
 
     zero = jnp.zeros((GROUP, knot_ref.shape[1]), F32)
     start = (zero, zero) if later else (zero,)
     sums = lax.fori_loop(0, knot_ref.shape[0] // GROUP, one_group, start, unroll=2)
     scalars = [(0, norm)] + [(1 + which, jnp.sum(part, keepdims=True)) for which, part in enumerate(sums)]
-    result = with_scalars(jnp.zeros((8, 128), F32), scalars)
-    for device in range(scalar_out.shape[0]):
-        scalar_out[device] = result
+    scalar_out[...] = with_scalars(jnp.zeros((8, 128), F32), scalars)
 
 
 def output_kernel(
-    live_ref, edge_ref, other_edge_ref, scalar_ref, star_0_ref, star_1_ref, att_0_ref, att_1_ref, table_0_ref,
-    table_1_ref, value_ref, image_0_ref, image_1_ref, star_out, att_out, cal_out, residual_out,
+    live_ref, edge_ref, other_edge_ref, scalar_ref, other_scalar_ref, star_0_ref, star_h_ref, att_0_ref,
+    att_h_ref, table_0_ref, table_h_ref, value_ref, image_0_ref, image_1_ref, star_out, att_out, cal_out,
+    residual_out,
 ):
     norm_0, square_0 = first_step(edge_ref[...] + other_edge_ref[...])
-    everyone = over_devices(scalar_ref)
+    everyone = scalar_ref[...] + other_scalar_ref[...]
     norm_1, square_1, cross = [picked(everyone, which) for which in range(3)]
+    step_0 = norm_0 / square_0
     ratio = norm_1 / norm_0
     step_1 = norm_1 / (square_1 + 2.0 * ratio * cross + ratio * ratio * square_0)
-    scale = norm_0 / square_0 + step_1 * ratio
-
-    def combined(old, new):
-        return scale * old + step_1 * new
-
-    star_out[...] = combined(star_0_ref[...], star_1_ref[...])
-    att_out[...] = combined(att_0_ref[...], att_1_ref[...])
-    cal = combined(table_0_ref[KNOT_ROWS:, :], table_1_ref[KNOT_ROWS:, :])
+    scale = step_0 + step_1 * ratio
+
+    def combined(old, change):
+        return scale * old + step_1 * (old - step_0 * change)
+
+    star_out[...] = combined(star_0_ref[...], star_h_ref[...])
+    att_out[...] = combined(att_0_ref[...], att_h_ref[...])
+    cal = combined(table_0_ref[KNOT_ROWS:, :], table_h_ref[KNOT_ROWS:, :])
     cal_out[...] = jnp.concatenate([cal[:, :128], cal[:, 128:]], axis=0)
     values = value_ref[...] * live_mask(live_ref, 0, value_ref.shape)
-    residual_out[...] = values - combined(image_0_ref[...], image_1_ref[...])
+    residual_out[...] = values - scale * image_0_ref[...] - step_1 * image_1_ref[...]
 
 
 def in_vmem(count):
@@ -409,17 +410,17 @@
     obs_star, obs_knot, obs_frac, star_coef, att_coef, cal_coef, tile_cal, live_tiles, obs_value
 ):
     n_stars, n_seg = lax.axis_size("stars"), lax.axis_size("seg")
-    count = n_stars * n_seg
     tile_count, width = obs_star.shape
     tile_row = tile_cal[None, :]
     place = lax.axis_index("seg").astype(jnp.int32)[None]
     image_shape = shaped(tile_count, width)
     table_shape = shaped(TABLE_ROWS, COARSE)
     star_shape = shaped(STAR_ROWS, COARSE)
-    scalar_shape, scalar_copies = shaped(8, 128), shaped(count, 8, 128)
-
-    def knot_backward(values, scalars, arrive):
-        observed = (obs_knot, obs_frac, att_coef, values, cal_coef, tile_row)
+    scalar_shape = shaped(8, 128)
+
+    def knot_backward(values, *scalars):
+        arrive = not scalars
+        observed = (values, cal_coef, tile_row, obs_knot, obs_frac, att_coef)
         scratch = [pltpu.VMEM((2 * KNOT_HALF, COARSE), F32)]
         if arrive:
             scratch += [pltpu.VMEM(array.shape, array.dtype) for array in observed]
@@ -427,19 +428,19 @@
         return pl.pallas_call(
             functools.partial(knot_backward_kernel, arrive),
             out_shape=shaped(n_stars, TABLE_ROWS // n_stars + 8, COARSE),
-            in_specs=in_smem(2) + (in_hbm if arrive else in_vmem)(len(observed)) + in_vmem(1),
+            in_specs=in_smem(2) + (in_hbm if arrive else in_vmem)(len(observed)) + in_vmem(len(scalars)),
             out_specs=in_vmem(1)[0],
             scratch_shapes=scratch,
             compiler_params=ARRIVE_PARAMS if arrive else PARAMS,
             cost_estimate=PASS_COST,
             name="knot_backward",
-        )(live_tiles, place, *observed, scalars)
+        )(live_tiles, place, *observed, *scalars)
 
     def star_backward(values, after):
         return pl.pallas_call(
             star_backward_kernel,
             out_shape=star_shape,
-            in_specs=in_smem(1) + in_vmem(3) + [pl.BlockSpec(memory_space=pl.ANY)],
+            in_specs=in_smem(1) + in_vmem(3) + in_hbm(1),
             out_specs=in_vmem(1)[0],
             scratch_shapes=[pltpu.VMEM((2 * STAR_ROWS, COARSE), F32)],
             compiler_params=PARAMS,
@@ -447,25 +448,25 @@
             name="star_backward",
         )(live_tiles, obs_star, star_coef, values, after)
 
-    def star_forward(own, other, *first):
+    def star_forward(*terms):
         return pl.pallas_call(
-            functools.partial(star_forward_kernel, n_seg, bool(first)),
-            out_shape=(image_shape, star_shape, scalar_shape),
-            in_specs=in_vmem(4 + len(first)),
-            out_specs=tuple(in_vmem(3)),
+            functools.partial(star_forward_kernel, n_seg),
+            out_shape=(image_shape, star_shape),
+            in_specs=in_vmem(2 + n_seg),
+            out_specs=tuple(in_vmem(2)),
             scratch_shapes=[pltpu.VMEM((2 * STAR_ROWS, COARSE), BF16)],
             compiler_params=PARAMS,
             cost_estimate=PASS_COST,
             name="star_forward",
-        )(obs_star, star_coef, own, other, *first)
-
-    def knot_forward(star_image, star_scalars, table, edge, other_edge, *first):
-        outs = (image_shape, table_shape) + ((scalar_copies,) if first else (shaped(1, 8, 128), scalar_shape))
+        )(obs_star, star_coef, *terms)
+
+    def knot_forward(*arrays):
+        later = len(arrays) > 5
         return pl.pallas_call(
-            functools.partial(knot_forward_kernel, n_stars, n_seg, bool(first)),
-            out_shape=outs,
-            in_specs=in_smem(2) + in_vmem(10 + len(first)),
-            out_specs=tuple(in_vmem(len(outs))),
+            functools.partial(knot_forward_kernel, n_stars, n_seg, later),
+            out_shape=(image_shape, table_shape, scalar_shape),
+            in_specs=in_smem(2) + in_vmem(5 + len(arrays)),
+            out_specs=tuple(in_vmem(3)),
             scratch_shapes=[
                 pltpu.VMEM((2 * KNOT_HALF, COARSE), BF16),
                 pltpu.VMEM((tile_count, width), F32),
@@ -473,22 +474,19 @@
             compiler_params=PARAMS,
             cost_estimate=PASS_COST,
             name="knot_forward",
-        )(
-            live_tiles, place, obs_knot, obs_frac, att_coef, cal_coef, tile_row, star_image,
-            star_scalars, table, edge, other_edge, *first,
-        )
+        )(live_tiles, place, obs_knot, obs_frac, att_coef, cal_coef, tile_row, *arrays)
 
     def swap(blocks, axes):
         return lax.all_to_all(blocks, axes, 0, 0)
 
-    def seg_terms(array):
-        distance = 1
-        while True:
-            other = lax.ppermute(array, "seg", [(i, i ^ distance) for i in range(n_seg)])
-            distance *= 2
-            if distance >= n_seg:
-                return array, other
-            array = array + other
+    def partner(array, axis, distance):
+        return lax.ppermute(array, axis, [(i, i ^ distance) for i in range(lax.axis_size(axis))])
+
+    def last_terms(array, *axes):
+        steps = [(axis, 1 << bit) for axis in axes for bit in range(lax.axis_size(axis).bit_length() - 1)]
+        for axis, distance in steps[:-1]:
+            array = array + partner(array, axis, distance)
+        return array, partner(array, *steps[-1])
 
     def table_sum(table):
         blocks = swap(table, "stars")
@@ -501,20 +499,21 @@
             cost_estimate=SMALL_COST,
             name="table_sum",
         )(blocks)
-        return (swap(copies, "stars").reshape(TABLE_ROWS, COARSE), *seg_terms(edge))
-
-    def half(values, scalars, arrive):
-        table = knot_backward(values, scalars, arrive)
+        return (swap(copies, "stars").reshape(TABLE_ROWS, COARSE), *last_terms(edge, "seg"))
+
+    def half(values, *scalars):
+        table = knot_backward(values, *scalars)
         star = star_backward(values, table)
-        return (*seg_terms(star), *table_sum(table))
-
-    own, other, table, edge, other_edge = half(obs_value, jnp.zeros((8, 128), F32), True)
-    star_image, star_0, star_scalars = star_forward(own, other)
-    image_0, table_0, scalars, ahead_0 = knot_forward(star_image, star_scalars, table, edge, other_edge)
-    own, other, table, edge, other_edge = half(image_0, scalars[0], False)
-    star_image, star_1, star_scalars = star_forward(own, other, edge, other_edge, star_0)
-    image_1, table_1, scalars = knot_forward(
-        star_image, star_scalars, table, edge, other_edge, table_0, ahead_0, image_0
+        stars = [star] + [partner(star, "seg", distance) for distance in range(1, n_seg)]
+        table, *edges = table_sum(table)
+        star_image, star = star_forward(*stars)
+        return star_image, star, table, edges
+
+    star_image, star_0, table, edges = half(obs_value)
+    image_0, table_0, scalars = knot_forward(star_image, star_0, table, *edges)
+    star_image, star_h, table, edges = half(image_0, scalars)
+    image_1, table_h, scalars = knot_forward(
+        star_image, star_h, table, *edges, star_0, table_0, image_0
     )
 
     def star_order(star):
@@ -527,15 +526,14 @@
     return pl.pallas_call(
         output_kernel,
         out_shape=(shaped(5, STAR_DEV), shaped(4, KNOT_DEV), shaped(CALB_DEV, width), image_shape),
-        in_specs=in_smem(1) + in_vmem(12),
+        in_specs=in_smem(1) + in_vmem(13),
         out_specs=tuple(in_vmem(4)),
         compiler_params=PARAMS,
         cost_estimate=SMALL_COST,
         name="outputs",
     )(
-        live_tiles, edge, other_edge, swap(scalars, ("stars", "seg")), star_order(star_0),
-        star_order(star_1), att_order(table_0), att_order(table_1), table_0, table_1, obs_value,
-        image_0, image_1,
+        live_tiles, *edges, *last_terms(scalars, "seg", "stars"), star_order(star_0), star_order(star_h),
+        att_order(table_0), att_order(table_h), table_0, table_h, obs_value, image_0, image_1,
     )
 
 

time: 105 us -> 124 us (1.18)
  blocking collectives: 0 us -> 34.9 us
  starting transfers between devices: 29.8 us -> 21.7 us
  waiting for transfers between devices: 24.6 us -> 19.6 us
  Pallas kernels: 46.3 us -> 44 us
    all_to_all x0 -> x2, blocking collectives: none -> 34.9 us  [swap(): return lax.all_to_all(blocks, axes, 0, 0)]
    all_to_all x5 -> x2, starting transfers between devices: 25.5 us -> 6.96 us  [swap(): return lax.all_to_all(blocks, axes, 0, 0)]
    all_to_all x5 -> x2, waiting for transfers between devices: 17.1 us -> 0.01 us  [swap(): return lax.all_to_all(blocks, axes, 0, 0)]
    ppermute x8 -> x15, waiting for transfers between devices: 7.52 us -> 19.6 us  [partner(): lax.ppermute(array, axis, [(i, i ^ distance) for i in range(lax.axis_size...]
    ppermute x8 -> x15, starting transfers between devices: 4.39 us -> 14.7 us  [partner(): lax.ppermute(array, axis, [(i, i ^ distance) for i in range(lax.axis_size...]
    pallas_call x2, Pallas kernels: 14.5 us -> 13.2 us  [knot_backward(): pl.pallas_call(functools.partial(knot_backward_kernel, arrive), out_shape...]
  transfers between devices with their start and end apart: 13 -> 17, of which waited for: 8 -> 11; matrix products, arithmetic and copies ran while one was open for 1% -> 1% of each run, Pallas kernels for 19% -> 15%
where the time goes in v4:
time: 124 us; the launch traced here: 123 us
  Pallas kernels  44 us (35%)
  blocking collectives  34.9 us (28%)
  starting transfers between devices  21.7 us (18%)
  waiting for transfers between devices  19.6 us (16%)
  local copies, waits for them, and re-layouts  1.68 us (1%)
  between operations  1.55 us (1%)
    all_to_all x2, blocking collectives, swap(): return lax.all_to_all(blocks, axes, 0, 0)  34.9 us
    ppermute x15, waiting for transfers between devices, partner(): lax.ppermute(array, axis, [(i, i ^ distance) for i in range(lax.axis_size...  19.6 us
    ppermute x15, starting transfers between devices, partner(): lax.ppermute(array, axis, [(i, i ^ distance) for i in range(lax.axis_size...  14.7 us
    pallas_call x2, Pallas kernels, knot_backward(): pl.pallas_call(functools.partial(knot_backward_kernel, arrive), out_shape...  13.2 us
    pallas_call x2, Pallas kernels, knot_forward(): pl.pallas_call(functools.partial(knot_forward_kernel, n_stars, n_seg, lat...  9.99 us
    pallas_call x2, Pallas kernels, star_forward(): pl.pallas_call(functools.partial(star_forward_kernel, n_seg), out_shape=(...  9.51 us
    pallas_call x2, Pallas kernels, star_backward(): pl.pallas_call(star_backward_kernel, out_shape=star_shape, in_specs=in_sm...  8.82 us
    all_to_all x2, starting transfers between devices, swap(): return lax.all_to_all(blocks, axes, 0, 0)  6.96 us
  transfers between devices with their start and end apart: 17, of which 11 were waited for; matrix products, arithmetic and copies ran while one was open for 1% of the time, Pallas kernels for 15%

profile of v4, /device:TPU:0, one launch (start us, length us, event | category | flops | bytes accessed | tf_op | source)
XLA Modules:
  0.0 123.5 jit_solution(29352790123083909)
XLA Ops:
  1.3 7.5 %knot_backward.2.after_ref = f32[8,40,256]{2,1,0:T(8,128)} custom-call(s32[1]{0:T(128)S(6)} %copy.17.live_ref, s32[1]{0:T(128)} %bitcast.place_ref, f32[128,128]{1,0:T(8,128)} %value_ref.3, f32[128,128]{1,0:T(8,128)} %cal_coef_ref.3, s32[1,128]{1,0:T(1,128)} %bitcast.10, s32[128,128]{1,0:T(8,128)} %knot_ref.3, f32[128,128]{1,0:T(8,128)} %frac_ref.3, ...), custom_call_target="tpu_custom_call" | custom-call | flops 3000000000 | bytes 1000000 | tf_op jit(solution)/shard_map/knot_backward/pallas_call | solution.py:428
  8.8 18.2 %all_to_all.20.block_ref = f32[8,40,256]{2,1,0:T(8,128)S(1)} all-to-all(f32[8,40,256]{2,1,0:T(8,128)} %knot_backward.2.after_ref), channel_id=1, replica_groups=mesh['stars'=8,'seg'=4] {'stars'}, dimensions={0} | all-to-all | bytes 655360 | tf_op jit(solution)/shard_map/all_to_all | solution.py:480
  27.7 3.5 %all-to-all-start.1 = ((f32[8,32,256]{2,1,0:T(8,128)}), f32[8,32,256]{2,1,0:T(8,128)S(1)}, u32[]{:S(2)}, u32[]{:S(2)}) async-start(f32[8,32,256]{2,1,0:T(8,128)} %get-tuple-element.20), calls=%async_computation.1 | async-start | bytes 524288 | tf_op jit(solution)/shard_map/all_to_all | solution.py:480
  31.3 4.4 %star_backward.2.refs_0_ = f32[160,256]{1,0:T(8,128)S(1)} custom-call(s32[1]{0:T(128)S(6)} %copy.17.live_ref, s32[128,128]{1,0:T(8,128)S(1)} %copy-done.4, f32[5,128,128]{2,1,0:T(8,128)S(1)} %copy-done.2, f32[128,128]{1,0:T(8,128)S(1)} %copy-done.1, f32[8,40,256]{2,1,0:T(8,128)S(1)} %copy-done), custom_call_target="tpu_custom_call" | custom-call | flops 3000000000 | bytes 1000000 | tf_op jit(solution)/shard_map/star_backward/pallas_call | solution.py:440
  38.8 1.6 %collective-permute-start.4 = (f32[8,128]{1,0:T(8,128)S(1)}, f32[8,128]{1,0:T(8,128)S(1)}, u32[]{:S(2)}, u32[]{:S(2)}) collective-permute-start(f32[8,128]{1,0:T(8,128)S(1)} %add.18.edge_ref), channel_id=1, source_target_pairs={{0,2},{1,3},{2,0},{3,1},{4,6},{5,7},{6,4},{7,5},{8,10},{9,11},{10,... | collective-permute-start | bytes 12296 | tf_op jit(solution)/shard_map/ppermute | solution.py:483
  40.4 1.8 %collective-permute-done.2.refs_3_ = f32[160,256]{1,0:T(8,128)S(1)} collective-permute-done((f32[160,256]{1,0:T(8,128)S(1)}, f32[160,256]{1,0:T(8,128)S(1)}, u32[]{:S(2)}, u32[]{:S(2)}) %collective-permute-start.2) | collective-permute-done | bytes 163872 | tf_op jit(solution)/shard_map/ppermute | solution.py:483
  42.2 3.6 %collective-permute-done.1.refs_2_ = f32[160,256]{1,0:T(8,128)S(1)} collective-permute-done((f32[160,256]{1,0:T(8,128)S(1)}, f32[160,256]{1,0:T(8,128)S(1)}, u32[]{:S(2)}, u32[]{:S(2)}) %collective-permute-start.1) | collective-permute-done | bytes 163872 | tf_op jit(solution)/shard_map/ppermute | solution.py:483
  45.8 4.8 %star_forward.2 = (f32[128,128]{1,0:T(8,128)S(1)}, f32[160,256]{1,0:T(8,128)S(1)}) custom-call(s32[128,128]{1,0:T(8,128)S(1)} %copy-done.4, f32[5,128,128]{2,1,0:T(8,128)S(1)} %copy-done.2, f32[160,256]{1,0:T(8,128)S(1)} %star_backward.2.refs_0_, f32[160,256]{1,0:T(8,128)S(1)} %collective-permute-done.refs_1_, ...), custom_call_target="tpu_custom_call" | custom-call | flops 3000000000 | bytes 1000000 | tf_op jit(solution)/shard_map/star_forward/pallas_call | solution.py:452
  51.2 5.0 %knot_forward.2 = (f32[128,128]{1,0:T(8,128)S(1)}, f32[256,256]{1,0:T(8,128)S(1)}, f32[8,128]{1,0:T(8,128)S(1)}) custom-call(s32[1]{0:T(128)S(6)} %copy.17.live_ref, s32[1]{0:T(128)} %bitcast.place_ref, s32[128,128]{1,0:T(8,128)S(1)} %copy-done.5, f32[128,128]{1,0:T(8,128)S(1)} %copy-done.6, f32[4,128,128]{2,1,0:T(8,128)S(1)} %copy-done.3, ...), custom_call_target="tpu_custom_call" | custom-call | flops 3000000000 | bytes 1000000 | tf_op jit(solution)/shard_map/knot_forward/pallas_call | solution.py:465
  56.2 5.8 %knot_backward.3.after_ref = f32[8,40,256]{2,1,0:T(8,128)S(1)} custom-call(s32[1]{0:T(128)S(6)} %copy.17.live_ref, s32[1]{0:T(128)} %bitcast.place_ref, f32[128,128]{1,0:T(8,128)S(1)} %get-tuple-element.22.refs_0_.value_ref.refs_2_.image_0_ref, f32[128,128]{1,0:T(8,128)S(1)} %copy-done.7, s32[1,128]{1,0:T(1,128)S(1)} %bitcast.12, s32[128,128]{1,0:T(8,128)S(1)} %copy-done.5, ...), custom_call_target="tpu_custom_call" | custom-call | flops 3000000000 | bytes 1000000 | tf_op jit(solution)/shard_map/knot_backward/pallas_call | solution.py:428
  62.0 16.8 %all_to_all.21.block_ref = f32[8,40,256]{2,1,0:T(8,128)S(1)} all-to-all(f32[8,40,256]{2,1,0:T(8,128)S(1)} %knot_backward.3.after_ref), channel_id=1, replica_groups=mesh['stars'=8,'seg'=4] {'stars'}, dimensions={0} | all-to-all | bytes 655360 | tf_op jit(solution)/shard_map/all_to_all | solution.py:480
  79.5 3.4 %all-to-all-start.3 = ((f32[8,32,256]{2,1,0:T(8,128)}), f32[8,32,256]{2,1,0:T(8,128)S(1)}, u32[]{:S(2)}, u32[]{:S(2)}) async-start(f32[8,32,256]{2,1,0:T(8,128)} %get-tuple-element.27), calls=%async_computation.3 | async-start | bytes 524288 | tf_op jit(solution)/shard_map/all_to_all | solution.py:480
  82.9 4.4 %star_backward.3.refs_0_ = f32[160,256]{1,0:T(8,128)S(1)} custom-call(s32[1]{0:T(128)S(6)} %copy.17.live_ref, s32[128,128]{1,0:T(8,128)S(1)} %copy-done.4, f32[5,128,128]{2,1,0:T(8,128)S(1)} %copy-done.2, f32[128,128]{1,0:T(8,128)S(1)} %get-tuple-element.22.refs_0_.value_ref.refs_2_.image_0_ref, f32[8,40,256]{2,1,0:T(8,128)S(1)} %knot_backward.3.after_ref), custom_call_target="tpu_custom_call" | custom-call | flops 3000000000 | bytes 1000000 | tf_op jit(solution)/shard_map/star_backward/pallas_call | solution.py:440
  90.9 3.0 %collective-permute-done.9.refs_3_ = f32[160,256]{1,0:T(8,128)S(1)} collective-permute-done((f32[160,256]{1,0:T(8,128)S(1)}, f32[160,256]{1,0:T(8,128)S(1)}, u32[]{:S(2)}, u32[]{:S(2)}) %collective-permute-start.9) | collective-permute-done | bytes 163872 | tf_op jit(solution)/shard_map/ppermute | solution.py:483
  93.9 1.9 %collective-permute-done.8.refs_2_ = f32[160,256]{1,0:T(8,128)S(1)} collective-permute-done((f32[160,256]{1,0:T(8,128)S(1)}, f32[160,256]{1,0:T(8,128)S(1)}, u32[]{:S(2)}, u32[]{:S(2)}) %collective-permute-start.8) | collective-permute-done | bytes 163872 | tf_op jit(solution)/shard_map/ppermute | solution.py:483
  95.8 4.8 %star_forward.3 = (f32[128,128]{1,0:T(8,128)S(1)}, f32[160,256]{1,0:T(8,128)S(1)}) custom-call(s32[128,128]{1,0:T(8,128)S(1)} %copy-done.4, f32[5,128,128]{2,1,0:T(8,128)S(1)} %copy-done.2, f32[160,256]{1,0:T(8,128)S(1)} %star_backward.3.refs_0_, f32[160,256]{1,0:T(8,128)S(1)} %collective-permute-done.7.refs_1_, ...), custom_call_target="tpu_custom_call" | custom-call | flops 3000000000 | bytes 1000000 | tf_op jit(solution)/shard_map/star_forward/pallas_call | solution.py:452
  100.6 5.0 %knot_forward.3 = (f32[128,128]{1,0:T(8,128)S(1)}, f32[256,256]{1,0:T(8,128)S(1)}, f32[8,128]{1,0:T(8,128)S(1)}) custom-call(s32[1]{0:T(128)S(6)} %copy.17.live_ref, s32[1]{0:T(128)} %bitcast.place_ref, s32[128,128]{1,0:T(8,128)S(1)} %copy-done.5, f32[128,128]{1,0:T(8,128)S(1)} %copy-done.6, f32[4,128,128]{2,1,0:T(8,128)S(1)} %copy-done.3, ...), custom_call_target="tpu_custom_call" | custom-call | flops 3000000000 | bytes 1000000 | tf_op jit(solution)/shard_map/knot_forward/pallas_call | solution.py:465
  107.2 1.7 %collective-permute-start.11 = (f32[8,128]{1,0:T(8,128)S(1)}, f32[8,128]{1,0:T(8,128)S(1)}, u32[]{:S(2)}, u32[]{:S(2)}) collective-permute-start(f32[8,128]{1,0:T(8,128)S(1)} %add.20), channel_id=1, source_target_pairs={{0,2},{1,3},{2,0},{3,1},{4,6},{5,7},{6,4},{7,5},{8,10},{9,11},{10,... | collective-permute-start | bytes 12296 | tf_op jit(solution)/shard_map/ppermute | solution.py:483
  108.9 1.9 %collective-permute-done.11 = f32[8,128]{1,0:T(8,128)S(1)} collective-permute-done((f32[8,128]{1,0:T(8,128)S(1)}, f32[8,128]{1,0:T(8,128)S(1)}, u32[]{:S(2)}, u32[]{:S(2)}) %collective-permute-start.11) | collective-permute-done | bytes 4128 | tf_op jit(solution)/shard_map/ppermute | solution.py:483
  110.8 1.7 %collective-permute-start.12 = (f32[8,128]{1,0:T(8,128)S(1)}, f32[8,128]{1,0:T(8,128)S(1)}, u32[]{:S(2)}, u32[]{:S(2)}) collective-permute-start(f32[8,128]{1,0:T(8,128)S(1)} %add.21), channel_id=1, source_target_pairs={{0,4},{4,0},{8,12},{12,8},{16,20},{20,16},{24,28},{28,24},{1,5},{5... | collective-permute-start | bytes 12296 | tf_op jit(solution)/shard_map/ppermute | solution.py:483
  112.5 1.9 %collective-permute-done.12 = f32[8,128]{1,0:T(8,128)S(1)} collective-permute-done((f32[8,128]{1,0:T(8,128)S(1)}, f32[8,128]{1,0:T(8,128)S(1)}, u32[]{:S(2)}, u32[]{:S(2)}) %collective-permute-start.12) | collective-permute-done | bytes 4128 | tf_op jit(solution)/shard_map/ppermute | solution.py:483
  114.4 1.7 %collective-permute-start.13 = (f32[8,128]{1,0:T(8,128)S(1)}, f32[8,128]{1,0:T(8,128)S(1)}, u32[]{:S(2)}, u32[]{:S(2)}) collective-permute-start(f32[8,128]{1,0:T(8,128)S(1)} %add.22), channel_id=1, source_target_pairs={{0,8},{4,12},{8,0},{12,4},{16,24},{20,28},{24,16},{28,20},{1,9},{5... | collective-permute-start | bytes 12296 | tf_op jit(solution)/shard_map/ppermute | solution.py:483
  116.1 1.9 %collective-permute-done.13 = f32[8,128]{1,0:T(8,128)S(1)} collective-permute-done((f32[8,128]{1,0:T(8,128)S(1)}, f32[8,128]{1,0:T(8,128)S(1)}, u32[]{:S(2)}, u32[]{:S(2)}) %collective-permute-start.13) | collective-permute-done | bytes 4128 | tf_op jit(solution)/shard_map/ppermute | solution.py:483
  118.0 2.6 %collective-permute-start.14 = (f32[8,128]{1,0:T(8,128)S(1)}, f32[8,128]{1,0:T(8,128)S(1)}, u32[]{:S(2)}, u32[]{:S(2)}) collective-permute-start(f32[8,128]{1,0:T(8,128)S(1)} %add.23.scalar_ref), channel_id=1, source_target_pairs={{0,16},{4,20},{8,24},{12,28},{16,0},{20,4},{24,8},{28,12},{1,17},{... | collective-permute-start | bytes 12296 | tf_op jit(solution)/shard_map/ppermute | solution.py:483
  (55 shorter events, 13.1 us)
Async XLA Ops:
  26.9 4.3 %copy-start.2 = (f32[5,128,128]{2,1,0:T(8,128)S(1)}, f32[5,128,128]{2,1,0:T(8,128)}, u32[]{:S(2)}) copy-start(f32[5,128,128]{2,1,0:T(8,128)} %star_coef_ref.7) | copy-start | bytes 983044
  27.7 3.6 %copy-start.1 = (f32[128,128]{1,0:T(8,128)S(1)}, f32[128,128]{1,0:T(8,128)}, u32[]{:S(2)}) copy-start(f32[128,128]{1,0:T(8,128)} %value_ref.3) | copy-start | bytes 196612
  27.7 3.6 %copy-start.4 = (s32[128,128]{1,0:T(8,128)S(1)}, s32[128,128]{1,0:T(8,128)}, u32[]{:S(2)}) copy-start(s32[128,128]{1,0:T(8,128)} %star_ref.7) | copy-start | bytes 196612
  27.7 22.9 %all-to-all-start.1 = ((f32[8,32,256]{2,1,0:T(8,128)}), f32[8,32,256]{2,1,0:T(8,128)S(1)}, u32[]{:S(2)}, u32[]{:S(2)}) async-start(f32[8,32,256]{2,1,0:T(8,128)} %get-tuple-element.20), calls=%async_computation.1 | async-start | bytes 524288 | tf_op jit(solution)/shard_map/all_to_all | solution.py:480
  35.7 6.5 %collective-permute-start.2 = (f32[160,256]{1,0:T(8,128)S(1)}, f32[160,256]{1,0:T(8,128)S(1)}, u32[]{:S(2)}, u32[]{:S(2)}) collective-permute-start(f32[160,256]{1,0:T(8,128)S(1)} %star_backward.2.refs_0_), channel_id=1, source_target_pairs={{0,3},{1,2},{2,1},{3,0},{4,7},{5,6},{6,5},{7,4},{8,11},{9,10},{10,... | collective-permute-start | bytes 491528 | tf_op jit(solution)/shard_map/ppermute | solution.py:483
  35.8 10.0 %collective-permute-start.1 = (f32[160,256]{1,0:T(8,128)S(1)}, f32[160,256]{1,0:T(8,128)S(1)}, u32[]{:S(2)}, u32[]{:S(2)}) collective-permute-start(f32[160,256]{1,0:T(8,128)S(1)} %star_backward.2.refs_0_), channel_id=1, source_target_pairs={{0,2},{1,3},{2,0},{3,1},{4,6},{5,7},{6,4},{7,5},{8,10},{9,11},{10,... | collective-permute-start | bytes 491528 | tf_op jit(solution)/shard_map/ppermute | solution.py:483
  37.3 8.5 %collective-permute-start = (f32[160,256]{1,0:T(8,128)S(1)}, f32[160,256]{1,0:T(8,128)S(1)}, u32[]{:S(2)}, u32[]{:S(2)}) collective-permute-start(f32[160,256]{1,0:T(8,128)S(1)} %star_backward.2.refs_0_), channel_id=1, source_target_pairs={{0,1},{1,0},{2,3},{3,2},{4,5},{5,4},{6,7},{7,6},{8,9},{9,8},{10,11... | collective-permute-start | bytes 491528 | tf_op jit(solution)/shard_map/ppermute | solution.py:483
  37.6 1.2 collective-permute-start.3
  38.8 11.8 %copy-start.3 = (f32[4,128,128]{2,1,0:T(8,128)S(1)}, f32[4,128,128]{2,1,0:T(8,128)}, u32[]{:S(2)}) copy-start(f32[4,128,128]{2,1,0:T(8,128)} %att_coef_ref.3) | copy-start | bytes 786436
  38.8 11.8 %copy-start.5 = (s32[128,128]{1,0:T(8,128)S(1)}, s32[128,128]{1,0:T(8,128)}, u32[]{:S(2)}) copy-start(s32[128,128]{1,0:T(8,128)} %knot_ref.3) | copy-start | bytes 196612
  38.8 11.8 %copy-start.6 = (f32[128,128]{1,0:T(8,128)S(1)}, f32[128,128]{1,0:T(8,128)}, u32[]{:S(2)}) copy-start(f32[128,128]{1,0:T(8,128)} %frac_ref.3) | copy-start | bytes 196612
  38.8 11.8 %copy-start.7 = (f32[128,128]{1,0:T(8,128)S(1)}, f32[128,128]{1,0:T(8,128)}, u32[]{:S(2)}) copy-start(f32[128,128]{1,0:T(8,128)} %cal_coef_ref.3) | copy-start | bytes 196612
  38.8 11.8 %collective-permute-start.4 = (f32[8,128]{1,0:T(8,128)S(1)}, f32[8,128]{1,0:T(8,128)S(1)}, u32[]{:S(2)}, u32[]{:S(2)}) collective-permute-start(f32[8,128]{1,0:T(8,128)S(1)} %add.18.edge_ref), channel_id=1, source_target_pairs={{0,2},{1,3},{2,0},{3,1},{4,6},{5,7},{6,4},{7,5},{8,10},{9,11},{10,... | collective-permute-start | bytes 12296 | tf_op jit(solution)/shard_map/ppermute | solution.py:483
  79.5 21.1 %all-to-all-start.3 = ((f32[8,32,256]{2,1,0:T(8,128)}), f32[8,32,256]{2,1,0:T(8,128)S(1)}, u32[]{:S(2)}, u32[]{:S(2)}) async-start(f32[8,32,256]{2,1,0:T(8,128)} %get-tuple-element.27), calls=%async_computation.3 | async-start | bytes 524288 | tf_op jit(solution)/shard_map/all_to_all | solution.py:480
  87.3 6.5 %collective-permute-start.9 = (f32[160,256]{1,0:T(8,128)S(1)}, f32[160,256]{1,0:T(8,128)S(1)}, u32[]{:S(2)}, u32[]{:S(2)}) collective-permute-start(f32[160,256]{1,0:T(8,128)S(1)} %star_backward.3.refs_0_), channel_id=1, source_target_pairs={{0,3},{1,2},{2,1},{3,0},{4,7},{5,6},{6,5},{7,4},{8,11},{9,10},{10,... | collective-permute-start | bytes 491528 | tf_op jit(solution)/shard_map/ppermute | solution.py:483
  87.4 8.4 %collective-permute-start.8 = (f32[160,256]{1,0:T(8,128)S(1)}, f32[160,256]{1,0:T(8,128)S(1)}, u32[]{:S(2)}, u32[]{:S(2)}) collective-permute-start(f32[160,256]{1,0:T(8,128)S(1)} %star_backward.3.refs_0_), channel_id=1, source_target_pairs={{0,2},{1,3},{2,0},{3,1},{4,6},{5,7},{6,4},{7,5},{8,10},{9,11},{10,... | collective-permute-start | bytes 491528 | tf_op jit(solution)/shard_map/ppermute | solution.py:483
  88.0 7.8 %collective-permute-start.7 = (f32[160,256]{1,0:T(8,128)S(1)}, f32[160,256]{1,0:T(8,128)S(1)}, u32[]{:S(2)}, u32[]{:S(2)}) collective-permute-start(f32[160,256]{1,0:T(8,128)S(1)} %star_backward.3.refs_0_), channel_id=1, source_target_pairs={{0,1},{1,0},{2,3},{3,2},{4,5},{5,4},{6,7},{7,6},{8,9},{9,8},{10,11... | collective-permute-start | bytes 491528 | tf_op jit(solution)/shard_map/ppermute | solution.py:483
  89.2 1.2 collective-permute-start.5
  90.4 10.1 %collective-permute-start.6 = (f32[8,128]{1,0:T(8,128)S(1)}, f32[8,128]{1,0:T(8,128)S(1)}, u32[]{:S(2)}, u32[]{:S(2)}) collective-permute-start(f32[8,128]{1,0:T(8,128)S(1)} %add.19.edge_ref), channel_id=1, source_target_pairs={{0,2},{1,3},{2,0},{3,1},{4,6},{5,7},{6,4},{7,5},{8,10},{9,11},{10,... | collective-permute-start | bytes 12296 | tf_op jit(solution)/shard_map/ppermute | solution.py:483
  105.6 1.5 %collective-permute-start.10 = (f32[8,128]{1,0:T(8,128)S(1)}, f32[8,128]{1,0:T(8,128)S(1)}, u32[]{:S(2)}, u32[]{:S(2)}) collective-permute-start(f32[8,128]{1,0:T(8,128)S(1)} %get-tuple-element.29), channel_id=1, source_target_pairs={{0,1},{1,0},{2,3},{3,2},{4,5},{5,4},{6,7},{7,6},{8,9},{9,8},{10,11... | collective-permute-start | bytes 12296 | tf_op jit(solution)/shard_map/ppermute | solution.py:483
  107.2 3.6 %collective-permute-start.11 = (f32[8,128]{1,0:T(8,128)S(1)}, f32[8,128]{1,0:T(8,128)S(1)}, u32[]{:S(2)}, u32[]{:S(2)}) collective-permute-start(f32[8,128]{1,0:T(8,128)S(1)} %add.20), channel_id=1, source_target_pairs={{0,2},{1,3},{2,0},{3,1},{4,6},{5,7},{6,4},{7,5},{8,10},{9,11},{10,... | collective-permute-start | bytes 12296 | tf_op jit(solution)/shard_map/ppermute | solution.py:483
  110.8 3.6 %collective-permute-start.12 = (f32[8,128]{1,0:T(8,128)S(1)}, f32[8,128]{1,0:T(8,128)S(1)}, u32[]{:S(2)}, u32[]{:S(2)}) collective-permute-start(f32[8,128]{1,0:T(8,128)S(1)} %add.21), channel_id=1, source_target_pairs={{0,4},{4,0},{8,12},{12,8},{16,20},{20,16},{24,28},{28,24},{1,5},{5... | collective-permute-start | bytes 12296 | tf_op jit(solution)/shard_map/ppermute | solution.py:483
  114.4 3.6 %collective-permute-start.13 = (f32[8,128]{1,0:T(8,128)S(1)}, f32[8,128]{1,0:T(8,128)S(1)}, u32[]{:S(2)}, u32[]{:S(2)}) collective-permute-start(f32[8,128]{1,0:T(8,128)S(1)} %add.22), channel_id=1, source_target_pairs={{0,8},{4,12},{8,0},{12,4},{16,24},{20,28},{24,16},{28,20},{1,9},{5... | collective-permute-start | bytes 12296 | tf_op jit(solution)/shard_map/ppermute | solution.py:483
  118.0 4.5 %collective-permute-start.14 = (f32[8,128]{1,0:T(8,128)S(1)}, f32[8,128]{1,0:T(8,128)S(1)}, u32[]{:S(2)}, u32[]{:S(2)}) collective-permute-start(f32[8,128]{1,0:T(8,128)S(1)} %add.23.scalar_ref), channel_id=1, source_target_pairs={{0,16},{4,20},{8,24},{12,28},{16,0},{20,4},{24,8},{28,12},{1,17},{... | collective-permute-start | bytes 12296 | tf_op jit(solution)/shard_map/ppermute | solution.py:483
  (2 other events, 4.2 us)

commit v5 on v4

--- a/solution.py
+++ b/solution.py
@@ -69,16 +69,19 @@
 
 
 def store_rows(out_ref, begin, rows):
-    block = out_ref.shape[1] - 8
+    block = out_ref.shape[1]
     for offset in range(0, rows.shape[0], 8):
         where = begin + offset
         out_ref[where // block, where % block : where % block + 8, :] = rows[offset : offset + 8]
 
 
-def knot_backward_kernel(arrive, live_ref, place_ref, *refs):
+def knot_backward_kernel(n_stars, arrive, live_ref, place_ref, *refs):
     observed, refs = refs[:6], refs[6:]
+    if not arrive:
+        scalar_ref, *refs = refs
+    block_outs, (table_out, knot_acc) = refs[:n_stars], refs[n_stars : n_stars + 2]
     if arrive:
-        table_out, knot_acc, *buffers, sems = refs
+        *buffers, sems = refs[n_stars + 2 :]
         copies = [
             pltpu.make_async_copy(source, target, sems.at[which])
             for which, (source, target) in enumerate(zip(observed, buffers))
@@ -86,8 +89,6 @@
         for copy in copies:
             copy.start()
         observed = buffers
-    else:
-        scalar_ref, table_out, knot_acc = refs
     value_ref, cal_coef_ref, tile_cal_ref, knot_ref, frac_ref, att_coef_ref = observed
     knot_acc[...] = jnp.zeros_like(knot_acc)
     if arrive:
@@ -154,11 +155,15 @@
     if not arrive:
         edges = edges + scalar_ref[...]
     edges = jnp.concatenate([edges, jnp.zeros_like(edges)], axis=1)
-    for device in range(table_out.shape[0]):
-        table_out[device, table_out.shape[1] - 8 :, :] = edges
-
-
-def star_backward_kernel(live_ref, star_ref, star_coef_ref, value_ref, after_ref, star_out, star_acc):
+    for distance, block_out in enumerate(block_outs):
+        block_out[:-8] = table_out[place_ref[1] ^ distance]
+        block_out[-8:] = edges
+
+
+def star_backward_kernel(
+    live_ref, star_ref, star_coef_ref, value_ref, after_ref, star_out, token_out, star_acc
+):
+    token_out[...] = jnp.zeros_like(token_out)
     star_acc[...] = jnp.zeros_like(star_acc)
 
     @pl.loop(0, star_ref.shape[0] // WIDE_GROUP)
@@ -187,14 +192,13 @@
     star_out[...] = star_acc[:STAR_ROWS] + star_acc[STAR_ROWS:]
 
 
-def sum_kernel(block_ref, out_ref, edge_out):
-    total = block_ref[0]
-    for device in range(1, block_ref.shape[0]):
-        total = total + block_ref[device]
-    rows = out_ref.shape[1]
-    for device in range(block_ref.shape[0]):
-        out_ref[device] = total[:rows]
-    edge_out[...] = total[rows:, :128]
+def sum_kernel(n_stars, after_ref, *refs):
+    block_refs, (part_out, edge_out) = refs[:n_stars], refs[n_stars:]
+    total = block_refs[0][...]
+    for block_ref in block_refs[1:]:
+        total = total + block_ref[...]
+    part_out[...] = total[:-8]
+    edge_out[...] = total[-8:, :128]
 
 
 def picked(array, which):
@@ -257,13 +261,14 @@
 
 def knot_forward_kernel(
     n_stars, n_seg, later, live_ref, place_ref, knot_ref, frac_ref, att_coef_ref, cal_coef_ref,
-    tile_cal_ref, star_image_ref, star_x_ref, table_x_ref, edge_ref, other_edge_ref, *refs,
+    tile_cal_ref, star_image_ref, star_x_ref, edge_ref, other_edge_ref, *refs,
 ):
+    part_refs, refs = refs[:n_stars], refs[n_stars:]
     if later:
         star_0_ref, table_0_ref, image_0_ref, image_ref, table_out, scalar_out = refs[:6]
     else:
         image_ref, table_out, scalar_out = refs[:3]
-    knot_parts_ref, cal_ref = refs[-2:]
+    table_ref, knot_parts_ref, cal_ref = refs[-3:]
     segment = place_ref[0]
     lane = lax.broadcasted_iota(jnp.int32, (8, 128), 1)
     row = lax.broadcasted_iota(jnp.int32, (8, 128), 0)
@@ -279,7 +284,9 @@
     ahead = jnp.where(lane % 2 == 0, own, 0.0) + pltpu.roll(jnp.where(lane % 2 == 1, after, 0.0), 127, 1)
     ahead = jnp.where((segment < n_seg - 1) & (lane < 8) & (row < 3), ahead, 0.0)
 
-    table = table_x_ref[...]
+    for distance, part_ref in enumerate(part_refs):
+        table_ref[place_ref[1] ^ distance] = part_ref[...]
+    table = table_ref[...].reshape(TABLE_ROWS, COARSE)
     pieces = []
     for comp in range(4):
         shifted = pltpu.roll(before, 128 - 2 * comp, 1) if comp else before
@@ -361,12 +368,12 @@
 
 
 def output_kernel(
-    live_ref, edge_ref, other_edge_ref, scalar_ref, other_scalar_ref, star_0_ref, star_h_ref, att_0_ref,
-    att_h_ref, table_0_ref, table_h_ref, value_ref, image_0_ref, image_1_ref, star_out, att_out, cal_out,
-    residual_out,
+    live_ref, edge_ref, other_edge_ref, star_0_ref, star_h_ref, att_0_ref, att_h_ref, table_0_ref,
+    table_h_ref, value_ref, image_0_ref, image_1_ref, *refs,
 ):
+    *scalar_refs, star_out, att_out, cal_out, residual_out = refs
     norm_0, square_0 = first_step(edge_ref[...] + other_edge_ref[...])
-    everyone = scalar_ref[...] + other_scalar_ref[...]
+    everyone = sum(scalar_ref[...] for scalar_ref in scalar_refs)
     norm_1, square_1, cross = [picked(everyone, which) for which in range(3)]
     step_0 = norm_0 / square_0
     ratio = norm_1 / norm_0
@@ -412,7 +419,8 @@
     n_stars, n_seg = lax.axis_size("stars"), lax.axis_size("seg")
     tile_count, width = obs_star.shape
     tile_row = tile_cal[None, :]
-    place = lax.axis_index("seg").astype(jnp.int32)[None]
+    place = jnp.stack([lax.axis_index("seg"), lax.axis_index("stars")]).astype(jnp.int32)
+    block_rows = TABLE_ROWS // n_stars
     image_shape = shaped(tile_count, width)
     table_shape = shaped(TABLE_ROWS, COARSE)
     star_shape = shaped(STAR_ROWS, COARSE)
@@ -421,15 +429,18 @@
     def knot_backward(values, *scalars):
         arrive = not scalars
         observed = (values, cal_coef, tile_row, obs_knot, obs_frac, att_coef)
-        scratch = [pltpu.VMEM((2 * KNOT_HALF, COARSE), F32)]
+        scratch = [
+            pltpu.VMEM((n_stars, block_rows, COARSE), F32),
+            pltpu.VMEM((2 * KNOT_HALF, COARSE), F32),
+        ]
         if arrive:
             scratch += [pltpu.VMEM(array.shape, array.dtype) for array in observed]
             scratch += [pltpu.SemaphoreType.DMA((len(observed),))]
         return pl.pallas_call(
-            functools.partial(knot_backward_kernel, arrive),
-            out_shape=shaped(n_stars, TABLE_ROWS // n_stars + 8, COARSE),
+            functools.partial(knot_backward_kernel, n_stars, arrive),
+            out_shape=(shaped(block_rows + 8, COARSE),) * n_stars,
             in_specs=in_smem(2) + (in_hbm if arrive else in_vmem)(len(observed)) + in_vmem(len(scalars)),
-            out_specs=in_vmem(1)[0],
+            out_specs=tuple(in_vmem(n_stars)),
             scratch_shapes=scratch,
             compiler_params=ARRIVE_PARAMS if arrive else PARAMS,
             cost_estimate=PASS_COST,
@@ -439,9 +450,9 @@
     def star_backward(values, after):
         return pl.pallas_call(
             star_backward_kernel,
-            out_shape=star_shape,
+            out_shape=(star_shape, scalar_shape),
             in_specs=in_smem(1) + in_vmem(3) + in_hbm(1),
-            out_specs=in_vmem(1)[0],
+            out_specs=tuple(in_vmem(2)),
             scratch_shapes=[pltpu.VMEM((2 * STAR_ROWS, COARSE), F32)],
             compiler_params=PARAMS,
             cost_estimate=PASS_COST,
@@ -461,13 +472,14 @@
         )(obs_star, star_coef, *terms)
 
     def knot_forward(*arrays):
-        later = len(arrays) > 5
+        later = len(arrays) > 4 + n_stars
         return pl.pallas_call(
             functools.partial(knot_forward_kernel, n_stars, n_seg, later),
             out_shape=(image_shape, table_shape, scalar_shape),
             in_specs=in_smem(2) + in_vmem(5 + len(arrays)),
             out_specs=tuple(in_vmem(3)),
             scratch_shapes=[
+                pltpu.VMEM((n_stars, block_rows, COARSE), F32),
                 pltpu.VMEM((2 * KNOT_HALF, COARSE), BF16),
                 pltpu.VMEM((tile_count, width), F32),
             ],
@@ -476,45 +488,40 @@
             name="knot_forward",
         )(live_tiles, place, obs_knot, obs_frac, att_coef, cal_coef, tile_row, *arrays)
 
-    def swap(blocks, axes):
-        return lax.all_to_all(blocks, axes, 0, 0)
-
     def partner(array, axis, distance):
         return lax.ppermute(array, axis, [(i, i ^ distance) for i in range(lax.axis_size(axis))])
 
-    def last_terms(array, *axes):
-        steps = [(axis, 1 << bit) for axis in axes for bit in range(lax.axis_size(axis).bit_length() - 1)]
-        for axis, distance in steps[:-1]:
-            array = array + partner(array, axis, distance)
-        return array, partner(array, *steps[-1])
-
-    def table_sum(table):
-        blocks = swap(table, "stars")
-        copies, edge = pl.pallas_call(
-            sum_kernel,
-            out_shape=(shaped(n_stars, TABLE_ROWS // n_stars, COARSE), scalar_shape),
-            in_specs=in_vmem(1),
+    def everyones(array, axis):
+        return [array] + [partner(array, axis, distance) for distance in range(1, lax.axis_size(axis))]
+
+    def table_sum(blocks, token):
+        return pl.pallas_call(
+            functools.partial(sum_kernel, n_stars),
+            out_shape=(shaped(block_rows, COARSE), scalar_shape),
+            in_specs=in_hbm(1) + in_vmem(n_stars),
             out_specs=tuple(in_vmem(2)),
             compiler_params=PARAMS,
             cost_estimate=SMALL_COST,
             name="table_sum",
-        )(blocks)
-        return (swap(copies, "stars").reshape(TABLE_ROWS, COARSE), *last_terms(edge, "seg"))
+        )(token, *blocks)
 
     def half(values, *scalars):
-        table = knot_backward(values, *scalars)
-        star = star_backward(values, table)
-        stars = [star] + [partner(star, "seg", distance) for distance in range(1, n_seg)]
-        table, *edges = table_sum(table)
-        star_image, star = star_forward(*stars)
-        return star_image, star, table, edges
-
-    star_image, star_0, table, edges = half(obs_value)
-    image_0, table_0, scalars = knot_forward(star_image, star_0, table, *edges)
-    star_image, star_h, table, edges = half(image_0, scalars)
-    image_1, table_h, scalars = knot_forward(
-        star_image, star_h, table, *edges, star_0, table_0, image_0
-    )
+        blocks = knot_backward(values, *scalars)
+        star, token = star_backward(values, blocks[0])
+        received = [partner(block, "stars", distance) for distance, block in enumerate(blocks) if distance]
+        part, edge = table_sum([blocks[0]] + received, token)
+        for distance in [1 << bit for bit in range(n_seg.bit_length() - 2)]:
+            edge = edge + partner(edge, "seg", distance)
+        star_image, star = star_forward(*everyones(star, "seg"))
+        return star_image, star, edge, partner(edge, "seg", n_seg // 2), *everyones(part, "stars")
+
+    first = half(obs_value)
+    star_0 = first[1]
+    image_0, table_0, scalars = knot_forward(*first)
+    second = half(image_0, scalars)
+    star_h, edges = second[1], second[2:4]
+    image_1, table_h, scalars = knot_forward(*second, star_0, table_0, image_0)
+    scalars = everyones(sum(everyones(scalars, "seg")), "stars")
 
     def star_order(star):
         return star.reshape(5, STAR_DEV)
@@ -526,14 +533,14 @@
     return pl.pallas_call(
         output_kernel,
         out_shape=(shaped(5, STAR_DEV), shaped(4, KNOT_DEV), shaped(CALB_DEV, width), image_shape),
-        in_specs=in_smem(1) + in_vmem(13),
+        in_specs=in_smem(1) + in_vmem(11 + n_stars),
         out_specs=tuple(in_vmem(4)),
         compiler_params=PARAMS,
         cost_estimate=SMALL_COST,
         name="outputs",
     )(
-        live_tiles, *edges, *last_terms(scalars, "seg", "stars"), star_order(star_0), star_order(star_h),
-        att_order(table_0), att_order(table_h), table_0, table_h, obs_value, image_0, image_1,
+        live_tiles, *edges, star_order(star_0), star_order(star_h), att_order(table_0), att_order(table_h),
+        table_0, table_h, obs_value, image_0, image_1, *scalars,
     )
 
 

time: 124 us -> 142 us (1.15)
  starting transfers between devices: 21.7 us -> 65.8 us
  blocking collectives: 34.9 us -> 0 us
  waiting for transfers between devices: 19.6 us -> 26.2 us
    ppermute x15 -> x48, starting transfers between devices: 14.7 us -> 65.8 us  [partner(): lax.ppermute(array, axis, [(i, i ^ distance) for i in range(lax.axis_size...]
    all_to_all x2 -> x0, blocking collectives: 34.9 us -> none  [swap(): return lax.all_to_all(blocks, axes, 0, 0)]
    all_to_all x2 -> x0, starting transfers between devices: 6.96 us -> none  [swap(): return lax.all_to_all(blocks, axes, 0, 0)]
    ppermute x15 -> x48, waiting for transfers between devices: 19.6 us -> 26.2 us  [partner(): lax.ppermute(array, axis, [(i, i ^ distance) for i in range(lax.axis_size...]
  transfers between devices with their start and end apart: 17 -> 48, of which waited for: 11 -> 18; matrix products, arithmetic and copies ran while one was open for 1% -> 1% of each run, Pallas kernels for 15% -> 13%
where the time goes in v5:
time: 142 us
  starting transfers between devices  65.8 us (46%)
  Pallas kernels  45 us (32%)
  waiting for transfers between devices  26.2 us (18%)
  local copies, waits for them, and re-layouts  2.45 us (2%)
  between operations  1.65 us (1%)
    ppermute x48, starting transfers between devices, partner(): lax.ppermute(array, axis, [(i, i ^ distance) for i in range(lax.axis_size...  65.8 us
    ppermute x48, waiting for transfers between devices, partner(): lax.ppermute(array, axis, [(i, i ^ distance) for i in range(lax.axis_size...  26.2 us
    pallas_call x2, Pallas kernels, knot_backward(): pl.pallas_call(functools.partial(knot_backward_kernel, n_stars, arrive),...  14.5 us
    pallas_call x2, Pallas kernels, knot_forward(): pl.pallas_call(functools.partial(knot_forward_kernel, n_stars, n_seg, lat...  11.1 us
    pallas_call x2, Pallas kernels, star_forward(): pl.pallas_call(functools.partial(star_forward_kernel, n_seg), out_shape=(...  9.52 us
    pallas_call x2, Pallas kernels, star_backward(): pl.pallas_call(star_backward_kernel, out_shape=(star_shape, scalar_shape)...  8.82 us
  transfers between devices with their start and end apart: 48, of which 18 were waited for; matrix products, arithmetic and copies ran while one was open for 1% of the time, Pallas kernels for 13%

profile of v5, /device:TPU:0, one launch (start us, length us, event | category | flops | bytes accessed | tf_op | source)
XLA Modules:
  0.0 141.7 jit_solution(17618199054012351922)
XLA Ops:
  1.9 8.2 %knot_backward.2 = (f32[40,256]{1,0:T(8,128)}, f32[40,256]{1,0:T(8,128)}, f32[40,256]{1,0:T(8,128)}, f32[40,256]{1,0:T(8,128)}, f32[40,256]{1,0:T(8,128)}, /*ind...) custom-call(s32[1]{0:T(128)S(6)} %copy.17.live_ref, s32[2]{0:T(128)} %pad_add_fusion.place_ref, ...), custom_call_target="tpu_custom_call" | custom-call | flops 3000000000 | bytes 1000000 | tf_op jit(solution)/shard_map/knot_backward/pallas_call | solution.py:439
  10.1 3.0 %collective-permute-start.3 = (f32[40,256]{1,0:T(8,128)}, f32[40,256]{1,0:T(8,128)S(1)}, u32[]{:S(2)}, u32[]{:S(2)}) collective-permute-start(f32[40,256]{1,0:T(8,128)} %get-tuple-element.43), channel_id=1, source_target_pairs={{0,4},{4,0},{8,12},{12,8},{16,20},{20,16},{24,28},{28,24},{1,5},{5... | collective-permute-start | bytes 122888 | tf_op jit(solution)/shard_map/ppermute | solution.py:492
  15.5 4.4 %star_backward.2 = (f32[160,256]{1,0:T(8,128)S(1)}, f32[8,128]{1,0:T(8,128)S(1)}) custom-call(s32[1]{0:T(128)S(6)} %copy.17.live_ref, s32[128,128]{1,0:T(8,128)S(1)} %copy-done.4, f32[5,128,128]{2,1,0:T(8,128)S(1)} %copy-done.2, f32[128,128]{1,0:T(8,128)S(1)} %copy-done, f32[40,256]{1,0:T(8,128)S(1)} %copy-done.1), custom_call_target="tpu_custom_call" | custom-call | flops 3000000000 | bytes 1000000 | tf_op jit(solution)/shard_map/star_backward/pallas_call | solution.py:451
  22.1 2.8 %collective-permute-start.6 = (f32[40,256]{1,0:T(8,128)S(1)}, f32[40,256]{1,0:T(8,128)S(1)}, u32[]{:S(2)}, u32[]{:S(2)}) collective-permute-start(f32[40,256]{1,0:T(8,128)S(1)} %copy-done.13), channel_id=1, source_target_pairs={{0,16},{4,20},{8,24},{12,28},{16,0},{20,4},{24,8},{28,12},{1,17},{... | collective-permute-start | bytes 122888 | tf_op jit(solution)/shard_map/ppermute | solution.py:492
  27.0 5.4 %collective-permute-start.8 = (f32[40,256]{1,0:T(8,128)S(1)}, f32[40,256]{1,0:T(8,128)S(1)}, u32[]{:S(2)}, u32[]{:S(2)}) collective-permute-start(f32[40,256]{1,0:T(8,128)S(1)} %copy-done.11), channel_id=1, source_target_pairs={{0,24},{4,28},{8,16},{12,20},{16,8},{20,12},{24,0},{28,4},{1,25},{... | collective-permute-start | bytes 122888 | tf_op jit(solution)/shard_map/ppermute | solution.py:492
  34.5 4.7 %collective-permute-done.9.refs_7_ = f32[40,256]{1,0:T(8,128)S(1)} collective-permute-done((f32[40,256]{1,0:T(8,128)S(1)}, f32[40,256]{1,0:T(8,128)S(1)}, u32[]{:S(2)}, u32[]{:S(2)}) %collective-permute-start.9) | collective-permute-done | bytes 40992 | tf_op jit(solution)/shard_map/ppermute | solution.py:492
  44.0 2.4 %collective-permute-start.17 = (f32[32,256]{1,0:T(8,128)S(1)}, f32[32,256]{1,0:T(8,128)S(1)}, u32[]{:S(2)}, u32[]{:S(2)}) collective-permute-start(f32[32,256]{1,0:T(8,128)S(1)} %get-tuple-element.51.refs_0_), channel_id=1, source_target_pairs={{0,24},{4,28},{8,16},{12,20},{16,8},{20,12},{24,0},{28,4},{1,25},{... | collective-permute-start | bytes 98312 | tf_op jit(solution)/shard_map/ppermute | solution.py:492
  46.4 2.5 %collective-permute-done.18.refs_7_ = f32[32,256]{1,0:T(8,128)S(1)} collective-permute-done((f32[32,256]{1,0:T(8,128)S(1)}, f32[32,256]{1,0:T(8,128)S(1)}, u32[]{:S(2)}, u32[]{:S(2)}) %collective-permute-start.18) | collective-permute-done | bytes 32800 | tf_op jit(solution)/shard_map/ppermute | solution.py:492
  49.8 2.5 %collective-permute-start.15 = (f32[32,256]{1,0:T(8,128)S(1)}, f32[32,256]{1,0:T(8,128)S(1)}, u32[]{:S(2)}, u32[]{:S(2)}) collective-permute-start(f32[32,256]{1,0:T(8,128)S(1)} %get-tuple-element.51.refs_0_), channel_id=1, source_target_pairs={{0,16},{4,20},{8,24},{12,28},{16,0},{20,4},{24,8},{28,12},{1,17},{... | collective-permute-start | bytes 98312 | tf_op jit(solution)/shard_map/ppermute | solution.py:492
  55.8 4.8 %star_forward.2 = (f32[128,128]{1,0:T(8,128)S(1)}, f32[160,256]{1,0:T(8,128)S(1)}) custom-call(s32[128,128]{1,0:T(8,128)S(1)} %copy-done.4, f32[5,128,128]{2,1,0:T(8,128)S(1)} %copy-done.2, f32[160,256]{1,0:T(8,128)S(1)} %get-tuple-element.39.refs_0_, f32[160,256]{1,0:T(8,128)S(1)} %collective-permute-done.refs_1_, ...), custom_call_target="tpu_custom_call" | custom-call | flops 3000000000 | bytes 1000000 | tf_op jit(solution)/shard_map/star_forward/pallas_call | solution.py:463
  61.3 5.5 %knot_forward.2 = (f32[128,128]{1,0:T(8,128)S(1)}, f32[256,256]{1,0:T(8,128)S(1)}, f32[8,128]{1,0:T(8,128)S(1)}) custom-call(s32[1]{0:T(128)S(6)} %copy.17.live_ref, s32[2]{0:T(128)S(1)} %copy-done.9, s32[128,128]{1,0:T(8,128)S(1)} %copy-done.5, f32[128,128]{1,0:T(8,128)S(1)} %copy-done.6, f32[4,128,128]{2,1,0:T(8,128)S(1)} %copy-done.3, ...), custom_call_target="tpu_custom_call" | custom-call | flops 3000000000 | bytes 1000000 | tf_op jit(solution)/shard_map/knot_forward/pallas_call | solution.py:476
  66.8 6.3 %knot_backward.3 = (f32[40,256]{1,0:T(8,128)S(1)}, f32[40,256]{1,0:T(8,128)S(1)}, f32[40,256]{1,0:T(8,128)S(1)}, f32[40,256]{1,0:T(8,128)S(1)}, f32[40,256]{1,0:...) custom-call(s32[1]{0:T(128)S(6)} %copy.17.live_ref, s32[2]{0:T(128)S(1)} %copy-done.9, ...), custom_call_target="tpu_custom_call" | custom-call | flops 3000000000 | bytes 1000000 | tf_op jit(solution)/shard_map/knot_backward/pallas_call | solution.py:439
  74.4 2.2 %collective-permute-start.21 = (f32[40,256]{1,0:T(8,128)S(1)}, f32[40,256]{1,0:T(8,128)S(1)}, u32[]{:S(2)}, u32[]{:S(2)}) collective-permute-start(f32[40,256]{1,0:T(8,128)S(1)} %get-tuple-element.58), channel_id=1, source_target_pairs={{0,12},{4,8},{8,4},{12,0},{16,28},{20,24},{24,20},{28,16},{1,13},{... | collective-permute-start | bytes 122888 | tf_op jit(solution)/shard_map/ppermute | solution.py:492
  76.6 4.4 %star_backward.3 = (f32[160,256]{1,0:T(8,128)S(1)}, f32[8,128]{1,0:T(8,128)S(1)}) custom-call(s32[1]{0:T(128)S(6)} %copy.17.live_ref, s32[128,128]{1,0:T(8,128)S(1)} %copy-done.4, f32[5,128,128]{2,1,0:T(8,128)S(1)} %copy-done.2, f32[128,128]{1,0:T(8,128)S(1)} %get-tuple-element.52.refs_0_.value_ref.refs_10_.image_0_ref, ...), custom_call_target="tpu_custom_call" | custom-call | flops 3000000000 | bytes 1000000 | tf_op jit(solution)/shard_map/star_backward/pallas_call | solution.py:451
  83.5 2.9 %collective-permute-start.23 = (f32[40,256]{1,0:T(8,128)S(1)}, f32[40,256]{1,0:T(8,128)S(1)}, u32[]{:S(2)}, u32[]{:S(2)}) collective-permute-start(f32[40,256]{1,0:T(8,128)S(1)} %get-tuple-element.60), channel_id=1, source_target_pairs={{0,20},{4,16},{8,28},{12,24},{16,4},{20,0},{24,12},{28,8},{1,21},{... | collective-permute-start | bytes 122888 | tf_op jit(solution)/shard_map/ppermute | solution.py:492
  86.3 2.8 %collective-permute-done.22.refs_4_ = f32[40,256]{1,0:T(8,128)S(1)} collective-permute-done((f32[40,256]{1,0:T(8,128)S(1)}, f32[40,256]{1,0:T(8,128)S(1)}, u32[]{:S(2)}, u32[]{:S(2)}) %collective-permute-start.22) | collective-permute-done | bytes 40992 | tf_op jit(solution)/shard_map/ppermute | solution.py:492
  90.5 3.1 %collective-permute-start.25 = (f32[40,256]{1,0:T(8,128)S(1)}, f32[40,256]{1,0:T(8,128)S(1)}, u32[]{:S(2)}, u32[]{:S(2)}) collective-permute-start(f32[40,256]{1,0:T(8,128)S(1)} %get-tuple-element.62), channel_id=1, source_target_pairs={{0,28},{4,24},{8,20},{12,16},{16,12},{20,8},{24,4},{28,0},{1,29},{... | collective-permute-start | bytes 122888 | tf_op jit(solution)/shard_map/ppermute | solution.py:492
  99.3 2.3 %collective-permute-start.37 = (f32[32,256]{1,0:T(8,128)S(1)}, f32[32,256]{1,0:T(8,128)S(1)}, u32[]{:S(2)}, u32[]{:S(2)}) collective-permute-start(f32[32,256]{1,0:T(8,128)S(1)} %get-tuple-element.68.refs_0_), channel_id=1, source_target_pairs={{0,28},{4,24},{8,20},{12,16},{16,12},{20,8},{24,4},{28,0},{1,29},{... | collective-permute-start | bytes 98312 | tf_op jit(solution)/shard_map/ppermute | solution.py:492
  102.1 2.4 %collective-permute-start.36 = (f32[32,256]{1,0:T(8,128)S(1)}, f32[32,256]{1,0:T(8,128)S(1)}, u32[]{:S(2)}, u32[]{:S(2)}) collective-permute-start(f32[32,256]{1,0:T(8,128)S(1)} %get-tuple-element.68.refs_0_), channel_id=1, source_target_pairs={{0,24},{4,28},{8,16},{12,20},{16,8},{20,12},{24,0},{28,4},{1,25},{... | collective-permute-start | bytes 98312 | tf_op jit(solution)/shard_map/ppermute | solution.py:492
  113.0 4.8 %star_forward.3 = (f32[128,128]{1,0:T(8,128)S(1)}, f32[160,256]{1,0:T(8,128)S(1)}) custom-call(s32[128,128]{1,0:T(8,128)S(1)} %copy-done.4, f32[5,128,128]{2,1,0:T(8,128)S(1)} %copy-done.2, f32[160,256]{1,0:T(8,128)S(1)} %get-tuple-element.64.refs_0_, f32[160,256]{1,0:T(8,128)S(1)} %collective-permute-done.28.refs_1_, ...), custom_call_target="tpu_custom_call" | custom-call | flops 3000000000 | bytes 1000000 | tf_op jit(solution)/shard_map/star_forward/pallas_call | solution.py:463
  117.8 5.6 %knot_forward.3 = (f32[128,128]{1,0:T(8,128)S(1)}, f32[256,256]{1,0:T(8,128)S(1)}, f32[8,128]{1,0:T(8,128)S(1)}) custom-call(s32[1]{0:T(128)S(6)} %copy.17.live_ref, s32[2]{0:T(128)S(1)} %copy-done.9, s32[128,128]{1,0:T(8,128)S(1)} %copy-done.5, f32[128,128]{1,0:T(8,128)S(1)} %copy-done.6, f32[4,128,128]{2,1,0:T(8,128)S(1)} %copy-done.3, ...), custom_call_target="tpu_custom_call" | custom-call | flops 3000000000 | bytes 1000000 | tf_op jit(solution)/shard_map/knot_forward/pallas_call | solution.py:476
  127.1 2.4 %collective-permute-start.47 = (f32[8,128]{1,0:T(8,128)S(1)}, f32[8,128]{1,0:T(8,128)S(1)}, u32[]{:S(2)}, u32[]{:S(2)}) collective-permute-start(f32[8,128]{1,0:T(8,128)S(1)} %add_add_fusion.refs_0_), channel_id=1, source_target_pairs={{0,28},{4,24},{8,20},{12,16},{16,12},{20,8},{24,4},{28,0},{1,29},{... | collective-permute-start | bytes 12296 | tf_op jit(solution)/shard_map/ppermute | solution.py:492
  131.4 3.4 %collective-permute-start.44 = (f32[8,128]{1,0:T(8,128)S(1)}, f32[8,128]{1,0:T(8,128)S(1)}, u32[]{:S(2)}, u32[]{:S(2)}) collective-permute-start(f32[8,128]{1,0:T(8,128)S(1)} %add_add_fusion.refs_0_), channel_id=1, source_target_pairs={{0,16},{4,20},{8,24},{12,28},{16,0},{20,4},{24,8},{28,12},{1,17},{... | collective-permute-start | bytes 12296 | tf_op jit(solution)/shard_map/ppermute | solution.py:492
  135.0 2.1 %collective-permute-start.42 = (f32[8,128]{1,0:T(8,128)S(1)}, f32[8,128]{1,0:T(8,128)S(1)}, u32[]{:S(2)}, u32[]{:S(2)}) collective-permute-start(f32[8,128]{1,0:T(8,128)S(1)} %add_add_fusion.refs_0_), channel_id=1, source_target_pairs={{0,8},{4,12},{8,0},{12,4},{16,24},{20,28},{24,16},{28,20},{1,9},{5... | collective-permute-start | bytes 12296 | tf_op jit(solution)/shard_map/ppermute | solution.py:492
  (123 shorter events, 49.1 us)
Async XLA Ops:
  10.1 11.9 %collective-permute-start.3 = (f32[40,256]{1,0:T(8,128)}, f32[40,256]{1,0:T(8,128)S(1)}, u32[]{:S(2)}, u32[]{:S(2)}) collective-permute-start(f32[40,256]{1,0:T(8,128)} %get-tuple-element.43), channel_id=1, source_target_pairs={{0,4},{4,0},{8,12},{12,8},{16,20},{20,16},{24,28},{28,24},{1,5},{5... | collective-permute-start | bytes 122888 | tf_op jit(solution)/shard_map/ppermute | solution.py:492
  13.1 8.9 %collective-permute-start.4 = (f32[40,256]{1,0:T(8,128)}, f32[40,256]{1,0:T(8,128)S(1)}, u32[]{:S(2)}, u32[]{:S(2)}) collective-permute-start(f32[40,256]{1,0:T(8,128)} %get-tuple-element.44), channel_id=1, source_target_pairs={{0,8},{4,12},{8,0},{12,4},{16,24},{20,28},{24,16},{28,20},{1,9},{5... | collective-permute-start | bytes 122888 | tf_op jit(solution)/shard_map/ppermute | solution.py:492
  14.7 10.2 %collective-permute-start.5 = (f32[40,256]{1,0:T(8,128)}, f32[40,256]{1,0:T(8,128)S(1)}, u32[]{:S(2)}, u32[]{:S(2)}) collective-permute-start(f32[40,256]{1,0:T(8,128)} %get-tuple-element.45), channel_id=1, source_target_pairs={{0,12},{4,8},{8,4},{12,0},{16,28},{20,24},{24,20},{28,16},{1,13},{... | collective-permute-start | bytes 122888 | tf_op jit(solution)/shard_map/ppermute | solution.py:492
  20.0 32.4 %collective-permute-start.2 = (f32[160,256]{1,0:T(8,128)S(1)}, f32[160,256]{1,0:T(8,128)S(1)}, u32[]{:S(2)}, u32[]{:S(2)}) collective-permute-start(f32[160,256]{1,0:T(8,128)S(1)} %get-tuple-element.39.refs_0_), channel_id=1, source_target_pairs={{0,3},{1,2},{2,1},{3,0},{4,7},{5,6},{6,5},{7,4},{8,11},{9,10},{10,... | collective-permute-start | bytes 491528 | tf_op jit(solution)/shard_map/ppermute | solution.py:492
  20.5 32.5 %collective-permute-start.1 = (f32[160,256]{1,0:T(8,128)S(1)}, f32[160,256]{1,0:T(8,128)S(1)}, u32[]{:S(2)}, u32[]{:S(2)}) collective-permute-start(f32[160,256]{1,0:T(8,128)S(1)} %get-tuple-element.39.refs_0_), channel_id=1, source_target_pairs={{0,2},{1,3},{2,0},{3,1},{4,6},{5,7},{6,4},{7,5},{8,10},{9,11},{10,... | collective-permute-start | bytes 491528 | tf_op jit(solution)/shard_map/ppermute | solution.py:492
  22.0 32.7 %collective-permute-start = (f32[160,256]{1,0:T(8,128)S(1)}, f32[160,256]{1,0:T(8,128)S(1)}, u32[]{:S(2)}, u32[]{:S(2)}) collective-permute-start(f32[160,256]{1,0:T(8,128)S(1)} %get-tuple-element.39.refs_0_), channel_id=1, source_target_pairs={{0,1},{1,0},{2,3},{3,2},{4,5},{5,4},{6,7},{7,6},{8,9},{9,8},{10,11... | collective-permute-start | bytes 491528 | tf_op jit(solution)/shard_map/ppermute | solution.py:492
  24.9 7.6 %collective-permute-start.7 = (f32[40,256]{1,0:T(8,128)S(1)}, f32[40,256]{1,0:T(8,128)S(1)}, u32[]{:S(2)}, u32[]{:S(2)}) collective-permute-start(f32[40,256]{1,0:T(8,128)S(1)} %copy-done.12), channel_id=1, source_target_pairs={{0,20},{4,16},{8,28},{12,24},{16,4},{20,0},{24,12},{28,8},{1,21},{... | collective-permute-start | bytes 122888 | tf_op jit(solution)/shard_map/ppermute | solution.py:492
  48.9 11.7 %collective-permute-start.16 = (f32[32,256]{1,0:T(8,128)S(1)}, f32[32,256]{1,0:T(8,128)S(1)}, u32[]{:S(2)}, u32[]{:S(2)}) collective-permute-start(f32[32,256]{1,0:T(8,128)S(1)} %get-tuple-element.51.refs_0_), channel_id=1, source_target_pairs={{0,20},{4,16},{8,28},{12,24},{16,4},{20,0},{24,12},{28,8},{1,21},{... | collective-permute-start | bytes 98312 | tf_op jit(solution)/shard_map/ppermute | solution.py:492
  49.8 10.8 %collective-permute-start.15 = (f32[32,256]{1,0:T(8,128)S(1)}, f32[32,256]{1,0:T(8,128)S(1)}, u32[]{:S(2)}, u32[]{:S(2)}) collective-permute-start(f32[32,256]{1,0:T(8,128)S(1)} %get-tuple-element.51.refs_0_), channel_id=1, source_target_pairs={{0,16},{4,20},{8,24},{12,28},{16,0},{20,4},{24,8},{28,12},{1,17},{... | collective-permute-start | bytes 98312 | tf_op jit(solution)/shard_map/ppermute | solution.py:492
  52.3 8.3 %collective-permute-start.14 = (f32[32,256]{1,0:T(8,128)S(1)}, f32[32,256]{1,0:T(8,128)S(1)}, u32[]{:S(2)}, u32[]{:S(2)}) collective-permute-start(f32[32,256]{1,0:T(8,128)S(1)} %get-tuple-element.51.refs_0_), channel_id=1, source_target_pairs={{0,12},{4,8},{8,4},{12,0},{16,28},{20,24},{24,20},{28,16},{1,13},{... | collective-permute-start | bytes 98312 | tf_op jit(solution)/shard_map/ppermute | solution.py:492
  53.0 7.6 %collective-permute-start.13 = (f32[32,256]{1,0:T(8,128)S(1)}, f32[32,256]{1,0:T(8,128)S(1)}, u32[]{:S(2)}, u32[]{:S(2)}) collective-permute-start(f32[32,256]{1,0:T(8,128)S(1)} %get-tuple-element.51.refs_0_), channel_id=1, source_target_pairs={{0,8},{4,12},{8,0},{12,4},{16,24},{20,28},{24,16},{28,20},{1,9},{5... | collective-permute-start | bytes 98312 | tf_op jit(solution)/shard_map/ppermute | solution.py:492
  73.2 8.5 %collective-permute-start.19 = (f32[40,256]{1,0:T(8,128)S(1)}, f32[40,256]{1,0:T(8,128)S(1)}, u32[]{:S(2)}, u32[]{:S(2)}) collective-permute-start(f32[40,256]{1,0:T(8,128)S(1)} %get-tuple-element.56), channel_id=1, source_target_pairs={{0,4},{4,0},{8,12},{12,8},{16,20},{20,16},{24,28},{28,24},{1,5},{5... | collective-permute-start | bytes 122888 | tf_op jit(solution)/shard_map/ppermute | solution.py:492
  74.1 8.9 %collective-permute-start.20 = (f32[40,256]{1,0:T(8,128)S(1)}, f32[40,256]{1,0:T(8,128)S(1)}, u32[]{:S(2)}, u32[]{:S(2)}) collective-permute-start(f32[40,256]{1,0:T(8,128)S(1)} %get-tuple-element.57), channel_id=1, source_target_pairs={{0,8},{4,12},{8,0},{12,4},{16,24},{20,28},{24,16},{28,20},{1,9},{5... | collective-permute-start | bytes 122888 | tf_op jit(solution)/shard_map/ppermute | solution.py:492
  74.4 9.0 %collective-permute-start.21 = (f32[40,256]{1,0:T(8,128)S(1)}, f32[40,256]{1,0:T(8,128)S(1)}, u32[]{:S(2)}, u32[]{:S(2)}) collective-permute-start(f32[40,256]{1,0:T(8,128)S(1)} %get-tuple-element.58), channel_id=1, source_target_pairs={{0,12},{4,8},{8,4},{12,0},{16,28},{20,24},{24,20},{28,16},{1,13},{... | collective-permute-start | bytes 122888 | tf_op jit(solution)/shard_map/ppermute | solution.py:492
  81.1 28.4 %collective-permute-start.30 = (f32[160,256]{1,0:T(8,128)S(1)}, f32[160,256]{1,0:T(8,128)S(1)}, u32[]{:S(2)}, u32[]{:S(2)}) collective-permute-start(f32[160,256]{1,0:T(8,128)S(1)} %get-tuple-element.64.refs_0_), channel_id=1, source_target_pairs={{0,3},{1,2},{2,1},{3,0},{4,7},{5,6},{6,5},{7,4},{8,11},{9,10},{10,... | collective-permute-start | bytes 491528 | tf_op jit(solution)/shard_map/ppermute | solution.py:492
  81.1 30.3 %collective-permute-start.29 = (f32[160,256]{1,0:T(8,128)S(1)}, f32[160,256]{1,0:T(8,128)S(1)}, u32[]{:S(2)}, u32[]{:S(2)}) collective-permute-start(f32[160,256]{1,0:T(8,128)S(1)} %get-tuple-element.64.refs_0_), channel_id=1, source_target_pairs={{0,2},{1,3},{2,0},{3,1},{4,6},{5,7},{6,4},{7,5},{8,10},{9,11},{10,... | collective-permute-start | bytes 491528 | tf_op jit(solution)/shard_map/ppermute | solution.py:492
  81.7 30.1 %collective-permute-start.28 = (f32[160,256]{1,0:T(8,128)S(1)}, f32[160,256]{1,0:T(8,128)S(1)}, u32[]{:S(2)}, u32[]{:S(2)}) collective-permute-start(f32[160,256]{1,0:T(8,128)S(1)} %get-tuple-element.64.refs_0_), channel_id=1, source_target_pairs={{0,1},{1,0},{2,3},{3,2},{4,5},{5,4},{6,7},{7,6},{8,9},{9,8},{10,11... | collective-permute-start | bytes 491528 | tf_op jit(solution)/shard_map/ppermute | solution.py:492
  105.9 11.8 %collective-permute-start.35 = (f32[32,256]{1,0:T(8,128)S(1)}, f32[32,256]{1,0:T(8,128)S(1)}, u32[]{:S(2)}, u32[]{:S(2)}) collective-permute-start(f32[32,256]{1,0:T(8,128)S(1)} %get-tuple-element.68.refs_0_), channel_id=1, source_target_pairs={{0,20},{4,16},{8,28},{12,24},{16,4},{20,0},{24,12},{28,8},{1,21},{... | collective-permute-start | bytes 98312 | tf_op jit(solution)/shard_map/ppermute | solution.py:492
  107.8 9.9 %collective-permute-start.34 = (f32[32,256]{1,0:T(8,128)S(1)}, f32[32,256]{1,0:T(8,128)S(1)}, u32[]{:S(2)}, u32[]{:S(2)}) collective-permute-start(f32[32,256]{1,0:T(8,128)S(1)} %get-tuple-element.68.refs_0_), channel_id=1, source_target_pairs={{0,16},{4,20},{8,24},{12,28},{16,0},{20,4},{24,8},{28,12},{1,17},{... | collective-permute-start | bytes 98312 | tf_op jit(solution)/shard_map/ppermute | solution.py:492
  109.5 8.3 %collective-permute-start.33 = (f32[32,256]{1,0:T(8,128)S(1)}, f32[32,256]{1,0:T(8,128)S(1)}, u32[]{:S(2)}, u32[]{:S(2)}) collective-permute-start(f32[32,256]{1,0:T(8,128)S(1)} %get-tuple-element.68.refs_0_), channel_id=1, source_target_pairs={{0,12},{4,8},{8,4},{12,0},{16,28},{20,24},{24,20},{28,16},{1,13},{... | collective-permute-start | bytes 98312 | tf_op jit(solution)/shard_map/ppermute | solution.py:492
  127.1 7.9 %collective-permute-start.47 = (f32[8,128]{1,0:T(8,128)S(1)}, f32[8,128]{1,0:T(8,128)S(1)}, u32[]{:S(2)}, u32[]{:S(2)}) collective-permute-start(f32[8,128]{1,0:T(8,128)S(1)} %add_add_fusion.refs_0_), channel_id=1, source_target_pairs={{0,28},{4,24},{8,20},{12,16},{16,12},{20,8},{24,4},{28,0},{1,29},{... | collective-permute-start | bytes 12296 | tf_op jit(solution)/shard_map/ppermute | solution.py:492
  129.6 7.6 %collective-permute-start.46 = (f32[8,128]{1,0:T(8,128)S(1)}, f32[8,128]{1,0:T(8,128)S(1)}, u32[]{:S(2)}, u32[]{:S(2)}) collective-permute-start(f32[8,128]{1,0:T(8,128)S(1)} %add_add_fusion.refs_0_), channel_id=1, source_target_pairs={{0,24},{4,28},{8,16},{12,20},{16,8},{20,12},{24,0},{28,4},{1,25},{... | collective-permute-start | bytes 12296 | tf_op jit(solution)/shard_map/ppermute | solution.py:492
  131.3 8.2 %collective-permute-start.45 = (f32[8,128]{1,0:T(8,128)S(1)}, f32[8,128]{1,0:T(8,128)S(1)}, u32[]{:S(2)}, u32[]{:S(2)}) collective-permute-start(f32[8,128]{1,0:T(8,128)S(1)} %add_add_fusion.refs_0_), channel_id=1, source_target_pairs={{0,20},{4,16},{8,28},{12,24},{16,4},{20,0},{24,12},{28,8},{1,21},{... | collective-permute-start | bytes 12296 | tf_op jit(solution)/shard_map/ppermute | solution.py:492
  131.4 8.0 %collective-permute-start.44 = (f32[8,128]{1,0:T(8,128)S(1)}, f32[8,128]{1,0:T(8,128)S(1)}, u32[]{:S(2)}, u32[]{:S(2)}) collective-permute-start(f32[8,128]{1,0:T(8,128)S(1)} %add_add_fusion.refs_0_), channel_id=1, source_target_pairs={{0,16},{4,20},{8,24},{12,28},{16,0},{20,4},{24,8},{28,12},{1,17},{... | collective-permute-start | bytes 12296 | tf_op jit(solution)/shard_map/ppermute | solution.py:492
  (38 other events, 279.7 us)

commit v6 on v4

--- a/solution.py
+++ b/solution.py
@@ -158,7 +158,10 @@
         table_out[device, table_out.shape[1] - 8 :, :] = edges
 
 
-def star_backward_kernel(live_ref, star_ref, star_coef_ref, value_ref, after_ref, star_out, star_acc):
+def star_backward_kernel(
+    live_ref, star_ref, star_coef_ref, value_ref, after_ref, star_out, token_out, star_acc
+):
+    token_out[...] = jnp.zeros_like(token_out)
     star_acc[...] = jnp.zeros_like(star_acc)
 
     @pl.loop(0, star_ref.shape[0] // WIDE_GROUP)
@@ -187,7 +190,7 @@
     star_out[...] = star_acc[:STAR_ROWS] + star_acc[STAR_ROWS:]
 
 
-def sum_kernel(block_ref, out_ref, edge_out):
+def sum_kernel(after_ref, block_ref, out_ref, edge_out):
     total = block_ref[0]
     for device in range(1, block_ref.shape[0]):
         total = total + block_ref[device]
@@ -361,12 +364,13 @@
 
 
 def output_kernel(
-    live_ref, edge_ref, other_edge_ref, scalar_ref, other_scalar_ref, star_0_ref, star_h_ref, att_0_ref,
-    att_h_ref, table_0_ref, table_h_ref, value_ref, image_0_ref, image_1_ref, star_out, att_out, cal_out,
-    residual_out,
+    live_ref, edge_ref, other_edge_ref, scalar_ref, star_0_ref, star_h_ref, att_0_ref, att_h_ref,
+    table_0_ref, table_h_ref, value_ref, image_0_ref, image_1_ref, star_out, att_out, cal_out, residual_out,
 ):
     norm_0, square_0 = first_step(edge_ref[...] + other_edge_ref[...])
-    everyone = scalar_ref[...] + other_scalar_ref[...]
+    everyone = scalar_ref[0]
+    for device in range(1, scalar_ref.shape[0]):
+        everyone = everyone + scalar_ref[device]
     norm_1, square_1, cross = [picked(everyone, which) for which in range(3)]
     step_0 = norm_0 / square_0
     ratio = norm_1 / norm_0
@@ -439,9 +443,9 @@
     def star_backward(values, after):
         return pl.pallas_call(
             star_backward_kernel,
-            out_shape=star_shape,
+            out_shape=(star_shape, scalar_shape),
             in_specs=in_smem(1) + in_vmem(3) + in_hbm(1),
-            out_specs=in_vmem(1)[0],
+            out_specs=tuple(in_vmem(2)),
             scratch_shapes=[pltpu.VMEM((2 * STAR_ROWS, COARSE), F32)],
             compiler_params=PARAMS,
             cost_estimate=PASS_COST,
@@ -482,30 +486,30 @@
     def partner(array, axis, distance):
         return lax.ppermute(array, axis, [(i, i ^ distance) for i in range(lax.axis_size(axis))])
 
-    def last_terms(array, *axes):
-        steps = [(axis, 1 << bit) for axis in axes for bit in range(lax.axis_size(axis).bit_length() - 1)]
-        for axis, distance in steps[:-1]:
-            array = array + partner(array, axis, distance)
-        return array, partner(array, *steps[-1])
-
-    def table_sum(table):
+    def everyones(array, axis):
+        return [array] + [partner(array, axis, distance) for distance in range(1, lax.axis_size(axis))]
+
+    def table_sum(table, token):
         blocks = swap(table, "stars")
         copies, edge = pl.pallas_call(
             sum_kernel,
             out_shape=(shaped(n_stars, TABLE_ROWS // n_stars, COARSE), scalar_shape),
-            in_specs=in_vmem(1),
+            in_specs=in_hbm(1) + in_vmem(1),
             out_specs=tuple(in_vmem(2)),
             compiler_params=PARAMS,
             cost_estimate=SMALL_COST,
             name="table_sum",
-        )(blocks)
-        return (swap(copies, "stars").reshape(TABLE_ROWS, COARSE), *last_terms(edge, "seg"))
+        )(token, blocks)
+        for distance in [1 << bit for bit in range(n_seg.bit_length() - 2)]:
+            edge = edge + partner(edge, "seg", distance)
+        table = swap(copies, "stars").reshape(TABLE_ROWS, COARSE)
+        return table, (edge, partner(edge, "seg", n_seg // 2))
 
     def half(values, *scalars):
         table = knot_backward(values, *scalars)
-        star = star_backward(values, table)
-        stars = [star] + [partner(star, "seg", distance) for distance in range(1, n_seg)]
-        table, *edges = table_sum(table)
+        star, token = star_backward(values, table)
+        stars = everyones(star, "seg")
+        table, edges = table_sum(table, token)
         star_image, star = star_forward(*stars)
         return star_image, star, table, edges
 
@@ -516,6 +520,9 @@
         star_image, star_h, table, *edges, star_0, table_0, image_0
     )
 
+    scalars = sum(everyones(scalars, "seg"))
+    scalars = swap(jnp.broadcast_to(scalars[None], (n_stars, *scalars.shape)), "stars")
+
     def star_order(star):
         return star.reshape(5, STAR_DEV)
 
@@ -526,14 +533,14 @@
     return pl.pallas_call(
         output_kernel,
         out_shape=(shaped(5, STAR_DEV), shaped(4, KNOT_DEV), shaped(CALB_DEV, width), image_shape),
-        in_specs=in_smem(1) + in_vmem(13),
+        in_specs=in_smem(1) + in_vmem(12),
         out_specs=tuple(in_vmem(4)),
         compiler_params=PARAMS,
         cost_estimate=SMALL_COST,
         name="outputs",
     )(
-        live_tiles, *edges, *last_terms(scalars, "seg", "stars"), star_order(star_0), star_order(star_h),
-        att_order(table_0), att_order(table_h), table_0, table_h, obs_value, image_0, image_1,
+        live_tiles, *edges, scalars, star_order(star_0), star_order(star_h), att_order(table_0),
+        att_order(table_h), table_0, table_h, obs_value, image_0, image_1,
     )
 
 

time: 124 us -> 117 us (0.944)
  blocking collectives: 34.9 us -> 0 us
  waiting for transfers between devices: 19.6 us -> 33.2 us
  starting transfers between devices: 21.7 us -> 34.6 us
    all_to_all x2 -> x0, blocking collectives: 34.9 us -> none  [swap(): return lax.all_to_all(blocks, axes, 0, 0)]
    all_to_all x2 -> x5, starting transfers between devices: 6.96 us -> 26.6 us  [swap(): return lax.all_to_all(blocks, axes, 0, 0)]
    all_to_all x2 -> x5, waiting for transfers between devices: 0.01 us -> 17.5 us  [swap(): return lax.all_to_all(blocks, axes, 0, 0)]
    ppermute x15 -> x13, starting transfers between devices: 14.7 us -> 7.94 us  [partner(): lax.ppermute(array, axis, [(i, i ^ distance) for i in range(lax.axis_size...]
    ppermute x15 -> x13, waiting for transfers between devices: 19.6 us -> 15.7 us  [partner(): lax.ppermute(array, axis, [(i, i ^ distance) for i in range(lax.axis_size...]
  transfers between devices with their start and end apart: 17 -> 18, of which waited for: 11 -> 11; matrix products, arithmetic and copies ran while one was open for 1% -> 1% of each run, Pallas kernels for 15% -> 16%
where the time goes in v6:
time: 117 us; the launch traced here: 116 us
  Pallas kernels  44.8 us (38%)
  starting transfers between devices  34.6 us (30%)
  waiting for transfers between devices  33.2 us (28%)
  local copies, waits for them, and re-layouts  2.3 us (2%)
  between operations  1.56 us (1%)
    all_to_all x5, starting transfers between devices, swap(): return lax.all_to_all(blocks, axes, 0, 0)  26.6 us
    all_to_all x5, waiting for transfers between devices, swap(): return lax.all_to_all(blocks, axes, 0, 0)  17.5 us
    ppermute x13, waiting for transfers between devices, partner(): lax.ppermute(array, axis, [(i, i ^ distance) for i in range(lax.axis_size...  15.7 us
    pallas_call x2, Pallas kernels, knot_backward(): pl.pallas_call(functools.partial(knot_backward_kernel, arrive), out_shape...  14 us
    pallas_call x2, Pallas kernels, knot_forward(): pl.pallas_call(functools.partial(knot_forward_kernel, n_stars, n_seg, lat...  9.98 us
    pallas_call x2, Pallas kernels, star_forward(): pl.pallas_call(functools.partial(star_forward_kernel, n_seg), out_shape=(...  9.52 us
    pallas_call x2, Pallas kernels, star_backward(): pl.pallas_call(star_backward_kernel, out_shape=(star_shape, scalar_shape)...  8.81 us
    ppermute x13, starting transfers between devices, partner(): lax.ppermute(array, axis, [(i, i ^ distance) for i in range(lax.axis_size...  7.94 us
  transfers between devices with their start and end apart: 18, of which 11 were waited for; matrix products, arithmetic and copies ran while one was open for 1% of the time, Pallas kernels for 16%

profile of v6, /device:TPU:0, one launch (start us, length us, event | category | flops | bytes accessed | tf_op | source)
XLA Modules:
  0.0 116.4 jit_solution(9938325150624915443)
XLA Ops:
  1.3 7.5 %knot_backward.2.after_ref = f32[8,40,256]{2,1,0:T(8,128)} custom-call(s32[1]{0:T(128)S(6)} %copy.17.live_ref, s32[1]{0:T(128)} %bitcast.place_ref, f32[128,128]{1,0:T(8,128)} %value_ref.3, f32[128,128]{1,0:T(8,128)} %cal_coef_ref.3, s32[1,128]{1,0:T(1,128)} %bitcast.10, s32[128,128]{1,0:T(8,128)} %knot_ref.3, f32[128,128]{1,0:T(8,128)} %frac_ref.3, ...), custom_call_target="tpu_custom_call" | custom-call | flops 3000000000 | bytes 1000000 | tf_op jit(solution)/shard_map/knot_backward/pallas_call | solution.py:432
  8.8 7.4 %all-to-all-start = ((f32[8,40,256]{2,1,0:T(8,128)}), f32[8,40,256]{2,1,0:T(8,128)S(1)}, u32[]{:S(2)}, u32[]{:S(2)}) async-start(f32[8,40,256]{2,1,0:T(8,128)} %knot_backward.2.after_ref), calls=%async_computation | async-start | bytes 655360 | tf_op jit(solution)/shard_map/all_to_all | solution.py:484
  16.3 4.4 %star_backward.2 = (f32[160,256]{1,0:T(8,128)S(1)}, f32[8,128]{1,0:T(8,128)S(1)}) custom-call(s32[1]{0:T(128)S(6)} %copy.17.live_ref, s32[128,128]{1,0:T(8,128)S(1)} %copy-done.4, f32[5,128,128]{2,1,0:T(8,128)S(1)} %copy-done.2, f32[128,128]{1,0:T(8,128)S(1)} %copy-done.1, f32[8,40,256]{2,1,0:T(8,128)S(1)} %copy-done), custom_call_target="tpu_custom_call" | custom-call | flops 3000000000 | bytes 1000000 | tf_op jit(solution)/shard_map/star_backward/pallas_call | solution.py:444
  20.7 5.9 %all-to-all-done.block_ref = f32[8,40,256]{2,1,0:T(8,128)S(1)} async-done(((f32[8,40,256]{2,1,0:T(8,128)}), f32[8,40,256]{2,1,0:T(8,128)S(1)}, u32[]{:S(2)}, u32[]{:S(2)}) %all-to-all-start) | async-done | bytes 327712 | tf_op jit(solution)/shard_map/all_to_all | solution.py:484
  27.3 3.6 %all-to-all-start.1 = ((f32[8,32,256]{2,1,0:T(8,128)}), f32[8,32,256]{2,1,0:T(8,128)S(1)}, u32[]{:S(2)}, u32[]{:S(2)}) async-start(f32[8,32,256]{2,1,0:T(8,128)} %get-tuple-element.26), calls=%async_computation.1 | async-start | bytes 524288 | tf_op jit(solution)/shard_map/all_to_all | solution.py:484
  31.1 1.4 %collective-permute-start.1 = (f32[160,256]{1,0:T(8,128)S(1)}, f32[160,256]{1,0:T(8,128)S(1)}, u32[]{:S(2)}, u32[]{:S(2)}) collective-permute-start(f32[160,256]{1,0:T(8,128)S(1)} %get-tuple-element.22.refs_0_), channel_id=1, source_target_pairs={{0,2},{1,3},{2,0},{3,1},{4,6},{5,7},{6,4},{7,5},{8,10},{9,11},{10,... | collective-permute-start | bytes 491528 | tf_op jit(solution)/shard_map/ppermute | solution.py:487
  33.9 1.6 %collective-permute-start.4 = (f32[8,128]{1,0:T(8,128)S(1)}, f32[8,128]{1,0:T(8,128)S(1)}, u32[]{:S(2)}, u32[]{:S(2)}) collective-permute-start(f32[8,128]{1,0:T(8,128)S(1)} %add.15.edge_ref), channel_id=1, source_target_pairs={{0,2},{1,3},{2,0},{3,1},{4,6},{5,7},{6,4},{7,5},{8,10},{9,11},{10,... | collective-permute-start | bytes 12296 | tf_op jit(solution)/shard_map/ppermute | solution.py:487
  35.5 1.8 %collective-permute-done.2.refs_3_ = f32[160,256]{1,0:T(8,128)S(1)} collective-permute-done((f32[160,256]{1,0:T(8,128)S(1)}, f32[160,256]{1,0:T(8,128)S(1)}, u32[]{:S(2)}, u32[]{:S(2)}) %collective-permute-start.2) | collective-permute-done | bytes 163872 | tf_op jit(solution)/shard_map/ppermute | solution.py:487
  37.3 3.6 %collective-permute-done.1.refs_2_ = f32[160,256]{1,0:T(8,128)S(1)} collective-permute-done((f32[160,256]{1,0:T(8,128)S(1)}, f32[160,256]{1,0:T(8,128)S(1)}, u32[]{:S(2)}, u32[]{:S(2)}) %collective-permute-start.1) | collective-permute-done | bytes 163872 | tf_op jit(solution)/shard_map/ppermute | solution.py:487
  40.9 4.8 %star_forward.2 = (f32[128,128]{1,0:T(8,128)S(1)}, f32[160,256]{1,0:T(8,128)S(1)}) custom-call(s32[128,128]{1,0:T(8,128)S(1)} %copy-done.4, f32[5,128,128]{2,1,0:T(8,128)S(1)} %copy-done.2, f32[160,256]{1,0:T(8,128)S(1)} %get-tuple-element.22.refs_0_, f32[160,256]{1,0:T(8,128)S(1)} %collective-permute-done.refs_1_, ...), custom_call_target="tpu_custom_call" | custom-call | flops 3000000000 | bytes 1000000 | tf_op jit(solution)/shard_map/star_forward/pallas_call | solution.py:456
  46.4 5.0 %knot_forward.2 = (f32[128,128]{1,0:T(8,128)S(1)}, f32[256,256]{1,0:T(8,128)S(1)}, f32[8,128]{1,0:T(8,128)S(1)}) custom-call(s32[1]{0:T(128)S(6)} %copy.17.live_ref, s32[1]{0:T(128)} %bitcast.place_ref, s32[128,128]{1,0:T(8,128)S(1)} %copy-done.5, f32[128,128]{1,0:T(8,128)S(1)} %copy-done.6, f32[4,128,128]{2,1,0:T(8,128)S(1)} %copy-done.3, ...), custom_call_target="tpu_custom_call" | custom-call | flops 3000000000 | bytes 1000000 | tf_op jit(solution)/shard_map/knot_forward/pallas_call | solution.py:469
  51.4 6.5 %knot_backward.3.after_ref = f32[8,40,256]{2,1,0:T(8,128)} custom-call(s32[1]{0:T(128)S(6)} %copy.17.live_ref, s32[1]{0:T(128)} %bitcast.place_ref, f32[128,128]{1,0:T(8,128)S(1)} %get-tuple-element.28.refs_0_.value_ref.refs_2_.image_0_ref, f32[128,128]{1,0:T(8,128)S(1)} %copy-done.7, s32[1,128]{1,0:T(1,128)S(1)} %bitcast.12, s32[128,128]{1,0:T(8,128)S(1)} %copy-done.5, ...), custom_call_target="tpu_custom_call" | custom-call | flops 3000000000 | bytes 1000000 | tf_op jit(solution)/shard_map/knot_backward/pallas_call | solution.py:432
  57.9 6.0 %all-to-all-start.2 = ((f32[8,40,256]{2,1,0:T(8,128)}), f32[8,40,256]{2,1,0:T(8,128)S(1)}, u32[]{:S(2)}, u32[]{:S(2)}) async-start(f32[8,40,256]{2,1,0:T(8,128)} %knot_backward.3.after_ref), calls=%async_computation.2 | async-start | bytes 655360 | tf_op jit(solution)/shard_map/all_to_all | solution.py:484
  63.8 4.4 %star_backward.3 = (f32[160,256]{1,0:T(8,128)S(1)}, f32[8,128]{1,0:T(8,128)S(1)}) custom-call(s32[1]{0:T(128)S(6)} %copy.17.live_ref, s32[128,128]{1,0:T(8,128)S(1)} %copy-done.4, f32[5,128,128]{2,1,0:T(8,128)S(1)} %copy-done.2, f32[128,128]{1,0:T(8,128)S(1)} %get-tuple-element.28.refs_0_.value_ref.refs_2_.image_0_ref, f32[8,40,256]{2,1,0:T(8,128)} %knot_backward.3.after_ref), custom_call_target="tpu_custom_call" | custom-call | flops 3000000000 | bytes 1000000 | tf_op jit(solution)/shard_map/star_backward/pallas_call | solution.py:444
  68.3 6.0 %all-to-all-done.2.block_ref = f32[8,40,256]{2,1,0:T(8,128)S(1)} async-done(((f32[8,40,256]{2,1,0:T(8,128)}), f32[8,40,256]{2,1,0:T(8,128)S(1)}, u32[]{:S(2)}, u32[]{:S(2)}) %all-to-all-start.2) | async-done | bytes 327712 | tf_op jit(solution)/shard_map/all_to_all | solution.py:484
  75.0 3.6 %all-to-all-start.3 = ((f32[8,32,256]{2,1,0:T(8,128)}), f32[8,32,256]{2,1,0:T(8,128)S(1)}, u32[]{:S(2)}, u32[]{:S(2)}) async-start(f32[8,32,256]{2,1,0:T(8,128)} %get-tuple-element.35), calls=%async_computation.3 | async-start | bytes 524288 | tf_op jit(solution)/shard_map/all_to_all | solution.py:484
  82.2 2.9 %collective-permute-done.9.refs_3_ = f32[160,256]{1,0:T(8,128)S(1)} collective-permute-done((f32[160,256]{1,0:T(8,128)S(1)}, f32[160,256]{1,0:T(8,128)S(1)}, u32[]{:S(2)}, u32[]{:S(2)}) %collective-permute-start.9) | collective-permute-done | bytes 163872 | tf_op jit(solution)/shard_map/ppermute | solution.py:487
  85.1 2.9 %collective-permute-done.8.refs_2_ = f32[160,256]{1,0:T(8,128)S(1)} collective-permute-done((f32[160,256]{1,0:T(8,128)S(1)}, f32[160,256]{1,0:T(8,128)S(1)}, u32[]{:S(2)}, u32[]{:S(2)}) %collective-permute-start.8) | collective-permute-done | bytes 163872 | tf_op jit(solution)/shard_map/ppermute | solution.py:487
  88.0 4.8 %star_forward.3 = (f32[128,128]{1,0:T(8,128)S(1)}, f32[160,256]{1,0:T(8,128)S(1)}) custom-call(s32[128,128]{1,0:T(8,128)S(1)} %copy-done.4, f32[5,128,128]{2,1,0:T(8,128)S(1)} %copy-done.2, f32[160,256]{1,0:T(8,128)S(1)} %get-tuple-element.32.refs_0_, f32[160,256]{1,0:T(8,128)S(1)} %collective-permute-done.7.refs_1_, ...), custom_call_target="tpu_custom_call" | custom-call | flops 3000000000 | bytes 1000000 | tf_op jit(solution)/shard_map/star_forward/pallas_call | solution.py:456
  92.8 5.0 %knot_forward.3 = (f32[128,128]{1,0:T(8,128)S(1)}, f32[256,256]{1,0:T(8,128)S(1)}, f32[8,128]{1,0:T(8,128)S(1)}) custom-call(s32[1]{0:T(128)S(6)} %copy.17.live_ref, s32[1]{0:T(128)} %bitcast.place_ref, s32[128,128]{1,0:T(8,128)S(1)} %copy-done.5, f32[128,128]{1,0:T(8,128)S(1)} %copy-done.6, f32[4,128,128]{2,1,0:T(8,128)S(1)} %copy-done.3, ...), custom_call_target="tpu_custom_call" | custom-call | flops 3000000000 | bytes 1000000 | tf_op jit(solution)/shard_map/knot_forward/pallas_call | solution.py:469
  98.5 1.2 %collective-permute-start.11 = (f32[8,128]{1,0:T(8,128)S(1)}, f32[8,128]{1,0:T(8,128)S(1)}, u32[]{:S(2)}, u32[]{:S(2)}) collective-permute-start(f32[8,128]{1,0:T(8,128)S(1)} %get-tuple-element.37), channel_id=1, source_target_pairs={{0,2},{1,3},{2,0},{3,1},{4,6},{5,7},{6,4},{7,5},{8,10},{9,11},{10,... | collective-permute-start | bytes 12296 | tf_op jit(solution)/shard_map/ppermute | solution.py:487
  100.9 1.2 %collective-permute-done.11 = f32[8,128]{1,0:T(8,128)S(1)} collective-permute-done((f32[8,128]{1,0:T(8,128)S(1)}, f32[8,128]{1,0:T(8,128)S(1)}, u32[]{:S(2)}, u32[]{:S(2)}) %collective-permute-start.11) | collective-permute-done | bytes 4128 | tf_op jit(solution)/shard_map/ppermute | solution.py:487
  102.7 6.0 %all-to-all-start.4 = ((f32[8,8,128]{2,1,0:T(8,128)}), f32[8,8,128]{2,1,0:T(8,128)S(1)}, u32[]{:S(2)}, u32[]{:S(2)}) async-start(f32[8,8,128]{2,1,0:T(8,128)} %broadcast_in_dim.14), calls=%async_computation.4 | async-start | bytes 65536 | tf_op jit(solution)/shard_map/all_to_all | solution.py:484
  109.8 5.6 %all-to-all-done.4.scalar_ref = f32[8,8,128]{2,1,0:T(8,128)S(1)} async-done(((f32[8,8,128]{2,1,0:T(8,128)}), f32[8,8,128]{2,1,0:T(8,128)S(1)}, u32[]{:S(2)}, u32[]{:S(2)}) %all-to-all-start.4) | async-done | bytes 32800 | tf_op jit(solution)/shard_map/all_to_all | solution.py:484
  (53 shorter events, 11.9 us)
Async XLA Ops:
  1.3 15.0 %copy-start.2 = (f32[5,128,128]{2,1,0:T(8,128)S(1)}, f32[5,128,128]{2,1,0:T(8,128)}, u32[]{:S(2)}) copy-start(f32[5,128,128]{2,1,0:T(8,128)} %star_coef_ref.7) | copy-start | bytes 983044
  8.8 7.4 %copy-start = (f32[8,40,256]{2,1,0:T(8,128)S(1)}, f32[8,40,256]{2,1,0:T(8,128)}, u32[]{:S(2)}) copy-start(f32[8,40,256]{2,1,0:T(8,128)} %knot_backward.2.after_ref) | copy-start | bytes 983044
  8.8 17.7 %all-to-all-start = ((f32[8,40,256]{2,1,0:T(8,128)}), f32[8,40,256]{2,1,0:T(8,128)S(1)}, u32[]{:S(2)}, u32[]{:S(2)}) async-start(f32[8,40,256]{2,1,0:T(8,128)} %knot_backward.2.after_ref), calls=%async_computation | async-start | bytes 655360 | tf_op jit(solution)/shard_map/all_to_all | solution.py:484
  27.3 18.4 %all-to-all-start.1 = ((f32[8,32,256]{2,1,0:T(8,128)}), f32[8,32,256]{2,1,0:T(8,128)S(1)}, u32[]{:S(2)}, u32[]{:S(2)}) async-start(f32[8,32,256]{2,1,0:T(8,128)} %get-tuple-element.26), calls=%async_computation.1 | async-start | bytes 524288 | tf_op jit(solution)/shard_map/all_to_all | solution.py:484
  30.9 6.4 %collective-permute-start.2 = (f32[160,256]{1,0:T(8,128)S(1)}, f32[160,256]{1,0:T(8,128)S(1)}, u32[]{:S(2)}, u32[]{:S(2)}) collective-permute-start(f32[160,256]{1,0:T(8,128)S(1)} %get-tuple-element.22.refs_0_), channel_id=1, source_target_pairs={{0,3},{1,2},{2,1},{3,0},{4,7},{5,6},{6,5},{7,4},{8,11},{9,10},{10,... | collective-permute-start | bytes 491528 | tf_op jit(solution)/shard_map/ppermute | solution.py:487
  31.1 9.8 %collective-permute-start.1 = (f32[160,256]{1,0:T(8,128)S(1)}, f32[160,256]{1,0:T(8,128)S(1)}, u32[]{:S(2)}, u32[]{:S(2)}) collective-permute-start(f32[160,256]{1,0:T(8,128)S(1)} %get-tuple-element.22.refs_0_), channel_id=1, source_target_pairs={{0,2},{1,3},{2,0},{3,1},{4,6},{5,7},{6,4},{7,5},{8,10},{9,11},{10,... | collective-permute-start | bytes 491528 | tf_op jit(solution)/shard_map/ppermute | solution.py:487
  32.5 8.5 %collective-permute-start = (f32[160,256]{1,0:T(8,128)S(1)}, f32[160,256]{1,0:T(8,128)S(1)}, u32[]{:S(2)}, u32[]{:S(2)}) collective-permute-start(f32[160,256]{1,0:T(8,128)S(1)} %get-tuple-element.22.refs_0_), channel_id=1, source_target_pairs={{0,1},{1,0},{2,3},{3,2},{4,5},{5,4},{6,7},{7,6},{8,9},{9,8},{10,11... | collective-permute-start | bytes 491528 | tf_op jit(solution)/shard_map/ppermute | solution.py:487
  32.7 1.2 %collective-permute-start.3 = (f32[8,128]{1,0:T(8,128)S(1)}, f32[8,128]{1,0:T(8,128)S(1)}, u32[]{:S(2)}, u32[]{:S(2)}) collective-permute-start(f32[8,128]{1,0:T(8,128)S(1)} %get-tuple-element.27), channel_id=1, source_target_pairs={{0,1},{1,0},{2,3},{3,2},{4,5},{5,4},{6,7},{7,6},{8,9},{9,8},{10,11... | collective-permute-start | bytes 12296 | tf_op jit(solution)/shard_map/ppermute | solution.py:487
  33.9 11.8 %copy-start.3 = (f32[4,128,128]{2,1,0:T(8,128)S(1)}, f32[4,128,128]{2,1,0:T(8,128)}, u32[]{:S(2)}) copy-start(f32[4,128,128]{2,1,0:T(8,128)} %att_coef_ref.3) | copy-start | bytes 786436
  33.9 11.8 %copy-start.5 = (s32[128,128]{1,0:T(8,128)S(1)}, s32[128,128]{1,0:T(8,128)}, u32[]{:S(2)}) copy-start(s32[128,128]{1,0:T(8,128)} %knot_ref.3) | copy-start | bytes 196612
  33.9 11.8 %copy-start.6 = (f32[128,128]{1,0:T(8,128)S(1)}, f32[128,128]{1,0:T(8,128)}, u32[]{:S(2)}) copy-start(f32[128,128]{1,0:T(8,128)} %frac_ref.3) | copy-start | bytes 196612
  33.9 11.9 %copy-start.7 = (f32[128,128]{1,0:T(8,128)S(1)}, f32[128,128]{1,0:T(8,128)}, u32[]{:S(2)}) copy-start(f32[128,128]{1,0:T(8,128)} %cal_coef_ref.3) | copy-start | bytes 196612
  33.9 11.8 %collective-permute-start.4 = (f32[8,128]{1,0:T(8,128)S(1)}, f32[8,128]{1,0:T(8,128)S(1)}, u32[]{:S(2)}, u32[]{:S(2)}) collective-permute-start(f32[8,128]{1,0:T(8,128)S(1)} %add.15.edge_ref), channel_id=1, source_target_pairs={{0,2},{1,3},{2,0},{3,1},{4,6},{5,7},{6,4},{7,5},{8,10},{9,11},{10,... | collective-permute-start | bytes 12296 | tf_op jit(solution)/shard_map/ppermute | solution.py:487
  57.9 16.4 %all-to-all-start.2 = ((f32[8,40,256]{2,1,0:T(8,128)}), f32[8,40,256]{2,1,0:T(8,128)S(1)}, u32[]{:S(2)}, u32[]{:S(2)}) async-start(f32[8,40,256]{2,1,0:T(8,128)} %knot_backward.3.after_ref), calls=%async_computation.2 | async-start | bytes 655360 | tf_op jit(solution)/shard_map/all_to_all | solution.py:484
  75.0 17.7 %all-to-all-start.3 = ((f32[8,32,256]{2,1,0:T(8,128)}), f32[8,32,256]{2,1,0:T(8,128)S(1)}, u32[]{:S(2)}, u32[]{:S(2)}) async-start(f32[8,32,256]{2,1,0:T(8,128)} %get-tuple-element.35), calls=%async_computation.3 | async-start | bytes 524288 | tf_op jit(solution)/shard_map/all_to_all | solution.py:484
  78.7 6.4 %collective-permute-start.9 = (f32[160,256]{1,0:T(8,128)S(1)}, f32[160,256]{1,0:T(8,128)S(1)}, u32[]{:S(2)}, u32[]{:S(2)}) collective-permute-start(f32[160,256]{1,0:T(8,128)S(1)} %get-tuple-element.32.refs_0_), channel_id=1, source_target_pairs={{0,3},{1,2},{2,1},{3,0},{4,7},{5,6},{6,5},{7,4},{8,11},{9,10},{10,... | collective-permute-start | bytes 491528 | tf_op jit(solution)/shard_map/ppermute | solution.py:487
  78.7 9.3 %collective-permute-start.8 = (f32[160,256]{1,0:T(8,128)S(1)}, f32[160,256]{1,0:T(8,128)S(1)}, u32[]{:S(2)}, u32[]{:S(2)}) collective-permute-start(f32[160,256]{1,0:T(8,128)S(1)} %get-tuple-element.32.refs_0_), channel_id=1, source_target_pairs={{0,2},{1,3},{2,0},{3,1},{4,6},{5,7},{6,4},{7,5},{8,10},{9,11},{10,... | collective-permute-start | bytes 491528 | tf_op jit(solution)/shard_map/ppermute | solution.py:487
  79.7 8.3 %collective-permute-start.7 = (f32[160,256]{1,0:T(8,128)S(1)}, f32[160,256]{1,0:T(8,128)S(1)}, u32[]{:S(2)}, u32[]{:S(2)}) collective-permute-start(f32[160,256]{1,0:T(8,128)S(1)} %get-tuple-element.32.refs_0_), channel_id=1, source_target_pairs={{0,1},{1,0},{2,3},{3,2},{4,5},{5,4},{6,7},{7,6},{8,9},{9,8},{10,11... | collective-permute-start | bytes 491528 | tf_op jit(solution)/shard_map/ppermute | solution.py:487
  80.5 1.2 %collective-permute-start.5 = (f32[8,128]{1,0:T(8,128)S(1)}, f32[8,128]{1,0:T(8,128)S(1)}, u32[]{:S(2)}, u32[]{:S(2)}) collective-permute-start(f32[8,128]{1,0:T(8,128)S(1)} %get-tuple-element.31), channel_id=1, source_target_pairs={{0,1},{1,0},{2,3},{3,2},{4,5},{5,4},{6,7},{7,6},{8,9},{9,8},{10,11... | collective-permute-start | bytes 12296 | tf_op jit(solution)/shard_map/ppermute | solution.py:487
  81.7 11.0 %collective-permute-start.6 = (f32[8,128]{1,0:T(8,128)S(1)}, f32[8,128]{1,0:T(8,128)S(1)}, u32[]{:S(2)}, u32[]{:S(2)}) collective-permute-start(f32[8,128]{1,0:T(8,128)S(1)} %add.16.edge_ref), channel_id=1, source_target_pairs={{0,2},{1,3},{2,0},{3,1},{4,6},{5,7},{6,4},{7,5},{8,10},{9,11},{10,... | collective-permute-start | bytes 12296 | tf_op jit(solution)/shard_map/ppermute | solution.py:487
  97.8 3.1 %collective-permute-start.12 = (f32[8,128]{1,0:T(8,128)S(1)}, f32[8,128]{1,0:T(8,128)S(1)}, u32[]{:S(2)}, u32[]{:S(2)}) collective-permute-start(f32[8,128]{1,0:T(8,128)S(1)} %get-tuple-element.37), channel_id=1, source_target_pairs={{0,3},{1,2},{2,1},{3,0},{4,7},{5,6},{6,5},{7,4},{8,11},{9,10},{10,... | collective-permute-start | bytes 12296 | tf_op jit(solution)/shard_map/ppermute | solution.py:487
  98.5 3.6 %collective-permute-start.11 = (f32[8,128]{1,0:T(8,128)S(1)}, f32[8,128]{1,0:T(8,128)S(1)}, u32[]{:S(2)}, u32[]{:S(2)}) collective-permute-start(f32[8,128]{1,0:T(8,128)S(1)} %get-tuple-element.37), channel_id=1, source_target_pairs={{0,2},{1,3},{2,0},{3,1},{4,6},{5,7},{6,4},{7,5},{8,10},{9,11},{10,... | collective-permute-start | bytes 12296 | tf_op jit(solution)/shard_map/ppermute | solution.py:487
  99.7 2.4 %collective-permute-start.10 = (f32[8,128]{1,0:T(8,128)S(1)}, f32[8,128]{1,0:T(8,128)S(1)}, u32[]{:S(2)}, u32[]{:S(2)}) collective-permute-start(f32[8,128]{1,0:T(8,128)S(1)} %get-tuple-element.37), channel_id=1, source_target_pairs={{0,1},{1,0},{2,3},{3,2},{4,5},{5,4},{6,7},{7,6},{8,9},{9,8},{10,11... | collective-permute-start | bytes 12296 | tf_op jit(solution)/shard_map/ppermute | solution.py:487
  102.7 12.7 %all-to-all-start.4 = ((f32[8,8,128]{2,1,0:T(8,128)}), f32[8,8,128]{2,1,0:T(8,128)S(1)}, u32[]{:S(2)}, u32[]{:S(2)}) async-start(f32[8,8,128]{2,1,0:T(8,128)} %broadcast_in_dim.14), calls=%async_computation.4 | async-start | bytes 65536 | tf_op jit(solution)/shard_map/all_to_all | solution.py:484
  (3 other events, 15.5 us)

commit v7 on v6

--- a/solution.py
+++ b/solution.py
@@ -69,7 +69,7 @@
 
 
 def store_rows(out_ref, begin, rows):
-    block = out_ref.shape[1] - 8
+    block = out_ref.shape[1]
     for offset in range(0, rows.shape[0], 8):
         where = begin + offset
         out_ref[where // block, where % block : where % block + 8, :] = rows[offset : offset + 8]
@@ -77,8 +77,11 @@
 
 def knot_backward_kernel(arrive, live_ref, place_ref, *refs):
     observed, refs = refs[:6], refs[6:]
+    if not arrive:
+        scalar_ref, *refs = refs
+    table_out, edge_out, knot_acc = refs[:3]
     if arrive:
-        table_out, knot_acc, *buffers, sems = refs
+        *buffers, sems = refs[3:]
         copies = [
             pltpu.make_async_copy(source, target, sems.at[which])
             for which, (source, target) in enumerate(zip(observed, buffers))
@@ -86,8 +89,6 @@
         for copy in copies:
             copy.start()
         observed = buffers
-    else:
-        scalar_ref, table_out, knot_acc = refs
     value_ref, cal_coef_ref, tile_cal_ref, knot_ref, frac_ref, att_coef_ref = observed
     knot_acc[...] = jnp.zeros_like(knot_acc)
     if arrive:
@@ -153,15 +154,12 @@
     edges = pltpu.roll(edges, SLOT * place_ref[0], 1)
     if not arrive:
         edges = edges + scalar_ref[...]
-    edges = jnp.concatenate([edges, jnp.zeros_like(edges)], axis=1)
-    for device in range(table_out.shape[0]):
-        table_out[device, table_out.shape[1] - 8 :, :] = edges
+    edge_out[...] = jnp.concatenate([edges, jnp.zeros_like(edges)], axis=1)
 
 
 def star_backward_kernel(
-    live_ref, star_ref, star_coef_ref, value_ref, after_ref, star_out, token_out, star_acc
+    live_ref, star_ref, star_coef_ref, value_ref, edge_ref, star_out, star_acc
 ):
-    token_out[...] = jnp.zeros_like(token_out)
     star_acc[...] = jnp.zeros_like(star_acc)
 
     @pl.loop(0, star_ref.shape[0] // WIDE_GROUP)
@@ -187,17 +185,19 @@
             jnp.concatenate(left, axis=1), jnp.concatenate(right, axis=1), ((1,), (1,))
         )
 
-    star_out[...] = star_acc[:STAR_ROWS] + star_acc[STAR_ROWS:]
-
-
-def sum_kernel(after_ref, block_ref, out_ref, edge_out):
+    star_out[:STAR_ROWS] = star_acc[:STAR_ROWS] + star_acc[STAR_ROWS:]
+    star_out[STAR_ROWS:] = edge_ref[...]
+
+
+def sum_kernel(block_ref, own_ref, other_ref, out_ref, star_out):
     total = block_ref[0]
     for device in range(1, block_ref.shape[0]):
         total = total + block_ref[device]
-    rows = out_ref.shape[1]
+    star = own_ref[...] + other_ref[...]
+    star_out[...] = star[:STAR_ROWS]
     for device in range(block_ref.shape[0]):
-        out_ref[device] = total[:rows]
-    edge_out[...] = total[rows:, :128]
+        out_ref[device, :-8] = total
+        out_ref[device, -8:] = star[STAR_ROWS:]
 
 
 def picked(array, which):
@@ -219,12 +219,8 @@
     return picked(edges, 0), picked(edges, 1)
 
 
-def star_forward_kernel(n_seg, star_ref, star_coef_ref, *refs):
-    term_refs, (image_ref, star_out, star_parts_ref) = refs[:n_seg], refs[n_seg:]
-    star_x = term_refs[0][...]
-    for term_ref in term_refs[1:]:
-        star_x = star_x + term_ref[...]
-    star_out[...] = star_x
+def star_forward_kernel(star_ref, star_coef_ref, star_x_ref, image_ref, star_parts_ref):
+    star_x = star_x_ref[...]
     star_high, star_low = two_parts(star_x)
     star_parts_ref[:STAR_ROWS] = star_high
     star_parts_ref[STAR_ROWS:] = star_low
@@ -260,7 +256,7 @@
 
 def knot_forward_kernel(
     n_stars, n_seg, later, live_ref, place_ref, knot_ref, frac_ref, att_coef_ref, cal_coef_ref,
-    tile_cal_ref, star_image_ref, star_x_ref, table_x_ref, edge_ref, other_edge_ref, *refs,
+    tile_cal_ref, star_image_ref, star_x_ref, block_ref, *refs,
 ):
     if later:
         star_0_ref, table_0_ref, image_0_ref, image_ref, table_out, scalar_out = refs[:6]
@@ -272,7 +268,9 @@
     row = lax.broadcasted_iota(jnp.int32, (8, 128), 0)
     wide_lane = lax.broadcasted_iota(jnp.int32, (8, COARSE), 1)
 
-    edges = edge_ref[...] + other_edge_ref[...]
+    edges = block_ref[0, -8:, :128]
+    for block in range(1, n_stars):
+        edges = edges + block_ref[block, -8:, :128]
 
     def slot(which):
         return pltpu.roll(edges, 128 - SLOT * jnp.clip(which, 0, n_seg - 1), 1)
@@ -282,7 +280,7 @@
     ahead = jnp.where(lane % 2 == 0, own, 0.0) + pltpu.roll(jnp.where(lane % 2 == 1, after, 0.0), 127, 1)
     ahead = jnp.where((segment < n_seg - 1) & (lane < 8) & (row < 3), ahead, 0.0)
 
-    table = table_x_ref[...]
+    table = block_ref[:, :-8, :].reshape(TABLE_ROWS, COARSE)
     pieces = []
     for comp in range(4):
         shifted = pltpu.roll(before, 128 - 2 * comp, 1) if comp else before
@@ -359,15 +357,19 @@
     zero = jnp.zeros((GROUP, knot_ref.shape[1]), F32)
     start = (zero, zero) if later else (zero,)
     sums = lax.fori_loop(0, knot_ref.shape[0] // GROUP, one_group, start, unroll=2)
-    scalars = [(0, norm)] + [(1 + which, jnp.sum(part, keepdims=True)) for which, part in enumerate(sums)]
-    scalar_out[...] = with_scalars(jnp.zeros((8, 128), F32), scalars)
+    scalars = [norm] + [jnp.sum(part, keepdims=True) for part in sums]
+    if later:
+        scalars += [norm_0, square_0]
+    scalars = with_scalars(jnp.zeros((8, 128), F32), list(enumerate(scalars)))
+    for device in range(scalar_out.shape[0]):
+        scalar_out[device] = scalars
 
 
 def output_kernel(
-    live_ref, edge_ref, other_edge_ref, scalar_ref, star_0_ref, star_h_ref, att_0_ref, att_h_ref,
-    table_0_ref, table_h_ref, value_ref, image_0_ref, image_1_ref, star_out, att_out, cal_out, residual_out,
+    live_ref, own_scalar_ref, scalar_ref, star_0_ref, star_h_ref, att_0_ref, att_h_ref, table_0_ref,
+    table_h_ref, value_ref, image_0_ref, image_1_ref, star_out, att_out, cal_out, residual_out,
 ):
-    norm_0, square_0 = first_step(edge_ref[...] + other_edge_ref[...])
+    norm_0, square_0 = [picked(own_scalar_ref[0], which) for which in (3, 4)]
     everyone = scalar_ref[0]
     for device in range(1, scalar_ref.shape[0]):
         everyone = everyone + scalar_ref[device]
@@ -420,7 +422,6 @@
     image_shape = shaped(tile_count, width)
     table_shape = shaped(TABLE_ROWS, COARSE)
     star_shape = shaped(STAR_ROWS, COARSE)
-    scalar_shape = shaped(8, 128)
 
     def knot_backward(values, *scalars):
         arrive = not scalars
@@ -431,44 +432,44 @@
             scratch += [pltpu.SemaphoreType.DMA((len(observed),))]
         return pl.pallas_call(
             functools.partial(knot_backward_kernel, arrive),
-            out_shape=shaped(n_stars, TABLE_ROWS // n_stars + 8, COARSE),
+            out_shape=(shaped(n_stars, TABLE_ROWS // n_stars, COARSE), shaped(8, COARSE)),
             in_specs=in_smem(2) + (in_hbm if arrive else in_vmem)(len(observed)) + in_vmem(len(scalars)),
-            out_specs=in_vmem(1)[0],
+            out_specs=tuple(in_vmem(2)),
             scratch_shapes=scratch,
             compiler_params=ARRIVE_PARAMS if arrive else PARAMS,
             cost_estimate=PASS_COST,
             name="knot_backward",
         )(live_tiles, place, *observed, *scalars)
 
-    def star_backward(values, after):
+    def star_backward(values, edges):
         return pl.pallas_call(
             star_backward_kernel,
-            out_shape=(star_shape, scalar_shape),
-            in_specs=in_smem(1) + in_vmem(3) + in_hbm(1),
-            out_specs=tuple(in_vmem(2)),
+            out_shape=shaped(STAR_ROWS + 8, COARSE),
+            in_specs=in_smem(1) + in_vmem(4),
+            out_specs=in_vmem(1)[0],
             scratch_shapes=[pltpu.VMEM((2 * STAR_ROWS, COARSE), F32)],
             compiler_params=PARAMS,
             cost_estimate=PASS_COST,
             name="star_backward",
-        )(live_tiles, obs_star, star_coef, values, after)
-
-    def star_forward(*terms):
+        )(live_tiles, obs_star, star_coef, values, edges)
+
+    def star_forward(star):
         return pl.pallas_call(
-            functools.partial(star_forward_kernel, n_seg),
-            out_shape=(image_shape, star_shape),
-            in_specs=in_vmem(2 + n_seg),
-            out_specs=tuple(in_vmem(2)),
+            star_forward_kernel,
+            out_shape=image_shape,
+            in_specs=in_vmem(3),
+            out_specs=in_vmem(1)[0],
             scratch_shapes=[pltpu.VMEM((2 * STAR_ROWS, COARSE), BF16)],
             compiler_params=PARAMS,
             cost_estimate=PASS_COST,
             name="star_forward",
-        )(obs_star, star_coef, *terms)
+        )(obs_star, star_coef, star)
 
     def knot_forward(*arrays):
-        later = len(arrays) > 5
+        later = len(arrays) > 3
         return pl.pallas_call(
             functools.partial(knot_forward_kernel, n_stars, n_seg, later),
-            out_shape=(image_shape, table_shape, scalar_shape),
+            out_shape=(image_shape, table_shape, shaped(n_stars * n_seg if later else 1, 8, 128)),
             in_specs=in_smem(2) + in_vmem(5 + len(arrays)),
             out_specs=tuple(in_vmem(3)),
             scratch_shapes=[
@@ -486,42 +487,27 @@
     def partner(array, axis, distance):
         return lax.ppermute(array, axis, [(i, i ^ distance) for i in range(lax.axis_size(axis))])
 
-    def everyones(array, axis):
-        return [array] + [partner(array, axis, distance) for distance in range(1, lax.axis_size(axis))]
-
-    def table_sum(table, token):
-        blocks = swap(table, "stars")
-        copies, edge = pl.pallas_call(
+    def half(values, *scalars):
+        table, edges = knot_backward(values, *scalars)
+        star = star_backward(values, edges)
+        distances = [1 << bit for bit in range(n_seg.bit_length() - 1)]
+        for distance in distances[:-1]:
+            star = star + partner(star, "seg", distance)
+        blocks, star = pl.pallas_call(
             sum_kernel,
-            out_shape=(shaped(n_stars, TABLE_ROWS // n_stars, COARSE), scalar_shape),
-            in_specs=in_hbm(1) + in_vmem(1),
+            out_shape=(shaped(n_stars, TABLE_ROWS // n_stars + 8, COARSE), star_shape),
+            in_specs=in_vmem(3),
             out_specs=tuple(in_vmem(2)),
             compiler_params=PARAMS,
             cost_estimate=SMALL_COST,
             name="table_sum",
-        )(token, blocks)
-        for distance in [1 << bit for bit in range(n_seg.bit_length() - 2)]:
-            edge = edge + partner(edge, "seg", distance)
-        table = swap(copies, "stars").reshape(TABLE_ROWS, COARSE)
-        return table, (edge, partner(edge, "seg", n_seg // 2))
-
-    def half(values, *scalars):
-        table = knot_backward(values, *scalars)
-        star, token = star_backward(values, table)
-        stars = everyones(star, "seg")
-        table, edges = table_sum(table, token)
-        star_image, star = star_forward(*stars)
-        return star_image, star, table, edges
-
-    star_image, star_0, table, edges = half(obs_value)
-    image_0, table_0, scalars = knot_forward(star_image, star_0, table, *edges)
-    star_image, star_h, table, edges = half(image_0, scalars)
-    image_1, table_h, scalars = knot_forward(
-        star_image, star_h, table, *edges, star_0, table_0, image_0
-    )
-
-    scalars = sum(everyones(scalars, "seg"))
-    scalars = swap(jnp.broadcast_to(scalars[None], (n_stars, *scalars.shape)), "stars")
+        )(swap(table, "stars"), star, partner(star, "seg", distances[-1]))
+        return star_forward(star), star, swap(blocks, "stars")
+
+    star_image, star_0, blocks = half(obs_value)
+    image_0, table_0, scalars = knot_forward(star_image, star_0, blocks)
+    star_image, star_h, blocks = half(image_0, scalars[0])
+    image_1, table_h, scalars = knot_forward(star_image, star_h, blocks, star_0, table_0, image_0)
 
     def star_order(star):
         return star.reshape(5, STAR_DEV)
@@ -533,14 +519,14 @@
     return pl.pallas_call(
         output_kernel,
         out_shape=(shaped(5, STAR_DEV), shaped(4, KNOT_DEV), shaped(CALB_DEV, width), image_shape),
-        in_specs=in_smem(1) + in_vmem(12),
+        in_specs=in_smem(1) + in_vmem(11),
         out_specs=tuple(in_vmem(4)),
         compiler_params=PARAMS,
         cost_estimate=SMALL_COST,
         name="outputs",
     )(
-        live_tiles, *edges, scalars, star_order(star_0), star_order(star_h), att_order(table_0),
-        att_order(table_h), table_0, table_h, obs_value, image_0, image_1,
+        live_tiles, scalars, swap(scalars, ("stars", "seg")), star_order(star_0), star_order(star_h),
+        att_order(table_0), att_order(table_h), table_0, table_h, obs_value, image_0, image_1,
     )
 
 

time: 117 us -> 109 us (0.932)
  starting transfers between devices: 34.6 us -> 30 us
  waiting for transfers between devices: 33.2 us -> 29.7 us
  Pallas kernels: 44.8 us -> 46.2 us
  local copies, waits for them, and re-layouts: 2.3 us -> 1.09 us
    ppermute x13 -> x4, starting transfers between devices: 7.94 us -> 3.31 us  [partner(): lax.ppermute(array, axis, [(i, i ^ distance) for i in range(lax.axis_size...]
    ppermute x13 -> x4, waiting for transfers between devices: 15.7 us -> 12.6 us  [partner(): lax.ppermute(array, axis, [(i, i ^ distance) for i in range(lax.axis_size...]
  transfers between devices with their start and end apart: 18 -> 9, of which waited for: 11 -> 7; matrix products, arithmetic and copies ran while one was open for 1% -> 1% of each run, Pallas kernels for 16% -> 17%
where the time goes in v7:
time: 109 us
  Pallas kernels  46.2 us (42%)
  starting transfers between devices  30 us (28%)
  waiting for transfers between devices  29.7 us (27%)
  between operations  1.53 us (1%)
  local copies, waits for them, and re-layouts  1.09 us (1%)
    all_to_all x5, starting transfers between devices, swap(): return lax.all_to_all(blocks, axes, 0, 0)  26.7 us
    all_to_all x5, waiting for transfers between devices, swap(): return lax.all_to_all(blocks, axes, 0, 0)  17.1 us
    pallas_call x2, Pallas kernels, knot_backward(): pl.pallas_call(functools.partial(knot_backward_kernel, arrive), out_shape...  13.8 us
    ppermute x4, waiting for transfers between devices, partner(): lax.ppermute(array, axis, [(i, i ^ distance) for i in range(lax.axis_size...  12.6 us
    pallas_call x2, Pallas kernels, knot_forward(): pl.pallas_call(functools.partial(knot_forward_kernel, n_stars, n_seg, lat...  10.7 us
    pallas_call x2, Pallas kernels, star_forward(): pl.pallas_call(star_forward_kernel, out_shape=image_shape, in_specs=in_vm...  9.47 us
    pallas_call x2, Pallas kernels, star_backward(): pl.pallas_call(star_backward_kernel, out_shape=shaped(STAR_ROWS + 8, COAR...  8.81 us
    ppermute x4, starting transfers between devices, partner(): lax.ppermute(array, axis, [(i, i ^ distance) for i in range(lax.axis_size...  3.31 us
  transfers between devices with their start and end apart: 9, of which 7 were waited for; matrix products, arithmetic and copies ran while one was open for 1% of the time, Pallas kernels for 17%

profile of v7, /device:TPU:0, one launch (start us, length us, event | category | flops | bytes accessed | tf_op | source)
XLA Modules:
  0.0 108.6 jit_solution(13003540212898485508)
XLA Ops:
  1.3 7.4 %knot_backward.2 = (f32[8,32,256]{2,1,0:T(8,128)}, f32[8,256]{1,0:T(8,128)}) custom-call(s32[1]{0:T(128)S(6)} %copy.17.live_ref, s32[1]{0:T(128)} %bitcast.place_ref, f32[128,128]{1,0:T(8,128)} %value_ref.3, f32[128,128]{1,0:T(8,128)} %cal_coef_ref.3, s32[1,128]{1,0:T(1,128)} %bitcast.7, s32[128,128]{1,0:T(8,128)} %knot_ref.3, f32[128,128]{1,0:T(8,128)} %frac_ref.3, ...), custom_call_target="tpu_custom_call" | custom-call | flops 3000000000 | bytes 1000000 | tf_op jit(solution)/shard_map/knot_backward/pallas_call | solution.py:433
  8.7 7.4 %all-to-all-start = ((f32[8,32,256]{2,1,0:T(8,128)}), f32[8,32,256]{2,1,0:T(8,128)S(1)}, u32[]{:S(2)}, u32[]{:S(2)}) async-start(f32[8,32,256]{2,1,0:T(8,128)} %get-tuple-element.18), calls=%async_computation | async-start | bytes 524288 | tf_op jit(solution)/shard_map/all_to_all | solution.py:485
  16.1 4.4 %star_backward.2 = f32[168,256]{1,0:T(8,128)S(1)} custom-call(s32[1]{0:T(128)S(6)} %copy.17.live_ref, s32[128,128]{1,0:T(8,128)S(1)} %copy-done.3, f32[5,128,128]{2,1,0:T(8,128)S(1)} %copy-done.1, f32[128,128]{1,0:T(8,128)S(1)} %copy-done, f32[8,256]{1,0:T(8,128)S(1)} %copy-done.8), custom_call_target="tpu_custom_call" | custom-call | flops 3000000000 | bytes 1000000 | tf_op jit(solution)/shard_map/star_backward/pallas_call | solution.py:445
  20.6 1.4 %collective-permute-done = f32[168,256]{1,0:T(8,128)S(1)} collective-permute-done((f32[168,256]{1,0:T(8,128)S(1)}, f32[168,256]{1,0:T(8,128)S(1)}, u32[]{:S(2)}, u32[]{:S(2)}) %collective-permute-start) | collective-permute-done | bytes 172064 | tf_op jit(solution)/shard_map/ppermute | solution.py:488
  22.1 1.6 %collective-permute-start.1 = (f32[168,256]{1,0:T(8,128)S(1)}, f32[168,256]{1,0:T(8,128)S(1)}, u32[]{:S(2)}, u32[]{:S(2)}) collective-permute-start(f32[168,256]{1,0:T(8,128)S(1)} %add.6.own_ref), channel_id=1, source_target_pairs={{0,2},{1,3},{2,0},{3,1},{4,6},{5,7},{6,4},{7,5},{8,10},{9,11},{10,... | collective-permute-start | bytes 516104 | tf_op jit(solution)/shard_map/ppermute | solution.py:488
  23.6 4.9 %collective-permute-done.1.other_ref = f32[168,256]{1,0:T(8,128)S(1)} collective-permute-done((f32[168,256]{1,0:T(8,128)S(1)}, f32[168,256]{1,0:T(8,128)S(1)}, u32[]{:S(2)}, u32[]{:S(2)}) %collective-permute-start.1) | collective-permute-done | bytes 172064 | tf_op jit(solution)/shard_map/ppermute | solution.py:488
  28.5 0.8 table_sum.2
  29.3 6.0 %all-to-all-start.1 = ((f32[8,40,256]{2,1,0:T(8,128)}), f32[8,40,256]{2,1,0:T(8,128)S(1)}, u32[]{:S(2)}, u32[]{:S(2)}) async-start(f32[8,40,256]{2,1,0:T(8,128)} %get-tuple-element.21), calls=%async_computation.1 | async-start | bytes 655360 | tf_op jit(solution)/shard_map/all_to_all | solution.py:485
  35.4 4.7 %star_forward.2.star_image_ref = f32[128,128]{1,0:T(8,128)S(1)} custom-call(s32[128,128]{1,0:T(8,128)S(1)} %copy-done.3, f32[5,128,128]{2,1,0:T(8,128)S(1)} %copy-done.1, f32[160,256]{1,0:T(8,128)S(1)} %get-tuple-element.20.star_x_ref.refs_0_), custom_call_target="tpu_custom_call" | custom-call | flops 3000000000 | bytes 1000000 | tf_op jit(solution)/shard_map/star_forward/pallas_call | solution.py:457
  40.1 5.0 %all-to-all-done.1.block_ref = f32[8,40,256]{2,1,0:T(8,128)S(1)} async-done(((f32[8,40,256]{2,1,0:T(8,128)}), f32[8,40,256]{2,1,0:T(8,128)S(1)}, u32[]{:S(2)}, u32[]{:S(2)}) %all-to-all-start.1) | async-done | bytes 327712 | tf_op jit(solution)/shard_map/all_to_all | solution.py:485
  45.1 5.0 %knot_forward.2 = (f32[128,128]{1,0:T(8,128)S(1)}, f32[256,256]{1,0:T(8,128)S(1)}, f32[1,8,128]{2,1,0:T(8,128)S(1)}) custom-call(s32[1]{0:T(128)S(6)} %copy.17.live_ref, s32[1]{0:T(128)} %bitcast.place_ref, s32[128,128]{1,0:T(8,128)S(1)} %copy-done.4, f32[128,128]{1,0:T(8,128)S(1)} %copy-done.5, f32[4,128,128]{2,1,0:T(8,128)S(1)} %copy-done.2, ...), custom_call_target="tpu_custom_call" | custom-call | flops 3000000000 | bytes 1000000 | tf_op jit(solution)/shard_map/knot_forward/pallas_call | solution.py:470
  50.1 6.4 %knot_backward.3 = (f32[8,32,256]{2,1,0:T(8,128)}, f32[8,256]{1,0:T(8,128)S(1)}) custom-call(s32[1]{0:T(128)S(6)} %copy.17.live_ref, s32[1]{0:T(128)} %bitcast.place_ref, f32[128,128]{1,0:T(8,128)S(1)} %get-tuple-element.22.refs_0_.value_ref.refs_2_.image_0_ref, f32[128,128]{1,0:T(8,128)S(1)} %copy-done.6, s32[1,128]{1,0:T(1,128)S(1)} %bitcast.9, ...), custom_call_target="tpu_custom_call" | custom-call | flops 3000000000 | bytes 1000000 | tf_op jit(solution)/shard_map/knot_backward/pallas_call | solution.py:433
  56.5 3.6 %all-to-all-start.2 = ((f32[8,32,256]{2,1,0:T(8,128)}), f32[8,32,256]{2,1,0:T(8,128)S(1)}, u32[]{:S(2)}, u32[]{:S(2)}) async-start(f32[8,32,256]{2,1,0:T(8,128)} %get-tuple-element.24), calls=%async_computation.2 | async-start | bytes 524288 | tf_op jit(solution)/shard_map/all_to_all | solution.py:485
  60.1 4.4 %star_backward.3 = f32[168,256]{1,0:T(8,128)S(1)} custom-call(s32[1]{0:T(128)S(6)} %copy.17.live_ref, s32[128,128]{1,0:T(8,128)S(1)} %copy-done.3, f32[5,128,128]{2,1,0:T(8,128)S(1)} %copy-done.1, f32[128,128]{1,0:T(8,128)S(1)} %get-tuple-element.22.refs_0_.value_ref.refs_2_.image_0_ref, f32[8,256]{1,0:T(8,128)S(1)} %get-tuple-element.25.edge_ref), custom_call_target="tpu_custom_call" | custom-call | flops 3000000000 | bytes 1000000 | tf_op jit(solution)/shard_map/star_backward/pallas_call | solution.py:445
  64.6 1.4 %collective-permute-done.2 = f32[168,256]{1,0:T(8,128)S(1)} collective-permute-done((f32[168,256]{1,0:T(8,128)S(1)}, f32[168,256]{1,0:T(8,128)S(1)}, u32[]{:S(2)}, u32[]{:S(2)}) %collective-permute-start.2) | collective-permute-done | bytes 172064 | tf_op jit(solution)/shard_map/ppermute | solution.py:488
  66.0 1.6 %collective-permute-start.3 = (f32[168,256]{1,0:T(8,128)S(1)}, f32[168,256]{1,0:T(8,128)S(1)}, u32[]{:S(2)}, u32[]{:S(2)}) collective-permute-start(f32[168,256]{1,0:T(8,128)S(1)} %add.7.own_ref), channel_id=1, source_target_pairs={{0,2},{1,3},{2,0},{3,1},{4,6},{5,7},{6,4},{7,5},{8,10},{9,11},{10,... | collective-permute-start | bytes 516104 | tf_op jit(solution)/shard_map/ppermute | solution.py:488
  67.6 4.9 %collective-permute-done.3.other_ref = f32[168,256]{1,0:T(8,128)S(1)} collective-permute-done((f32[168,256]{1,0:T(8,128)S(1)}, f32[168,256]{1,0:T(8,128)S(1)}, u32[]{:S(2)}, u32[]{:S(2)}) %collective-permute-start.3) | collective-permute-done | bytes 172064 | tf_op jit(solution)/shard_map/ppermute | solution.py:488
  73.3 6.0 %all-to-all-start.3 = ((f32[8,40,256]{2,1,0:T(8,128)}), f32[8,40,256]{2,1,0:T(8,128)S(1)}, u32[]{:S(2)}, u32[]{:S(2)}) async-start(f32[8,40,256]{2,1,0:T(8,128)} %get-tuple-element.27), calls=%async_computation.3 | async-start | bytes 655360 | tf_op jit(solution)/shard_map/all_to_all | solution.py:485
  79.3 4.7 %star_forward.3.star_image_ref = f32[128,128]{1,0:T(8,128)S(1)} custom-call(s32[128,128]{1,0:T(8,128)S(1)} %copy-done.3, f32[5,128,128]{2,1,0:T(8,128)S(1)} %copy-done.1, f32[160,256]{1,0:T(8,128)S(1)} %get-tuple-element.26.star_x_ref), custom_call_target="tpu_custom_call" | custom-call | flops 3000000000 | bytes 1000000 | tf_op jit(solution)/shard_map/star_forward/pallas_call | solution.py:457
  84.0 5.0 %all-to-all-done.3.block_ref = f32[8,40,256]{2,1,0:T(8,128)S(1)} async-done(((f32[8,40,256]{2,1,0:T(8,128)}), f32[8,40,256]{2,1,0:T(8,128)S(1)}, u32[]{:S(2)}, u32[]{:S(2)}) %all-to-all-start.3) | async-done | bytes 327712 | tf_op jit(solution)/shard_map/all_to_all | solution.py:485
  89.0 5.7 %knot_forward.3 = (f32[128,128]{1,0:T(8,128)S(1)}, f32[256,256]{1,0:T(8,128)S(1)}, f32[32,8,128]{2,1,0:T(8,128)}) custom-call(s32[1]{0:T(128)S(6)} %copy.17.live_ref, s32[1]{0:T(128)} %bitcast.place_ref, s32[128,128]{1,0:T(8,128)S(1)} %copy-done.4, f32[128,128]{1,0:T(8,128)S(1)} %copy-done.5, f32[4,128,128]{2,1,0:T(8,128)S(1)} %copy-done.2, ...), custom_call_target="tpu_custom_call" | custom-call | flops 3000000000 | bytes 1000000 | tf_op jit(solution)/shard_map/knot_forward/pallas_call | solution.py:470
  94.7 3.7 %all-to-all-start.4 = ((f32[32,8,128]{2,1,0:T(8,128)}), f32[32,8,128]{2,1,0:T(8,128)S(1)}, u32[]{:S(2)}, u32[]{:S(2)}) async-start(f32[32,8,128]{2,1,0:T(8,128)} %get-tuple-element.29.own_scalar_ref), calls=%async_computation.4 | async-start | bytes 262144 | tf_op jit(solution)/shard_map/all_to_all | solution.py:485
  99.5 7.1 %all-to-all-done.4.scalar_ref = f32[32,8,128]{2,1,0:T(8,128)S(1)} async-done(((f32[32,8,128]{2,1,0:T(8,128)}), f32[32,8,128]{2,1,0:T(8,128)S(1)}, u32[]{:S(2)}, u32[]{:S(2)}) %all-to-all-start.4) | async-done | bytes 131104 | tf_op jit(solution)/shard_map/all_to_all | solution.py:485
  106.6 1.9 %outputs.1 = (f32[5,8192]{1,0:T(8,128)}, f32[4,8192]{1,0:T(4,128)}, f32[256,128]{1,0:T(8,128)}, f32[128,128]{1,0:T(8,128)}) custom-call(s32[1]{0:T(128)S(6)} %copy.17.live_ref, f32[32,8,128]{2,1,0:T(8,128)} %get-tuple-element.29.own_scalar_ref, f32[32,8,128]{2,1,0:T(8,128)S(1)} %all-to-all-done.4.scalar_ref, f32[5,8192]{1,0:T(8,128)S(1)} %reshape.26.star_0_ref, ...), custom_call_target="tpu_custom_call" | custom-call | flops 1000000 | bytes 600000 | tf_op jit(solution)/shard_map/outputs/pallas_call | solution.py:519
  (33 shorter events, 2.1 us)
Async XLA Ops:
  8.7 7.4 %copy-start.1 = (f32[5,128,128]{2,1,0:T(8,128)S(1)}, f32[5,128,128]{2,1,0:T(8,128)}, u32[]{:S(2)}) copy-start(f32[5,128,128]{2,1,0:T(8,128)} %star_coef_ref.7) | copy-start | bytes 983044
  8.7 7.4 %copy-start = (f32[128,128]{1,0:T(8,128)S(1)}, f32[128,128]{1,0:T(8,128)}, u32[]{:S(2)}) copy-start(f32[128,128]{1,0:T(8,128)} %value_ref.3) | copy-start | bytes 196612
  8.7 7.4 %copy-start.3 = (s32[128,128]{1,0:T(8,128)S(1)}, s32[128,128]{1,0:T(8,128)}, u32[]{:S(2)}) copy-start(s32[128,128]{1,0:T(8,128)} %star_ref.7) | copy-start | bytes 196612
  8.7 7.4 %copy-start.8 = (f32[8,256]{1,0:T(8,128)S(1)}, f32[8,256]{1,0:T(8,128)}, u32[]{:S(2)}) copy-start(f32[8,256]{1,0:T(8,128)} %get-tuple-element.19.edge_ref) | copy-start | bytes 24580
  8.7 19.8 %all-to-all-start = ((f32[8,32,256]{2,1,0:T(8,128)}), f32[8,32,256]{2,1,0:T(8,128)S(1)}, u32[]{:S(2)}, u32[]{:S(2)}) async-start(f32[8,32,256]{2,1,0:T(8,128)} %get-tuple-element.18), calls=%async_computation | async-start | bytes 524288 | tf_op jit(solution)/shard_map/all_to_all | solution.py:485
  20.6 1.5 %collective-permute-start = (f32[168,256]{1,0:T(8,128)S(1)}, f32[168,256]{1,0:T(8,128)S(1)}, u32[]{:S(2)}, u32[]{:S(2)}) collective-permute-start(f32[168,256]{1,0:T(8,128)S(1)} %star_backward.2), channel_id=1, source_target_pairs={{0,1},{1,0},{2,3},{3,2},{4,5},{5,4},{6,7},{7,6},{8,9},{9,8},{10,11... | collective-permute-start | bytes 516104 | tf_op jit(solution)/shard_map/ppermute | solution.py:488
  22.1 6.5 %collective-permute-start.1 = (f32[168,256]{1,0:T(8,128)S(1)}, f32[168,256]{1,0:T(8,128)S(1)}, u32[]{:S(2)}, u32[]{:S(2)}) collective-permute-start(f32[168,256]{1,0:T(8,128)S(1)} %add.6.own_ref), channel_id=1, source_target_pairs={{0,2},{1,3},{2,0},{3,1},{4,6},{5,7},{6,4},{7,5},{8,10},{9,11},{10,... | collective-permute-start | bytes 516104 | tf_op jit(solution)/shard_map/ppermute | solution.py:488
  29.3 15.7 %all-to-all-start.1 = ((f32[8,40,256]{2,1,0:T(8,128)}), f32[8,40,256]{2,1,0:T(8,128)S(1)}, u32[]{:S(2)}, u32[]{:S(2)}) async-start(f32[8,40,256]{2,1,0:T(8,128)} %get-tuple-element.21), calls=%async_computation.1 | async-start | bytes 655360 | tf_op jit(solution)/shard_map/all_to_all | solution.py:485
  35.3 9.8 %copy-start.2 = (f32[4,128,128]{2,1,0:T(8,128)S(1)}, f32[4,128,128]{2,1,0:T(8,128)}, u32[]{:S(2)}) copy-start(f32[4,128,128]{2,1,0:T(8,128)} %att_coef_ref.3) | copy-start | bytes 786436
  35.3 9.8 %copy-start.4 = (s32[128,128]{1,0:T(8,128)S(1)}, s32[128,128]{1,0:T(8,128)}, u32[]{:S(2)}) copy-start(s32[128,128]{1,0:T(8,128)} %knot_ref.3) | copy-start | bytes 196612
  35.3 9.7 %copy-start.5 = (f32[128,128]{1,0:T(8,128)S(1)}, f32[128,128]{1,0:T(8,128)}, u32[]{:S(2)}) copy-start(f32[128,128]{1,0:T(8,128)} %frac_ref.3) | copy-start | bytes 196612
  35.3 9.7 %copy-start.6 = (f32[128,128]{1,0:T(8,128)S(1)}, f32[128,128]{1,0:T(8,128)}, u32[]{:S(2)}) copy-start(f32[128,128]{1,0:T(8,128)} %cal_coef_ref.3) | copy-start | bytes 196612
  35.4 9.7 %copy-start.7 = (s32[128]{0:T(128)S(1)}, s32[128]{0:T(128)}, u32[]{:S(2)}) copy-start(s32[128]{0:T(128)} %param.15) | copy-start | bytes 1540
  56.5 16.0 %all-to-all-start.2 = ((f32[8,32,256]{2,1,0:T(8,128)}), f32[8,32,256]{2,1,0:T(8,128)S(1)}, u32[]{:S(2)}, u32[]{:S(2)}) async-start(f32[8,32,256]{2,1,0:T(8,128)} %get-tuple-element.24), calls=%async_computation.2 | async-start | bytes 524288 | tf_op jit(solution)/shard_map/all_to_all | solution.py:485
  64.5 1.5 %collective-permute-start.2 = (f32[168,256]{1,0:T(8,128)S(1)}, f32[168,256]{1,0:T(8,128)S(1)}, u32[]{:S(2)}, u32[]{:S(2)}) collective-permute-start(f32[168,256]{1,0:T(8,128)S(1)} %star_backward.3), channel_id=1, source_target_pairs={{0,1},{1,0},{2,3},{3,2},{4,5},{5,4},{6,7},{7,6},{8,9},{9,8},{10,11... | collective-permute-start | bytes 516104 | tf_op jit(solution)/shard_map/ppermute | solution.py:488
  66.0 6.5 %collective-permute-start.3 = (f32[168,256]{1,0:T(8,128)S(1)}, f32[168,256]{1,0:T(8,128)S(1)}, u32[]{:S(2)}, u32[]{:S(2)}) collective-permute-start(f32[168,256]{1,0:T(8,128)S(1)} %add.7.own_ref), channel_id=1, source_target_pairs={{0,2},{1,3},{2,0},{3,1},{4,6},{5,7},{6,4},{7,5},{8,10},{9,11},{10,... | collective-permute-start | bytes 516104 | tf_op jit(solution)/shard_map/ppermute | solution.py:488
  73.3 15.7 %all-to-all-start.3 = ((f32[8,40,256]{2,1,0:T(8,128)}), f32[8,40,256]{2,1,0:T(8,128)S(1)}, u32[]{:S(2)}, u32[]{:S(2)}) async-start(f32[8,40,256]{2,1,0:T(8,128)} %get-tuple-element.27), calls=%async_computation.3 | async-start | bytes 655360 | tf_op jit(solution)/shard_map/all_to_all | solution.py:485
  94.7 11.9 %all-to-all-start.4 = ((f32[32,8,128]{2,1,0:T(8,128)}), f32[32,8,128]{2,1,0:T(8,128)S(1)}, u32[]{:S(2)}, u32[]{:S(2)}) async-start(f32[32,8,128]{2,1,0:T(8,128)} %get-tuple-element.29.own_scalar_ref), calls=%async_computation.4 | async-start | bytes 262144 | tf_op jit(solution)/shard_map/all_to_all | solution.py:485

commit v8 on v7

--- a/solution.py
+++ b/solution.py
@@ -12,8 +12,7 @@
 CALB_DEV = 256
 FINE = 32
 COARSE = 256
-GROUP = 8
-WIDE_GROUP = 16
+GROUP = 16
 SLOT = 8
 STAR_ROWS = 5 * FINE
 KNOT_ROWS = 4 * FINE
@@ -34,8 +33,12 @@
 
 
 def one_hot(index_row, size):
-    rows, _ = rows_and_columns((size, index_row.shape[1]))
-    return jnp.where(rows == index_row, 1.0, 0.0).astype(BF16)
+    width = index_row.shape[1]
+    row = jnp.broadcast_to(index_row.astype(F32), (16, width)).astype(BF16)
+    rows = jnp.concatenate([row] * (size // 16), axis=0)
+    places, _ = rows_and_columns((size, width))
+    places = places.astype(F32).astype(BF16)
+    return jnp.where(places == rows, jnp.ones((), BF16), jnp.zeros((), BF16))
 
 
 def spline_weights(fraction):
@@ -75,28 +78,43 @@
         out_ref[where // block, where % block : where % block + 8, :] = rows[offset : offset + 8]
 
 
-def knot_backward_kernel(arrive, live_ref, place_ref, *refs):
-    observed, refs = refs[:6], refs[6:]
-    if not arrive:
-        scalar_ref, *refs = refs
-    table_out, edge_out, knot_acc = refs[:3]
-    if arrive:
-        *buffers, sems = refs[3:]
-        copies = [
-            pltpu.make_async_copy(source, target, sems.at[which])
-            for which, (source, target) in enumerate(zip(observed, buffers))
-        ]
-        for copy in copies:
-            copy.start()
-        observed = buffers
-    value_ref, cal_coef_ref, tile_cal_ref, knot_ref, frac_ref, att_coef_ref = observed
-    knot_acc[...] = jnp.zeros_like(knot_acc)
-    if arrive:
-        for copy in copies[:3]:
-            copy.wait()
-
-    values = value_ref[...]
-    values = values * live_mask(live_ref, 0, values.shape) * cal_coef_ref[...]
+def scatter(first, values, observed, knot_acc, star_acc):
+    knot_ref, frac_ref, att_coef_ref, star_ref, star_coef_ref = observed
+    rows = pl.ds(first, GROUP)
+    knot, star = knot_ref[rows, :], star_ref[rows, :]
+    knot_coarse, knot_fine = knot >> 5, knot & (FINE - 1)
+    star_coarse, star_fine = star & (COARSE - 1), star >> 8
+    weights = spline_weights(frac_ref[rows, :])
+    terms = [att_coef_ref[comp, rows, :] * values for comp in range(4)]
+    parts = [two_parts(star_coef_ref[comp, rows, :] * values) for comp in range(5)]
+    parts = [pair[half].astype(F32) for half in range(2) for pair in parts]
+    width = knot.shape[1]
+    fine_rows, _ = rows_and_columns((FINE, width))
+    knot_left, knot_right, star_left, star_right = [], [], [], []
+    for tile in range(GROUP):
+        here = slice(tile, tile + 1)
+        knot_right.append(one_hot(knot_coarse[here], COARSE))
+        columns = weight_columns(weights, knot_fine, tile)
+        spread = jnp.concatenate(
+            [term[here] * columns[:FINE] for term in terms]
+            + [term[here] * columns[FINE:] for term in terms],
+            axis=0,
+        )
+        knot_left.append(jnp.concatenate(two_parts(spread), axis=0))
+        star_right.append(one_hot(star_coarse[here], COARSE))
+        chosen = fine_rows == star_fine[here]
+        star_left.append(
+            jnp.concatenate([jnp.where(chosen, part[here], 0.0) for part in parts], axis=0).astype(BF16)
+        )
+    knot_acc[...] += product(
+        jnp.concatenate(knot_left, axis=1), jnp.concatenate(knot_right, axis=1), ((1,), (1,))
+    )
+    star_acc[...] += product(
+        jnp.concatenate(star_left, axis=1), jnp.concatenate(star_right, axis=1), ((1,), (1,))
+    )
+
+
+def scatter_calibration(values, tile_cal_ref, table_out):
     blocks = product(
         one_hot(tile_cal_ref[...], CALB_DEV), jnp.concatenate(two_parts(values), axis=1), ((1,), (0,))
     )
@@ -104,35 +122,9 @@
     blocks = blocks[:, :width] + blocks[:, width:]
     blocks = jnp.concatenate([blocks[: CALB_DEV // 2], blocks[CALB_DEV // 2 :]], axis=1)
     store_rows(table_out, KNOT_ROWS, blocks)
-    if arrive:
-        for copy in copies[3:]:
-            copy.wait()
-
-    @pl.loop(0, knot_ref.shape[0] // WIDE_GROUP)
-    def _(group):
-        first = pl.multiple_of(group * WIDE_GROUP, WIDE_GROUP)
-        rows = pl.ds(first, WIDE_GROUP)
-        knot = knot_ref[rows, :]
-        values = value_ref[rows, :]
-        values = values * live_mask(live_ref, first, values.shape)
-        coarse, fine = knot >> 5, knot & (FINE - 1)
-        weights = spline_weights(frac_ref[rows, :])
-        terms = [att_coef_ref[comp, rows, :] * values for comp in range(4)]
-        left, right = [], []
-        for tile in range(WIDE_GROUP):
-            here = slice(tile, tile + 1)
-            right.append(one_hot(coarse[here], COARSE))
-            columns = weight_columns(weights, fine, tile)
-            spread = jnp.concatenate(
-                [term[here] * columns[:FINE] for term in terms]
-                + [term[here] * columns[FINE:] for term in terms],
-                axis=0,
-            )
-            left.append(jnp.concatenate(two_parts(spread), axis=0))
-        knot_acc[...] += product(
-            jnp.concatenate(left, axis=1), jnp.concatenate(right, axis=1), ((1,), (1,))
-        )
-
+
+
+def scatter_end(place_ref, scalars, knot_acc, star_acc, table_out, star_out):
     lane = lax.broadcasted_iota(jnp.int32, (8, 128), 1)
     row = lax.broadcasted_iota(jnp.int32, (8, 128), 0)
     wide_lane = lax.broadcasted_iota(jnp.int32, (8, COARSE), 1)
@@ -151,42 +143,37 @@
         head = pltpu.roll(head, 2 * comp + 1, 1)
         edges = jnp.where((lane == 2 * comp) & (row < 3), tail, edges)
         edges = jnp.where((lane == 2 * comp + 1) & (row < 3), head, edges)
-    edges = pltpu.roll(edges, SLOT * place_ref[0], 1)
-    if not arrive:
-        edges = edges + scalar_ref[...]
-    edge_out[...] = jnp.concatenate([edges, jnp.zeros_like(edges)], axis=1)
-
-
-def star_backward_kernel(
-    live_ref, star_ref, star_coef_ref, value_ref, edge_ref, star_out, star_acc
-):
+    edges = with_scalars(pltpu.roll(edges, SLOT * place_ref[0], 1), scalars)
+    star_out[:STAR_ROWS] = star_acc[:STAR_ROWS] + star_acc[STAR_ROWS:]
+    star_out[STAR_ROWS:] = jnp.concatenate([edges, jnp.zeros_like(edges)], axis=1)
+
+
+def first_kernel(live_ref, place_ref, *refs):
+    sources, (table_out, star_out, knot_acc, star_acc) = refs[:8], refs[8:12]
+    buffers, sems = refs[12:20], refs[20]
+    copies = [
+        pltpu.make_async_copy(source, target, sems.at[which])
+        for which, (source, target) in enumerate(zip(sources, buffers))
+    ]
+    for copy in copies:
+        copy.start()
+    value_ref, cal_coef_ref, tile_cal_ref, *observed = buffers
+    knot_acc[...] = jnp.zeros_like(knot_acc)
     star_acc[...] = jnp.zeros_like(star_acc)
-
-    @pl.loop(0, star_ref.shape[0] // WIDE_GROUP)
+    for copy in copies[:3]:
+        copy.wait()
+    values = value_ref[...] * live_mask(live_ref, 0, value_ref.shape)
+    scatter_calibration(values * cal_coef_ref[...], tile_cal_ref, table_out)
+    for copy in copies[3:]:
+        copy.wait()
+
+    @pl.loop(0, value_ref.shape[0] // GROUP)
     def _(group):
-        first = pl.multiple_of(group * WIDE_GROUP, WIDE_GROUP)
-        rows = pl.ds(first, WIDE_GROUP)
-        star = star_ref[rows, :]
-        values = value_ref[rows, :]
-        values = values * live_mask(live_ref, first, values.shape)
-        coarse, fine = star & (COARSE - 1), star >> 8
-        parts = [two_parts(star_coef_ref[comp, rows, :] * values) for comp in range(5)]
-        parts = [pair[half].astype(F32) for half in range(2) for pair in parts]
-        left, right = [], []
-        fine_rows, _ = rows_and_columns((FINE, star.shape[1]))
-        for tile in range(WIDE_GROUP):
-            here = slice(tile, tile + 1)
-            right.append(one_hot(coarse[here], COARSE))
-            chosen = fine_rows == fine[here]
-            left.append(
-                jnp.concatenate([jnp.where(chosen, part[here], 0.0) for part in parts], axis=0).astype(BF16)
-            )
-        star_acc[...] += product(
-            jnp.concatenate(left, axis=1), jnp.concatenate(right, axis=1), ((1,), (1,))
-        )
-
-    star_out[:STAR_ROWS] = star_acc[:STAR_ROWS] + star_acc[STAR_ROWS:]
-    star_out[STAR_ROWS:] = edge_ref[...]
+        first = pl.multiple_of(group * GROUP, GROUP)
+        values = value_ref[pl.ds(first, GROUP), :]
+        scatter(first, values * live_mask(live_ref, first, values.shape), observed, knot_acc, star_acc)
+
+    scatter_end(place_ref, [], knot_acc, star_acc, table_out, star_out)
 
 
 def sum_kernel(block_ref, own_ref, other_ref, out_ref, star_out):
@@ -225,7 +212,7 @@
     star_parts_ref[:STAR_ROWS] = star_high
     star_parts_ref[STAR_ROWS:] = star_low
 
-    @pl.loop(0, star_ref.shape[0] // GROUP, unroll=2)
+    @pl.loop(0, star_ref.shape[0] // GROUP)
     def _(group):
         rows = pl.ds(pl.multiple_of(group * GROUP, GROUP), GROUP)
         star = star_ref[rows, :]
@@ -254,20 +241,10 @@
         image_ref[rows, :] = jnp.concatenate(image_rows, axis=0)
 
 
-def knot_forward_kernel(
-    n_stars, n_seg, later, live_ref, place_ref, knot_ref, frac_ref, att_coef_ref, cal_coef_ref,
-    tile_cal_ref, star_image_ref, star_x_ref, block_ref, *refs,
-):
-    if later:
-        star_0_ref, table_0_ref, image_0_ref, image_ref, table_out, scalar_out = refs[:6]
-    else:
-        image_ref, table_out, scalar_out = refs[:3]
-    knot_parts_ref, cal_ref = refs[-2:]
+def received_table(n_stars, n_seg, place_ref, block_ref):
     segment = place_ref[0]
     lane = lax.broadcasted_iota(jnp.int32, (8, 128), 1)
     row = lax.broadcasted_iota(jnp.int32, (8, 128), 0)
-    wide_lane = lax.broadcasted_iota(jnp.int32, (8, COARSE), 1)
-
     edges = block_ref[0, -8:, :128]
     for block in range(1, n_stars):
         edges = edges + block_ref[block, -8:, :128]
@@ -288,20 +265,11 @@
         top = table[comp * FINE : comp * FINE + 8]
         pieces.append(top + jnp.concatenate([shifted, jnp.zeros_like(shifted)], axis=1))
         pieces.append(table[comp * FINE + 8 : (comp + 1) * FINE])
-    table = jnp.concatenate(pieces + [table[KNOT_ROWS:]], axis=0)
-    table_out[...] = table
-    if later:
-        norm_0, square_0 = first_step(edges)
-        step = norm_0 / square_0
-        star_change = star_0_ref[...] - step * star_x_ref[...]
-        table_change = table_0_ref[...] - step * table
-    else:
-        star_change, table_change = star_x_ref[...], table
-    norm = (
-        jnp.sum(star_change * star_change, keepdims=True) / n_seg
-        + jnp.sum(table_change * table_change, keepdims=True) / n_stars
-    )
-
+    return jnp.concatenate(pieces + [table[KNOT_ROWS:]], axis=0), ahead, edges
+
+
+def gather_ready(table, ahead, cal_coef_ref, tile_cal_ref, star_image_ref, knot_parts_ref, cal_ref):
+    wide_lane = lax.broadcasted_iota(jnp.int32, (8, COARSE), 1)
     beyond = []
     for comp in range(4):
         moved = pltpu.roll(table[comp * FINE : comp * FINE + 8], COARSE - 1, 1)
@@ -317,49 +285,103 @@
     )
     cal_ref[...] = (rows[:, :128] + rows[:, 128:]) * cal_coef_ref[...] + star_image_ref[...]
 
+
+def gather(first, live_ref, observed, knot_parts_ref, cal_ref):
+    knot_ref, frac_ref, att_coef_ref = observed
+    rows = pl.ds(first, GROUP)
+    knot = knot_ref[rows, :]
+    coarse, fine = knot >> 5, knot & (FINE - 1)
+    weights = spline_weights(frac_ref[rows, :])
+    coef = [att_coef_ref[comp, rows, :] for comp in range(4)]
+    tiles = [slice(tile, tile + 1) for tile in range(GROUP)]
+    hot = jnp.concatenate([one_hot(coarse[here], COARSE) for here in tiles], axis=1)
+    found = product(knot_parts_ref[...], hot, ((1,), (0,)))
+    width = knot.shape[1]
+    image_rows = []
+    for tile, here in enumerate(tiles):
+        across = slice(tile * width, (tile + 1) * width)
+
+        def part(begin, size):
+            return (
+                found[begin : begin + size, across]
+                + found[KNOT_HALF + begin : KNOT_HALF + begin + size, across]
+            )
+
+        columns = weight_columns(weights, fine, tile)
+        main = sum(coef[comp][here] * part(comp * FINE, FINE) for comp in range(4))
+        past = sum(coef[comp][here] * part(KNOT_ROWS + comp * 8, 8) for comp in range(4))
+        both = main * columns[:FINE]
+        both = both[:8] + both[8:16] + both[16:24] + both[24:] + past * columns[FINE:]
+        image_rows.append(jnp.sum(both, axis=0, keepdims=True))
+    image = jnp.concatenate(image_rows, axis=0) + cal_ref[rows, :]
+    return image * live_mask(live_ref, first, image.shape)
+
+
+def squares(array):
+    return jnp.sum(array * array, keepdims=True)
+
+
+def middle_kernel(
+    n_stars, n_seg, live_ref, place_ref, knot_ref, frac_ref, att_coef_ref, star_ref, star_coef_ref,
+    cal_coef_ref, tile_cal_ref, star_image_ref, star_x_ref, block_ref, image_ref, table_out, scatter_out,
+    star_out, knot_parts_ref, cal_ref, knot_acc, star_acc,
+):
+    table, ahead, _ = received_table(n_stars, n_seg, place_ref, block_ref)
+    table_out[...] = table
+    norm = squares(star_x_ref[...]) / n_seg + squares(table) / n_stars
+    gather_ready(table, ahead, cal_coef_ref, tile_cal_ref, star_image_ref, knot_parts_ref, cal_ref)
+    knot_acc[...] = jnp.zeros_like(knot_acc)
+    star_acc[...] = jnp.zeros_like(star_acc)
+    observed = (knot_ref, frac_ref, att_coef_ref)
+    every = (knot_ref, frac_ref, att_coef_ref, star_ref, star_coef_ref)
+    groups = knot_ref.shape[0] // GROUP
+    image = gather(0, live_ref, observed, knot_parts_ref, cal_ref)
+    image_ref[:GROUP, :] = image
+
+    def one_group(group, total):
+        first = pl.multiple_of(group * GROUP, GROUP)
+        following = pl.multiple_of(first + GROUP, GROUP)
+        values = image_ref[pl.ds(first, GROUP), :]
+        image = gather(following, live_ref, observed, knot_parts_ref, cal_ref)
+        scatter(first, values, every, knot_acc, star_acc)
+        image_ref[pl.ds(following, GROUP), :] = image
+        return total + image * image
+
+    total = lax.fori_loop(0, groups - 1, one_group, image * image)
+    first = (groups - 1) * GROUP
+    scatter(first, image_ref[first:, :], every, knot_acc, star_acc)
+    scatter_calibration(image_ref[...] * cal_coef_ref[...], tile_cal_ref, scatter_out)
+    scalars = [(0, norm), (1, jnp.sum(total, keepdims=True))]
+    scatter_end(place_ref, scalars, knot_acc, star_acc, scatter_out, star_out)
+
+
+def last_kernel(
+    n_stars, n_seg, live_ref, place_ref, knot_ref, frac_ref, att_coef_ref, cal_coef_ref, tile_cal_ref,
+    star_image_ref, star_x_ref, block_ref, star_0_ref, table_0_ref, image_0_ref, image_ref, table_out,
+    scalar_out, knot_parts_ref, cal_ref,
+):
+    table, ahead, edges = received_table(n_stars, n_seg, place_ref, block_ref)
+    table_out[...] = table
+    norm_0, square_0 = first_step(edges)
+    step = norm_0 / square_0
+    norm = (
+        squares(star_0_ref[...] - step * star_x_ref[...]) / n_seg
+        + squares(table_0_ref[...] - step * table) / n_stars
+    )
+    gather_ready(table, ahead, cal_coef_ref, tile_cal_ref, star_image_ref, knot_parts_ref, cal_ref)
+
     def one_group(group, sums):
         first = pl.multiple_of(group * GROUP, GROUP)
         rows = pl.ds(first, GROUP)
-        knot = knot_ref[rows, :]
-        coarse, fine = knot >> 5, knot & (FINE - 1)
-        weights = spline_weights(frac_ref[rows, :])
-        coef = [att_coef_ref[comp, rows, :] for comp in range(4)]
-        tiles = [slice(tile, tile + 1) for tile in range(GROUP)]
-        hot = jnp.concatenate([one_hot(coarse[here], COARSE) for here in tiles], axis=1)
-        found = product(knot_parts_ref[...], hot, ((1,), (0,)))
-        width = knot.shape[1]
-        image_rows = []
-        for tile, here in enumerate(tiles):
-            across = slice(tile * width, (tile + 1) * width)
-
-            def part(begin, size):
-                return (
-                    found[begin : begin + size, across]
-                    + found[KNOT_HALF + begin : KNOT_HALF + begin + size, across]
-                )
-
-            columns = weight_columns(weights, fine, tile)
-            main = sum(coef[comp][here] * part(comp * FINE, FINE) for comp in range(4))
-            past = sum(coef[comp][here] * part(KNOT_ROWS + comp * 8, 8) for comp in range(4))
-            both = main * columns[:FINE]
-            both = both[:8] + both[8:16] + both[16:24] + both[24:] + past * columns[FINE:]
-            image_rows.append(jnp.sum(both, axis=0, keepdims=True))
-        image = jnp.concatenate(image_rows, axis=0) + cal_ref[rows, :]
-        image = image * live_mask(live_ref, first, image.shape)
-        if later:
-            image_0 = image_0_ref[rows, :]
-            image = image_0 - step * image
-            image_ref[rows, :] = image
-            return sums[0] + image * image, sums[1] + image * image_0
+        image_0 = image_0_ref[rows, :]
+        image = gather(first, live_ref, (knot_ref, frac_ref, att_coef_ref), knot_parts_ref, cal_ref)
+        image = image_0 - step * image
         image_ref[rows, :] = image
-        return (sums[0] + image * image,)
+        return sums[0] + image * image, sums[1] + image * image_0
 
     zero = jnp.zeros((GROUP, knot_ref.shape[1]), F32)
-    start = (zero, zero) if later else (zero,)
-    sums = lax.fori_loop(0, knot_ref.shape[0] // GROUP, one_group, start, unroll=2)
-    scalars = [norm] + [jnp.sum(part, keepdims=True) for part in sums]
-    if later:
-        scalars += [norm_0, square_0]
+    sums = lax.fori_loop(0, knot_ref.shape[0] // GROUP, one_group, (zero, zero))
+    scalars = [norm] + [jnp.sum(part, keepdims=True) for part in sums] + [norm_0, square_0]
     scalars = with_scalars(jnp.zeros((8, 128), F32), list(enumerate(scalars)))
     for device in range(scalar_out.shape[0]):
         scalar_out[device] = scalars
@@ -422,36 +444,49 @@
     image_shape = shaped(tile_count, width)
     table_shape = shaped(TABLE_ROWS, COARSE)
     star_shape = shaped(STAR_ROWS, COARSE)
-
-    def knot_backward(values, *scalars):
-        arrive = not scalars
-        observed = (values, cal_coef, tile_row, obs_knot, obs_frac, att_coef)
-        scratch = [pltpu.VMEM((2 * KNOT_HALF, COARSE), F32)]
-        if arrive:
-            scratch += [pltpu.VMEM(array.shape, array.dtype) for array in observed]
-            scratch += [pltpu.SemaphoreType.DMA((len(observed),))]
+    sent_shapes = (shaped(n_stars, TABLE_ROWS // n_stars, COARSE), shaped(STAR_ROWS + 8, COARSE))
+    sums = [pltpu.VMEM((2 * KNOT_HALF, COARSE), F32), pltpu.VMEM((2 * STAR_ROWS, COARSE), F32)]
+    ready = [pltpu.VMEM((2 * KNOT_HALF, COARSE), BF16), pltpu.VMEM((tile_count, width), F32)]
+
+    def first_scatter():
+        observed = (obs_value, cal_coef, tile_row, obs_knot, obs_frac, att_coef, obs_star, star_coef)
+        buffers = [pltpu.VMEM(array.shape, array.dtype) for array in observed]
         return pl.pallas_call(
-            functools.partial(knot_backward_kernel, arrive),
-            out_shape=(shaped(n_stars, TABLE_ROWS // n_stars, COARSE), shaped(8, COARSE)),
-            in_specs=in_smem(2) + (in_hbm if arrive else in_vmem)(len(observed)) + in_vmem(len(scalars)),
+            first_kernel,
+            out_shape=sent_shapes,
+            in_specs=in_smem(2) + in_hbm(len(observed)),
             out_specs=tuple(in_vmem(2)),
-            scratch_shapes=scratch,
-            compiler_params=ARRIVE_PARAMS if arrive else PARAMS,
+            scratch_shapes=sums + buffers + [pltpu.SemaphoreType.DMA((len(observed),))],
+            compiler_params=ARRIVE_PARAMS,
             cost_estimate=PASS_COST,
-            name="knot_backward",
-        )(live_tiles, place, *observed, *scalars)
-
-    def star_backward(values, edges):
+            name="first_scatter",
+        )(live_tiles, place, *observed)
+
+    def middle(*received):
+        observed = (obs_knot, obs_frac, att_coef, obs_star, star_coef, cal_coef, tile_row)
         return pl.pallas_call(
-            star_backward_kernel,
-            out_shape=shaped(STAR_ROWS + 8, COARSE),
-            in_specs=in_smem(1) + in_vmem(4),
-            out_specs=in_vmem(1)[0],
-            scratch_shapes=[pltpu.VMEM((2 * STAR_ROWS, COARSE), F32)],
+            functools.partial(middle_kernel, n_stars, n_seg),
+            out_shape=(image_shape, table_shape, *sent_shapes),
+            in_specs=in_smem(2) + in_vmem(len(observed) + len(received)),
+            out_specs=tuple(in_vmem(4)),
+            scratch_shapes=ready + sums,
             compiler_params=PARAMS,
             cost_estimate=PASS_COST,
-            name="star_backward",
-        )(live_tiles, obs_star, star_coef, values, edges)
+            name="gather_and_scatter",
+        )(live_tiles, place, *observed, *received)
+
+    def last_gather(*received):
+        observed = (obs_knot, obs_frac, att_coef, cal_coef, tile_row)
+        return pl.pallas_call(
+            functools.partial(last_kernel, n_stars, n_seg),
+            out_shape=(image_shape, table_shape, shaped(n_stars * n_seg, 8, 128)),
+            in_specs=in_smem(2) + in_vmem(len(observed) + len(received)),
+            out_specs=tuple(in_vmem(3)),
+            scratch_shapes=ready,
+            compiler_params=PARAMS,
+            cost_estimate=PASS_COST,
+            name="last_gather",
+        )(live_tiles, place, *observed, *received)
 
     def star_forward(star):
         return pl.pallas_call(
@@ -465,31 +500,13 @@
             name="star_forward",
         )(obs_star, star_coef, star)
 
-    def knot_forward(*arrays):
-        later = len(arrays) > 3
-        return pl.pallas_call(
-            functools.partial(knot_forward_kernel, n_stars, n_seg, later),
-            out_shape=(image_shape, table_shape, shaped(n_stars * n_seg if later else 1, 8, 128)),
-            in_specs=in_smem(2) + in_vmem(5 + len(arrays)),
-            out_specs=tuple(in_vmem(3)),
-            scratch_shapes=[
-                pltpu.VMEM((2 * KNOT_HALF, COARSE), BF16),
-                pltpu.VMEM((tile_count, width), F32),
-            ],
-            compiler_params=PARAMS,
-            cost_estimate=PASS_COST,
-            name="knot_forward",
-        )(live_tiles, place, obs_knot, obs_frac, att_coef, cal_coef, tile_row, *arrays)
-
     def swap(blocks, axes):
         return lax.all_to_all(blocks, axes, 0, 0)
 
     def partner(array, axis, distance):
         return lax.ppermute(array, axis, [(i, i ^ distance) for i in range(lax.axis_size(axis))])
 
-    def half(values, *scalars):
-        table, edges = knot_backward(values, *scalars)
-        star = star_backward(values, edges)
+    def reduced(table, star):
         distances = [1 << bit for bit in range(n_seg.bit_length() - 1)]
         for distance in distances[:-1]:
             star = star + partner(star, "seg", distance)
@@ -504,10 +521,12 @@
         )(swap(table, "stars"), star, partner(star, "seg", distances[-1]))
         return star_forward(star), star, swap(blocks, "stars")
 
-    star_image, star_0, blocks = half(obs_value)
-    image_0, table_0, scalars = knot_forward(star_image, star_0, blocks)
-    star_image, star_h, blocks = half(image_0, scalars[0])
-    image_1, table_h, scalars = knot_forward(star_image, star_h, blocks, star_0, table_0, image_0)
+    first = reduced(*first_scatter())
+    star_0 = first[1]
+    image_0, table_0, *sent = middle(*first)
+    second = reduced(*sent)
+    star_h = second[1]
+    image_1, table_h, scalars = last_gather(*second, star_0, table_0, image_0)
 
     def star_order(star):
         return star.reshape(5, STAR_DEV)

time: 109 us -> 102 us (0.936)
  Pallas kernels: 46.2 us -> 38.1 us
  waiting for transfers between devices: 29.7 us -> 32.2 us
  starting transfers between devices: 30 us -> 28.5 us
    pallas_call x8 -> x5, Pallas kernels: 34.8 us -> 27.7 us  [the longest x1 11.3 us: middle(): pl.pallas_call(functools.partial(middle_kernel, n_stars, n_seg), out_shap...]
    all_to_all x5, waiting for transfers between devices: 17.1 us -> 19.6 us  [swap(): return lax.all_to_all(blocks, axes, 0, 0)]
    all_to_all x5, starting transfers between devices: 26.7 us -> 25.2 us  [swap(): return lax.all_to_all(blocks, axes, 0, 0)]
  transfers between devices with their start and end apart: 9 -> 9, of which waited for: 7 -> 9; matrix products, arithmetic and copies ran while one was open for 1% -> 1% of each run, Pallas kernels for 17% -> 8%
where the time goes in v8:
time: 102 us; the launch traced here: 101 us
  Pallas kernels  38.1 us (37%)
  waiting for transfers between devices  32.2 us (32%)
  starting transfers between devices  28.5 us (28%)
  between operations  1.48 us (1%)
  local copies, waits for them, and re-layouts  1.08 us (1%)
    all_to_all x5, starting transfers between devices, swap(): return lax.all_to_all(blocks, axes, 0, 0)  25.2 us
    all_to_all x5, waiting for transfers between devices, swap(): return lax.all_to_all(blocks, axes, 0, 0)  19.6 us
    ppermute x4, waiting for transfers between devices, partner(): lax.ppermute(array, axis, [(i, i ^ distance) for i in range(lax.axis_size...  12.6 us
    pallas_call x1, Pallas kernels, middle(): pl.pallas_call(functools.partial(middle_kernel, n_stars, n_seg), out_shap...  11.3 us
    pallas_call x1, Pallas kernels, first_scatter(): pl.pallas_call(first_kernel, out_shape=sent_shapes, in_specs=in_smem(2) +...  9.42 us
    pallas_call x2, Pallas kernels, star_forward(): pl.pallas_call(star_forward_kernel, out_shape=image_shape, in_specs=in_vm...  8.5 us
    pallas_call x1, Pallas kernels, last_gather(): pl.pallas_call(functools.partial(last_kernel, n_stars, n_seg), out_shape=...  5.41 us
    ppermute x4, starting transfers between devices, partner(): lax.ppermute(array, axis, [(i, i ^ distance) for i in range(lax.axis_size...  3.24 us
  transfers between devices with their start and end apart: 9, of which 9 were waited for; matrix products, arithmetic and copies ran while one was open for 1% of the time, Pallas kernels for 8%

profile of v8, /device:TPU:0, one launch (start us, length us, event | category | flops | bytes accessed | tf_op | source)
XLA Modules:
  0.0 101.4 jit_solution(14892152759010655380)
XLA Ops:
  1.3 9.4 %first_scatter.1 = (f32[8,32,256]{2,1,0:T(8,128)}, f32[168,256]{1,0:T(8,128)}) custom-call(s32[1]{0:T(128)S(6)} %copy.17.live_ref, s32[1]{0:T(128)} %bitcast.place_ref, f32[128,128]{1,0:T(8,128)} %value_ref.1, f32[128,128]{1,0:T(8,128)} %cal_coef_ref.3, s32[1,128]{1,0:T(1,128)} %bitcast.6, s32[128,128]{1,0:T(8,128)} %knot_ref.3, f32[128,128]{1,0:T(8,128)} %frac_ref.3, ...), custom_call_target="tpu_custom_call" | custom-call | flops 3000000000 | bytes 1000000 | tf_op jit(solution)/shard_map/first_scatter/pallas_call | solution.py:454
  10.7 7.4 %all-to-all-start = ((f32[8,32,256]{2,1,0:T(8,128)}), f32[8,32,256]{2,1,0:T(8,128)S(1)}, u32[]{:S(2)}, u32[]{:S(2)}) async-start(f32[8,32,256]{2,1,0:T(8,128)} %get-tuple-element.17), calls=%async_computation | async-start | bytes 524288 | tf_op jit(solution)/shard_map/all_to_all | solution.py:504
  18.2 1.4 %collective-permute-done = f32[168,256]{1,0:T(8,128)S(1)} collective-permute-done((f32[168,256]{1,0:T(8,128)S(1)}, f32[168,256]{1,0:T(8,128)S(1)}, u32[]{:S(2)}, u32[]{:S(2)}) %collective-permute-start) | collective-permute-done | bytes 172064 | tf_op jit(solution)/shard_map/ppermute | solution.py:507
  19.6 1.6 %collective-permute-start.1 = (f32[168,256]{1,0:T(8,128)S(1)}, f32[168,256]{1,0:T(8,128)S(1)}, u32[]{:S(2)}, u32[]{:S(2)}) collective-permute-start(f32[168,256]{1,0:T(8,128)S(1)} %add.6.own_ref), channel_id=1, source_target_pairs={{0,2},{1,3},{2,0},{3,1},{4,6},{5,7},{6,4},{7,5},{8,10},{9,11},{10,... | collective-permute-start | bytes 516104 | tf_op jit(solution)/shard_map/ppermute | solution.py:507
  21.2 4.9 %collective-permute-done.1.other_ref = f32[168,256]{1,0:T(8,128)S(1)} collective-permute-done((f32[168,256]{1,0:T(8,128)S(1)}, f32[168,256]{1,0:T(8,128)S(1)}, u32[]{:S(2)}, u32[]{:S(2)}) %collective-permute-start.1) | collective-permute-done | bytes 172064 | tf_op jit(solution)/shard_map/ppermute | solution.py:507
  26.1 0.9 all-to-all-done.block_ref
  27.0 0.8 table_sum.2
  27.8 5.1 %all-to-all-start.1 = ((f32[8,40,256]{2,1,0:T(8,128)}), f32[8,40,256]{2,1,0:T(8,128)S(1)}, u32[]{:S(2)}, u32[]{:S(2)}) async-start(f32[8,40,256]{2,1,0:T(8,128)} %get-tuple-element.20), calls=%async_computation.1 | async-start | bytes 655360 | tf_op jit(solution)/shard_map/all_to_all | solution.py:504
  33.0 4.2 %star_forward.2.star_image_ref = f32[128,128]{1,0:T(8,128)S(1)} custom-call(s32[128,128]{1,0:T(8,128)S(1)} %copy-done.3, f32[5,128,128]{2,1,0:T(8,128)S(1)} %copy-done.1, f32[160,256]{1,0:T(8,128)S(1)} %get-tuple-element.19.star_x_ref.star_0_ref), custom_call_target="tpu_custom_call" | custom-call | flops 3000000000 | bytes 1000000 | tf_op jit(solution)/shard_map/star_forward/pallas_call | solution.py:492
  37.3 5.4 %all-to-all-done.1.block_ref = f32[8,40,256]{2,1,0:T(8,128)S(1)} async-done(((f32[8,40,256]{2,1,0:T(8,128)}), f32[8,40,256]{2,1,0:T(8,128)S(1)}, u32[]{:S(2)}, u32[]{:S(2)}) %all-to-all-start.1) | async-done | bytes 327712 | tf_op jit(solution)/shard_map/all_to_all | solution.py:504
  42.7 11.3 %gather_and_scatter.1 = (f32[128,128]{1,0:T(8,128)S(1)}, f32[256,256]{1,0:T(8,128)S(1)}, f32[8,32,256]{2,1,0:T(8,128)}, f32[168,256]{1,0:T(8,128)S(1)}) custom-call(s32[1]{0:T(128)S(6)} %copy.17.live_ref, s32[1]{0:T(128)} %bitcast.place_ref, s32[128,128]{1,0:T(8,128)S(1)} %copy-done.4, f32[128,128]{1,0:T(8,128)S(1)} %copy-done.5, ...), custom_call_target="tpu_custom_call" | custom-call | flops 3000000000 | bytes 1000000 | tf_op jit(solution)/shard_map/gather_and_scatter/pallas_call | solution.py:467
  54.0 3.6 %all-to-all-start.2 = ((f32[8,32,256]{2,1,0:T(8,128)}), f32[8,32,256]{2,1,0:T(8,128)S(1)}, u32[]{:S(2)}, u32[]{:S(2)}) async-start(f32[8,32,256]{2,1,0:T(8,128)} %get-tuple-element.21), calls=%async_computation.2 | async-start | bytes 524288 | tf_op jit(solution)/shard_map/all_to_all | solution.py:504
  57.7 1.4 %collective-permute-done.2 = f32[168,256]{1,0:T(8,128)S(1)} collective-permute-done((f32[168,256]{1,0:T(8,128)S(1)}, f32[168,256]{1,0:T(8,128)S(1)}, u32[]{:S(2)}, u32[]{:S(2)}) %collective-permute-start.2) | collective-permute-done | bytes 172064 | tf_op jit(solution)/shard_map/ppermute | solution.py:507
  59.1 1.6 %collective-permute-start.3 = (f32[168,256]{1,0:T(8,128)S(1)}, f32[168,256]{1,0:T(8,128)S(1)}, u32[]{:S(2)}, u32[]{:S(2)}) collective-permute-start(f32[168,256]{1,0:T(8,128)S(1)} %add.7.own_ref), channel_id=1, source_target_pairs={{0,2},{1,3},{2,0},{3,1},{4,6},{5,7},{6,4},{7,5},{8,10},{9,11},{10,... | collective-permute-start | bytes 516104 | tf_op jit(solution)/shard_map/ppermute | solution.py:507
  60.7 4.9 %collective-permute-done.3.other_ref = f32[168,256]{1,0:T(8,128)S(1)} collective-permute-done((f32[168,256]{1,0:T(8,128)S(1)}, f32[168,256]{1,0:T(8,128)S(1)}, u32[]{:S(2)}, u32[]{:S(2)}) %collective-permute-start.3) | collective-permute-done | bytes 172064 | tf_op jit(solution)/shard_map/ppermute | solution.py:507
  65.6 0.6 all-to-all-done.2.block_ref
  66.2 0.8 table_sum.3
  67.0 5.4 %all-to-all-start.3 = ((f32[8,40,256]{2,1,0:T(8,128)}), f32[8,40,256]{2,1,0:T(8,128)S(1)}, u32[]{:S(2)}, u32[]{:S(2)}) async-start(f32[8,40,256]{2,1,0:T(8,128)} %get-tuple-element.24), calls=%async_computation.3 | async-start | bytes 655360 | tf_op jit(solution)/shard_map/all_to_all | solution.py:504
  72.3 4.2 %star_forward.3.star_image_ref = f32[128,128]{1,0:T(8,128)S(1)} custom-call(s32[128,128]{1,0:T(8,128)S(1)} %copy-done.3, f32[5,128,128]{2,1,0:T(8,128)S(1)} %copy-done.1, f32[160,256]{1,0:T(8,128)S(1)} %get-tuple-element.23.star_x_ref), custom_call_target="tpu_custom_call" | custom-call | flops 3000000000 | bytes 1000000 | tf_op jit(solution)/shard_map/star_forward/pallas_call | solution.py:492
  76.6 5.5 %all-to-all-done.3.block_ref = f32[8,40,256]{2,1,0:T(8,128)S(1)} async-done(((f32[8,40,256]{2,1,0:T(8,128)}), f32[8,40,256]{2,1,0:T(8,128)S(1)}, u32[]{:S(2)}, u32[]{:S(2)}) %all-to-all-start.3) | async-done | bytes 327712 | tf_op jit(solution)/shard_map/all_to_all | solution.py:504
  82.1 5.4 %last_gather.1 = (f32[128,128]{1,0:T(8,128)S(1)}, f32[256,256]{1,0:T(8,128)S(1)}, f32[32,8,128]{2,1,0:T(8,128)}) custom-call(s32[1]{0:T(128)S(6)} %copy.17.live_ref, s32[1]{0:T(128)} %bitcast.place_ref, s32[128,128]{1,0:T(8,128)S(1)} %copy-done.4, f32[128,128]{1,0:T(8,128)S(1)} %copy-done.5, f32[4,128,128]{2,1,0:T(8,128)S(1)} %copy-done.2, ...), custom_call_target="tpu_custom_call" | custom-call | flops 3000000000 | bytes 1000000 | tf_op jit(solution)/shard_map/last_gather/pallas_call | solution.py:480
  87.5 3.7 %all-to-all-start.4 = ((f32[32,8,128]{2,1,0:T(8,128)}), f32[32,8,128]{2,1,0:T(8,128)S(1)}, u32[]{:S(2)}, u32[]{:S(2)}) async-start(f32[32,8,128]{2,1,0:T(8,128)} %get-tuple-element.27.own_scalar_ref), calls=%async_computation.4 | async-start | bytes 262144 | tf_op jit(solution)/shard_map/all_to_all | solution.py:504
  92.3 7.1 %all-to-all-done.4.scalar_ref = f32[32,8,128]{2,1,0:T(8,128)S(1)} async-done(((f32[32,8,128]{2,1,0:T(8,128)}), f32[32,8,128]{2,1,0:T(8,128)S(1)}, u32[]{:S(2)}, u32[]{:S(2)}) %all-to-all-start.4) | async-done | bytes 131104 | tf_op jit(solution)/shard_map/all_to_all | solution.py:504
  99.4 1.9 %outputs.1 = (f32[5,8192]{1,0:T(8,128)}, f32[4,8192]{1,0:T(4,128)}, f32[256,128]{1,0:T(8,128)}, f32[128,128]{1,0:T(8,128)}) custom-call(s32[1]{0:T(128)S(6)} %copy.17.live_ref, f32[32,8,128]{2,1,0:T(8,128)} %get-tuple-element.27.own_scalar_ref, f32[32,8,128]{2,1,0:T(8,128)S(1)} %all-to-all-done.4.scalar_ref, f32[5,8192]{1,0:T(8,128)S(1)} %reshape.26.star_0_ref, ...), custom_call_target="tpu_custom_call" | custom-call | flops 1000000 | bytes 600000 | tf_op jit(solution)/shard_map/outputs/pallas_call | solution.py:538
  (30 shorter events, 1.2 us)
Async XLA Ops:
  10.7 7.4 %copy-start.8 = (f32[168,256]{1,0:T(8,128)S(1)}, f32[168,256]{1,0:T(8,128)}, u32[]{:S(2)}) copy-start(f32[168,256]{1,0:T(8,128)} %get-tuple-element.18) | copy-start | bytes 516100
  10.7 16.3 %all-to-all-start = ((f32[8,32,256]{2,1,0:T(8,128)}), f32[8,32,256]{2,1,0:T(8,128)S(1)}, u32[]{:S(2)}, u32[]{:S(2)}) async-start(f32[8,32,256]{2,1,0:T(8,128)} %get-tuple-element.17), calls=%async_computation | async-start | bytes 524288 | tf_op jit(solution)/shard_map/all_to_all | solution.py:504
  18.1 1.5 %collective-permute-start = (f32[168,256]{1,0:T(8,128)S(1)}, f32[168,256]{1,0:T(8,128)S(1)}, u32[]{:S(2)}, u32[]{:S(2)}) collective-permute-start(f32[168,256]{1,0:T(8,128)S(1)} %copy-done.8), channel_id=1, source_target_pairs={{0,1},{1,0},{2,3},{3,2},{4,5},{5,4},{6,7},{7,6},{8,9},{9,8},{10,11... | collective-permute-start | bytes 516104 | tf_op jit(solution)/shard_map/ppermute | solution.py:507
  19.6 6.5 %collective-permute-start.1 = (f32[168,256]{1,0:T(8,128)S(1)}, f32[168,256]{1,0:T(8,128)S(1)}, u32[]{:S(2)}, u32[]{:S(2)}) collective-permute-start(f32[168,256]{1,0:T(8,128)S(1)} %add.6.own_ref), channel_id=1, source_target_pairs={{0,2},{1,3},{2,0},{3,1},{4,6},{5,7},{6,4},{7,5},{8,10},{9,11},{10,... | collective-permute-start | bytes 516104 | tf_op jit(solution)/shard_map/ppermute | solution.py:507
  27.8 5.1 %copy-start.1 = (f32[5,128,128]{2,1,0:T(8,128)S(1)}, f32[5,128,128]{2,1,0:T(8,128)}, u32[]{:S(2)}) copy-start(f32[5,128,128]{2,1,0:T(8,128)} %star_coef_ref.5) | copy-start | bytes 983044
  27.8 5.2 %copy-start.3 = (s32[128,128]{1,0:T(8,128)S(1)}, s32[128,128]{1,0:T(8,128)}, u32[]{:S(2)}) copy-start(s32[128,128]{1,0:T(8,128)} %star_ref.5) | copy-start | bytes 196612
  27.8 14.9 %all-to-all-start.1 = ((f32[8,40,256]{2,1,0:T(8,128)}), f32[8,40,256]{2,1,0:T(8,128)S(1)}, u32[]{:S(2)}, u32[]{:S(2)}) async-start(f32[8,40,256]{2,1,0:T(8,128)} %get-tuple-element.20), calls=%async_computation.1 | async-start | bytes 655360 | tf_op jit(solution)/shard_map/all_to_all | solution.py:504
  33.0 9.7 %copy-start.2 = (f32[4,128,128]{2,1,0:T(8,128)S(1)}, f32[4,128,128]{2,1,0:T(8,128)}, u32[]{:S(2)}) copy-start(f32[4,128,128]{2,1,0:T(8,128)} %att_coef_ref.3) | copy-start | bytes 786436
  33.0 9.7 %copy-start.4 = (s32[128,128]{1,0:T(8,128)S(1)}, s32[128,128]{1,0:T(8,128)}, u32[]{:S(2)}) copy-start(s32[128,128]{1,0:T(8,128)} %knot_ref.3) | copy-start | bytes 196612
  33.0 9.7 %copy-start.5 = (f32[128,128]{1,0:T(8,128)S(1)}, f32[128,128]{1,0:T(8,128)}, u32[]{:S(2)}) copy-start(f32[128,128]{1,0:T(8,128)} %frac_ref.3) | copy-start | bytes 196612
  33.0 9.7 %copy-start.6 = (f32[128,128]{1,0:T(8,128)S(1)}, f32[128,128]{1,0:T(8,128)}, u32[]{:S(2)}) copy-start(f32[128,128]{1,0:T(8,128)} %cal_coef_ref.3) | copy-start | bytes 196612
  33.0 9.7 %copy-start.7 = (s32[128]{0:T(128)S(1)}, s32[128]{0:T(128)}, u32[]{:S(2)}) copy-start(s32[128]{0:T(128)} %param.15) | copy-start | bytes 1540
  54.0 12.2 %all-to-all-start.2 = ((f32[8,32,256]{2,1,0:T(8,128)}), f32[8,32,256]{2,1,0:T(8,128)S(1)}, u32[]{:S(2)}, u32[]{:S(2)}) async-start(f32[8,32,256]{2,1,0:T(8,128)} %get-tuple-element.21), calls=%async_computation.2 | async-start | bytes 524288 | tf_op jit(solution)/shard_map/all_to_all | solution.py:504
  57.7 1.4 %collective-permute-start.2 = (f32[168,256]{1,0:T(8,128)S(1)}, f32[168,256]{1,0:T(8,128)S(1)}, u32[]{:S(2)}, u32[]{:S(2)}) collective-permute-start(f32[168,256]{1,0:T(8,128)S(1)} %get-tuple-element.22), channel_id=1, source_target_pairs={{0,1},{1,0},{2,3},{3,2},{4,5},{5,4},{6,7},{7,6},{8,9},{9,8},{10,11... | collective-permute-start | bytes 516104 | tf_op jit(solution)/shard_map/ppermute | solution.py:507
  59.1 6.5 %collective-permute-start.3 = (f32[168,256]{1,0:T(8,128)S(1)}, f32[168,256]{1,0:T(8,128)S(1)}, u32[]{:S(2)}, u32[]{:S(2)}) collective-permute-start(f32[168,256]{1,0:T(8,128)S(1)} %add.7.own_ref), channel_id=1, source_target_pairs={{0,2},{1,3},{2,0},{3,1},{4,6},{5,7},{6,4},{7,5},{8,10},{9,11},{10,... | collective-permute-start | bytes 516104 | tf_op jit(solution)/shard_map/ppermute | solution.py:507
  67.0 15.1 %all-to-all-start.3 = ((f32[8,40,256]{2,1,0:T(8,128)}), f32[8,40,256]{2,1,0:T(8,128)S(1)}, u32[]{:S(2)}, u32[]{:S(2)}) async-start(f32[8,40,256]{2,1,0:T(8,128)} %get-tuple-element.24), calls=%async_computation.3 | async-start | bytes 655360 | tf_op jit(solution)/shard_map/all_to_all | solution.py:504
  87.5 11.9 %all-to-all-start.4 = ((f32[32,8,128]{2,1,0:T(8,128)}), f32[32,8,128]{2,1,0:T(8,128)S(1)}, u32[]{:S(2)}, u32[]{:S(2)}) async-start(f32[32,8,128]{2,1,0:T(8,128)} %get-tuple-element.27.own_scalar_ref), calls=%async_computation.4 | async-start | bytes 262144 | tf_op jit(solution)/shard_map/all_to_all | solution.py:504
  92.0 7.4 %copy-start = (f32[128,128]{1,0:T(8,128)S(1)}, f32[128,128]{1,0:T(8,128)}, u32[]{:S(2)}) copy-start(f32[128,128]{1,0:T(8,128)} %value_ref.1) | copy-start | bytes 196612

commit v9 on v8

--- a/solution.py
+++ b/solution.py
@@ -20,7 +20,8 @@
 BF16 = jnp.bfloat16
 F32 = jnp.float32
 SCALAR_LANE = 64
-KNOT_HALF = KNOT_ROWS + 32
+PAST_ROWS = 16
+KNOT_HALF = KNOT_ROWS + PAST_ROWS
 
 
 def two_parts(values):
@@ -32,13 +33,18 @@
     return lax.broadcasted_iota(jnp.int32, shape, 0), lax.broadcasted_iota(jnp.int32, shape, 1)
 
 
+def packed_rows(row, size):
+    wide = jnp.broadcast_to(row.astype(F32), (16, row.shape[1])).astype(BF16)
+    return jnp.concatenate([wide] * (size // 16), axis=0)
+
+
+def matches(index_row, size):
+    places, _ = rows_and_columns((size, index_row.shape[1]))
+    return places.astype(F32).astype(BF16) == packed_rows(index_row, size)
+
+
 def one_hot(index_row, size):
-    width = index_row.shape[1]
-    row = jnp.broadcast_to(index_row.astype(F32), (16, width)).astype(BF16)
-    rows = jnp.concatenate([row] * (size // 16), axis=0)
-    places, _ = rows_and_columns((size, width))
-    places = places.astype(F32).astype(BF16)
-    return jnp.where(places == rows, jnp.ones((), BF16), jnp.zeros((), BF16))
+    return jnp.where(matches(index_row, size), jnp.ones((), BF16), jnp.zeros((), BF16))
 
 
 def spline_weights(fraction):
@@ -53,12 +59,28 @@
     )
 
 
-def weight_columns(weights, fine, tile):
-    rows, _ = rows_and_columns((FINE + 8, weights[0].shape[1]))
-    behind = rows - fine[tile : tile + 1]
+def weight_columns(weights, fine_row, tile, places):
+    behind = places - fine_row
     result = jnp.zeros(behind.shape, F32)
     for offset in range(4):
         result = jnp.where(behind == offset, weights[offset][tile : tile + 1], result)
+    return result
+
+
+def near_and_past(weights, fine, tile):
+    width = fine.shape[1]
+    fine_row = fine[tile : tile + 1]
+    near, _ = rows_and_columns((FINE, width))
+    past, _ = rows_and_columns((PAST_ROWS, width))
+    past = FINE + (past & 3)
+    return weight_columns(weights, fine_row, tile, near), weight_columns(weights, fine_row, tile, past)
+
+
+def past_terms(terms, here):
+    rows, _ = rows_and_columns((PAST_ROWS, terms[0].shape[1]))
+    result = jnp.broadcast_to(terms[3][here], rows.shape)
+    for comp in range(2, -1, -1):
+        result = jnp.where(rows < 4 * (comp + 1), terms[comp][here], result)
     return result
 
 
@@ -88,23 +110,22 @@
     terms = [att_coef_ref[comp, rows, :] * values for comp in range(4)]
     parts = [two_parts(star_coef_ref[comp, rows, :] * values) for comp in range(5)]
     parts = [pair[half].astype(F32) for half in range(2) for pair in parts]
-    width = knot.shape[1]
-    fine_rows, _ = rows_and_columns((FINE, width))
     knot_left, knot_right, star_left, star_right = [], [], [], []
     for tile in range(GROUP):
         here = slice(tile, tile + 1)
         knot_right.append(one_hot(knot_coarse[here], COARSE))
-        columns = weight_columns(weights, knot_fine, tile)
+        near, past = near_and_past(weights, knot_fine, tile)
         spread = jnp.concatenate(
-            [term[here] * columns[:FINE] for term in terms]
-            + [term[here] * columns[FINE:] for term in terms],
-            axis=0,
+            [term[here] * near for term in terms] + [past_terms(terms, here) * past], axis=0
         )
         knot_left.append(jnp.concatenate(two_parts(spread), axis=0))
         star_right.append(one_hot(star_coarse[here], COARSE))
-        chosen = fine_rows == star_fine[here]
+        chosen = matches(star_fine[here], FINE)
         star_left.append(
-            jnp.concatenate([jnp.where(chosen, part[here], 0.0) for part in parts], axis=0).astype(BF16)
+            jnp.concatenate(
+                [jnp.where(chosen, packed_rows(part[here], FINE), jnp.zeros((), BF16)) for part in parts],
+                axis=0,
+            )
         )
     knot_acc[...] += product(
         jnp.concatenate(knot_left, axis=1), jnp.concatenate(knot_right, axis=1), ((1,), (1,))
@@ -128,12 +149,15 @@
     lane = lax.broadcasted_iota(jnp.int32, (8, 128), 1)
     row = lax.broadcasted_iota(jnp.int32, (8, 128), 0)
     wide_lane = lax.broadcasted_iota(jnp.int32, (8, COARSE), 1)
+    wide_row = lax.broadcasted_iota(jnp.int32, (8, COARSE), 0)
     edges = jnp.zeros((8, 128), F32)
     for comp in range(4):
-        begin, past = comp * FINE, KNOT_ROWS + comp * 8
+        begin, past = comp * FINE, KNOT_ROWS + comp // 2 * 8
         main = knot_acc[begin : begin + FINE] + knot_acc[KNOT_HALF + begin : KNOT_HALF + begin + FINE]
         beyond = knot_acc[past : past + 8] + knot_acc[KNOT_HALF + past : KNOT_HALF + past + 8]
-        moved = pltpu.roll(beyond, 1, 1)
+        if comp % 2:
+            beyond = pltpu.roll(beyond, 4, 0)
+        moved = pltpu.roll(jnp.where(wide_row < 3, beyond, 0.0), 1, 1)
         top = main[:8] + jnp.where(wide_lane > 0, moved, 0.0)
         store_rows(table_out, begin, top)
         store_rows(table_out, begin + 8, main[8:])
@@ -182,9 +206,9 @@
         total = total + block_ref[device]
     star = own_ref[...] + other_ref[...]
     star_out[...] = star[:STAR_ROWS]
+    total = jnp.concatenate([total[:, :128], total[:, 128:], star[STAR_ROWS:, :128]], axis=0)
     for device in range(block_ref.shape[0]):
-        out_ref[device, :-8] = total
-        out_ref[device, -8:] = star[STAR_ROWS:]
+        out_ref[device] = total
 
 
 def picked(array, which):
@@ -245,9 +269,9 @@
     segment = place_ref[0]
     lane = lax.broadcasted_iota(jnp.int32, (8, 128), 1)
     row = lax.broadcasted_iota(jnp.int32, (8, 128), 0)
-    edges = block_ref[0, -8:, :128]
+    edges = block_ref[0, -8:, :]
     for block in range(1, n_stars):
-        edges = edges + block_ref[block, -8:, :128]
+        edges = edges + block_ref[block, -8:, :]
 
     def slot(which):
         return pltpu.roll(edges, 128 - SLOT * jnp.clip(which, 0, n_seg - 1), 1)
@@ -257,7 +281,9 @@
     ahead = jnp.where(lane % 2 == 0, own, 0.0) + pltpu.roll(jnp.where(lane % 2 == 1, after, 0.0), 127, 1)
     ahead = jnp.where((segment < n_seg - 1) & (lane < 8) & (row < 3), ahead, 0.0)
 
-    table = block_ref[:, :-8, :].reshape(TABLE_ROWS, COARSE)
+    size = TABLE_ROWS // n_stars
+    table = jnp.concatenate([block_ref[:, :size, :], block_ref[:, size : 2 * size, :]], axis=2)
+    table = table.reshape(TABLE_ROWS, COARSE)
     pieces = []
     for comp in range(4):
         shifted = pltpu.roll(before, 128 - 2 * comp, 1) if comp else before
@@ -270,11 +296,14 @@
 
 def gather_ready(table, ahead, cal_coef_ref, tile_cal_ref, star_image_ref, knot_parts_ref, cal_ref):
     wide_lane = lax.broadcasted_iota(jnp.int32, (8, COARSE), 1)
+    row = lax.broadcasted_iota(jnp.int32, (8, COARSE), 0)
     beyond = []
     for comp in range(4):
         moved = pltpu.roll(table[comp * FINE : comp * FINE + 8], COARSE - 1, 1)
         last = pltpu.roll(ahead, 127 - 2 * comp, 1)
-        beyond.append(jnp.where(wide_lane == COARSE - 1, jnp.concatenate([last, last], axis=1), moved))
+        moved = jnp.where(wide_lane == COARSE - 1, jnp.concatenate([last, last], axis=1), moved)
+        beyond.append(pltpu.roll(moved, 4, 0) if comp % 2 else moved)
+    beyond = [jnp.where(row < 4, beyond[0], beyond[1]), jnp.where(row < 4, beyond[2], beyond[3])]
     knot_high, knot_low = two_parts(jnp.concatenate([table[:KNOT_ROWS]] + beyond, axis=0))
     knot_parts_ref[:KNOT_HALF] = knot_high
     knot_parts_ref[KNOT_HALF:] = knot_low
@@ -307,11 +336,10 @@
                 + found[KNOT_HALF + begin : KNOT_HALF + begin + size, across]
             )
 
-        columns = weight_columns(weights, fine, tile)
-        main = sum(coef[comp][here] * part(comp * FINE, FINE) for comp in range(4))
-        past = sum(coef[comp][here] * part(KNOT_ROWS + comp * 8, 8) for comp in range(4))
-        both = main * columns[:FINE]
-        both = both[:8] + both[8:16] + both[16:24] + both[24:] + past * columns[FINE:]
+        near, past = near_and_past(weights, fine, tile)
+        near = near * sum(coef[comp][here] * part(comp * FINE, FINE) for comp in range(4))
+        past = past * past_terms(coef, here) * part(KNOT_ROWS, PAST_ROWS)
+        both = near[:8] + near[8:16] + near[16:24] + near[24:] + past[:8] + past[8:]
         image_rows.append(jnp.sum(both, axis=0, keepdims=True))
     image = jnp.concatenate(image_rows, axis=0) + cal_ref[rows, :]
     return image * live_mask(live_ref, first, image.shape)
@@ -358,7 +386,7 @@
 def last_kernel(
     n_stars, n_seg, live_ref, place_ref, knot_ref, frac_ref, att_coef_ref, cal_coef_ref, tile_cal_ref,
     star_image_ref, star_x_ref, block_ref, star_0_ref, table_0_ref, image_0_ref, image_ref, table_out,
-    scalar_out, knot_parts_ref, cal_ref,
+    scalar_out, own_scalar_out, knot_parts_ref, cal_ref,
 ):
     table, ahead, edges = received_table(n_stars, n_seg, place_ref, block_ref)
     table_out[...] = table
@@ -383,6 +411,7 @@
     sums = lax.fori_loop(0, knot_ref.shape[0] // GROUP, one_group, (zero, zero))
     scalars = [norm] + [jnp.sum(part, keepdims=True) for part in sums] + [norm_0, square_0]
     scalars = with_scalars(jnp.zeros((8, 128), F32), list(enumerate(scalars)))
+    own_scalar_out[...] = scalars
     for device in range(scalar_out.shape[0]):
         scalar_out[device] = scalars
 
@@ -391,7 +420,7 @@
     live_ref, own_scalar_ref, scalar_ref, star_0_ref, star_h_ref, att_0_ref, att_h_ref, table_0_ref,
     table_h_ref, value_ref, image_0_ref, image_1_ref, star_out, att_out, cal_out, residual_out,
 ):
-    norm_0, square_0 = [picked(own_scalar_ref[0], which) for which in (3, 4)]
+    norm_0, square_0 = [picked(own_scalar_ref[...], which) for which in (3, 4)]
     everyone = scalar_ref[0]
     for device in range(1, scalar_ref.shape[0]):
         everyone = everyone + scalar_ref[device]
@@ -479,9 +508,9 @@
         observed = (obs_knot, obs_frac, att_coef, cal_coef, tile_row)
         return pl.pallas_call(
             functools.partial(last_kernel, n_stars, n_seg),
-            out_shape=(image_shape, table_shape, shaped(n_stars * n_seg, 8, 128)),
+            out_shape=(image_shape, table_shape, shaped(n_stars * n_seg, 8, 128), shaped(8, 128)),
             in_specs=in_smem(2) + in_vmem(len(observed) + len(received)),
-            out_specs=tuple(in_vmem(3)),
+            out_specs=tuple(in_vmem(4)),
             scratch_shapes=ready,
             compiler_params=PARAMS,
             cost_estimate=PASS_COST,
@@ -512,7 +541,7 @@
             star = star + partner(star, "seg", distance)
         blocks, star = pl.pallas_call(
             sum_kernel,
-            out_shape=(shaped(n_stars, TABLE_ROWS // n_stars + 8, COARSE), star_shape),
+            out_shape=(shaped(n_stars, 2 * TABLE_ROWS // n_stars + 8, 128), star_shape),
             in_specs=in_vmem(3),
             out_specs=tuple(in_vmem(2)),
             compiler_params=PARAMS,
@@ -526,7 +555,7 @@
     image_0, table_0, *sent = middle(*first)
     second = reduced(*sent)
     star_h = second[1]
-    image_1, table_h, scalars = last_gather(*second, star_0, table_0, image_0)
+    image_1, table_h, scalars, own_scalars = last_gather(*second, star_0, table_0, image_0)
 
     def star_order(star):
         return star.reshape(5, STAR_DEV)
@@ -544,7 +573,7 @@
         cost_estimate=SMALL_COST,
         name="outputs",
     )(
-        live_tiles, scalars, swap(scalars, ("stars", "seg")), star_order(star_0), star_order(star_h),
+        live_tiles, own_scalars, swap(scalars, ("stars", "seg")), star_order(star_0), star_order(star_h),
         att_order(table_0), att_order(table_h), table_0, table_h, obs_value, image_0, image_1,
     )
 

time: 102 us -> 99.4 us (0.975)
  waiting for transfers between devices: 32.2 us -> 30.8 us
  Pallas kernels: 38.1 us -> 36.9 us
    all_to_all x5, waiting for transfers between devices: 19.6 us -> 18.2 us  [swap(): return lax.all_to_all(blocks, axes, 0, 0)]
  transfers between devices with their start and end apart: 9 -> 9, of which waited for: 9 -> 9; matrix products, arithmetic and copies ran while one was open for 1% -> 1% of each run, Pallas kernels for 8% -> 9%
where the time goes in v9:
time: 99.4 us; the launch traced here: 98.8 us
  Pallas kernels  36.9 us (37%)
  waiting for transfers between devices  30.8 us (31%)
  starting transfers between devices  28.5 us (29%)
  between operations  1.48 us (1%)
  local copies, waits for them, and re-layouts  1.08 us (1%)
    all_to_all x5, starting transfers between devices, swap(): return lax.all_to_all(blocks, axes, 0, 0)  25.2 us
    all_to_all x5, waiting for transfers between devices, swap(): return lax.all_to_all(blocks, axes, 0, 0)  18.2 us
    ppermute x4, waiting for transfers between devices, partner(): lax.ppermute(array, axis, [(i, i ^ distance) for i in range(lax.axis_size...  12.6 us
    pallas_call x1, Pallas kernels, middle(): pl.pallas_call(functools.partial(middle_kernel, n_stars, n_seg), out_shap...  11.5 us
    pallas_call x1, Pallas kernels, first_scatter(): pl.pallas_call(first_kernel, out_shape=sent_shapes, in_specs=in_smem(2) +...  9.24 us
    pallas_call x2, Pallas kernels, star_forward(): pl.pallas_call(star_forward_kernel, out_shape=image_shape, in_specs=in_vm...  8.5 us
    pallas_call x1, Pallas kernels, last_gather(): pl.pallas_call(functools.partial(last_kernel, n_stars, n_seg), out_shape=...  5.13 us
    ppermute x4, starting transfers between devices, partner(): lax.ppermute(array, axis, [(i, i ^ distance) for i in range(lax.axis_size...  3.24 us
  transfers between devices with their start and end apart: 9, of which 9 were waited for; matrix products, arithmetic and copies ran while one was open for 1% of the time, Pallas kernels for 9%

profile of v9, /device:TPU:0, one launch (start us, length us, event | category | flops | bytes accessed | tf_op | source)
XLA Modules:
  0.0 98.8 jit_solution(11366307238062880924)
XLA Ops:
  1.3 9.2 %first_scatter.1 = (f32[8,32,256]{2,1,0:T(8,128)}, f32[168,256]{1,0:T(8,128)}) custom-call(s32[1]{0:T(128)S(6)} %copy.17.live_ref, s32[1]{0:T(128)} %bitcast.place_ref, f32[128,128]{1,0:T(8,128)} %value_ref.1, f32[128,128]{1,0:T(8,128)} %cal_coef_ref.3, s32[1,128]{1,0:T(1,128)} %bitcast.6, s32[128,128]{1,0:T(8,128)} %knot_ref.3, f32[128,128]{1,0:T(8,128)} %frac_ref.3, ...), custom_call_target="tpu_custom_call" | custom-call | flops 3000000000 | bytes 1000000 | tf_op jit(solution)/shard_map/first_scatter/pallas_call | solution.py:483
  10.5 7.4 %all-to-all-start = ((f32[8,32,256]{2,1,0:T(8,128)}), f32[8,32,256]{2,1,0:T(8,128)S(1)}, u32[]{:S(2)}, u32[]{:S(2)}) async-start(f32[8,32,256]{2,1,0:T(8,128)} %get-tuple-element.18), calls=%async_computation | async-start | bytes 524288 | tf_op jit(solution)/shard_map/all_to_all | solution.py:533
  18.0 1.4 %collective-permute-done = f32[168,256]{1,0:T(8,128)S(1)} collective-permute-done((f32[168,256]{1,0:T(8,128)S(1)}, f32[168,256]{1,0:T(8,128)S(1)}, u32[]{:S(2)}, u32[]{:S(2)}) %collective-permute-start) | collective-permute-done | bytes 172064 | tf_op jit(solution)/shard_map/ppermute | solution.py:536
  19.4 1.6 %collective-permute-start.1 = (f32[168,256]{1,0:T(8,128)S(1)}, f32[168,256]{1,0:T(8,128)S(1)}, u32[]{:S(2)}, u32[]{:S(2)}) collective-permute-start(f32[168,256]{1,0:T(8,128)S(1)} %add.6.own_ref), channel_id=1, source_target_pairs={{0,2},{1,3},{2,0},{3,1},{4,6},{5,7},{6,4},{7,5},{8,10},{9,11},{10,... | collective-permute-start | bytes 516104 | tf_op jit(solution)/shard_map/ppermute | solution.py:536
  21.0 4.9 %collective-permute-done.1.other_ref = f32[168,256]{1,0:T(8,128)S(1)} collective-permute-done((f32[168,256]{1,0:T(8,128)S(1)}, f32[168,256]{1,0:T(8,128)S(1)}, u32[]{:S(2)}, u32[]{:S(2)}) %collective-permute-start.1) | collective-permute-done | bytes 172064 | tf_op jit(solution)/shard_map/ppermute | solution.py:536
  25.9 0.9 all-to-all-done.block_ref
  26.9 0.7 table_sum.2
  27.6 5.1 %all-to-all-start.1 = ((f32[8,72,128]{2,1,0:T(8,128)}), f32[8,72,128]{2,1,0:T(8,128)S(1)}, u32[]{:S(2)}, u32[]{:S(2)}) async-start(f32[8,72,128]{2,1,0:T(8,128)} %get-tuple-element.21), calls=%async_computation.1 | async-start | bytes 589824 | tf_op jit(solution)/shard_map/all_to_all | solution.py:533
  32.8 4.2 %star_forward.2.star_image_ref = f32[128,128]{1,0:T(8,128)S(1)} custom-call(s32[128,128]{1,0:T(8,128)S(1)} %copy-done.3, f32[5,128,128]{2,1,0:T(8,128)S(1)} %copy-done.1, f32[160,256]{1,0:T(8,128)S(1)} %get-tuple-element.20.star_x_ref.star_0_ref), custom_call_target="tpu_custom_call" | custom-call | flops 3000000000 | bytes 1000000 | tf_op jit(solution)/shard_map/star_forward/pallas_call | solution.py:521
  37.1 4.7 %all-to-all-done.1.block_ref = f32[8,72,128]{2,1,0:T(8,128)S(1)} async-done(((f32[8,72,128]{2,1,0:T(8,128)}), f32[8,72,128]{2,1,0:T(8,128)S(1)}, u32[]{:S(2)}, u32[]{:S(2)}) %all-to-all-start.1) | async-done | bytes 294944 | tf_op jit(solution)/shard_map/all_to_all | solution.py:533
  41.8 11.5 %gather_and_scatter.1 = (f32[128,128]{1,0:T(8,128)S(1)}, f32[256,256]{1,0:T(8,128)S(1)}, f32[8,32,256]{2,1,0:T(8,128)}, f32[168,256]{1,0:T(8,128)S(1)}) custom-call(s32[1]{0:T(128)S(6)} %copy.17.live_ref, s32[1]{0:T(128)} %bitcast.place_ref, s32[128,128]{1,0:T(8,128)S(1)} %copy-done.4, f32[128,128]{1,0:T(8,128)S(1)} %copy-done.5, ...), custom_call_target="tpu_custom_call" | custom-call | flops 3000000000 | bytes 1000000 | tf_op jit(solution)/shard_map/gather_and_scatter/pallas_call | solution.py:496
  53.4 3.6 %all-to-all-start.2 = ((f32[8,32,256]{2,1,0:T(8,128)}), f32[8,32,256]{2,1,0:T(8,128)S(1)}, u32[]{:S(2)}, u32[]{:S(2)}) async-start(f32[8,32,256]{2,1,0:T(8,128)} %get-tuple-element.22), calls=%async_computation.2 | async-start | bytes 524288 | tf_op jit(solution)/shard_map/all_to_all | solution.py:533
  57.0 1.4 %collective-permute-done.2 = f32[168,256]{1,0:T(8,128)S(1)} collective-permute-done((f32[168,256]{1,0:T(8,128)S(1)}, f32[168,256]{1,0:T(8,128)S(1)}, u32[]{:S(2)}, u32[]{:S(2)}) %collective-permute-start.2) | collective-permute-done | bytes 172064 | tf_op jit(solution)/shard_map/ppermute | solution.py:536
  58.4 1.6 %collective-permute-start.3 = (f32[168,256]{1,0:T(8,128)S(1)}, f32[168,256]{1,0:T(8,128)S(1)}, u32[]{:S(2)}, u32[]{:S(2)}) collective-permute-start(f32[168,256]{1,0:T(8,128)S(1)} %add.7.own_ref), channel_id=1, source_target_pairs={{0,2},{1,3},{2,0},{3,1},{4,6},{5,7},{6,4},{7,5},{8,10},{9,11},{10,... | collective-permute-start | bytes 516104 | tf_op jit(solution)/shard_map/ppermute | solution.py:536
  60.0 4.9 %collective-permute-done.3.other_ref = f32[168,256]{1,0:T(8,128)S(1)} collective-permute-done((f32[168,256]{1,0:T(8,128)S(1)}, f32[168,256]{1,0:T(8,128)S(1)}, u32[]{:S(2)}, u32[]{:S(2)}) %collective-permute-start.3) | collective-permute-done | bytes 172064 | tf_op jit(solution)/shard_map/ppermute | solution.py:536
  64.9 0.6 all-to-all-done.2.block_ref
  65.5 0.7 table_sum.3
  66.3 5.4 %all-to-all-start.3 = ((f32[8,72,128]{2,1,0:T(8,128)}), f32[8,72,128]{2,1,0:T(8,128)S(1)}, u32[]{:S(2)}, u32[]{:S(2)}) async-start(f32[8,72,128]{2,1,0:T(8,128)} %get-tuple-element.25), calls=%async_computation.3 | async-start | bytes 589824 | tf_op jit(solution)/shard_map/all_to_all | solution.py:533
  71.7 4.2 %star_forward.3.star_image_ref = f32[128,128]{1,0:T(8,128)S(1)} custom-call(s32[128,128]{1,0:T(8,128)S(1)} %copy-done.3, f32[5,128,128]{2,1,0:T(8,128)S(1)} %copy-done.1, f32[160,256]{1,0:T(8,128)S(1)} %get-tuple-element.24.star_x_ref), custom_call_target="tpu_custom_call" | custom-call | flops 3000000000 | bytes 1000000 | tf_op jit(solution)/shard_map/star_forward/pallas_call | solution.py:521
  75.9 4.8 %all-to-all-done.3.block_ref = f32[8,72,128]{2,1,0:T(8,128)S(1)} async-done(((f32[8,72,128]{2,1,0:T(8,128)}), f32[8,72,128]{2,1,0:T(8,128)S(1)}, u32[]{:S(2)}, u32[]{:S(2)}) %all-to-all-start.3) | async-done | bytes 294944 | tf_op jit(solution)/shard_map/all_to_all | solution.py:533
  80.7 5.1 %last_gather.1 = (f32[128,128]{1,0:T(8,128)S(1)}, f32[256,256]{1,0:T(8,128)S(1)}, f32[32,8,128]{2,1,0:T(8,128)}, f32[8,128]{1,0:T(8,128)S(1)}) custom-call(s32[1]{0:T(128)S(6)} %copy.17.live_ref, s32[1]{0:T(128)} %bitcast.place_ref, s32[128,128]{1,0:T(8,128)S(1)} %copy-done.4, f32[128,128]{1,0:T(8,128)S(1)} %copy-done.5, f32[4,128,128]{2,1,0:T(8,128)S(1)} %copy-done.2, ...), custom_call_target="tpu_custom_call" | custom-call | flops 3000000000 | bytes 1000000 | tf_op jit(solution)/shard_map/last_gather/pallas_call | solution.py:509
  85.8 3.7 %all-to-all-start.4 = ((f32[32,8,128]{2,1,0:T(8,128)}), f32[32,8,128]{2,1,0:T(8,128)S(1)}, u32[]{:S(2)}, u32[]{:S(2)}) async-start(f32[32,8,128]{2,1,0:T(8,128)} %get-tuple-element.29), calls=%async_computation.4 | async-start | bytes 262144 | tf_op jit(solution)/shard_map/all_to_all | solution.py:533
  90.6 7.1 %all-to-all-done.4.scalar_ref = f32[32,8,128]{2,1,0:T(8,128)S(1)} async-done(((f32[32,8,128]{2,1,0:T(8,128)}), f32[32,8,128]{2,1,0:T(8,128)S(1)}, u32[]{:S(2)}, u32[]{:S(2)}) %all-to-all-start.4) | async-done | bytes 131104 | tf_op jit(solution)/shard_map/all_to_all | solution.py:533
  97.8 1.0 %outputs.1 = (f32[5,8192]{1,0:T(8,128)}, f32[4,8192]{1,0:T(4,128)}, f32[256,128]{1,0:T(8,128)}, f32[128,128]{1,0:T(8,128)}) custom-call(s32[1]{0:T(128)S(6)} %copy.17.live_ref, f32[8,128]{1,0:T(8,128)S(1)} %get-tuple-element.28.own_scalar_ref, f32[32,8,128]{2,1,0:T(8,128)S(1)} %all-to-all-done.4.scalar_ref, f32[5,8192]{1,0:T(8,128)S(1)} %reshape.26.star_0_ref, ...), custom_call_target="tpu_custom_call" | custom-call | flops 1000000 | bytes 600000 | tf_op jit(solution)/shard_map/outputs/pallas_call | solution.py:567
  (30 shorter events, 1.2 us)
Async XLA Ops:
  10.5 7.4 %copy-start.8 = (f32[168,256]{1,0:T(8,128)S(1)}, f32[168,256]{1,0:T(8,128)}, u32[]{:S(2)}) copy-start(f32[168,256]{1,0:T(8,128)} %get-tuple-element.19) | copy-start | bytes 516100
  10.5 16.3 %all-to-all-start = ((f32[8,32,256]{2,1,0:T(8,128)}), f32[8,32,256]{2,1,0:T(8,128)S(1)}, u32[]{:S(2)}, u32[]{:S(2)}) async-start(f32[8,32,256]{2,1,0:T(8,128)} %get-tuple-element.18), calls=%async_computation | async-start | bytes 524288 | tf_op jit(solution)/shard_map/all_to_all | solution.py:533
  17.9 1.5 %collective-permute-start = (f32[168,256]{1,0:T(8,128)S(1)}, f32[168,256]{1,0:T(8,128)S(1)}, u32[]{:S(2)}, u32[]{:S(2)}) collective-permute-start(f32[168,256]{1,0:T(8,128)S(1)} %copy-done.8), channel_id=1, source_target_pairs={{0,1},{1,0},{2,3},{3,2},{4,5},{5,4},{6,7},{7,6},{8,9},{9,8},{10,11... | collective-permute-start | bytes 516104 | tf_op jit(solution)/shard_map/ppermute | solution.py:536
  19.4 6.5 %collective-permute-start.1 = (f32[168,256]{1,0:T(8,128)S(1)}, f32[168,256]{1,0:T(8,128)S(1)}, u32[]{:S(2)}, u32[]{:S(2)}) collective-permute-start(f32[168,256]{1,0:T(8,128)S(1)} %add.6.own_ref), channel_id=1, source_target_pairs={{0,2},{1,3},{2,0},{3,1},{4,6},{5,7},{6,4},{7,5},{8,10},{9,11},{10,... | collective-permute-start | bytes 516104 | tf_op jit(solution)/shard_map/ppermute | solution.py:536
  27.6 5.1 %copy-start.1 = (f32[5,128,128]{2,1,0:T(8,128)S(1)}, f32[5,128,128]{2,1,0:T(8,128)}, u32[]{:S(2)}) copy-start(f32[5,128,128]{2,1,0:T(8,128)} %star_coef_ref.5) | copy-start | bytes 983044
  27.6 5.1 %copy-start.3 = (s32[128,128]{1,0:T(8,128)S(1)}, s32[128,128]{1,0:T(8,128)}, u32[]{:S(2)}) copy-start(s32[128,128]{1,0:T(8,128)} %star_ref.5) | copy-start | bytes 196612
  27.6 14.2 %all-to-all-start.1 = ((f32[8,72,128]{2,1,0:T(8,128)}), f32[8,72,128]{2,1,0:T(8,128)S(1)}, u32[]{:S(2)}, u32[]{:S(2)}) async-start(f32[8,72,128]{2,1,0:T(8,128)} %get-tuple-element.21), calls=%async_computation.1 | async-start | bytes 589824 | tf_op jit(solution)/shard_map/all_to_all | solution.py:533
  32.8 9.0 %copy-start.2 = (f32[4,128,128]{2,1,0:T(8,128)S(1)}, f32[4,128,128]{2,1,0:T(8,128)}, u32[]{:S(2)}) copy-start(f32[4,128,128]{2,1,0:T(8,128)} %att_coef_ref.3) | copy-start | bytes 786436
  32.8 9.0 %copy-start.4 = (s32[128,128]{1,0:T(8,128)S(1)}, s32[128,128]{1,0:T(8,128)}, u32[]{:S(2)}) copy-start(s32[128,128]{1,0:T(8,128)} %knot_ref.3) | copy-start | bytes 196612
  32.8 9.0 %copy-start.5 = (f32[128,128]{1,0:T(8,128)S(1)}, f32[128,128]{1,0:T(8,128)}, u32[]{:S(2)}) copy-start(f32[128,128]{1,0:T(8,128)} %frac_ref.3) | copy-start | bytes 196612
  32.8 9.0 %copy-start.6 = (f32[128,128]{1,0:T(8,128)S(1)}, f32[128,128]{1,0:T(8,128)}, u32[]{:S(2)}) copy-start(f32[128,128]{1,0:T(8,128)} %cal_coef_ref.3) | copy-start | bytes 196612
  32.8 9.0 %copy-start.7 = (s32[128]{0:T(128)S(1)}, s32[128]{0:T(128)}, u32[]{:S(2)}) copy-start(s32[128]{0:T(128)} %param.15) | copy-start | bytes 1540
  53.4 12.2 %all-to-all-start.2 = ((f32[8,32,256]{2,1,0:T(8,128)}), f32[8,32,256]{2,1,0:T(8,128)S(1)}, u32[]{:S(2)}, u32[]{:S(2)}) async-start(f32[8,32,256]{2,1,0:T(8,128)} %get-tuple-element.22), calls=%async_computation.2 | async-start | bytes 524288 | tf_op jit(solution)/shard_map/all_to_all | solution.py:533
  57.0 1.4 %collective-permute-start.2 = (f32[168,256]{1,0:T(8,128)S(1)}, f32[168,256]{1,0:T(8,128)S(1)}, u32[]{:S(2)}, u32[]{:S(2)}) collective-permute-start(f32[168,256]{1,0:T(8,128)S(1)} %get-tuple-element.23), channel_id=1, source_target_pairs={{0,1},{1,0},{2,3},{3,2},{4,5},{5,4},{6,7},{7,6},{8,9},{9,8},{10,11... | collective-permute-start | bytes 516104 | tf_op jit(solution)/shard_map/ppermute | solution.py:536
  58.4 6.5 %collective-permute-start.3 = (f32[168,256]{1,0:T(8,128)S(1)}, f32[168,256]{1,0:T(8,128)S(1)}, u32[]{:S(2)}, u32[]{:S(2)}) collective-permute-start(f32[168,256]{1,0:T(8,128)S(1)} %add.7.own_ref), channel_id=1, source_target_pairs={{0,2},{1,3},{2,0},{3,1},{4,6},{5,7},{6,4},{7,5},{8,10},{9,11},{10,... | collective-permute-start | bytes 516104 | tf_op jit(solution)/shard_map/ppermute | solution.py:536
  66.3 14.4 %all-to-all-start.3 = ((f32[8,72,128]{2,1,0:T(8,128)}), f32[8,72,128]{2,1,0:T(8,128)S(1)}, u32[]{:S(2)}, u32[]{:S(2)}) async-start(f32[8,72,128]{2,1,0:T(8,128)} %get-tuple-element.25), calls=%async_computation.3 | async-start | bytes 589824 | tf_op jit(solution)/shard_map/all_to_all | solution.py:533
  85.8 11.9 %all-to-all-start.4 = ((f32[32,8,128]{2,1,0:T(8,128)}), f32[32,8,128]{2,1,0:T(8,128)S(1)}, u32[]{:S(2)}, u32[]{:S(2)}) async-start(f32[32,8,128]{2,1,0:T(8,128)} %get-tuple-element.29), calls=%async_computation.4 | async-start | bytes 262144 | tf_op jit(solution)/shard_map/all_to_all | solution.py:533
  90.4 7.4 %copy-start = (f32[128,128]{1,0:T(8,128)S(1)}, f32[128,128]{1,0:T(8,128)}, u32[]{:S(2)}) copy-start(f32[128,128]{1,0:T(8,128)} %value_ref.1) | copy-start | bytes 196612

commit v10 on v9

--- a/solution.py
+++ b/solution.py
@@ -100,7 +100,7 @@
         out_ref[where // block, where % block : where % block + 8, :] = rows[offset : offset + 8]
 
 
-def scatter(first, values, observed, knot_acc, star_acc):
+def prepare(first, values, observed, buffers):
     knot_ref, frac_ref, att_coef_ref, star_ref, star_coef_ref = observed
     rows = pl.ds(first, GROUP)
     knot, star = knot_ref[rows, :], star_ref[rows, :]
@@ -110,29 +110,28 @@
     terms = [att_coef_ref[comp, rows, :] * values for comp in range(4)]
     parts = [two_parts(star_coef_ref[comp, rows, :] * values) for comp in range(5)]
     parts = [pair[half].astype(F32) for half in range(2) for pair in parts]
-    knot_left, knot_right, star_left, star_right = [], [], [], []
+    width = knot.shape[1]
+    knot_left, knot_right, star_left, star_right = buffers
     for tile in range(GROUP):
         here = slice(tile, tile + 1)
-        knot_right.append(one_hot(knot_coarse[here], COARSE))
+        across = slice(tile * width, (tile + 1) * width)
+        knot_right[:, across] = one_hot(knot_coarse[here], COARSE)
         near, past = near_and_past(weights, knot_fine, tile)
         spread = jnp.concatenate(
             [term[here] * near for term in terms] + [past_terms(terms, here) * past], axis=0
         )
-        knot_left.append(jnp.concatenate(two_parts(spread), axis=0))
-        star_right.append(one_hot(star_coarse[here], COARSE))
+        knot_left[:, across] = jnp.concatenate(two_parts(spread), axis=0)
+        star_right[:, across] = one_hot(star_coarse[here], COARSE)
         chosen = matches(star_fine[here], FINE)
-        star_left.append(
-            jnp.concatenate(
-                [jnp.where(chosen, packed_rows(part[here], FINE), jnp.zeros((), BF16)) for part in parts],
-                axis=0,
-            )
+        star_left[:, across] = jnp.concatenate(
+            [jnp.where(chosen, packed_rows(part[here], FINE), jnp.zeros((), BF16)) for part in parts], axis=0
         )
-    knot_acc[...] += product(
-        jnp.concatenate(knot_left, axis=1), jnp.concatenate(knot_right, axis=1), ((1,), (1,))
-    )
-    star_acc[...] += product(
-        jnp.concatenate(star_left, axis=1), jnp.concatenate(star_right, axis=1), ((1,), (1,))
-    )
+
+
+def multiply(buffers, knot_acc, star_acc):
+    knot_left, knot_right, star_left, star_right = buffers
+    knot_acc[...] += product(knot_left[...], knot_right[...], ((1,), (1,)))
+    star_acc[...] += product(star_left[...], star_right[...], ((1,), (1,)))
 
 
 def scatter_calibration(values, tile_cal_ref, table_out):
@@ -174,7 +173,7 @@
 
 def first_kernel(live_ref, place_ref, *refs):
     sources, (table_out, star_out, knot_acc, star_acc) = refs[:8], refs[8:12]
-    buffers, sems = refs[12:20], refs[20]
+    even, odd, buffers, sems = refs[12:16], refs[16:20], refs[20:28], refs[28]
     copies = [
         pltpu.make_async_copy(source, target, sems.at[which])
         for which, (source, target) in enumerate(zip(sources, buffers))
@@ -191,12 +190,24 @@
     for copy in copies[3:]:
         copy.wait()
 
-    @pl.loop(0, value_ref.shape[0] // GROUP)
-    def _(group):
-        first = pl.multiple_of(group * GROUP, GROUP)
+    def build(group, target):
+        first = group * GROUP if isinstance(group, int) else pl.multiple_of(group * GROUP, GROUP)
         values = value_ref[pl.ds(first, GROUP), :]
-        scatter(first, values * live_mask(live_ref, first, values.shape), observed, knot_acc, star_acc)
-
+        prepare(first, values * live_mask(live_ref, first, values.shape), observed, target)
+
+    groups = value_ref.shape[0] // GROUP
+    build(0, even)
+
+    @pl.loop(0, groups // 2 - 1)
+    def _(pair):
+        multiply(even, knot_acc, star_acc)
+        build(2 * pair + 1, odd)
+        multiply(odd, knot_acc, star_acc)
+        build(2 * pair + 2, even)
+
+    multiply(even, knot_acc, star_acc)
+    build(groups - 1, odd)
+    multiply(odd, knot_acc, star_acc)
     scatter_end(place_ref, [], knot_acc, star_acc, table_out, star_out)
 
 
@@ -230,22 +241,41 @@
     return picked(edges, 0), picked(edges, 1)
 
 
-def star_forward_kernel(star_ref, star_coef_ref, star_x_ref, image_ref, star_parts_ref):
-    star_x = star_x_ref[...]
-    star_high, star_low = two_parts(star_x)
+def in_turn(groups, make, use, even, odd, sums=()):
+    make(0, even)
+
+    def pair(index, sums):
+        first = 2 * index
+        make(first + 1, odd)
+        sums = use(first, even, sums)
+        make(first + 2, even)
+        return use(first + 1, odd, sums)
+
+    sums = lax.fori_loop(0, groups // 2 - 1, pair, sums)
+    make(groups - 1, odd)
+    return use(groups - 1, odd, use(groups - 2, even, sums))
+
+
+def group_rows(group):
+    return pl.ds(group * GROUP if isinstance(group, int) else pl.multiple_of(group * GROUP, GROUP), GROUP)
+
+
+def star_forward_kernel(star_ref, star_coef_ref, star_x_ref, image_ref, star_parts_ref, even, odd):
+    star_high, star_low = two_parts(star_x_ref[...])
     star_parts_ref[:STAR_ROWS] = star_high
     star_parts_ref[STAR_ROWS:] = star_low
-
-    @pl.loop(0, star_ref.shape[0] // GROUP)
-    def _(group):
-        rows = pl.ds(pl.multiple_of(group * GROUP, GROUP), GROUP)
-        star = star_ref[rows, :]
-        coarse, fine = star & (COARSE - 1), star >> 8
+    tiles = [slice(tile, tile + 1) for tile in range(GROUP)]
+
+    def make(group, target):
+        coarse = star_ref[group_rows(group), :] & (COARSE - 1)
+        hot = jnp.concatenate([one_hot(coarse[here], COARSE) for here in tiles], axis=1)
+        target[...] = product(star_parts_ref[...], hot, ((1,), (0,)))
+
+    def use(group, found, sums):
+        rows = group_rows(group)
+        fine = star_ref[rows, :] >> 8
         coef = [star_coef_ref[comp, rows, :] for comp in range(5)]
-        tiles = [slice(tile, tile + 1) for tile in range(GROUP)]
-        hot = jnp.concatenate([one_hot(coarse[here], COARSE) for here in tiles], axis=1)
-        found = product(star_parts_ref[...], hot, ((1,), (0,)))
-        width = star.shape[1]
+        width = fine.shape[1]
         fine_rows, _ = rows_and_columns((FINE, width))
         image_rows = []
         for tile, here in enumerate(tiles):
@@ -263,6 +293,9 @@
             both = both[:8] + both[8:16] + both[16:24] + both[24:]
             image_rows.append(jnp.sum(both, axis=0, keepdims=True))
         image_ref[rows, :] = jnp.concatenate(image_rows, axis=0)
+        return sums
+
+    in_turn(star_ref.shape[0] // GROUP, make, use, even, odd)
 
 
 def received_table(n_stars, n_seg, place_ref, block_ref):
@@ -315,19 +348,22 @@
     cal_ref[...] = (rows[:, :128] + rows[:, 128:]) * cal_coef_ref[...] + star_image_ref[...]
 
 
-def gather(first, live_ref, observed, knot_parts_ref, cal_ref):
+def gather_products(group, knot_ref, knot_parts_ref):
+    coarse = knot_ref[group_rows(group), :] >> 5
+    hot = [one_hot(coarse[tile : tile + 1], COARSE) for tile in range(GROUP)]
+    return product(knot_parts_ref[...], jnp.concatenate(hot, axis=1), ((1,), (0,)))
+
+
+def gather_image(group, found, live_ref, observed, cal_ref):
     knot_ref, frac_ref, att_coef_ref = observed
-    rows = pl.ds(first, GROUP)
-    knot = knot_ref[rows, :]
-    coarse, fine = knot >> 5, knot & (FINE - 1)
+    rows = group_rows(group)
+    fine = knot_ref[rows, :] & (FINE - 1)
     weights = spline_weights(frac_ref[rows, :])
     coef = [att_coef_ref[comp, rows, :] for comp in range(4)]
-    tiles = [slice(tile, tile + 1) for tile in range(GROUP)]
-    hot = jnp.concatenate([one_hot(coarse[here], COARSE) for here in tiles], axis=1)
-    found = product(knot_parts_ref[...], hot, ((1,), (0,)))
-    width = knot.shape[1]
+    width = fine.shape[1]
     image_rows = []
-    for tile, here in enumerate(tiles):
+    for tile in range(GROUP):
+        here = slice(tile, tile + 1)
         across = slice(tile * width, (tile + 1) * width)
 
         def part(begin, size):
@@ -342,7 +378,7 @@
         both = near[:8] + near[8:16] + near[16:24] + near[24:] + past[:8] + past[8:]
         image_rows.append(jnp.sum(both, axis=0, keepdims=True))
     image = jnp.concatenate(image_rows, axis=0) + cal_ref[rows, :]
-    return image * live_mask(live_ref, first, image.shape)
+    return image * live_mask(live_ref, group * GROUP, image.shape)
 
 
 def squares(array):
@@ -352,7 +388,7 @@
 def middle_kernel(
     n_stars, n_seg, live_ref, place_ref, knot_ref, frac_ref, att_coef_ref, star_ref, star_coef_ref,
     cal_coef_ref, tile_cal_ref, star_image_ref, star_x_ref, block_ref, image_ref, table_out, scatter_out,
-    star_out, knot_parts_ref, cal_ref, knot_acc, star_acc,
+    star_out, knot_parts_ref, cal_ref, knot_acc, star_acc, *buffers,
 ):
     table, ahead, _ = received_table(n_stars, n_seg, place_ref, block_ref)
     table_out[...] = table
@@ -363,21 +399,27 @@
     observed = (knot_ref, frac_ref, att_coef_ref)
     every = (knot_ref, frac_ref, att_coef_ref, star_ref, star_coef_ref)
     groups = knot_ref.shape[0] // GROUP
-    image = gather(0, live_ref, observed, knot_parts_ref, cal_ref)
-    image_ref[:GROUP, :] = image
-
-    def one_group(group, total):
-        first = pl.multiple_of(group * GROUP, GROUP)
-        following = pl.multiple_of(first + GROUP, GROUP)
-        values = image_ref[pl.ds(first, GROUP), :]
-        image = gather(following, live_ref, observed, knot_parts_ref, cal_ref)
-        scatter(first, values, every, knot_acc, star_acc)
-        image_ref[pl.ds(following, GROUP), :] = image
-        return total + image * image
-
-    total = lax.fori_loop(0, groups - 1, one_group, image * image)
-    first = (groups - 1) * GROUP
-    scatter(first, image_ref[first:, :], every, knot_acc, star_acc)
+    even, odd = buffers[:4], buffers[4:]
+
+    def build(group, target):
+        found = gather_products(group, knot_ref, knot_parts_ref)
+        image = gather_image(group, found, live_ref, observed, cal_ref)
+        image_ref[group_rows(group), :] = image
+        prepare(group_rows(group).start, image, every, target)
+        return image * image
+
+    total = build(0, even)
+
+    def pair(index, total):
+        multiply(even, knot_acc, star_acc)
+        total = total + build(2 * index + 1, odd)
+        multiply(odd, knot_acc, star_acc)
+        return total + build(2 * index + 2, even)
+
+    total = lax.fori_loop(0, groups // 2 - 1, pair, total)
+    multiply(even, knot_acc, star_acc)
+    total = total + build(groups - 1, odd)
+    multiply(odd, knot_acc, star_acc)
     scatter_calibration(image_ref[...] * cal_coef_ref[...], tile_cal_ref, scatter_out)
     scalars = [(0, norm), (1, jnp.sum(total, keepdims=True))]
     scatter_end(place_ref, scalars, knot_acc, star_acc, scatter_out, star_out)
@@ -386,7 +428,7 @@
 def last_kernel(
     n_stars, n_seg, live_ref, place_ref, knot_ref, frac_ref, att_coef_ref, cal_coef_ref, tile_cal_ref,
     star_image_ref, star_x_ref, block_ref, star_0_ref, table_0_ref, image_0_ref, image_ref, table_out,
-    scalar_out, own_scalar_out, knot_parts_ref, cal_ref,
+    scalar_out, own_scalar_out, knot_parts_ref, cal_ref, even, odd,
 ):
     table, ahead, edges = received_table(n_stars, n_seg, place_ref, block_ref)
     table_out[...] = table
@@ -398,17 +440,19 @@
     )
     gather_ready(table, ahead, cal_coef_ref, tile_cal_ref, star_image_ref, knot_parts_ref, cal_ref)
 
-    def one_group(group, sums):
-        first = pl.multiple_of(group * GROUP, GROUP)
-        rows = pl.ds(first, GROUP)
+    def make(group, target):
+        target[...] = gather_products(group, knot_ref, knot_parts_ref)
+
+    def use(group, found, sums):
+        rows = group_rows(group)
         image_0 = image_0_ref[rows, :]
-        image = gather(first, live_ref, (knot_ref, frac_ref, att_coef_ref), knot_parts_ref, cal_ref)
+        image = gather_image(group, found, live_ref, (knot_ref, frac_ref, att_coef_ref), cal_ref)
         image = image_0 - step * image
         image_ref[rows, :] = image
         return sums[0] + image * image, sums[1] + image * image_0
 
     zero = jnp.zeros((GROUP, knot_ref.shape[1]), F32)
-    sums = lax.fori_loop(0, knot_ref.shape[0] // GROUP, one_group, (zero, zero))
+    sums = in_turn(knot_ref.shape[0] // GROUP, make, use, even, odd, (zero, zero))
     scalars = [norm] + [jnp.sum(part, keepdims=True) for part in sums] + [norm_0, square_0]
     scalars = with_scalars(jnp.zeros((8, 128), F32), list(enumerate(scalars)))
     own_scalar_out[...] = scalars
@@ -475,6 +519,9 @@
     star_shape = shaped(STAR_ROWS, COARSE)
     sent_shapes = (shaped(n_stars, TABLE_ROWS // n_stars, COARSE), shaped(STAR_ROWS + 8, COARSE))
     sums = [pltpu.VMEM((2 * KNOT_HALF, COARSE), F32), pltpu.VMEM((2 * STAR_ROWS, COARSE), F32)]
+    lanes = GROUP * width
+    sizes = (2 * KNOT_HALF, COARSE, 2 * STAR_ROWS, COARSE)
+    turns = [pltpu.VMEM((size, lanes), BF16) for size in sizes] * 2
     ready = [pltpu.VMEM((2 * KNOT_HALF, COARSE), BF16), pltpu.VMEM((tile_count, width), F32)]
 
     def first_scatter():
@@ -485,7 +532,7 @@
             out_shape=sent_shapes,
             in_specs=in_smem(2) + in_hbm(len(observed)),
             out_specs=tuple(in_vmem(2)),
-            scratch_shapes=sums + buffers + [pltpu.SemaphoreType.DMA((len(observed),))],
+            scratch_shapes=sums + turns + buffers + [pltpu.SemaphoreType.DMA((len(observed),))],
             compiler_params=ARRIVE_PARAMS,
             cost_estimate=PASS_COST,
             name="first_scatter",
@@ -498,7 +545,7 @@
             out_shape=(image_shape, table_shape, *sent_shapes),
             in_specs=in_smem(2) + in_vmem(len(observed) + len(received)),
             out_specs=tuple(in_vmem(4)),
-            scratch_shapes=ready + sums,
+            scratch_shapes=ready + sums + turns,
             compiler_params=PARAMS,
             cost_estimate=PASS_COST,
             name="gather_and_scatter",
@@ -511,7 +558,7 @@
             out_shape=(image_shape, table_shape, shaped(n_stars * n_seg, 8, 128), shaped(8, 128)),
             in_specs=in_smem(2) + in_vmem(len(observed) + len(received)),
             out_specs=tuple(in_vmem(4)),
-            scratch_shapes=ready,
+            scratch_shapes=ready + [pltpu.VMEM((2 * KNOT_HALF, lanes), F32)] * 2,
             compiler_params=PARAMS,
             cost_estimate=PASS_COST,
             name="last_gather",
@@ -523,7 +570,7 @@
             out_shape=image_shape,
             in_specs=in_vmem(3),
             out_specs=in_vmem(1)[0],
-            scratch_shapes=[pltpu.VMEM((2 * STAR_ROWS, COARSE), BF16)],
+            scratch_shapes=[pltpu.VMEM((2 * STAR_ROWS, COARSE), BF16)] + [pltpu.VMEM((2 * STAR_ROWS, lanes), F32)] * 2,
             compiler_params=PARAMS,
             cost_estimate=PASS_COST,
             name="star_forward",

time: 99.4 us -> 110 us (1.11)
  Pallas kernels: 36.9 us -> 46.4 us
    pallas_call x1, Pallas kernels: 11.5 us -> 17.2 us  [middle(): pl.pallas_call(functools.partial(middle_kernel, n_stars, n_seg), out_shap...]
    pallas_call x1, Pallas kernels: 9.24 us -> 13.9 us  [first_scatter(): pl.pallas_call(first_kernel, out_shape=sent_shapes, in_specs=in_smem(2) +...]
  transfers between devices with their start and end apart: 9 -> 9, of which waited for: 9 -> 9; matrix products, arithmetic and copies ran while one was open for 1% -> 1% of each run, Pallas kernels for 9% -> 7%
where the time goes in v10:
time: 110 us; the launch traced here: 109 us
  Pallas kernels  46.4 us (42%)
  waiting for transfers between devices  31.6 us (29%)
  starting transfers between devices  28.5 us (26%)
  between operations  1.48 us (1%)
    all_to_all x5, starting transfers between devices, swap(): return lax.all_to_all(blocks, axes, 0, 0)  25.2 us
    all_to_all x5, waiting for transfers between devices, swap(): return lax.all_to_all(blocks, axes, 0, 0)  19 us
    pallas_call x1, Pallas kernels, middle(): pl.pallas_call(functools.partial(middle_kernel, n_stars, n_seg), out_shap...  17.2 us
    pallas_call x1, Pallas kernels, first_scatter(): pl.pallas_call(first_kernel, out_shape=sent_shapes, in_specs=in_smem(2) +...  13.9 us
    ppermute x4, waiting for transfers between devices, partner(): lax.ppermute(array, axis, [(i, i ^ distance) for i in range(lax.axis_size...  12.6 us
    pallas_call x2, Pallas kernels, star_forward(): pl.pallas_call(star_forward_kernel, out_shape=image_shape, in_specs=in_vm...  7.64 us
    pallas_call x1, Pallas kernels, last_gather(): pl.pallas_call(functools.partial(last_kernel, n_stars, n_seg), out_shape=...  5.23 us
    ppermute x4, starting transfers between devices, partner(): lax.ppermute(array, axis, [(i, i ^ distance) for i in range(lax.axis_size...  3.24 us
  transfers between devices with their start and end apart: 9, of which 9 were waited for; matrix products, arithmetic and copies ran while one was open for 1% of the time, Pallas kernels for 7%

profile of v10, /device:TPU:0, one launch (start us, length us, event | category | flops | bytes accessed | tf_op | source)
XLA Modules:
  0.0 109.1 jit_solution(9792485651499001355)
XLA Ops:
  1.3 13.9 %first_scatter.1 = (f32[8,32,256]{2,1,0:T(8,128)}, f32[168,256]{1,0:T(8,128)}) custom-call(s32[1]{0:T(128)S(6)} %copy.17.live_ref, s32[1]{0:T(128)} %bitcast.place_ref, f32[128,128]{1,0:T(8,128)} %value_ref.1, f32[128,128]{1,0:T(8,128)} %cal_coef_ref.3, s32[1,128]{1,0:T(1,128)} %bitcast.6, s32[128,128]{1,0:T(8,128)} %knot_ref.3, f32[128,128]{1,0:T(8,128)} %frac_ref.3, ...), custom_call_target="tpu_custom_call" | custom-call | flops 3000000000 | bytes 1000000 | tf_op jit(solution)/shard_map/first_scatter/pallas_call | solution.py:530
  15.2 7.4 %all-to-all-start = ((f32[8,32,256]{2,1,0:T(8,128)}), f32[8,32,256]{2,1,0:T(8,128)S(1)}, u32[]{:S(2)}, u32[]{:S(2)}) async-start(f32[8,32,256]{2,1,0:T(8,128)} %get-tuple-element.18), calls=%async_computation | async-start | bytes 524288 | tf_op jit(solution)/shard_map/all_to_all | solution.py:580
  22.6 1.4 %collective-permute-done = f32[168,256]{1,0:T(8,128)S(1)} collective-permute-done((f32[168,256]{1,0:T(8,128)S(1)}, f32[168,256]{1,0:T(8,128)S(1)}, u32[]{:S(2)}, u32[]{:S(2)}) %collective-permute-start) | collective-permute-done | bytes 172064 | tf_op jit(solution)/shard_map/ppermute | solution.py:583
  24.1 1.6 %collective-permute-start.1 = (f32[168,256]{1,0:T(8,128)S(1)}, f32[168,256]{1,0:T(8,128)S(1)}, u32[]{:S(2)}, u32[]{:S(2)}) collective-permute-start(f32[168,256]{1,0:T(8,128)S(1)} %add.6.own_ref), channel_id=1, source_target_pairs={{0,2},{1,3},{2,0},{3,1},{4,6},{5,7},{6,4},{7,5},{8,10},{9,11},{10,... | collective-permute-start | bytes 516104 | tf_op jit(solution)/shard_map/ppermute | solution.py:583
  25.7 4.9 %collective-permute-done.1.other_ref = f32[168,256]{1,0:T(8,128)S(1)} collective-permute-done((f32[168,256]{1,0:T(8,128)S(1)}, f32[168,256]{1,0:T(8,128)S(1)}, u32[]{:S(2)}, u32[]{:S(2)}) %collective-permute-start.1) | collective-permute-done | bytes 172064 | tf_op jit(solution)/shard_map/ppermute | solution.py:583
  30.6 0.9 all-to-all-done.block_ref
  31.5 0.7 table_sum.2
  32.2 5.1 %all-to-all-start.1 = ((f32[8,72,128]{2,1,0:T(8,128)}), f32[8,72,128]{2,1,0:T(8,128)S(1)}, u32[]{:S(2)}, u32[]{:S(2)}) async-start(f32[8,72,128]{2,1,0:T(8,128)} %get-tuple-element.21), calls=%async_computation.1 | async-start | bytes 589824 | tf_op jit(solution)/shard_map/all_to_all | solution.py:580
  37.5 3.8 %star_forward.2.star_image_ref = f32[128,128]{1,0:T(8,128)S(1)} custom-call(s32[128,128]{1,0:T(8,128)S(1)} %copy-done.3, f32[5,128,128]{2,1,0:T(8,128)S(1)} %copy-done.1, f32[160,256]{1,0:T(8,128)S(1)} %get-tuple-element.20.star_x_ref.star_0_ref), custom_call_target="tpu_custom_call" | custom-call | flops 3000000000 | bytes 1000000 | tf_op jit(solution)/shard_map/star_forward/pallas_call | solution.py:568
  41.3 5.2 %all-to-all-done.1.block_ref = f32[8,72,128]{2,1,0:T(8,128)S(1)} async-done(((f32[8,72,128]{2,1,0:T(8,128)}), f32[8,72,128]{2,1,0:T(8,128)S(1)}, u32[]{:S(2)}, u32[]{:S(2)}) %all-to-all-start.1) | async-done | bytes 294944 | tf_op jit(solution)/shard_map/all_to_all | solution.py:580
  46.5 17.2 %gather_and_scatter.1 = (f32[128,128]{1,0:T(8,128)S(1)}, f32[256,256]{1,0:T(8,128)S(1)}, f32[8,32,256]{2,1,0:T(8,128)}, f32[168,256]{1,0:T(8,128)S(1)}) custom-call(s32[1]{0:T(128)S(6)} %copy.17.live_ref, s32[1]{0:T(128)} %bitcast.place_ref, s32[128,128]{1,0:T(8,128)S(1)} %copy-done.4, f32[128,128]{1,0:T(8,128)S(1)} %copy-done.5, ...), custom_call_target="tpu_custom_call" | custom-call | flops 3000000000 | bytes 1000000 | tf_op jit(solution)/shard_map/gather_and_scatter/pallas_call | solution.py:543
  63.6 3.6 %all-to-all-start.2 = ((f32[8,32,256]{2,1,0:T(8,128)}), f32[8,32,256]{2,1,0:T(8,128)S(1)}, u32[]{:S(2)}, u32[]{:S(2)}) async-start(f32[8,32,256]{2,1,0:T(8,128)} %get-tuple-element.22), calls=%async_computation.2 | async-start | bytes 524288 | tf_op jit(solution)/shard_map/all_to_all | solution.py:580
  67.3 1.4 %collective-permute-done.2 = f32[168,256]{1,0:T(8,128)S(1)} collective-permute-done((f32[168,256]{1,0:T(8,128)S(1)}, f32[168,256]{1,0:T(8,128)S(1)}, u32[]{:S(2)}, u32[]{:S(2)}) %collective-permute-start.2) | collective-permute-done | bytes 172064 | tf_op jit(solution)/shard_map/ppermute | solution.py:583
  68.7 1.6 %collective-permute-start.3 = (f32[168,256]{1,0:T(8,128)S(1)}, f32[168,256]{1,0:T(8,128)S(1)}, u32[]{:S(2)}, u32[]{:S(2)}) collective-permute-start(f32[168,256]{1,0:T(8,128)S(1)} %add.7.own_ref), channel_id=1, source_target_pairs={{0,2},{1,3},{2,0},{3,1},{4,6},{5,7},{6,4},{7,5},{8,10},{9,11},{10,... | collective-permute-start | bytes 516104 | tf_op jit(solution)/shard_map/ppermute | solution.py:583
  70.3 4.9 %collective-permute-done.3.other_ref = f32[168,256]{1,0:T(8,128)S(1)} collective-permute-done((f32[168,256]{1,0:T(8,128)S(1)}, f32[168,256]{1,0:T(8,128)S(1)}, u32[]{:S(2)}, u32[]{:S(2)}) %collective-permute-start.3) | collective-permute-done | bytes 172064 | tf_op jit(solution)/shard_map/ppermute | solution.py:583
  75.2 0.6 all-to-all-done.2.block_ref
  75.8 0.7 table_sum.3
  76.5 5.4 %all-to-all-start.3 = ((f32[8,72,128]{2,1,0:T(8,128)}), f32[8,72,128]{2,1,0:T(8,128)S(1)}, u32[]{:S(2)}, u32[]{:S(2)}) async-start(f32[8,72,128]{2,1,0:T(8,128)} %get-tuple-element.25), calls=%async_computation.3 | async-start | bytes 589824 | tf_op jit(solution)/shard_map/all_to_all | solution.py:580
  81.9 3.8 %star_forward.3.star_image_ref = f32[128,128]{1,0:T(8,128)S(1)} custom-call(s32[128,128]{1,0:T(8,128)S(1)} %copy-done.3, f32[5,128,128]{2,1,0:T(8,128)S(1)} %copy-done.1, f32[160,256]{1,0:T(8,128)S(1)} %get-tuple-element.24.star_x_ref), custom_call_target="tpu_custom_call" | custom-call | flops 3000000000 | bytes 1000000 | tf_op jit(solution)/shard_map/star_forward/pallas_call | solution.py:568
  85.7 5.2 %all-to-all-done.3.block_ref = f32[8,72,128]{2,1,0:T(8,128)S(1)} async-done(((f32[8,72,128]{2,1,0:T(8,128)}), f32[8,72,128]{2,1,0:T(8,128)S(1)}, u32[]{:S(2)}, u32[]{:S(2)}) %all-to-all-start.3) | async-done | bytes 294944 | tf_op jit(solution)/shard_map/all_to_all | solution.py:580
  91.0 5.2 %last_gather.1 = (f32[128,128]{1,0:T(8,128)S(1)}, f32[256,256]{1,0:T(8,128)S(1)}, f32[32,8,128]{2,1,0:T(8,128)}, f32[8,128]{1,0:T(8,128)S(1)}) custom-call(s32[1]{0:T(128)S(6)} %copy.17.live_ref, s32[1]{0:T(128)} %bitcast.place_ref, s32[128,128]{1,0:T(8,128)S(1)} %copy-done.4, f32[128,128]{1,0:T(8,128)S(1)} %copy-done.5, f32[4,128,128]{2,1,0:T(8,128)S(1)} %copy-done.2, ...), custom_call_target="tpu_custom_call" | custom-call | flops 3000000000 | bytes 1000000 | tf_op jit(solution)/shard_map/last_gather/pallas_call | solution.py:556
  96.2 3.7 %all-to-all-start.4 = ((f32[32,8,128]{2,1,0:T(8,128)}), f32[32,8,128]{2,1,0:T(8,128)S(1)}, u32[]{:S(2)}, u32[]{:S(2)}) async-start(f32[32,8,128]{2,1,0:T(8,128)} %get-tuple-element.29), calls=%async_computation.4 | async-start | bytes 262144 | tf_op jit(solution)/shard_map/all_to_all | solution.py:580
  101.0 7.1 %all-to-all-done.4.scalar_ref = f32[32,8,128]{2,1,0:T(8,128)S(1)} async-done(((f32[32,8,128]{2,1,0:T(8,128)}), f32[32,8,128]{2,1,0:T(8,128)S(1)}, u32[]{:S(2)}, u32[]{:S(2)}) %all-to-all-start.4) | async-done | bytes 131104 | tf_op jit(solution)/shard_map/all_to_all | solution.py:580
  108.1 1.0 outputs.1
  (30 shorter events, 1.2 us)
Async XLA Ops:
  15.2 7.4 %copy-start.8 = (f32[168,256]{1,0:T(8,128)S(1)}, f32[168,256]{1,0:T(8,128)}, u32[]{:S(2)}) copy-start(f32[168,256]{1,0:T(8,128)} %get-tuple-element.19) | copy-start | bytes 516100
  15.2 16.3 %all-to-all-start = ((f32[8,32,256]{2,1,0:T(8,128)}), f32[8,32,256]{2,1,0:T(8,128)S(1)}, u32[]{:S(2)}, u32[]{:S(2)}) async-start(f32[8,32,256]{2,1,0:T(8,128)} %get-tuple-element.18), calls=%async_computation | async-start | bytes 524288 | tf_op jit(solution)/shard_map/all_to_all | solution.py:580
  22.6 1.5 %collective-permute-start = (f32[168,256]{1,0:T(8,128)S(1)}, f32[168,256]{1,0:T(8,128)S(1)}, u32[]{:S(2)}, u32[]{:S(2)}) collective-permute-start(f32[168,256]{1,0:T(8,128)S(1)} %copy-done.8), channel_id=1, source_target_pairs={{0,1},{1,0},{2,3},{3,2},{4,5},{5,4},{6,7},{7,6},{8,9},{9,8},{10,11... | collective-permute-start | bytes 516104 | tf_op jit(solution)/shard_map/ppermute | solution.py:583
  24.1 6.5 %collective-permute-start.1 = (f32[168,256]{1,0:T(8,128)S(1)}, f32[168,256]{1,0:T(8,128)S(1)}, u32[]{:S(2)}, u32[]{:S(2)}) collective-permute-start(f32[168,256]{1,0:T(8,128)S(1)} %add.6.own_ref), channel_id=1, source_target_pairs={{0,2},{1,3},{2,0},{3,1},{4,6},{5,7},{6,4},{7,5},{8,10},{9,11},{10,... | collective-permute-start | bytes 516104 | tf_op jit(solution)/shard_map/ppermute | solution.py:583
  32.2 5.1 %copy-start.1 = (f32[5,128,128]{2,1,0:T(8,128)S(1)}, f32[5,128,128]{2,1,0:T(8,128)}, u32[]{:S(2)}) copy-start(f32[5,128,128]{2,1,0:T(8,128)} %star_coef_ref.5) | copy-start | bytes 983044
  32.2 5.2 %copy-start.3 = (s32[128,128]{1,0:T(8,128)S(1)}, s32[128,128]{1,0:T(8,128)}, u32[]{:S(2)}) copy-start(s32[128,128]{1,0:T(8,128)} %star_ref.5) | copy-start | bytes 196612
  32.2 14.2 %all-to-all-start.1 = ((f32[8,72,128]{2,1,0:T(8,128)}), f32[8,72,128]{2,1,0:T(8,128)S(1)}, u32[]{:S(2)}, u32[]{:S(2)}) async-start(f32[8,72,128]{2,1,0:T(8,128)} %get-tuple-element.21), calls=%async_computation.1 | async-start | bytes 589824 | tf_op jit(solution)/shard_map/all_to_all | solution.py:580
  37.4 9.0 %copy-start.2 = (f32[4,128,128]{2,1,0:T(8,128)S(1)}, f32[4,128,128]{2,1,0:T(8,128)}, u32[]{:S(2)}) copy-start(f32[4,128,128]{2,1,0:T(8,128)} %att_coef_ref.3) | copy-start | bytes 786436
  37.4 9.0 %copy-start.4 = (s32[128,128]{1,0:T(8,128)S(1)}, s32[128,128]{1,0:T(8,128)}, u32[]{:S(2)}) copy-start(s32[128,128]{1,0:T(8,128)} %knot_ref.3) | copy-start | bytes 196612
  37.4 9.0 %copy-start.5 = (f32[128,128]{1,0:T(8,128)S(1)}, f32[128,128]{1,0:T(8,128)}, u32[]{:S(2)}) copy-start(f32[128,128]{1,0:T(8,128)} %frac_ref.3) | copy-start | bytes 196612
  37.4 9.0 %copy-start.6 = (f32[128,128]{1,0:T(8,128)S(1)}, f32[128,128]{1,0:T(8,128)}, u32[]{:S(2)}) copy-start(f32[128,128]{1,0:T(8,128)} %cal_coef_ref.3) | copy-start | bytes 196612
  37.4 9.0 %copy-start.7 = (s32[128]{0:T(128)S(1)}, s32[128]{0:T(128)}, u32[]{:S(2)}) copy-start(s32[128]{0:T(128)} %param.15) | copy-start | bytes 1540
  63.6 12.2 %all-to-all-start.2 = ((f32[8,32,256]{2,1,0:T(8,128)}), f32[8,32,256]{2,1,0:T(8,128)S(1)}, u32[]{:S(2)}, u32[]{:S(2)}) async-start(f32[8,32,256]{2,1,0:T(8,128)} %get-tuple-element.22), calls=%async_computation.2 | async-start | bytes 524288 | tf_op jit(solution)/shard_map/all_to_all | solution.py:580
  67.2 1.4 %collective-permute-start.2 = (f32[168,256]{1,0:T(8,128)S(1)}, f32[168,256]{1,0:T(8,128)S(1)}, u32[]{:S(2)}, u32[]{:S(2)}) collective-permute-start(f32[168,256]{1,0:T(8,128)S(1)} %get-tuple-element.23), channel_id=1, source_target_pairs={{0,1},{1,0},{2,3},{3,2},{4,5},{5,4},{6,7},{7,6},{8,9},{9,8},{10,11... | collective-permute-start | bytes 516104 | tf_op jit(solution)/shard_map/ppermute | solution.py:583
  68.7 6.5 %collective-permute-start.3 = (f32[168,256]{1,0:T(8,128)S(1)}, f32[168,256]{1,0:T(8,128)S(1)}, u32[]{:S(2)}, u32[]{:S(2)}) collective-permute-start(f32[168,256]{1,0:T(8,128)S(1)} %add.7.own_ref), channel_id=1, source_target_pairs={{0,2},{1,3},{2,0},{3,1},{4,6},{5,7},{6,4},{7,5},{8,10},{9,11},{10,... | collective-permute-start | bytes 516104 | tf_op jit(solution)/shard_map/ppermute | solution.py:583
  76.5 14.4 %all-to-all-start.3 = ((f32[8,72,128]{2,1,0:T(8,128)}), f32[8,72,128]{2,1,0:T(8,128)S(1)}, u32[]{:S(2)}, u32[]{:S(2)}) async-start(f32[8,72,128]{2,1,0:T(8,128)} %get-tuple-element.25), calls=%async_computation.3 | async-start | bytes 589824 | tf_op jit(solution)/shard_map/all_to_all | solution.py:580
  96.2 11.9 %all-to-all-start.4 = ((f32[32,8,128]{2,1,0:T(8,128)}), f32[32,8,128]{2,1,0:T(8,128)S(1)}, u32[]{:S(2)}, u32[]{:S(2)}) async-start(f32[32,8,128]{2,1,0:T(8,128)} %get-tuple-element.29), calls=%async_computation.4 | async-start | bytes 262144 | tf_op jit(solution)/shard_map/all_to_all | solution.py:580
  100.7 7.4 %copy-start = (f32[128,128]{1,0:T(8,128)S(1)}, f32[128,128]{1,0:T(8,128)}, u32[]{:S(2)}) copy-start(f32[128,128]{1,0:T(8,128)} %value_ref.1) | copy-start | bytes 196612

commit v11 on v9

--- a/solution.py
+++ b/solution.py
@@ -100,26 +100,67 @@
         out_ref[where // block, where % block : where % block + 8, :] = rows[offset : offset + 8]
 
 
-def scatter(first, values, observed, knot_acc, star_acc):
-    knot_ref, frac_ref, att_coef_ref, star_ref, star_coef_ref = observed
-    rows = pl.ds(first, GROUP)
-    knot, star = knot_ref[rows, :], star_ref[rows, :]
-    knot_coarse, knot_fine = knot >> 5, knot & (FINE - 1)
-    star_coarse, star_fine = star & (COARSE - 1), star >> 8
-    weights = spline_weights(frac_ref[rows, :])
+class Fresh:
+    def __init__(self, knot_ref, frac_ref, star_ref):
+        self.refs = knot_ref, frac_ref, star_ref
+
+    def at(self, group):
+        rows = group_rows(group)
+        knot_ref, frac_ref, star_ref = self.refs
+        knot, star = knot_ref[rows, :], star_ref[rows, :]
+        weights = spline_weights(frac_ref[rows, :])
+        knot_hot = [one_hot((knot >> 5)[tile : tile + 1], COARSE) for tile in range(GROUP)]
+        star_hot = [one_hot((star & (COARSE - 1))[tile : tile + 1], COARSE) for tile in range(GROUP)]
+        columns = [near_and_past(weights, knot & (FINE - 1), tile) for tile in range(GROUP)]
+        return columns, jnp.concatenate(knot_hot, axis=1), jnp.concatenate(star_hot, axis=1)
+
+
+class Stored:
+    def __init__(self, column_ref, knot_hot_ref, star_hot_ref):
+        self.refs = column_ref, knot_hot_ref, star_hot_ref
+
+    def columns(self, group):
+        column_ref = self.refs[0]
+        result = []
+        for tile in range(GROUP):
+            both = column_ref[group * GROUP + tile]
+            result.append((both[:FINE], both[FINE:]))
+        return result
+
+    def at(self, group):
+        return self.columns(group), self.refs[1][group], self.refs[2][group]
+
+
+def group_rows(group):
+    return pl.ds(group * GROUP if isinstance(group, int) else pl.multiple_of(group * GROUP, GROUP), GROUP)
+
+
+def factor_kernel(knot_ref, frac_ref, star_ref, after_ref, column_out, knot_hot_out, star_hot_out):
+    @pl.loop(0, knot_ref.shape[0] // GROUP)
+    def _(group):
+        columns, knot_hot, star_hot = Fresh(knot_ref, frac_ref, star_ref).at(group)
+        knot_hot_out[group] = knot_hot
+        star_hot_out[group] = star_hot
+        for tile in range(GROUP):
+            column_out[group * GROUP + tile] = jnp.concatenate(columns[tile], axis=0)
+
+
+def scatter(group, values, factors, coefs, knot_acc, star_acc):
+    att_coef_ref, star_ref, star_coef_ref = coefs
+    rows = group_rows(group)
+    star_fine = star_ref[rows, :] >> 8
+    columns, knot_hot, star_hot = factors.at(group)
     terms = [att_coef_ref[comp, rows, :] * values for comp in range(4)]
     parts = [two_parts(star_coef_ref[comp, rows, :] * values) for comp in range(5)]
     parts = [pair[half].astype(F32) for half in range(2) for pair in parts]
-    knot_left, knot_right, star_left, star_right = [], [], [], []
+    knot_left, star_left = [], []
     for tile in range(GROUP):
         here = slice(tile, tile + 1)
-        knot_right.append(one_hot(knot_coarse[here], COARSE))
-        near, past = near_and_past(weights, knot_fine, tile)
+        near, past = columns[tile]
         spread = jnp.concatenate(
             [term[here] * near for term in terms] + [past_terms(terms, here) * past], axis=0
         )
         knot_left.append(jnp.concatenate(two_parts(spread), axis=0))
-        star_right.append(one_hot(star_coarse[here], COARSE))
         chosen = matches(star_fine[here], FINE)
         star_left.append(
             jnp.concatenate(
@@ -128,10 +169,10 @@
             )
         )
     knot_acc[...] += product(
-        jnp.concatenate(knot_left, axis=1), jnp.concatenate(knot_right, axis=1), ((1,), (1,))
+        jnp.concatenate(knot_left, axis=1), knot_hot, ((1,), (1,))
     )
     star_acc[...] += product(
-        jnp.concatenate(star_left, axis=1), jnp.concatenate(star_right, axis=1), ((1,), (1,))
+        jnp.concatenate(star_left, axis=1), star_hot, ((1,), (1,))
     )
 
 
@@ -181,7 +222,8 @@
     ]
     for copy in copies:
         copy.start()
-    value_ref, cal_coef_ref, tile_cal_ref, *observed = buffers
+    value_ref, cal_coef_ref, tile_cal_ref, knot_ref, frac_ref, att_coef_ref, star_ref, star_coef_ref = buffers
+    factors, coefs = Fresh(knot_ref, frac_ref, star_ref), (att_coef_ref, star_ref, star_coef_ref)
     knot_acc[...] = jnp.zeros_like(knot_acc)
     star_acc[...] = jnp.zeros_like(star_acc)
     for copy in copies[:3]:
@@ -193,9 +235,9 @@
 
     @pl.loop(0, value_ref.shape[0] // GROUP)
     def _(group):
-        first = pl.multiple_of(group * GROUP, GROUP)
-        values = value_ref[pl.ds(first, GROUP), :]
-        scatter(first, values * live_mask(live_ref, first, values.shape), observed, knot_acc, star_acc)
+        values = value_ref[group_rows(group), :]
+        values = values * live_mask(live_ref, group * GROUP, values.shape)
+        scatter(group, values, factors, coefs, knot_acc, star_acc)
 
     scatter_end(place_ref, [], knot_acc, star_acc, table_out, star_out)
 
@@ -230,7 +272,7 @@
     return picked(edges, 0), picked(edges, 1)
 
 
-def star_forward_kernel(star_ref, star_coef_ref, star_x_ref, image_ref, star_parts_ref):
+def star_forward_kernel(star_ref, star_coef_ref, star_hot_ref, star_x_ref, image_ref, star_parts_ref):
     star_x = star_x_ref[...]
     star_high, star_low = two_parts(star_x)
     star_parts_ref[:STAR_ROWS] = star_high
@@ -240,11 +282,10 @@
     def _(group):
         rows = pl.ds(pl.multiple_of(group * GROUP, GROUP), GROUP)
         star = star_ref[rows, :]
-        coarse, fine = star & (COARSE - 1), star >> 8
+        fine = star >> 8
         coef = [star_coef_ref[comp, rows, :] for comp in range(5)]
         tiles = [slice(tile, tile + 1) for tile in range(GROUP)]
-        hot = jnp.concatenate([one_hot(coarse[here], COARSE) for here in tiles], axis=1)
-        found = product(star_parts_ref[...], hot, ((1,), (0,)))
+        found = product(star_parts_ref[...], star_hot_ref[group], ((1,), (0,)))
         width = star.shape[1]
         fine_rows, _ = rows_and_columns((FINE, width))
         image_rows = []
@@ -315,19 +356,15 @@
     cal_ref[...] = (rows[:, :128] + rows[:, 128:]) * cal_coef_ref[...] + star_image_ref[...]
 
 
-def gather(first, live_ref, observed, knot_parts_ref, cal_ref):
-    knot_ref, frac_ref, att_coef_ref = observed
-    rows = pl.ds(first, GROUP)
-    knot = knot_ref[rows, :]
-    coarse, fine = knot >> 5, knot & (FINE - 1)
-    weights = spline_weights(frac_ref[rows, :])
+def gather(group, live_ref, factors, att_coef_ref, knot_parts_ref, cal_ref):
+    rows = group_rows(group)
     coef = [att_coef_ref[comp, rows, :] for comp in range(4)]
-    tiles = [slice(tile, tile + 1) for tile in range(GROUP)]
-    hot = jnp.concatenate([one_hot(coarse[here], COARSE) for here in tiles], axis=1)
-    found = product(knot_parts_ref[...], hot, ((1,), (0,)))
-    width = knot.shape[1]
+    columns = factors.columns(group)
+    found = product(knot_parts_ref[...], factors.refs[1][group], ((1,), (0,)))
+    width = cal_ref.shape[1]
     image_rows = []
-    for tile, here in enumerate(tiles):
+    for tile in range(GROUP):
+        here = slice(tile, tile + 1)
         across = slice(tile * width, (tile + 1) * width)
 
         def part(begin, size):
@@ -336,13 +373,13 @@
                 + found[KNOT_HALF + begin : KNOT_HALF + begin + size, across]
             )
 
-        near, past = near_and_past(weights, fine, tile)
+        near, past = columns[tile]
         near = near * sum(coef[comp][here] * part(comp * FINE, FINE) for comp in range(4))
         past = past * past_terms(coef, here) * part(KNOT_ROWS, PAST_ROWS)
         both = near[:8] + near[8:16] + near[16:24] + near[24:] + past[:8] + past[8:]
         image_rows.append(jnp.sum(both, axis=0, keepdims=True))
     image = jnp.concatenate(image_rows, axis=0) + cal_ref[rows, :]
-    return image * live_mask(live_ref, first, image.shape)
+    return image * live_mask(live_ref, group * GROUP, image.shape)
 
 
 def squares(array):
@@ -350,8 +387,8 @@
 
 
 def middle_kernel(
-    n_stars, n_seg, live_ref, place_ref, knot_ref, frac_ref, att_coef_ref, star_ref, star_coef_ref,
-    cal_coef_ref, tile_cal_ref, star_image_ref, star_x_ref, block_ref, image_ref, table_out, scatter_out,
+    n_stars, n_seg, live_ref, place_ref, column_ref, knot_hot_ref, star_hot_ref, att_coef_ref, star_ref,
+    star_coef_ref, cal_coef_ref, tile_cal_ref, star_image_ref, star_x_ref, block_ref, image_ref, table_out, scatter_out,
     star_out, knot_parts_ref, cal_ref, knot_acc, star_acc,
 ):
     table, ahead, _ = received_table(n_stars, n_seg, place_ref, block_ref)
@@ -360,31 +397,28 @@
     gather_ready(table, ahead, cal_coef_ref, tile_cal_ref, star_image_ref, knot_parts_ref, cal_ref)
     knot_acc[...] = jnp.zeros_like(knot_acc)
     star_acc[...] = jnp.zeros_like(star_acc)
-    observed = (knot_ref, frac_ref, att_coef_ref)
-    every = (knot_ref, frac_ref, att_coef_ref, star_ref, star_coef_ref)
-    groups = knot_ref.shape[0] // GROUP
-    image = gather(0, live_ref, observed, knot_parts_ref, cal_ref)
+    factors = Stored(column_ref, knot_hot_ref, star_hot_ref)
+    coefs = (att_coef_ref, star_ref, star_coef_ref)
+    groups = star_ref.shape[0] // GROUP
+    image = gather(0, live_ref, factors, att_coef_ref, knot_parts_ref, cal_ref)
     image_ref[:GROUP, :] = image
 
     def one_group(group, total):
-        first = pl.multiple_of(group * GROUP, GROUP)
-        following = pl.multiple_of(first + GROUP, GROUP)
-        values = image_ref[pl.ds(first, GROUP), :]
-        image = gather(following, live_ref, observed, knot_parts_ref, cal_ref)
-        scatter(first, values, every, knot_acc, star_acc)
-        image_ref[pl.ds(following, GROUP), :] = image
+        values = image_ref[group_rows(group), :]
+        image = gather(group + 1, live_ref, factors, att_coef_ref, knot_parts_ref, cal_ref)
+        scatter(group, values, factors, coefs, knot_acc, star_acc)
+        image_ref[group_rows(group + 1), :] = image
         return total + image * image
 
     total = lax.fori_loop(0, groups - 1, one_group, image * image)
-    first = (groups - 1) * GROUP
-    scatter(first, image_ref[first:, :], every, knot_acc, star_acc)
+    scatter(groups - 1, image_ref[group_rows(groups - 1), :], factors, coefs, knot_acc, star_acc)
     scatter_calibration(image_ref[...] * cal_coef_ref[...], tile_cal_ref, scatter_out)
     scalars = [(0, norm), (1, jnp.sum(total, keepdims=True))]
     scatter_end(place_ref, scalars, knot_acc, star_acc, scatter_out, star_out)
 
 
 def last_kernel(
-    n_stars, n_seg, live_ref, place_ref, knot_ref, frac_ref, att_coef_ref, cal_coef_ref, tile_cal_ref,
+    n_stars, n_seg, live_ref, place_ref, column_ref, knot_hot_ref, att_coef_ref, cal_coef_ref, tile_cal_ref,
     star_image_ref, star_x_ref, block_ref, star_0_ref, table_0_ref, image_0_ref, image_ref, table_out,
     scalar_out, own_scalar_out, knot_parts_ref, cal_ref,
 ):
@@ -398,17 +432,18 @@
     )
     gather_ready(table, ahead, cal_coef_ref, tile_cal_ref, star_image_ref, knot_parts_ref, cal_ref)
 
+    factors = Stored(column_ref, knot_hot_ref, None)
+
     def one_group(group, sums):
-        first = pl.multiple_of(group * GROUP, GROUP)
-        rows = pl.ds(first, GROUP)
+        rows = group_rows(group)
         image_0 = image_0_ref[rows, :]
-        image = gather(first, live_ref, (knot_ref, frac_ref, att_coef_ref), knot_parts_ref, cal_ref)
+        image = gather(group, live_ref, factors, att_coef_ref, knot_parts_ref, cal_ref)
         image = image_0 - step * image
         image_ref[rows, :] = image
         return sums[0] + image * image, sums[1] + image * image_0
 
-    zero = jnp.zeros((GROUP, knot_ref.shape[1]), F32)
-    sums = lax.fori_loop(0, knot_ref.shape[0] // GROUP, one_group, (zero, zero))
+    zero = jnp.zeros((GROUP, image_ref.shape[1]), F32)
+    sums = lax.fori_loop(0, image_ref.shape[0] // GROUP, one_group, (zero, zero))
     scalars = [norm] + [jnp.sum(part, keepdims=True) for part in sums] + [norm_0, square_0]
     scalars = with_scalars(jnp.zeros((8, 128), F32), list(enumerate(scalars)))
     own_scalar_out[...] = scalars
@@ -458,7 +493,7 @@
 
 
 ARRIVE_PARAMS = pltpu.CompilerParams(vmem_limit_bytes=60 * 1024 * 1024)
-PARAMS = pltpu.CompilerParams(vmem_limit_bytes=40 * 1024 * 1024)
+PARAMS = pltpu.CompilerParams(vmem_limit_bytes=32 * 1024 * 1024)
 PASS_COST = pl.CostEstimate(flops=3_000_000_000, bytes_accessed=1_000_000, transcendentals=0)
 SMALL_COST = pl.CostEstimate(flops=1_000_000, bytes_accessed=600_000, transcendentals=0)
 
@@ -491,8 +526,21 @@
             name="first_scatter",
         )(live_tiles, place, *observed)
 
+    def factors(after):
+        groups = tile_count // GROUP
+        hot_shape = jax.ShapeDtypeStruct((groups, COARSE, GROUP * width), BF16)
+        return pl.pallas_call(
+            factor_kernel,
+            out_shape=(shaped(tile_count, FINE + PAST_ROWS, width), hot_shape, hot_shape),
+            in_specs=in_vmem(3) + [pl.BlockSpec(memory_space=pl.ANY)],
+            out_specs=tuple(in_vmem(3)),
+            compiler_params=PARAMS,
+            cost_estimate=PASS_COST,
+            name="factors",
+        )(obs_knot, obs_frac, obs_star, after)
+
     def middle(*received):
-        observed = (obs_knot, obs_frac, att_coef, obs_star, star_coef, cal_coef, tile_row)
+        observed = (*made, att_coef, obs_star, star_coef, cal_coef, tile_row)
         return pl.pallas_call(
             functools.partial(middle_kernel, n_stars, n_seg),
             out_shape=(image_shape, table_shape, *sent_shapes),
@@ -505,7 +553,7 @@
         )(live_tiles, place, *observed, *received)
 
     def last_gather(*received):
-        observed = (obs_knot, obs_frac, att_coef, cal_coef, tile_row)
+        observed = (*made[:2], att_coef, cal_coef, tile_row)
         return pl.pallas_call(
             functools.partial(last_kernel, n_stars, n_seg),
             out_shape=(image_shape, table_shape, shaped(n_stars * n_seg, 8, 128), shaped(8, 128)),
@@ -521,13 +569,13 @@
         return pl.pallas_call(
             star_forward_kernel,
             out_shape=image_shape,
-            in_specs=in_vmem(3),
+            in_specs=in_vmem(4),
             out_specs=in_vmem(1)[0],
             scratch_shapes=[pltpu.VMEM((2 * STAR_ROWS, COARSE), BF16)],
             compiler_params=PARAMS,
             cost_estimate=PASS_COST,
             name="star_forward",
-        )(obs_star, star_coef, star)
+        )(obs_star, star_coef, made[2], star)
 
     def swap(blocks, axes):
         return lax.all_to_all(blocks, axes, 0, 0)
@@ -550,7 +598,9 @@
         )(swap(table, "stars"), star, partner(star, "seg", distances[-1]))
         return star_forward(star), star, swap(blocks, "stars")
 
-    first = reduced(*first_scatter())
+    sent = first_scatter()
+    made = factors(sent[1])
+    first = reduced(*sent)
     star_0 = first[1]
     image_0, table_0, *sent = middle(*first)
     second = reduced(*sent)

time: 99.4 us -> 147 us (1.48); the launches traced: 98.8 us -> 145 us
  local copies, waits for them, and re-layouts: 1.08 us -> 50.8 us
  waiting for transfers between devices: 30.8 us -> 16.8 us
  starting transfers between devices: 28.5 us -> 34.5 us
  Pallas kernels: 36.9 us -> 39.4 us
  other arithmetic: 0.05 us -> 1.89 us
    unnamed x18 -> x86, local copies, waits for them, and re-layouts: 0.05 us -> 47 us
    all_to_all x5, waiting for transfers between devices: 18.2 us -> 4.42 us  [swap(): return lax.all_to_all(blocks, axes, 0, 0)]
    all_to_all x5, starting transfers between devices: 25.2 us -> 31.3 us  [swap(): return lax.all_to_all(blocks, axes, 0, 0)]
    pallas_call x0 -> x1, Pallas kernels: none -> 2.96 us  [factors(): pl.pallas_call(factor_kernel, out_shape=(shaped(tile_count, FINE + PAST_R...]
    add x2, other arithmetic: 0.05 us -> 1.89 us  [reduced(): star = star + partner(star, 'seg', distance)]
    reshape x2, local copies, waits for them, and re-layouts: 0.1 us -> 1.93 us  [star_order(): return star.reshape(5, STAR_DEV)]
  transfers between devices with their start and end apart: 9 -> 9, of which waited for: 9 -> 5; matrix products, arithmetic and copies ran while one was open for 1% -> 4% of each run, Pallas kernels for 9% -> 8%
where the time goes in v11:
time: 147 us; the launch traced here: 145 us
  local copies, waits for them, and re-layouts  50.8 us (35%)
  Pallas kernels  39.4 us (27%)
  starting transfers between devices  34.5 us (23%)
  waiting for transfers between devices  16.8 us (11%)
  other arithmetic  1.89 us (1%)
  between operations  1.55 us (1%)
    unnamed x86, local copies, waits for them, and re-layouts  47 us
    all_to_all x5, starting transfers between devices, swap(): return lax.all_to_all(blocks, axes, 0, 0)  31.3 us
    ppermute x4, waiting for transfers between devices, partner(): lax.ppermute(array, axis, [(i, i ^ distance) for i in range(lax.axis_size...  12.3 us
    pallas_call x1, Pallas kernels, middle(): pl.pallas_call(functools.partial(middle_kernel, n_stars, n_seg), out_shap...  10.6 us
    pallas_call x1, Pallas kernels, first_scatter(): pl.pallas_call(first_kernel, out_shape=sent_shapes, in_specs=in_smem(2) +...  9.25 us
    pallas_call x2, Pallas kernels, star_forward(): pl.pallas_call(star_forward_kernel, out_shape=image_shape, in_specs=in_vm...  8.45 us
    pallas_call x1, Pallas kernels, last_gather(): pl.pallas_call(functools.partial(last_kernel, n_stars, n_seg), out_shape=...  5.39 us
    all_to_all x5, waiting for transfers between devices, swap(): return lax.all_to_all(blocks, axes, 0, 0)  4.42 us
  transfers between devices with their start and end apart: 9, of which 5 were waited for; matrix products, arithmetic and copies ran while one was open for 4% of the time, Pallas kernels for 8%

profile of v11, /device:TPU:0, one launch (start us, length us, event | category | flops | bytes accessed | tf_op | source)
XLA Modules:
  0.0 144.8 jit_solution(9278745943897658239)
XLA Ops:
  1.3 9.2 %first_scatter.1 = (f32[8,32,256]{2,1,0:T(8,128)}, f32[168,256]{1,0:T(8,128)}) custom-call(s32[1]{0:T(128)S(6)} %copy.17.live_ref, s32[1]{0:T(128)} %bitcast.place_ref, f32[128,128]{1,0:T(8,128)} %value_ref.1, f32[128,128]{1,0:T(8,128)} %cal_coef_ref.3, s32[1,128]{1,0:T(1,128)} %bitcast.6, s32[128,128]{1,0:T(8,128)} %knot_ref.1, f32[128,128]{1,0:T(8,128)} %frac_ref.1, ...), custom_call_target="tpu_custom_call" | custom-call | flops 3000000000 | bytes 1000000 | tf_op jit(solution)/shard_map/first_scatter/pallas_call | solution.py:518
  10.6 7.3 %all-to-all-start = ((f32[8,32,256]{2,1,0:T(8,128)}), f32[8,32,256]{2,1,0:T(8,128)S(1)}, u32[]{:S(2)}, u32[]{:S(2)}) async-start(f32[8,32,256]{2,1,0:T(8,128)} %get-tuple-element.25), calls=%async_computation | async-start | bytes 524288 | tf_op jit(solution)/shard_map/all_to_all | solution.py:581
  17.8 1.6 %collective-permute-done = f32[168,256]{1,0:T(8,128)S(1)} collective-permute-done((f32[168,256]{1,0:T(8,128)}, f32[168,256]{1,0:T(8,128)S(1)}, u32[]{:S(2)}, u32[]{:S(2)}) %collective-permute-start) | collective-permute-done | bytes 172064 | tf_op jit(solution)/shard_map/ppermute | solution.py:584
  20.4 1.6 %collective-permute-start.1 = (f32[168,256]{1,0:T(8,128)S(1)}, f32[168,256]{1,0:T(8,128)S(1)}, u32[]{:S(2)}, u32[]{:S(2)}) collective-permute-start(f32[168,256]{1,0:T(8,128)S(1)} %add.6.own_ref), channel_id=1, source_target_pairs={{0,2},{1,3},{2,0},{3,1},{4,6},{5,7},{6,4},{7,5},{8,10},{9,11},{10,... | collective-permute-start | bytes 516104 | tf_op jit(solution)/shard_map/ppermute | solution.py:584
  22.0 4.9 %collective-permute-done.1.other_ref = f32[168,256]{1,0:T(8,128)S(1)} collective-permute-done((f32[168,256]{1,0:T(8,128)S(1)}, f32[168,256]{1,0:T(8,128)S(1)}, u32[]{:S(2)}, u32[]{:S(2)}) %collective-permute-start.1) | collective-permute-done | bytes 172064 | tf_op jit(solution)/shard_map/ppermute | solution.py:584
  28.3 6.0 %all-to-all-start.1 = ((f32[8,72,128]{2,1,0:T(8,128)}), f32[8,72,128]{2,1,0:T(8,128)}, u32[]{:S(2)}, u32[]{:S(2)}) async-start(f32[8,72,128]{2,1,0:T(8,128)} %get-tuple-element.27), calls=%async_computation.1 | async-start | bytes 589824 | tf_op jit(solution)/shard_map/all_to_all | solution.py:581
  36.9 3.0 %factors.1 = (f32[128,48,128]{2,1,0:T(8,128)S(1)}, bf16[8,256,2048]{2,1,0:T(8,128)(2,1)S(1)}, bf16[8,256,2048]{2,1,0:T(8,128)(2,1)S(1)}) custom-call(s32[128,128]{1,0:T(8,128)S(1)} %copy-done.41, f32[128,128]{1,0:T(8,128)S(1)} %copy-done.42, s32[128,128]{1,0:T(8,128)S(1)} %copy-done.30, f32[168,256]{1,0:T(8,128)S(1)} %copy-done.25), custom_call_target="tpu_custom_call" | custom-call | flops 3000000000 | bytes 1000000 | tf_op jit(solution)/shard_map/factors/pallas_call | solution.py:532
  39.9 3.3 %copy-done = bf16[8,256,2048]{2,1,0:T(8,128)(2,1)} copy-done((bf16[8,256,2048]{2,1,0:T(8,128)(2,1)}, bf16[8,256,2048]{2,1,0:T(8,128)(2,1)S(1)}, u32[]{:S(2)}) %copy-start) | copy-done | bytes 8388632
  44.2 4.2 %star_forward.2.star_image_ref = f32[128,128]{1,0:T(8,128)S(1)} custom-call(s32[128,128]{1,0:T(8,128)S(1)} %copy-done.30, f32[5,128,128]{2,1,0:T(8,128)S(1)} %copy-done.19, bf16[8,256,2048]{2,1,0:T(8,128)(2,1)S(1)} %get-tuple-element.24.star_hot_ref, f32[160,256]{1,0:T(8,128)S(1)} %copy-done.7), custom_call_target="tpu_custom_call" | custom-call | flops 3000000000 | bytes 1000000 | tf_op jit(solution)/shard_map/star_forward/pallas_call | solution.py:569
  48.4 3.3 %copy-done.3 = bf16[8,256,2048]{2,1,0:T(8,128)(2,1)} copy-done((bf16[8,256,2048]{2,1,0:T(8,128)(2,1)}, bf16[8,256,2048]{2,1,0:T(8,128)(2,1)S(1)}, u32[]{:S(2)}) %copy-start.3) | copy-done | bytes 8388632
  52.4 3.4 %copy-done.1 = bf16[8,256,2048]{2,1,0:T(8,128)(2,1)S(1)} copy-done((bf16[8,256,2048]{2,1,0:T(8,128)(2,1)S(1)}, bf16[8,256,2048]{2,1,0:T(8,128)(2,1)}, u32[]{:S(2)}) %copy-start.1) | copy-done | bytes 8388632
  55.7 3.4 %copy-done.4 = bf16[8,256,2048]{2,1,0:T(8,128)(2,1)S(1)} copy-done((bf16[8,256,2048]{2,1,0:T(8,128)(2,1)S(1)}, bf16[8,256,2048]{2,1,0:T(8,128)(2,1)}, u32[]{:S(2)}) %copy-start.4) | copy-done | bytes 8388632
  63.6 10.6 %gather_and_scatter.1 = (f32[128,128]{1,0:T(8,128)S(1)}, f32[256,256]{1,0:T(8,128)S(1)}, f32[8,32,256]{2,1,0:T(8,128)S(1)}, f32[168,256]{1,0:T(8,128)S(1)}) custom-call(s32[1]{0:T(128)S(6)} %copy.17.live_ref, s32[1]{0:T(128)} %bitcast.place_ref, f32[128,48,128]{2,1,0:T(8,128)S(1)} %get-tuple-element.22.column_ref, bf16[8,256,2048]{2,1,0:T(8,128)(2,1)S(1)} %copy-done.1, ...), custom_call_target="tpu_custom_call" | custom-call | flops 3000000000 | bytes 1000000 | tf_op jit(solution)/shard_map/gather_and_scatter/pallas_call | solution.py:544
  75.6 6.0 %all-to-all-start.2 = ((f32[8,32,256]{2,1,0:T(8,128)}), f32[8,32,256]{2,1,0:T(8,128)}, u32[]{:S(2)}, u32[]{:S(2)}) async-start(f32[8,32,256]{2,1,0:T(8,128)} %copy-done.24), calls=%async_computation.2 | async-start | bytes 524288 | tf_op jit(solution)/shard_map/all_to_all | solution.py:581
  81.6 1.6 %collective-permute-done.2 = f32[168,256]{1,0:T(8,128)S(1)} collective-permute-done((f32[168,256]{1,0:T(8,128)}, f32[168,256]{1,0:T(8,128)S(1)}, u32[]{:S(2)}, u32[]{:S(2)}) %collective-permute-start.2) | collective-permute-done | bytes 172064 | tf_op jit(solution)/shard_map/ppermute | solution.py:584
  84.2 1.6 %collective-permute-start.3 = (f32[168,256]{1,0:T(8,128)S(1)}, f32[168,256]{1,0:T(8,128)S(1)}, u32[]{:S(2)}, u32[]{:S(2)}) collective-permute-start(f32[168,256]{1,0:T(8,128)S(1)} %add.7.own_ref), channel_id=1, source_target_pairs={{0,2},{1,3},{2,0},{3,1},{4,6},{5,7},{6,4},{7,5},{8,10},{9,11},{10,... | collective-permute-start | bytes 516104 | tf_op jit(solution)/shard_map/ppermute | solution.py:584
  86.4 4.2 %collective-permute-done.3.other_ref = f32[168,256]{1,0:T(8,128)S(1)} collective-permute-done((f32[168,256]{1,0:T(8,128)S(1)}, f32[168,256]{1,0:T(8,128)S(1)}, u32[]{:S(2)}, u32[]{:S(2)}) %collective-permute-start.3) | collective-permute-done | bytes 172064 | tf_op jit(solution)/shard_map/ppermute | solution.py:584
  95.5 6.0 %all-to-all-start.3 = ((f32[8,72,128]{2,1,0:T(8,128)}), f32[8,72,128]{2,1,0:T(8,128)}, u32[]{:S(2)}, u32[]{:S(2)}) async-start(f32[8,72,128]{2,1,0:T(8,128)} %copy-done.22), calls=%async_computation.3 | async-start | bytes 589824 | tf_op jit(solution)/shard_map/all_to_all | solution.py:581
  101.5 3.4 %copy-done.5 = bf16[8,256,2048]{2,1,0:T(8,128)(2,1)S(1)} copy-done((bf16[8,256,2048]{2,1,0:T(8,128)(2,1)S(1)}, bf16[8,256,2048]{2,1,0:T(8,128)(2,1)}, u32[]{:S(2)}) %copy-start.5) | copy-done | bytes 8388632
  107.6 4.2 %star_forward.3.star_image_ref = f32[128,128]{1,0:T(8,128)S(1)} custom-call(s32[128,128]{1,0:T(8,128)S(1)} %copy-done.32, f32[5,128,128]{2,1,0:T(8,128)S(1)} %copy-done.21, bf16[8,256,2048]{2,1,0:T(8,128)(2,1)S(1)} %copy-done.5, f32[160,256]{1,0:T(8,128)S(1)} %copy-done.15), custom_call_target="tpu_custom_call" | custom-call | flops 3000000000 | bytes 1000000 | tf_op jit(solution)/shard_map/star_forward/pallas_call | solution.py:569
  112.5 3.4 %copy-done.2 = bf16[8,256,2048]{2,1,0:T(8,128)(2,1)S(1)} copy-done((bf16[8,256,2048]{2,1,0:T(8,128)(2,1)S(1)}, bf16[8,256,2048]{2,1,0:T(8,128)(2,1)}, u32[]{:S(2)}) %copy-start.2) | copy-done | bytes 8388632
  119.5 5.4 %last_gather.1 = (f32[128,128]{1,0:T(8,128)S(1)}, f32[256,256]{1,0:T(8,128)S(1)}, f32[32,8,128]{2,1,0:T(8,128)S(1)}, f32[8,128]{1,0:T(8,128)S(1)}) custom-call(s32[1]{0:T(128)S(6)} %copy.17.live_ref, s32[1]{0:T(128)} %bitcast.place_ref, f32[128,48,128]{2,1,0:T(8,128)S(1)} %get-tuple-element.22.column_ref, bf16[8,256,2048]{2,1,0:T(8,128)(2,1)S(1)} %copy-done.2, ...), custom_call_target="tpu_custom_call" | custom-call | flops 3000000000 | bytes 1000000 | tf_op jit(solution)/shard_map/last_gather/pallas_call | solution.py:557
  126.9 6.0 %all-to-all-start.4 = ((f32[32,8,128]{2,1,0:T(8,128)}), f32[32,8,128]{2,1,0:T(8,128)S(1)}, u32[]{:S(2)}, u32[]{:S(2)}) async-start(f32[32,8,128]{2,1,0:T(8,128)} %copy-done.29), calls=%async_computation.4 | async-start | bytes 262144 | tf_op jit(solution)/shard_map/all_to_all | solution.py:581
  136.8 4.4 %all-to-all-done.4.scalar_ref = f32[32,8,128]{2,1,0:T(8,128)S(1)} async-done(((f32[32,8,128]{2,1,0:T(8,128)}), f32[32,8,128]{2,1,0:T(8,128)S(1)}, u32[]{:S(2)}, u32[]{:S(2)}) %all-to-all-start.4) | async-done | bytes 131104 | tf_op jit(solution)/shard_map/all_to_all | solution.py:581
  (99 shorter events, 35.4 us)
Async XLA Ops:
  0.6 33.7 %copy-start.42 = (f32[128,128]{1,0:T(8,128)S(1)}, f32[128,128]{1,0:T(8,128)}, u32[]{:S(2)}) copy-start(f32[128,128]{1,0:T(8,128)} %frac_ref.1) | copy-start | bytes 196612
  10.6 16.3 %all-to-all-start = ((f32[8,32,256]{2,1,0:T(8,128)}), f32[8,32,256]{2,1,0:T(8,128)S(1)}, u32[]{:S(2)}, u32[]{:S(2)}) async-start(f32[8,32,256]{2,1,0:T(8,128)} %get-tuple-element.25), calls=%async_computation | async-start | bytes 524288 | tf_op jit(solution)/shard_map/all_to_all | solution.py:581
  17.8 1.6 %collective-permute-start = (f32[168,256]{1,0:T(8,128)}, f32[168,256]{1,0:T(8,128)S(1)}, u32[]{:S(2)}, u32[]{:S(2)}) collective-permute-start(f32[168,256]{1,0:T(8,128)} %get-tuple-element.21.after_ref), channel_id=1, source_target_pairs={{0,1},{1,0},{2,3},{3,2},{4,5},{5,4},{6,7},{7,6},{8,9},{9,8},{10,11... | collective-permute-start | bytes 516104 | tf_op jit(solution)/shard_map/ppermute | solution.py:584
  20.4 6.5 %collective-permute-start.1 = (f32[168,256]{1,0:T(8,128)S(1)}, f32[168,256]{1,0:T(8,128)S(1)}, u32[]{:S(2)}, u32[]{:S(2)}) collective-permute-start(f32[168,256]{1,0:T(8,128)S(1)} %add.6.own_ref), channel_id=1, source_target_pairs={{0,2},{1,3},{2,0},{3,1},{4,6},{5,7},{6,4},{7,5},{8,10},{9,11},{10,... | collective-permute-start | bytes 516104 | tf_op jit(solution)/shard_map/ppermute | solution.py:584
  28.3 24.0 %all-to-all-start.1 = ((f32[8,72,128]{2,1,0:T(8,128)}), f32[8,72,128]{2,1,0:T(8,128)}, u32[]{:S(2)}, u32[]{:S(2)}) async-start(f32[8,72,128]{2,1,0:T(8,128)} %get-tuple-element.27), calls=%async_computation.1 | async-start | bytes 589824 | tf_op jit(solution)/shard_map/all_to_all | solution.py:581
  36.9 6.3 %copy-start.7 = (f32[160,256]{1,0:T(8,128)S(1)}, f32[160,256]{1,0:T(8,128)}, u32[]{:S(2)}) copy-start(f32[160,256]{1,0:T(8,128)} %copy-done.6) | copy-start | bytes 491524
  36.9 15.4 %copy-start.23 = (f32[128,128]{1,0:T(8,128)S(1)}, f32[128,128]{1,0:T(8,128)}, u32[]{:S(2)}) copy-start(f32[128,128]{1,0:T(8,128)} %cal_coef_ref.3) | copy-start | bytes 196612
  36.9 15.4 %copy-start.40 = (s32[128]{0:T(128)S(1)}, s32[128]{0:T(128)}, u32[]{:S(2)}) copy-start(s32[128]{0:T(128)} %param.15) | copy-start | bytes 1540
  39.9 3.3 %copy-start = (bf16[8,256,2048]{2,1,0:T(8,128)(2,1)}, bf16[8,256,2048]{2,1,0:T(8,128)(2,1)S(1)}, u32[]{:S(2)}) copy-start(bf16[8,256,2048]{2,1,0:T(8,128)(2,1)S(1)} %get-tuple-element.23.knot_hot_ref) | copy-start | bytes 25165828
  43.2 1.0 copy-start.19
  48.4 3.3 %copy-start.3 = (bf16[8,256,2048]{2,1,0:T(8,128)(2,1)}, bf16[8,256,2048]{2,1,0:T(8,128)(2,1)S(1)}, u32[]{:S(2)}) copy-start(bf16[8,256,2048]{2,1,0:T(8,128)(2,1)S(1)} %get-tuple-element.24.star_hot_ref) | copy-start | bytes 25165828
  52.3 3.4 %copy-start.1 = (bf16[8,256,2048]{2,1,0:T(8,128)(2,1)S(1)}, bf16[8,256,2048]{2,1,0:T(8,128)(2,1)}, u32[]{:S(2)}) copy-start(bf16[8,256,2048]{2,1,0:T(8,128)(2,1)} %copy-done) | copy-start | bytes 25165828
  55.7 3.4 %copy-start.4 = (bf16[8,256,2048]{2,1,0:T(8,128)(2,1)S(1)}, bf16[8,256,2048]{2,1,0:T(8,128)(2,1)}, u32[]{:S(2)}) copy-start(bf16[8,256,2048]{2,1,0:T(8,128)(2,1)} %copy-done.3) | copy-start | bytes 25165828
  60.0 0.9 copy-start.10
  61.0 1.0 copy-start.20
  75.6 15.7 %all-to-all-start.2 = ((f32[8,32,256]{2,1,0:T(8,128)}), f32[8,32,256]{2,1,0:T(8,128)}, u32[]{:S(2)}, u32[]{:S(2)}) async-start(f32[8,32,256]{2,1,0:T(8,128)} %copy-done.24), calls=%async_computation.2 | async-start | bytes 524288 | tf_op jit(solution)/shard_map/all_to_all | solution.py:581
  81.6 1.6 %collective-permute-start.2 = (f32[168,256]{1,0:T(8,128)}, f32[168,256]{1,0:T(8,128)S(1)}, u32[]{:S(2)}, u32[]{:S(2)}) collective-permute-start(f32[168,256]{1,0:T(8,128)} %copy-done.26), channel_id=1, source_target_pairs={{0,1},{1,0},{2,3},{3,2},{4,5},{5,4},{6,7},{7,6},{8,9},{9,8},{10,11... | collective-permute-start | bytes 516104 | tf_op jit(solution)/shard_map/ppermute | solution.py:584
  84.2 6.5 %collective-permute-start.3 = (f32[168,256]{1,0:T(8,128)S(1)}, f32[168,256]{1,0:T(8,128)S(1)}, u32[]{:S(2)}, u32[]{:S(2)}) collective-permute-start(f32[168,256]{1,0:T(8,128)S(1)} %add.7.own_ref), channel_id=1, source_target_pairs={{0,2},{1,3},{2,0},{3,1},{4,6},{5,7},{6,4},{7,5},{8,10},{9,11},{10,... | collective-permute-start | bytes 516104 | tf_op jit(solution)/shard_map/ppermute | solution.py:584
  95.5 17.0 %all-to-all-start.3 = ((f32[8,72,128]{2,1,0:T(8,128)}), f32[8,72,128]{2,1,0:T(8,128)}, u32[]{:S(2)}, u32[]{:S(2)}) async-start(f32[8,72,128]{2,1,0:T(8,128)} %copy-done.22), calls=%async_computation.3 | async-start | bytes 589824 | tf_op jit(solution)/shard_map/all_to_all | solution.py:581
  101.5 3.4 %copy-start.5 = (bf16[8,256,2048]{2,1,0:T(8,128)(2,1)S(1)}, bf16[8,256,2048]{2,1,0:T(8,128)(2,1)}, u32[]{:S(2)}) copy-start(bf16[8,256,2048]{2,1,0:T(8,128)(2,1)} %copy-done.3) | copy-start | bytes 25165828
  105.8 1.0 copy-start.21
  112.5 3.4 %copy-start.2 = (bf16[8,256,2048]{2,1,0:T(8,128)(2,1)S(1)}, bf16[8,256,2048]{2,1,0:T(8,128)(2,1)}, u32[]{:S(2)}) copy-start(bf16[8,256,2048]{2,1,0:T(8,128)(2,1)} %copy-done) | copy-start | bytes 25165828
  126.9 14.3 %all-to-all-start.4 = ((f32[32,8,128]{2,1,0:T(8,128)}), f32[32,8,128]{2,1,0:T(8,128)S(1)}, u32[]{:S(2)}, u32[]{:S(2)}) async-start(f32[32,8,128]{2,1,0:T(8,128)} %copy-done.29), calls=%async_computation.4 | async-start | bytes 262144 | tf_op jit(solution)/shard_map/all_to_all | solution.py:581
  141.2 1.0 copy-start.18
  (28 other events, 22.1 us)

commit v12 on v9

--- a/solution.py
+++ b/solution.py
@@ -13,6 +13,7 @@
 FINE = 32
 COARSE = 256
 GROUP = 16
+FIRST_GROUP = 32
 SLOT = 8
 STAR_ROWS = 5 * FINE
 KNOT_ROWS = 4 * FINE
@@ -100,9 +101,9 @@
         out_ref[where // block, where % block : where % block + 8, :] = rows[offset : offset + 8]
 
 
-def scatter(first, values, observed, knot_acc, star_acc):
+def scatter(first, size, values, observed, knot_acc, star_acc):
     knot_ref, frac_ref, att_coef_ref, star_ref, star_coef_ref = observed
-    rows = pl.ds(first, GROUP)
+    rows = pl.ds(first, size)
     knot, star = knot_ref[rows, :], star_ref[rows, :]
     knot_coarse, knot_fine = knot >> 5, knot & (FINE - 1)
     star_coarse, star_fine = star & (COARSE - 1), star >> 8
@@ -111,7 +112,7 @@
     parts = [two_parts(star_coef_ref[comp, rows, :] * values) for comp in range(5)]
     parts = [pair[half].astype(F32) for half in range(2) for pair in parts]
     knot_left, knot_right, star_left, star_right = [], [], [], []
-    for tile in range(GROUP):
+    for tile in range(size):
         here = slice(tile, tile + 1)
         knot_right.append(one_hot(knot_coarse[here], COARSE))
         near, past = near_and_past(weights, knot_fine, tile)
@@ -175,12 +176,19 @@
 def first_kernel(live_ref, place_ref, *refs):
     sources, (table_out, star_out, knot_acc, star_acc) = refs[:8], refs[8:12]
     buffers, sems = refs[12:20], refs[20]
-    copies = [
-        pltpu.make_async_copy(source, target, sems.at[which])
-        for which, (source, target) in enumerate(zip(sources, buffers))
-    ]
-    for copy in copies:
-        copy.start()
+    half = sources[0].shape[0] // 2
+    copies = []
+
+    def begin(source, target, *place):
+        source, target = (source.at[place], target.at[place]) if place else (source, target)
+        copies.append(pltpu.make_async_copy(source, target, sems.at[len(copies)]))
+        copies[-1].start()
+
+    for source, target in zip(sources[:3], buffers):
+        begin(source, target)
+    for rows in (slice(0, half), slice(half, 2 * half)):
+        for source, target in zip(sources[3:], buffers[3:]):
+            begin(source, target, *[slice(None)] * (len(source.shape) - 2), rows)
     value_ref, cal_coef_ref, tile_cal_ref, *observed = buffers
     knot_acc[...] = jnp.zeros_like(knot_acc)
     star_acc[...] = jnp.zeros_like(star_acc)
@@ -188,14 +196,20 @@
         copy.wait()
     values = value_ref[...] * live_mask(live_ref, 0, value_ref.shape)
     scatter_calibration(values * cal_coef_ref[...], tile_cal_ref, table_out)
-    for copy in copies[3:]:
+    for copy in copies[3:8]:
         copy.wait()
 
-    @pl.loop(0, value_ref.shape[0] // GROUP)
+    @pl.loop(0, value_ref.shape[0] // FIRST_GROUP)
     def _(group):
-        first = pl.multiple_of(group * GROUP, GROUP)
-        values = value_ref[pl.ds(first, GROUP), :]
-        scatter(first, values * live_mask(live_ref, first, values.shape), observed, knot_acc, star_acc)
+        @pl.when(group * FIRST_GROUP == half)
+        def _():
+            for copy in copies[8:]:
+                copy.wait()
+
+        first = pl.multiple_of(group * FIRST_GROUP, FIRST_GROUP)
+        values = value_ref[pl.ds(first, FIRST_GROUP), :]
+        values = values * live_mask(live_ref, first, values.shape)
+        scatter(first, FIRST_GROUP, values, observed, knot_acc, star_acc)
 
     scatter_end(place_ref, [], knot_acc, star_acc, table_out, star_out)
 
@@ -371,13 +385,13 @@
         following = pl.multiple_of(first + GROUP, GROUP)
         values = image_ref[pl.ds(first, GROUP), :]
         image = gather(following, live_ref, observed, knot_parts_ref, cal_ref)
-        scatter(first, values, every, knot_acc, star_acc)
+        scatter(first, GROUP, values, every, knot_acc, star_acc)
         image_ref[pl.ds(following, GROUP), :] = image
         return total + image * image
 
     total = lax.fori_loop(0, groups - 1, one_group, image * image)
     first = (groups - 1) * GROUP
-    scatter(first, image_ref[first:, :], every, knot_acc, star_acc)
+    scatter(first, GROUP, image_ref[first:, :], every, knot_acc, star_acc)
     scatter_calibration(image_ref[...] * cal_coef_ref[...], tile_cal_ref, scatter_out)
     scalars = [(0, norm), (1, jnp.sum(total, keepdims=True))]
     scatter_end(place_ref, scalars, knot_acc, star_acc, scatter_out, star_out)
@@ -485,7 +499,7 @@
             out_shape=sent_shapes,
             in_specs=in_smem(2) + in_hbm(len(observed)),
             out_specs=tuple(in_vmem(2)),
-            scratch_shapes=sums + buffers + [pltpu.SemaphoreType.DMA((len(observed),))],
+            scratch_shapes=sums + buffers + [pltpu.SemaphoreType.DMA((13,))],
             compiler_params=ARRIVE_PARAMS,
             cost_estimate=PASS_COST,
             name="first_scatter",

time: 99.4 us -> 98.5 us (level)
  no operation moved by 1% of the time
where the time goes in v12:
time: 98.5 us; the launch traced here: 97.9 us
  Pallas kernels  36 us (37%)
  waiting for transfers between devices  30.8 us (31%)
  starting transfers between devices  28.5 us (29%)
  between operations  1.48 us (2%)
  local copies, waits for them, and re-layouts  1.08 us (1%)
    all_to_all x5, starting transfers between devices, swap(): return lax.all_to_all(blocks, axes, 0, 0)  25.2 us
    all_to_all x5, waiting for transfers between devices, swap(): return lax.all_to_all(blocks, axes, 0, 0)  18.2 us
    ppermute x4, waiting for transfers between devices, partner(): lax.ppermute(array, axis, [(i, i ^ distance) for i in range(lax.axis_size...  12.6 us
    pallas_call x1, Pallas kernels, middle(): pl.pallas_call(functools.partial(middle_kernel, n_stars, n_seg), out_shap...  11.5 us
    pallas_call x2, Pallas kernels, star_forward(): pl.pallas_call(star_forward_kernel, out_shape=image_shape, in_specs=in_vm...  8.5 us
    pallas_call x1, Pallas kernels, first_scatter(): pl.pallas_call(first_kernel, out_shape=sent_shapes, in_specs=in_smem(2) +...  8.36 us
    pallas_call x1, Pallas kernels, last_gather(): pl.pallas_call(functools.partial(last_kernel, n_stars, n_seg), out_shape=...  5.13 us
    ppermute x4, starting transfers between devices, partner(): lax.ppermute(array, axis, [(i, i ^ distance) for i in range(lax.axis_size...  3.24 us
  transfers between devices with their start and end apart: 9, of which 9 were waited for; matrix products, arithmetic and copies ran while one was open for 1% of the time, Pallas kernels for 9%

profile of v12, /device:TPU:0, one launch (start us, length us, event | category | flops | bytes accessed | tf_op | source)
XLA Modules:
  0.0 97.9 jit_solution(12849506027199301780)
XLA Ops:
  1.3 8.4 %first_scatter.1 = (f32[8,32,256]{2,1,0:T(8,128)}, f32[168,256]{1,0:T(8,128)}) custom-call(s32[1]{0:T(128)S(6)} %copy.17.live_ref, s32[1]{0:T(128)} %bitcast.place_ref, f32[128,128]{1,0:T(8,128)} %value_ref.1, f32[128,128]{1,0:T(8,128)} %cal_coef_ref.3, s32[1,128]{1,0:T(1,128)} %bitcast.6, s32[128,128]{1,0:T(8,128)} %knot_ref.3, f32[128,128]{1,0:T(8,128)} %frac_ref.3, ...), custom_call_target="tpu_custom_call" | custom-call | flops 3000000000 | bytes 1000000 | tf_op jit(solution)/shard_map/first_scatter/pallas_call | solution.py:497
  9.7 7.4 %all-to-all-start = ((f32[8,32,256]{2,1,0:T(8,128)}), f32[8,32,256]{2,1,0:T(8,128)S(1)}, u32[]{:S(2)}, u32[]{:S(2)}) async-start(f32[8,32,256]{2,1,0:T(8,128)} %get-tuple-element.18), calls=%async_computation | async-start | bytes 524288 | tf_op jit(solution)/shard_map/all_to_all | solution.py:547
  17.1 1.4 %collective-permute-done = f32[168,256]{1,0:T(8,128)S(1)} collective-permute-done((f32[168,256]{1,0:T(8,128)S(1)}, f32[168,256]{1,0:T(8,128)S(1)}, u32[]{:S(2)}, u32[]{:S(2)}) %collective-permute-start) | collective-permute-done | bytes 172064 | tf_op jit(solution)/shard_map/ppermute | solution.py:550
  18.5 1.6 %collective-permute-start.1 = (f32[168,256]{1,0:T(8,128)S(1)}, f32[168,256]{1,0:T(8,128)S(1)}, u32[]{:S(2)}, u32[]{:S(2)}) collective-permute-start(f32[168,256]{1,0:T(8,128)S(1)} %add.6.own_ref), channel_id=1, source_target_pairs={{0,2},{1,3},{2,0},{3,1},{4,6},{5,7},{6,4},{7,5},{8,10},{9,11},{10,... | collective-permute-start | bytes 516104 | tf_op jit(solution)/shard_map/ppermute | solution.py:550
  20.1 4.9 %collective-permute-done.1.other_ref = f32[168,256]{1,0:T(8,128)S(1)} collective-permute-done((f32[168,256]{1,0:T(8,128)S(1)}, f32[168,256]{1,0:T(8,128)S(1)}, u32[]{:S(2)}, u32[]{:S(2)}) %collective-permute-start.1) | collective-permute-done | bytes 172064 | tf_op jit(solution)/shard_map/ppermute | solution.py:550
  25.0 0.9 all-to-all-done.block_ref
  26.0 0.7 table_sum.2
  26.7 5.1 %all-to-all-start.1 = ((f32[8,72,128]{2,1,0:T(8,128)}), f32[8,72,128]{2,1,0:T(8,128)S(1)}, u32[]{:S(2)}, u32[]{:S(2)}) async-start(f32[8,72,128]{2,1,0:T(8,128)} %get-tuple-element.21), calls=%async_computation.1 | async-start | bytes 589824 | tf_op jit(solution)/shard_map/all_to_all | solution.py:547
  31.9 4.3 %star_forward.2.star_image_ref = f32[128,128]{1,0:T(8,128)S(1)} custom-call(s32[128,128]{1,0:T(8,128)S(1)} %copy-done.3, f32[5,128,128]{2,1,0:T(8,128)S(1)} %copy-done.1, f32[160,256]{1,0:T(8,128)S(1)} %get-tuple-element.20.star_x_ref.star_0_ref), custom_call_target="tpu_custom_call" | custom-call | flops 3000000000 | bytes 1000000 | tf_op jit(solution)/shard_map/star_forward/pallas_call | solution.py:535
  36.2 4.7 %all-to-all-done.1.block_ref = f32[8,72,128]{2,1,0:T(8,128)S(1)} async-done(((f32[8,72,128]{2,1,0:T(8,128)}), f32[8,72,128]{2,1,0:T(8,128)S(1)}, u32[]{:S(2)}, u32[]{:S(2)}) %all-to-all-start.1) | async-done | bytes 294944 | tf_op jit(solution)/shard_map/all_to_all | solution.py:547
  40.9 11.5 %gather_and_scatter.1 = (f32[128,128]{1,0:T(8,128)S(1)}, f32[256,256]{1,0:T(8,128)S(1)}, f32[8,32,256]{2,1,0:T(8,128)}, f32[168,256]{1,0:T(8,128)S(1)}) custom-call(s32[1]{0:T(128)S(6)} %copy.17.live_ref, s32[1]{0:T(128)} %bitcast.place_ref, s32[128,128]{1,0:T(8,128)S(1)} %copy-done.4, f32[128,128]{1,0:T(8,128)S(1)} %copy-done.5, ...), custom_call_target="tpu_custom_call" | custom-call | flops 3000000000 | bytes 1000000 | tf_op jit(solution)/shard_map/gather_and_scatter/pallas_call | solution.py:510
  52.5 3.6 %all-to-all-start.2 = ((f32[8,32,256]{2,1,0:T(8,128)}), f32[8,32,256]{2,1,0:T(8,128)S(1)}, u32[]{:S(2)}, u32[]{:S(2)}) async-start(f32[8,32,256]{2,1,0:T(8,128)} %get-tuple-element.22), calls=%async_computation.2 | async-start | bytes 524288 | tf_op jit(solution)/shard_map/all_to_all | solution.py:547
  56.1 1.4 %collective-permute-done.2 = f32[168,256]{1,0:T(8,128)S(1)} collective-permute-done((f32[168,256]{1,0:T(8,128)S(1)}, f32[168,256]{1,0:T(8,128)S(1)}, u32[]{:S(2)}, u32[]{:S(2)}) %collective-permute-start.2) | collective-permute-done | bytes 172064 | tf_op jit(solution)/shard_map/ppermute | solution.py:550
  57.5 1.6 %collective-permute-start.3 = (f32[168,256]{1,0:T(8,128)S(1)}, f32[168,256]{1,0:T(8,128)S(1)}, u32[]{:S(2)}, u32[]{:S(2)}) collective-permute-start(f32[168,256]{1,0:T(8,128)S(1)} %add.7.own_ref), channel_id=1, source_target_pairs={{0,2},{1,3},{2,0},{3,1},{4,6},{5,7},{6,4},{7,5},{8,10},{9,11},{10,... | collective-permute-start | bytes 516104 | tf_op jit(solution)/shard_map/ppermute | solution.py:550
  59.1 4.9 %collective-permute-done.3.other_ref = f32[168,256]{1,0:T(8,128)S(1)} collective-permute-done((f32[168,256]{1,0:T(8,128)S(1)}, f32[168,256]{1,0:T(8,128)S(1)}, u32[]{:S(2)}, u32[]{:S(2)}) %collective-permute-start.3) | collective-permute-done | bytes 172064 | tf_op jit(solution)/shard_map/ppermute | solution.py:550
  64.0 0.6 all-to-all-done.2.block_ref
  64.6 0.7 table_sum.3
  65.4 5.4 %all-to-all-start.3 = ((f32[8,72,128]{2,1,0:T(8,128)}), f32[8,72,128]{2,1,0:T(8,128)S(1)}, u32[]{:S(2)}, u32[]{:S(2)}) async-start(f32[8,72,128]{2,1,0:T(8,128)} %get-tuple-element.25), calls=%async_computation.3 | async-start | bytes 589824 | tf_op jit(solution)/shard_map/all_to_all | solution.py:547
  70.8 4.2 %star_forward.3.star_image_ref = f32[128,128]{1,0:T(8,128)S(1)} custom-call(s32[128,128]{1,0:T(8,128)S(1)} %copy-done.3, f32[5,128,128]{2,1,0:T(8,128)S(1)} %copy-done.1, f32[160,256]{1,0:T(8,128)S(1)} %get-tuple-element.24.star_x_ref), custom_call_target="tpu_custom_call" | custom-call | flops 3000000000 | bytes 1000000 | tf_op jit(solution)/shard_map/star_forward/pallas_call | solution.py:535
  75.0 4.8 %all-to-all-done.3.block_ref = f32[8,72,128]{2,1,0:T(8,128)S(1)} async-done(((f32[8,72,128]{2,1,0:T(8,128)}), f32[8,72,128]{2,1,0:T(8,128)S(1)}, u32[]{:S(2)}, u32[]{:S(2)}) %all-to-all-start.3) | async-done | bytes 294944 | tf_op jit(solution)/shard_map/all_to_all | solution.py:547
  79.8 5.1 %last_gather.1 = (f32[128,128]{1,0:T(8,128)S(1)}, f32[256,256]{1,0:T(8,128)S(1)}, f32[32,8,128]{2,1,0:T(8,128)}, f32[8,128]{1,0:T(8,128)S(1)}) custom-call(s32[1]{0:T(128)S(6)} %copy.17.live_ref, s32[1]{0:T(128)} %bitcast.place_ref, s32[128,128]{1,0:T(8,128)S(1)} %copy-done.4, f32[128,128]{1,0:T(8,128)S(1)} %copy-done.5, f32[4,128,128]{2,1,0:T(8,128)S(1)} %copy-done.2, ...), custom_call_target="tpu_custom_call" | custom-call | flops 3000000000 | bytes 1000000 | tf_op jit(solution)/shard_map/last_gather/pallas_call | solution.py:523
  85.0 3.7 %all-to-all-start.4 = ((f32[32,8,128]{2,1,0:T(8,128)}), f32[32,8,128]{2,1,0:T(8,128)S(1)}, u32[]{:S(2)}, u32[]{:S(2)}) async-start(f32[32,8,128]{2,1,0:T(8,128)} %get-tuple-element.29), calls=%async_computation.4 | async-start | bytes 262144 | tf_op jit(solution)/shard_map/all_to_all | solution.py:547
  89.7 7.1 %all-to-all-done.4.scalar_ref = f32[32,8,128]{2,1,0:T(8,128)S(1)} async-done(((f32[32,8,128]{2,1,0:T(8,128)}), f32[32,8,128]{2,1,0:T(8,128)S(1)}, u32[]{:S(2)}, u32[]{:S(2)}) %all-to-all-start.4) | async-done | bytes 131104 | tf_op jit(solution)/shard_map/all_to_all | solution.py:547
  96.9 1.0 %outputs.1 = (f32[5,8192]{1,0:T(8,128)}, f32[4,8192]{1,0:T(4,128)}, f32[256,128]{1,0:T(8,128)}, f32[128,128]{1,0:T(8,128)}) custom-call(s32[1]{0:T(128)S(6)} %copy.17.live_ref, f32[8,128]{1,0:T(8,128)S(1)} %get-tuple-element.28.own_scalar_ref, f32[32,8,128]{2,1,0:T(8,128)S(1)} %all-to-all-done.4.scalar_ref, f32[5,8192]{1,0:T(8,128)S(1)} %reshape.26.star_0_ref, ...), custom_call_target="tpu_custom_call" | custom-call | flops 1000000 | bytes 600000 | tf_op jit(solution)/shard_map/outputs/pallas_call | solution.py:581
  (30 shorter events, 1.2 us)
Async XLA Ops:
  9.6 7.4 %copy-start.8 = (f32[168,256]{1,0:T(8,128)S(1)}, f32[168,256]{1,0:T(8,128)}, u32[]{:S(2)}) copy-start(f32[168,256]{1,0:T(8,128)} %get-tuple-element.19) | copy-start | bytes 516100
  9.7 16.3 %all-to-all-start = ((f32[8,32,256]{2,1,0:T(8,128)}), f32[8,32,256]{2,1,0:T(8,128)S(1)}, u32[]{:S(2)}, u32[]{:S(2)}) async-start(f32[8,32,256]{2,1,0:T(8,128)} %get-tuple-element.18), calls=%async_computation | async-start | bytes 524288 | tf_op jit(solution)/shard_map/all_to_all | solution.py:547
  17.0 1.5 %collective-permute-start = (f32[168,256]{1,0:T(8,128)S(1)}, f32[168,256]{1,0:T(8,128)S(1)}, u32[]{:S(2)}, u32[]{:S(2)}) collective-permute-start(f32[168,256]{1,0:T(8,128)S(1)} %copy-done.8), channel_id=1, source_target_pairs={{0,1},{1,0},{2,3},{3,2},{4,5},{5,4},{6,7},{7,6},{8,9},{9,8},{10,11... | collective-permute-start | bytes 516104 | tf_op jit(solution)/shard_map/ppermute | solution.py:550
  18.5 6.5 %collective-permute-start.1 = (f32[168,256]{1,0:T(8,128)S(1)}, f32[168,256]{1,0:T(8,128)S(1)}, u32[]{:S(2)}, u32[]{:S(2)}) collective-permute-start(f32[168,256]{1,0:T(8,128)S(1)} %add.6.own_ref), channel_id=1, source_target_pairs={{0,2},{1,3},{2,0},{3,1},{4,6},{5,7},{6,4},{7,5},{8,10},{9,11},{10,... | collective-permute-start | bytes 516104 | tf_op jit(solution)/shard_map/ppermute | solution.py:550
  26.7 5.1 %copy-start.1 = (f32[5,128,128]{2,1,0:T(8,128)S(1)}, f32[5,128,128]{2,1,0:T(8,128)}, u32[]{:S(2)}) copy-start(f32[5,128,128]{2,1,0:T(8,128)} %star_coef_ref.5) | copy-start | bytes 983044
  26.7 5.2 %copy-start.3 = (s32[128,128]{1,0:T(8,128)S(1)}, s32[128,128]{1,0:T(8,128)}, u32[]{:S(2)}) copy-start(s32[128,128]{1,0:T(8,128)} %star_ref.5) | copy-start | bytes 196612
  26.7 14.2 %all-to-all-start.1 = ((f32[8,72,128]{2,1,0:T(8,128)}), f32[8,72,128]{2,1,0:T(8,128)S(1)}, u32[]{:S(2)}, u32[]{:S(2)}) async-start(f32[8,72,128]{2,1,0:T(8,128)} %get-tuple-element.21), calls=%async_computation.1 | async-start | bytes 589824 | tf_op jit(solution)/shard_map/all_to_all | solution.py:547
  31.9 9.0 %copy-start.2 = (f32[4,128,128]{2,1,0:T(8,128)S(1)}, f32[4,128,128]{2,1,0:T(8,128)}, u32[]{:S(2)}) copy-start(f32[4,128,128]{2,1,0:T(8,128)} %att_coef_ref.3) | copy-start | bytes 786436
  31.9 9.0 %copy-start.4 = (s32[128,128]{1,0:T(8,128)S(1)}, s32[128,128]{1,0:T(8,128)}, u32[]{:S(2)}) copy-start(s32[128,128]{1,0:T(8,128)} %knot_ref.3) | copy-start | bytes 196612
  31.9 9.0 %copy-start.5 = (f32[128,128]{1,0:T(8,128)S(1)}, f32[128,128]{1,0:T(8,128)}, u32[]{:S(2)}) copy-start(f32[128,128]{1,0:T(8,128)} %frac_ref.3) | copy-start | bytes 196612
  31.9 9.0 %copy-start.6 = (f32[128,128]{1,0:T(8,128)S(1)}, f32[128,128]{1,0:T(8,128)}, u32[]{:S(2)}) copy-start(f32[128,128]{1,0:T(8,128)} %cal_coef_ref.3) | copy-start | bytes 196612
  31.9 9.0 %copy-start.7 = (s32[128]{0:T(128)S(1)}, s32[128]{0:T(128)}, u32[]{:S(2)}) copy-start(s32[128]{0:T(128)} %param.15) | copy-start | bytes 1540
  52.5 12.2 %all-to-all-start.2 = ((f32[8,32,256]{2,1,0:T(8,128)}), f32[8,32,256]{2,1,0:T(8,128)S(1)}, u32[]{:S(2)}, u32[]{:S(2)}) async-start(f32[8,32,256]{2,1,0:T(8,128)} %get-tuple-element.22), calls=%async_computation.2 | async-start | bytes 524288 | tf_op jit(solution)/shard_map/all_to_all | solution.py:547
  56.1 1.4 %collective-permute-start.2 = (f32[168,256]{1,0:T(8,128)S(1)}, f32[168,256]{1,0:T(8,128)S(1)}, u32[]{:S(2)}, u32[]{:S(2)}) collective-permute-start(f32[168,256]{1,0:T(8,128)S(1)} %get-tuple-element.23), channel_id=1, source_target_pairs={{0,1},{1,0},{2,3},{3,2},{4,5},{5,4},{6,7},{7,6},{8,9},{9,8},{10,11... | collective-permute-start | bytes 516104 | tf_op jit(solution)/shard_map/ppermute | solution.py:550
  57.5 6.5 %collective-permute-start.3 = (f32[168,256]{1,0:T(8,128)S(1)}, f32[168,256]{1,0:T(8,128)S(1)}, u32[]{:S(2)}, u32[]{:S(2)}) collective-permute-start(f32[168,256]{1,0:T(8,128)S(1)} %add.7.own_ref), channel_id=1, source_target_pairs={{0,2},{1,3},{2,0},{3,1},{4,6},{5,7},{6,4},{7,5},{8,10},{9,11},{10,... | collective-permute-start | bytes 516104 | tf_op jit(solution)/shard_map/ppermute | solution.py:550
  65.4 14.5 %all-to-all-start.3 = ((f32[8,72,128]{2,1,0:T(8,128)}), f32[8,72,128]{2,1,0:T(8,128)S(1)}, u32[]{:S(2)}, u32[]{:S(2)}) async-start(f32[8,72,128]{2,1,0:T(8,128)} %get-tuple-element.25), calls=%async_computation.3 | async-start | bytes 589824 | tf_op jit(solution)/shard_map/all_to_all | solution.py:547
  85.0 11.9 %all-to-all-start.4 = ((f32[32,8,128]{2,1,0:T(8,128)}), f32[32,8,128]{2,1,0:T(8,128)S(1)}, u32[]{:S(2)}, u32[]{:S(2)}) async-start(f32[32,8,128]{2,1,0:T(8,128)} %get-tuple-element.29), calls=%async_computation.4 | async-start | bytes 262144 | tf_op jit(solution)/shard_map/all_to_all | solution.py:547
  89.5 7.4 %copy-start = (f32[128,128]{1,0:T(8,128)S(1)}, f32[128,128]{1,0:T(8,128)}, u32[]{:S(2)}) copy-start(f32[128,128]{1,0:T(8,128)} %value_ref.1) | copy-start | bytes 196612

commit v13 on v12

--- a/solution.py
+++ b/solution.py
@@ -13,7 +13,7 @@
 FINE = 32
 COARSE = 256
 GROUP = 16
-FIRST_GROUP = 32
+WIDE_GROUP = 32
 SLOT = 8
 STAR_ROWS = 5 * FINE
 KNOT_ROWS = 4 * FINE
@@ -101,21 +101,29 @@
         out_ref[where // block, where % block : where % block + 8, :] = rows[offset : offset + 8]
 
 
-def scatter(first, size, values, observed, knot_acc, star_acc):
-    knot_ref, frac_ref, att_coef_ref, star_ref, star_coef_ref = observed
-    rows = pl.ds(first, size)
-    knot, star = knot_ref[rows, :], star_ref[rows, :]
-    knot_coarse, knot_fine = knot >> 5, knot & (FINE - 1)
+def knot_factors(first, knot_ref, frac_ref):
+    rows = pl.ds(first, WIDE_GROUP)
+    knot = knot_ref[rows, :]
+    coarse, fine = knot >> 5, knot & (FINE - 1)
+    weights = spline_weights(frac_ref[rows, :])
+    hot = [one_hot(coarse[tile : tile + 1], COARSE) for tile in range(WIDE_GROUP)]
+    columns = [near_and_past(weights, fine, tile) for tile in range(WIDE_GROUP)]
+    return jnp.concatenate(hot, axis=1), columns
+
+
+def scatter(first, factors, values, observed, knot_acc, star_acc):
+    att_coef_ref, star_ref, star_coef_ref = observed
+    rows = pl.ds(first, WIDE_GROUP)
+    knot_hot, columns = factors
+    star = star_ref[rows, :]
     star_coarse, star_fine = star & (COARSE - 1), star >> 8
-    weights = spline_weights(frac_ref[rows, :])
     terms = [att_coef_ref[comp, rows, :] * values for comp in range(4)]
     parts = [two_parts(star_coef_ref[comp, rows, :] * values) for comp in range(5)]
     parts = [pair[half].astype(F32) for half in range(2) for pair in parts]
-    knot_left, knot_right, star_left, star_right = [], [], [], []
-    for tile in range(size):
+    knot_left, star_left, star_right = [], [], []
+    for tile in range(WIDE_GROUP):
         here = slice(tile, tile + 1)
-        knot_right.append(one_hot(knot_coarse[here], COARSE))
-        near, past = near_and_past(weights, knot_fine, tile)
+        near, past = columns[tile]
         spread = jnp.concatenate(
             [term[here] * near for term in terms] + [past_terms(terms, here) * past], axis=0
         )
@@ -129,7 +137,7 @@
             )
         )
     knot_acc[...] += product(
-        jnp.concatenate(knot_left, axis=1), jnp.concatenate(knot_right, axis=1), ((1,), (1,))
+        jnp.concatenate(knot_left, axis=1), knot_hot, ((1,), (1,))
     )
     star_acc[...] += product(
         jnp.concatenate(star_left, axis=1), jnp.concatenate(star_right, axis=1), ((1,), (1,))
@@ -189,7 +197,7 @@
     for rows in (slice(0, half), slice(half, 2 * half)):
         for source, target in zip(sources[3:], buffers[3:]):
             begin(source, target, *[slice(None)] * (len(source.shape) - 2), rows)
-    value_ref, cal_coef_ref, tile_cal_ref, *observed = buffers
+    value_ref, cal_coef_ref, tile_cal_ref, knot_ref, frac_ref, *observed = buffers
     knot_acc[...] = jnp.zeros_like(knot_acc)
     star_acc[...] = jnp.zeros_like(star_acc)
     for copy in copies[:3]:
@@ -199,17 +207,17 @@
     for copy in copies[3:8]:
         copy.wait()
 
-    @pl.loop(0, value_ref.shape[0] // FIRST_GROUP)
+    @pl.loop(0, value_ref.shape[0] // WIDE_GROUP)
     def _(group):
-        @pl.when(group * FIRST_GROUP == half)
+        @pl.when(group * WIDE_GROUP == half)
         def _():
             for copy in copies[8:]:
                 copy.wait()
 
-        first = pl.multiple_of(group * FIRST_GROUP, FIRST_GROUP)
-        values = value_ref[pl.ds(first, FIRST_GROUP), :]
+        first = pl.multiple_of(group * WIDE_GROUP, WIDE_GROUP)
+        values = value_ref[pl.ds(first, WIDE_GROUP), :]
         values = values * live_mask(live_ref, first, values.shape)
-        scatter(first, FIRST_GROUP, values, observed, knot_acc, star_acc)
+        scatter(first, knot_factors(first, knot_ref, frac_ref), values, observed, knot_acc, star_acc)
 
     scatter_end(place_ref, [], knot_acc, star_acc, table_out, star_out)
 
@@ -329,19 +337,15 @@
     cal_ref[...] = (rows[:, :128] + rows[:, 128:]) * cal_coef_ref[...] + star_image_ref[...]
 
 
-def gather(first, live_ref, observed, knot_parts_ref, cal_ref):
-    knot_ref, frac_ref, att_coef_ref = observed
-    rows = pl.ds(first, GROUP)
-    knot = knot_ref[rows, :]
-    coarse, fine = knot >> 5, knot & (FINE - 1)
-    weights = spline_weights(frac_ref[rows, :])
+def gather(first, live_ref, factors, att_coef_ref, knot_parts_ref, cal_ref):
+    rows = pl.ds(first, WIDE_GROUP)
     coef = [att_coef_ref[comp, rows, :] for comp in range(4)]
-    tiles = [slice(tile, tile + 1) for tile in range(GROUP)]
-    hot = jnp.concatenate([one_hot(coarse[here], COARSE) for here in tiles], axis=1)
+    hot, columns = factors
     found = product(knot_parts_ref[...], hot, ((1,), (0,)))
-    width = knot.shape[1]
+    width = cal_ref.shape[1]
     image_rows = []
-    for tile, here in enumerate(tiles):
+    for tile in range(WIDE_GROUP):
+        here = slice(tile, tile + 1)
         across = slice(tile * width, (tile + 1) * width)
 
         def part(begin, size):
@@ -350,7 +354,7 @@
                 + found[KNOT_HALF + begin : KNOT_HALF + begin + size, across]
             )
 
-        near, past = near_and_past(weights, fine, tile)
+        near, past = columns[tile]
         near = near * sum(coef[comp][here] * part(comp * FINE, FINE) for comp in range(4))
         past = past * past_terms(coef, here) * part(KNOT_ROWS, PAST_ROWS)
         both = near[:8] + near[8:16] + near[16:24] + near[24:] + past[:8] + past[8:]
@@ -374,24 +378,16 @@
     gather_ready(table, ahead, cal_coef_ref, tile_cal_ref, star_image_ref, knot_parts_ref, cal_ref)
     knot_acc[...] = jnp.zeros_like(knot_acc)
     star_acc[...] = jnp.zeros_like(star_acc)
-    observed = (knot_ref, frac_ref, att_coef_ref)
-    every = (knot_ref, frac_ref, att_coef_ref, star_ref, star_coef_ref)
-    groups = knot_ref.shape[0] // GROUP
-    image = gather(0, live_ref, observed, knot_parts_ref, cal_ref)
-    image_ref[:GROUP, :] = image
-
     def one_group(group, total):
-        first = pl.multiple_of(group * GROUP, GROUP)
-        following = pl.multiple_of(first + GROUP, GROUP)
-        values = image_ref[pl.ds(first, GROUP), :]
-        image = gather(following, live_ref, observed, knot_parts_ref, cal_ref)
-        scatter(first, GROUP, values, every, knot_acc, star_acc)
-        image_ref[pl.ds(following, GROUP), :] = image
+        first = pl.multiple_of(group * WIDE_GROUP, WIDE_GROUP)
+        factors = knot_factors(first, knot_ref, frac_ref)
+        image = gather(first, live_ref, factors, att_coef_ref, knot_parts_ref, cal_ref)
+        image_ref[pl.ds(first, WIDE_GROUP), :] = image
+        scatter(first, factors, image, (att_coef_ref, star_ref, star_coef_ref), knot_acc, star_acc)
         return total + image * image
 
-    total = lax.fori_loop(0, groups - 1, one_group, image * image)
-    first = (groups - 1) * GROUP
-    scatter(first, GROUP, image_ref[first:, :], every, knot_acc, star_acc)
+    zero = jnp.zeros((WIDE_GROUP, knot_ref.shape[1]), F32)
+    total = lax.fori_loop(0, knot_ref.shape[0] // WIDE_GROUP, one_group, zero)
     scatter_calibration(image_ref[...] * cal_coef_ref[...], tile_cal_ref, scatter_out)
     scalars = [(0, norm), (1, jnp.sum(total, keepdims=True))]
     scatter_end(place_ref, scalars, knot_acc, star_acc, scatter_out, star_out)
@@ -413,16 +409,17 @@
     gather_ready(table, ahead, cal_coef_ref, tile_cal_ref, star_image_ref, knot_parts_ref, cal_ref)
 
     def one_group(group, sums):
-        first = pl.multiple_of(group * GROUP, GROUP)
-        rows = pl.ds(first, GROUP)
+        first = pl.multiple_of(group * WIDE_GROUP, WIDE_GROUP)
+        rows = pl.ds(first, WIDE_GROUP)
         image_0 = image_0_ref[rows, :]
-        image = gather(first, live_ref, (knot_ref, frac_ref, att_coef_ref), knot_parts_ref, cal_ref)
+        factors = knot_factors(first, knot_ref, frac_ref)
+        image = gather(first, live_ref, factors, att_coef_ref, knot_parts_ref, cal_ref)
         image = image_0 - step * image
         image_ref[rows, :] = image
         return sums[0] + image * image, sums[1] + image * image_0
 
-    zero = jnp.zeros((GROUP, knot_ref.shape[1]), F32)
-    sums = lax.fori_loop(0, knot_ref.shape[0] // GROUP, one_group, (zero, zero))
+    zero = jnp.zeros((WIDE_GROUP, knot_ref.shape[1]), F32)
+    sums = lax.fori_loop(0, knot_ref.shape[0] // WIDE_GROUP, one_group, (zero, zero))
     scalars = [norm] + [jnp.sum(part, keepdims=True) for part in sums] + [norm_0, square_0]
     scalars = with_scalars(jnp.zeros((8, 128), F32), list(enumerate(scalars)))
     own_scalar_out[...] = scalars

time: 98.5 us -> 96.5 us (0.980)
  Pallas kernels: 36 us -> 34 us
    pallas_call x1, Pallas kernels: 11.5 us -> 10.2 us  [middle(): pl.pallas_call(functools.partial(middle_kernel, n_stars, n_seg), out_shap...]
where the time goes in v13:
time: 96.5 us; the launch traced here: 95.8 us
  Pallas kernels  34 us (35%)
  waiting for transfers between devices  30.8 us (32%)
  starting transfers between devices  28.5 us (30%)
  between operations  1.48 us (2%)
  local copies, waits for them, and re-layouts  1.08 us (1%)
    all_to_all x5, starting transfers between devices, swap(): return lax.all_to_all(blocks, axes, 0, 0)  25.2 us
    all_to_all x5, waiting for transfers between devices, swap(): return lax.all_to_all(blocks, axes, 0, 0)  18.2 us
    ppermute x4, waiting for transfers between devices, partner(): lax.ppermute(array, axis, [(i, i ^ distance) for i in range(lax.axis_size...  12.6 us
    pallas_call x1, Pallas kernels, middle(): pl.pallas_call(functools.partial(middle_kernel, n_stars, n_seg), out_shap...  10.2 us
    pallas_call x2, Pallas kernels, star_forward(): pl.pallas_call(star_forward_kernel, out_shape=image_shape, in_specs=in_vm...  8.5 us
    pallas_call x1, Pallas kernels, first_scatter(): pl.pallas_call(first_kernel, out_shape=sent_shapes, in_specs=in_smem(2) +...  8.36 us
    pallas_call x1, Pallas kernels, last_gather(): pl.pallas_call(functools.partial(last_kernel, n_stars, n_seg), out_shape=...  4.42 us
    ppermute x4, starting transfers between devices, partner(): lax.ppermute(array, axis, [(i, i ^ distance) for i in range(lax.axis_size...  3.25 us
  transfers between devices with their start and end apart: 9, of which 9 were waited for; matrix products, arithmetic and copies ran while one was open for 1% of the time, Pallas kernels for 9%

profile of v13, /device:TPU:0, one launch (start us, length us, event | category | flops | bytes accessed | tf_op | source)
XLA Modules:
  0.0 95.8 jit_solution(8324365829631160078)
XLA Ops:
  1.3 8.4 %first_scatter.1 = (f32[8,32,256]{2,1,0:T(8,128)}, f32[168,256]{1,0:T(8,128)}) custom-call(s32[1]{0:T(128)S(6)} %copy.17.live_ref, s32[1]{0:T(128)} %bitcast.place_ref, f32[128,128]{1,0:T(8,128)} %value_ref.1, f32[128,128]{1,0:T(8,128)} %cal_coef_ref.3, s32[1,128]{1,0:T(1,128)} %bitcast.6, s32[128,128]{1,0:T(8,128)} %knot_ref.3, f32[128,128]{1,0:T(8,128)} %frac_ref.3, ...), custom_call_target="tpu_custom_call" | custom-call | flops 3000000000 | bytes 1000000 | tf_op jit(solution)/shard_map/first_scatter/pallas_call | solution.py:494
  9.7 7.4 %all-to-all-start = ((f32[8,32,256]{2,1,0:T(8,128)}), f32[8,32,256]{2,1,0:T(8,128)S(1)}, u32[]{:S(2)}, u32[]{:S(2)}) async-start(f32[8,32,256]{2,1,0:T(8,128)} %get-tuple-element.18), calls=%async_computation | async-start | bytes 524288 | tf_op jit(solution)/shard_map/all_to_all | solution.py:544
  17.1 1.4 %collective-permute-done = f32[168,256]{1,0:T(8,128)S(1)} collective-permute-done((f32[168,256]{1,0:T(8,128)S(1)}, f32[168,256]{1,0:T(8,128)S(1)}, u32[]{:S(2)}, u32[]{:S(2)}) %collective-permute-start) | collective-permute-done | bytes 172064 | tf_op jit(solution)/shard_map/ppermute | solution.py:547
  18.5 1.6 %collective-permute-start.1 = (f32[168,256]{1,0:T(8,128)S(1)}, f32[168,256]{1,0:T(8,128)S(1)}, u32[]{:S(2)}, u32[]{:S(2)}) collective-permute-start(f32[168,256]{1,0:T(8,128)S(1)} %add.6.own_ref), channel_id=1, source_target_pairs={{0,2},{1,3},{2,0},{3,1},{4,6},{5,7},{6,4},{7,5},{8,10},{9,11},{10,... | collective-permute-start | bytes 516104 | tf_op jit(solution)/shard_map/ppermute | solution.py:547
  20.1 4.9 %collective-permute-done.1.other_ref = f32[168,256]{1,0:T(8,128)S(1)} collective-permute-done((f32[168,256]{1,0:T(8,128)S(1)}, f32[168,256]{1,0:T(8,128)S(1)}, u32[]{:S(2)}, u32[]{:S(2)}) %collective-permute-start.1) | collective-permute-done | bytes 172064 | tf_op jit(solution)/shard_map/ppermute | solution.py:547
  25.0 0.9 all-to-all-done.block_ref
  26.0 0.7 table_sum.2
  26.7 5.1 %all-to-all-start.1 = ((f32[8,72,128]{2,1,0:T(8,128)}), f32[8,72,128]{2,1,0:T(8,128)S(1)}, u32[]{:S(2)}, u32[]{:S(2)}) async-start(f32[8,72,128]{2,1,0:T(8,128)} %get-tuple-element.21), calls=%async_computation.1 | async-start | bytes 589824 | tf_op jit(solution)/shard_map/all_to_all | solution.py:544
  31.9 4.3 %star_forward.2.star_image_ref = f32[128,128]{1,0:T(8,128)S(1)} custom-call(s32[128,128]{1,0:T(8,128)S(1)} %copy-done.3, f32[5,128,128]{2,1,0:T(8,128)S(1)} %copy-done.1, f32[160,256]{1,0:T(8,128)S(1)} %get-tuple-element.20.star_x_ref.star_0_ref), custom_call_target="tpu_custom_call" | custom-call | flops 3000000000 | bytes 1000000 | tf_op jit(solution)/shard_map/star_forward/pallas_call | solution.py:532
  36.2 4.7 %all-to-all-done.1.block_ref = f32[8,72,128]{2,1,0:T(8,128)S(1)} async-done(((f32[8,72,128]{2,1,0:T(8,128)}), f32[8,72,128]{2,1,0:T(8,128)S(1)}, u32[]{:S(2)}, u32[]{:S(2)}) %all-to-all-start.1) | async-done | bytes 294944 | tf_op jit(solution)/shard_map/all_to_all | solution.py:544
  40.9 10.2 %gather_and_scatter.1 = (f32[128,128]{1,0:T(8,128)S(1)}, f32[256,256]{1,0:T(8,128)S(1)}, f32[8,32,256]{2,1,0:T(8,128)}, f32[168,256]{1,0:T(8,128)S(1)}) custom-call(s32[1]{0:T(128)S(6)} %copy.17.live_ref, s32[1]{0:T(128)} %bitcast.place_ref, s32[128,128]{1,0:T(8,128)S(1)} %copy-done.4, f32[128,128]{1,0:T(8,128)S(1)} %copy-done.5, ...), custom_call_target="tpu_custom_call" | custom-call | flops 3000000000 | bytes 1000000 | tf_op jit(solution)/shard_map/gather_and_scatter/pallas_call | solution.py:507
  51.1 3.6 %all-to-all-start.2 = ((f32[8,32,256]{2,1,0:T(8,128)}), f32[8,32,256]{2,1,0:T(8,128)S(1)}, u32[]{:S(2)}, u32[]{:S(2)}) async-start(f32[8,32,256]{2,1,0:T(8,128)} %get-tuple-element.22), calls=%async_computation.2 | async-start | bytes 524288 | tf_op jit(solution)/shard_map/all_to_all | solution.py:544
  54.8 1.4 %collective-permute-done.2 = f32[168,256]{1,0:T(8,128)S(1)} collective-permute-done((f32[168,256]{1,0:T(8,128)S(1)}, f32[168,256]{1,0:T(8,128)S(1)}, u32[]{:S(2)}, u32[]{:S(2)}) %collective-permute-start.2) | collective-permute-done | bytes 172064 | tf_op jit(solution)/shard_map/ppermute | solution.py:547
  56.2 1.6 %collective-permute-start.3 = (f32[168,256]{1,0:T(8,128)S(1)}, f32[168,256]{1,0:T(8,128)S(1)}, u32[]{:S(2)}, u32[]{:S(2)}) collective-permute-start(f32[168,256]{1,0:T(8,128)S(1)} %add.7.own_ref), channel_id=1, source_target_pairs={{0,2},{1,3},{2,0},{3,1},{4,6},{5,7},{6,4},{7,5},{8,10},{9,11},{10,... | collective-permute-start | bytes 516104 | tf_op jit(solution)/shard_map/ppermute | solution.py:547
  57.8 4.9 %collective-permute-done.3.other_ref = f32[168,256]{1,0:T(8,128)S(1)} collective-permute-done((f32[168,256]{1,0:T(8,128)S(1)}, f32[168,256]{1,0:T(8,128)S(1)}, u32[]{:S(2)}, u32[]{:S(2)}) %collective-permute-start.3) | collective-permute-done | bytes 172064 | tf_op jit(solution)/shard_map/ppermute | solution.py:547
  62.7 0.6 all-to-all-done.2.block_ref
  63.3 0.7 table_sum.3
  64.0 5.4 %all-to-all-start.3 = ((f32[8,72,128]{2,1,0:T(8,128)}), f32[8,72,128]{2,1,0:T(8,128)S(1)}, u32[]{:S(2)}, u32[]{:S(2)}) async-start(f32[8,72,128]{2,1,0:T(8,128)} %get-tuple-element.25), calls=%async_computation.3 | async-start | bytes 589824 | tf_op jit(solution)/shard_map/all_to_all | solution.py:544
  69.4 4.2 %star_forward.3.star_image_ref = f32[128,128]{1,0:T(8,128)S(1)} custom-call(s32[128,128]{1,0:T(8,128)S(1)} %copy-done.3, f32[5,128,128]{2,1,0:T(8,128)S(1)} %copy-done.1, f32[160,256]{1,0:T(8,128)S(1)} %get-tuple-element.24.star_x_ref), custom_call_target="tpu_custom_call" | custom-call | flops 3000000000 | bytes 1000000 | tf_op jit(solution)/shard_map/star_forward/pallas_call | solution.py:532
  73.7 4.8 %all-to-all-done.3.block_ref = f32[8,72,128]{2,1,0:T(8,128)S(1)} async-done(((f32[8,72,128]{2,1,0:T(8,128)}), f32[8,72,128]{2,1,0:T(8,128)S(1)}, u32[]{:S(2)}, u32[]{:S(2)}) %all-to-all-start.3) | async-done | bytes 294944 | tf_op jit(solution)/shard_map/all_to_all | solution.py:544
  78.5 4.4 %last_gather.1 = (f32[128,128]{1,0:T(8,128)S(1)}, f32[256,256]{1,0:T(8,128)S(1)}, f32[32,8,128]{2,1,0:T(8,128)}, f32[8,128]{1,0:T(8,128)S(1)}) custom-call(s32[1]{0:T(128)S(6)} %copy.17.live_ref, s32[1]{0:T(128)} %bitcast.place_ref, s32[128,128]{1,0:T(8,128)S(1)} %copy-done.4, f32[128,128]{1,0:T(8,128)S(1)} %copy-done.5, f32[4,128,128]{2,1,0:T(8,128)S(1)} %copy-done.2, ...), custom_call_target="tpu_custom_call" | custom-call | flops 3000000000 | bytes 1000000 | tf_op jit(solution)/shard_map/last_gather/pallas_call | solution.py:520
  82.9 3.7 %all-to-all-start.4 = ((f32[32,8,128]{2,1,0:T(8,128)}), f32[32,8,128]{2,1,0:T(8,128)S(1)}, u32[]{:S(2)}, u32[]{:S(2)}) async-start(f32[32,8,128]{2,1,0:T(8,128)} %get-tuple-element.29), calls=%async_computation.4 | async-start | bytes 262144 | tf_op jit(solution)/shard_map/all_to_all | solution.py:544
  87.7 7.1 %all-to-all-done.4.scalar_ref = f32[32,8,128]{2,1,0:T(8,128)S(1)} async-done(((f32[32,8,128]{2,1,0:T(8,128)}), f32[32,8,128]{2,1,0:T(8,128)S(1)}, u32[]{:S(2)}, u32[]{:S(2)}) %all-to-all-start.4) | async-done | bytes 131104 | tf_op jit(solution)/shard_map/all_to_all | solution.py:544
  94.8 1.0 %outputs.1 = (f32[5,8192]{1,0:T(8,128)}, f32[4,8192]{1,0:T(4,128)}, f32[256,128]{1,0:T(8,128)}, f32[128,128]{1,0:T(8,128)}) custom-call(s32[1]{0:T(128)S(6)} %copy.17.live_ref, f32[8,128]{1,0:T(8,128)S(1)} %get-tuple-element.28.own_scalar_ref, f32[32,8,128]{2,1,0:T(8,128)S(1)} %all-to-all-done.4.scalar_ref, f32[5,8192]{1,0:T(8,128)S(1)} %reshape.26.star_0_ref, ...), custom_call_target="tpu_custom_call" | custom-call | flops 1000000 | bytes 600000 | tf_op jit(solution)/shard_map/outputs/pallas_call | solution.py:578
  (30 shorter events, 1.2 us)
Async XLA Ops:
  9.7 7.4 %copy-start.8 = (f32[168,256]{1,0:T(8,128)S(1)}, f32[168,256]{1,0:T(8,128)}, u32[]{:S(2)}) copy-start(f32[168,256]{1,0:T(8,128)} %get-tuple-element.19) | copy-start | bytes 516100
  9.7 16.3 %all-to-all-start = ((f32[8,32,256]{2,1,0:T(8,128)}), f32[8,32,256]{2,1,0:T(8,128)S(1)}, u32[]{:S(2)}, u32[]{:S(2)}) async-start(f32[8,32,256]{2,1,0:T(8,128)} %get-tuple-element.18), calls=%async_computation | async-start | bytes 524288 | tf_op jit(solution)/shard_map/all_to_all | solution.py:544
  17.0 1.5 %collective-permute-start = (f32[168,256]{1,0:T(8,128)S(1)}, f32[168,256]{1,0:T(8,128)S(1)}, u32[]{:S(2)}, u32[]{:S(2)}) collective-permute-start(f32[168,256]{1,0:T(8,128)S(1)} %copy-done.8), channel_id=1, source_target_pairs={{0,1},{1,0},{2,3},{3,2},{4,5},{5,4},{6,7},{7,6},{8,9},{9,8},{10,11... | collective-permute-start | bytes 516104 | tf_op jit(solution)/shard_map/ppermute | solution.py:547
  18.5 6.5 %collective-permute-start.1 = (f32[168,256]{1,0:T(8,128)S(1)}, f32[168,256]{1,0:T(8,128)S(1)}, u32[]{:S(2)}, u32[]{:S(2)}) collective-permute-start(f32[168,256]{1,0:T(8,128)S(1)} %add.6.own_ref), channel_id=1, source_target_pairs={{0,2},{1,3},{2,0},{3,1},{4,6},{5,7},{6,4},{7,5},{8,10},{9,11},{10,... | collective-permute-start | bytes 516104 | tf_op jit(solution)/shard_map/ppermute | solution.py:547
  26.7 5.1 %copy-start.1 = (f32[5,128,128]{2,1,0:T(8,128)S(1)}, f32[5,128,128]{2,1,0:T(8,128)}, u32[]{:S(2)}) copy-start(f32[5,128,128]{2,1,0:T(8,128)} %star_coef_ref.5) | copy-start | bytes 983044
  26.7 5.1 %copy-start.3 = (s32[128,128]{1,0:T(8,128)S(1)}, s32[128,128]{1,0:T(8,128)}, u32[]{:S(2)}) copy-start(s32[128,128]{1,0:T(8,128)} %star_ref.5) | copy-start | bytes 196612
  26.7 14.2 %all-to-all-start.1 = ((f32[8,72,128]{2,1,0:T(8,128)}), f32[8,72,128]{2,1,0:T(8,128)S(1)}, u32[]{:S(2)}, u32[]{:S(2)}) async-start(f32[8,72,128]{2,1,0:T(8,128)} %get-tuple-element.21), calls=%async_computation.1 | async-start | bytes 589824 | tf_op jit(solution)/shard_map/all_to_all | solution.py:544
  31.9 9.0 %copy-start.2 = (f32[4,128,128]{2,1,0:T(8,128)S(1)}, f32[4,128,128]{2,1,0:T(8,128)}, u32[]{:S(2)}) copy-start(f32[4,128,128]{2,1,0:T(8,128)} %att_coef_ref.3) | copy-start | bytes 786436
  31.9 9.0 %copy-start.4 = (s32[128,128]{1,0:T(8,128)S(1)}, s32[128,128]{1,0:T(8,128)}, u32[]{:S(2)}) copy-start(s32[128,128]{1,0:T(8,128)} %knot_ref.3) | copy-start | bytes 196612
  31.9 9.0 %copy-start.5 = (f32[128,128]{1,0:T(8,128)S(1)}, f32[128,128]{1,0:T(8,128)}, u32[]{:S(2)}) copy-start(f32[128,128]{1,0:T(8,128)} %frac_ref.3) | copy-start | bytes 196612
  31.9 9.0 %copy-start.6 = (f32[128,128]{1,0:T(8,128)S(1)}, f32[128,128]{1,0:T(8,128)}, u32[]{:S(2)}) copy-start(f32[128,128]{1,0:T(8,128)} %cal_coef_ref.3) | copy-start | bytes 196612
  31.9 9.0 %copy-start.7 = (s32[128]{0:T(128)S(1)}, s32[128]{0:T(128)}, u32[]{:S(2)}) copy-start(s32[128]{0:T(128)} %param.15) | copy-start | bytes 1540
  51.1 12.2 %all-to-all-start.2 = ((f32[8,32,256]{2,1,0:T(8,128)}), f32[8,32,256]{2,1,0:T(8,128)S(1)}, u32[]{:S(2)}, u32[]{:S(2)}) async-start(f32[8,32,256]{2,1,0:T(8,128)} %get-tuple-element.22), calls=%async_computation.2 | async-start | bytes 524288 | tf_op jit(solution)/shard_map/all_to_all | solution.py:544
  54.7 1.4 %collective-permute-start.2 = (f32[168,256]{1,0:T(8,128)S(1)}, f32[168,256]{1,0:T(8,128)S(1)}, u32[]{:S(2)}, u32[]{:S(2)}) collective-permute-start(f32[168,256]{1,0:T(8,128)S(1)} %get-tuple-element.23), channel_id=1, source_target_pairs={{0,1},{1,0},{2,3},{3,2},{4,5},{5,4},{6,7},{7,6},{8,9},{9,8},{10,11... | collective-permute-start | bytes 516104 | tf_op jit(solution)/shard_map/ppermute | solution.py:547
  56.2 6.5 %collective-permute-start.3 = (f32[168,256]{1,0:T(8,128)S(1)}, f32[168,256]{1,0:T(8,128)S(1)}, u32[]{:S(2)}, u32[]{:S(2)}) collective-permute-start(f32[168,256]{1,0:T(8,128)S(1)} %add.7.own_ref), channel_id=1, source_target_pairs={{0,2},{1,3},{2,0},{3,1},{4,6},{5,7},{6,4},{7,5},{8,10},{9,11},{10,... | collective-permute-start | bytes 516104 | tf_op jit(solution)/shard_map/ppermute | solution.py:547
  64.0 14.4 %all-to-all-start.3 = ((f32[8,72,128]{2,1,0:T(8,128)}), f32[8,72,128]{2,1,0:T(8,128)S(1)}, u32[]{:S(2)}, u32[]{:S(2)}) async-start(f32[8,72,128]{2,1,0:T(8,128)} %get-tuple-element.25), calls=%async_computation.3 | async-start | bytes 589824 | tf_op jit(solution)/shard_map/all_to_all | solution.py:544
  82.9 11.9 %all-to-all-start.4 = ((f32[32,8,128]{2,1,0:T(8,128)}), f32[32,8,128]{2,1,0:T(8,128)S(1)}, u32[]{:S(2)}, u32[]{:S(2)}) async-start(f32[32,8,128]{2,1,0:T(8,128)} %get-tuple-element.29), calls=%async_computation.4 | async-start | bytes 262144 | tf_op jit(solution)/shard_map/all_to_all | solution.py:544
  87.4 7.4 %copy-start = (f32[128,128]{1,0:T(8,128)S(1)}, f32[128,128]{1,0:T(8,128)}, u32[]{:S(2)}) copy-start(f32[128,128]{1,0:T(8,128)} %value_ref.1) | copy-start | bytes 196612

commit v14 on v13

--- a/solution.py
+++ b/solution.py
@@ -13,7 +13,7 @@
 FINE = 32
 COARSE = 256
 GROUP = 16
-WIDE_GROUP = 32
+WIDE_GROUP = 64
 SLOT = 8
 STAR_ROWS = 5 * FINE
 KNOT_ROWS = 4 * FINE

time: 96.5 us -> 95.1 us (0.985)
  Pallas kernels: 34 us -> 32.6 us
where the time goes in v14:
time: 95.1 us; the launch traced here: 94.5 us
  Pallas kernels  32.6 us (34%)
  waiting for transfers between devices  30.8 us (32%)
  starting transfers between devices  28.5 us (30%)
  between operations  1.48 us (2%)
  local copies, waits for them, and re-layouts  1.08 us (1%)
    all_to_all x5, starting transfers between devices, swap(): return lax.all_to_all(blocks, axes, 0, 0)  25.2 us
    all_to_all x5, waiting for transfers between devices, swap(): return lax.all_to_all(blocks, axes, 0, 0)  18.2 us
    ppermute x4, waiting for transfers between devices, partner(): lax.ppermute(array, axis, [(i, i ^ distance) for i in range(lax.axis_size...  12.6 us
    pallas_call x1, Pallas kernels, middle(): pl.pallas_call(functools.partial(middle_kernel, n_stars, n_seg), out_shap...  9.55 us
    pallas_call x2, Pallas kernels, star_forward(): pl.pallas_call(star_forward_kernel, out_shape=image_shape, in_specs=in_vm...  8.5 us
    pallas_call x1, Pallas kernels, first_scatter(): pl.pallas_call(first_kernel, out_shape=sent_shapes, in_specs=in_smem(2) +...  7.92 us
    pallas_call x1, Pallas kernels, last_gather(): pl.pallas_call(functools.partial(last_kernel, n_stars, n_seg), out_shape=...  4.09 us
    ppermute x4, starting transfers between devices, partner(): lax.ppermute(array, axis, [(i, i ^ distance) for i in range(lax.axis_size...  3.24 us
  transfers between devices with their start and end apart: 9, of which 9 were waited for; matrix products, arithmetic and copies ran while one was open for 1% of the time, Pallas kernels for 9%

profile of v14, /device:TPU:0, one launch (start us, length us, event | category | flops | bytes accessed | tf_op | source)
XLA Modules:
  0.0 94.5 jit_solution(15168839010238794256)
XLA Ops:
  1.3 7.9 %first_scatter.1 = (f32[8,32,256]{2,1,0:T(8,128)}, f32[168,256]{1,0:T(8,128)}) custom-call(s32[1]{0:T(128)S(6)} %copy.17.live_ref, s32[1]{0:T(128)} %bitcast.place_ref, f32[128,128]{1,0:T(8,128)} %value_ref.1, f32[128,128]{1,0:T(8,128)} %cal_coef_ref.3, s32[1,128]{1,0:T(1,128)} %bitcast.6, s32[128,128]{1,0:T(8,128)} %knot_ref.3, f32[128,128]{1,0:T(8,128)} %frac_ref.3, ...), custom_call_target="tpu_custom_call" | custom-call | flops 3000000000 | bytes 1000000 | tf_op jit(solution)/shard_map/first_scatter/pallas_call | solution.py:494
  9.2 7.4 %all-to-all-start = ((f32[8,32,256]{2,1,0:T(8,128)}), f32[8,32,256]{2,1,0:T(8,128)S(1)}, u32[]{:S(2)}, u32[]{:S(2)}) async-start(f32[8,32,256]{2,1,0:T(8,128)} %get-tuple-element.18), calls=%async_computation | async-start | bytes 524288 | tf_op jit(solution)/shard_map/all_to_all | solution.py:544
  16.7 1.4 %collective-permute-done = f32[168,256]{1,0:T(8,128)S(1)} collective-permute-done((f32[168,256]{1,0:T(8,128)S(1)}, f32[168,256]{1,0:T(8,128)S(1)}, u32[]{:S(2)}, u32[]{:S(2)}) %collective-permute-start) | collective-permute-done | bytes 172064 | tf_op jit(solution)/shard_map/ppermute | solution.py:547
  18.1 1.6 %collective-permute-start.1 = (f32[168,256]{1,0:T(8,128)S(1)}, f32[168,256]{1,0:T(8,128)S(1)}, u32[]{:S(2)}, u32[]{:S(2)}) collective-permute-start(f32[168,256]{1,0:T(8,128)S(1)} %add.6.own_ref), channel_id=1, source_target_pairs={{0,2},{1,3},{2,0},{3,1},{4,6},{5,7},{6,4},{7,5},{8,10},{9,11},{10,... | collective-permute-start | bytes 516104 | tf_op jit(solution)/shard_map/ppermute | solution.py:547
  19.7 4.9 %collective-permute-done.1.other_ref = f32[168,256]{1,0:T(8,128)S(1)} collective-permute-done((f32[168,256]{1,0:T(8,128)S(1)}, f32[168,256]{1,0:T(8,128)S(1)}, u32[]{:S(2)}, u32[]{:S(2)}) %collective-permute-start.1) | collective-permute-done | bytes 172064 | tf_op jit(solution)/shard_map/ppermute | solution.py:547
  24.6 0.9 all-to-all-done.block_ref
  25.5 0.7 table_sum.2
  26.3 5.1 %all-to-all-start.1 = ((f32[8,72,128]{2,1,0:T(8,128)}), f32[8,72,128]{2,1,0:T(8,128)S(1)}, u32[]{:S(2)}, u32[]{:S(2)}) async-start(f32[8,72,128]{2,1,0:T(8,128)} %get-tuple-element.21), calls=%async_computation.1 | async-start | bytes 589824 | tf_op jit(solution)/shard_map/all_to_all | solution.py:544
  31.5 4.2 %star_forward.2.star_image_ref = f32[128,128]{1,0:T(8,128)S(1)} custom-call(s32[128,128]{1,0:T(8,128)S(1)} %copy-done.3, f32[5,128,128]{2,1,0:T(8,128)S(1)} %copy-done.1, f32[160,256]{1,0:T(8,128)S(1)} %get-tuple-element.20.star_x_ref.star_0_ref), custom_call_target="tpu_custom_call" | custom-call | flops 3000000000 | bytes 1000000 | tf_op jit(solution)/shard_map/star_forward/pallas_call | solution.py:532
  35.8 4.7 %all-to-all-done.1.block_ref = f32[8,72,128]{2,1,0:T(8,128)S(1)} async-done(((f32[8,72,128]{2,1,0:T(8,128)}), f32[8,72,128]{2,1,0:T(8,128)S(1)}, u32[]{:S(2)}, u32[]{:S(2)}) %all-to-all-start.1) | async-done | bytes 294944 | tf_op jit(solution)/shard_map/all_to_all | solution.py:544
  40.5 9.6 %gather_and_scatter.1 = (f32[128,128]{1,0:T(8,128)S(1)}, f32[256,256]{1,0:T(8,128)S(1)}, f32[8,32,256]{2,1,0:T(8,128)}, f32[168,256]{1,0:T(8,128)S(1)}) custom-call(s32[1]{0:T(128)S(6)} %copy.17.live_ref, s32[1]{0:T(128)} %bitcast.place_ref, s32[128,128]{1,0:T(8,128)S(1)} %copy-done.4, f32[128,128]{1,0:T(8,128)S(1)} %copy-done.5, ...), custom_call_target="tpu_custom_call" | custom-call | flops 3000000000 | bytes 1000000 | tf_op jit(solution)/shard_map/gather_and_scatter/pallas_call | solution.py:507
  50.1 3.6 %all-to-all-start.2 = ((f32[8,32,256]{2,1,0:T(8,128)}), f32[8,32,256]{2,1,0:T(8,128)S(1)}, u32[]{:S(2)}, u32[]{:S(2)}) async-start(f32[8,32,256]{2,1,0:T(8,128)} %get-tuple-element.22), calls=%async_computation.2 | async-start | bytes 524288 | tf_op jit(solution)/shard_map/all_to_all | solution.py:544
  53.7 1.4 %collective-permute-done.2 = f32[168,256]{1,0:T(8,128)S(1)} collective-permute-done((f32[168,256]{1,0:T(8,128)S(1)}, f32[168,256]{1,0:T(8,128)S(1)}, u32[]{:S(2)}, u32[]{:S(2)}) %collective-permute-start.2) | collective-permute-done | bytes 172064 | tf_op jit(solution)/shard_map/ppermute | solution.py:547
  55.1 1.6 %collective-permute-start.3 = (f32[168,256]{1,0:T(8,128)S(1)}, f32[168,256]{1,0:T(8,128)S(1)}, u32[]{:S(2)}, u32[]{:S(2)}) collective-permute-start(f32[168,256]{1,0:T(8,128)S(1)} %add.7.own_ref), channel_id=1, source_target_pairs={{0,2},{1,3},{2,0},{3,1},{4,6},{5,7},{6,4},{7,5},{8,10},{9,11},{10,... | collective-permute-start | bytes 516104 | tf_op jit(solution)/shard_map/ppermute | solution.py:547
  56.7 4.9 %collective-permute-done.3.other_ref = f32[168,256]{1,0:T(8,128)S(1)} collective-permute-done((f32[168,256]{1,0:T(8,128)S(1)}, f32[168,256]{1,0:T(8,128)S(1)}, u32[]{:S(2)}, u32[]{:S(2)}) %collective-permute-start.3) | collective-permute-done | bytes 172064 | tf_op jit(solution)/shard_map/ppermute | solution.py:547
  61.6 0.6 all-to-all-done.2.block_ref
  62.2 0.7 table_sum.3
  63.0 5.4 %all-to-all-start.3 = ((f32[8,72,128]{2,1,0:T(8,128)}), f32[8,72,128]{2,1,0:T(8,128)S(1)}, u32[]{:S(2)}, u32[]{:S(2)}) async-start(f32[8,72,128]{2,1,0:T(8,128)} %get-tuple-element.25), calls=%async_computation.3 | async-start | bytes 589824 | tf_op jit(solution)/shard_map/all_to_all | solution.py:544
  68.4 4.2 %star_forward.3.star_image_ref = f32[128,128]{1,0:T(8,128)S(1)} custom-call(s32[128,128]{1,0:T(8,128)S(1)} %copy-done.3, f32[5,128,128]{2,1,0:T(8,128)S(1)} %copy-done.1, f32[160,256]{1,0:T(8,128)S(1)} %get-tuple-element.24.star_x_ref), custom_call_target="tpu_custom_call" | custom-call | flops 3000000000 | bytes 1000000 | tf_op jit(solution)/shard_map/star_forward/pallas_call | solution.py:532
  72.6 4.8 %all-to-all-done.3.block_ref = f32[8,72,128]{2,1,0:T(8,128)S(1)} async-done(((f32[8,72,128]{2,1,0:T(8,128)}), f32[8,72,128]{2,1,0:T(8,128)S(1)}, u32[]{:S(2)}, u32[]{:S(2)}) %all-to-all-start.3) | async-done | bytes 294944 | tf_op jit(solution)/shard_map/all_to_all | solution.py:544
  77.4 4.1 %last_gather.1 = (f32[128,128]{1,0:T(8,128)S(1)}, f32[256,256]{1,0:T(8,128)S(1)}, f32[32,8,128]{2,1,0:T(8,128)}, f32[8,128]{1,0:T(8,128)S(1)}) custom-call(s32[1]{0:T(128)S(6)} %copy.17.live_ref, s32[1]{0:T(128)} %bitcast.place_ref, s32[128,128]{1,0:T(8,128)S(1)} %copy-done.4, f32[128,128]{1,0:T(8,128)S(1)} %copy-done.5, f32[4,128,128]{2,1,0:T(8,128)S(1)} %copy-done.2, ...), custom_call_target="tpu_custom_call" | custom-call | flops 3000000000 | bytes 1000000 | tf_op jit(solution)/shard_map/last_gather/pallas_call | solution.py:520
  81.5 3.7 %all-to-all-start.4 = ((f32[32,8,128]{2,1,0:T(8,128)}), f32[32,8,128]{2,1,0:T(8,128)S(1)}, u32[]{:S(2)}, u32[]{:S(2)}) async-start(f32[32,8,128]{2,1,0:T(8,128)} %get-tuple-element.29), calls=%async_computation.4 | async-start | bytes 262144 | tf_op jit(solution)/shard_map/all_to_all | solution.py:544
  86.3 7.1 %all-to-all-done.4.scalar_ref = f32[32,8,128]{2,1,0:T(8,128)S(1)} async-done(((f32[32,8,128]{2,1,0:T(8,128)}), f32[32,8,128]{2,1,0:T(8,128)S(1)}, u32[]{:S(2)}, u32[]{:S(2)}) %all-to-all-start.4) | async-done | bytes 131104 | tf_op jit(solution)/shard_map/all_to_all | solution.py:544
  93.4 1.0 %outputs.1 = (f32[5,8192]{1,0:T(8,128)}, f32[4,8192]{1,0:T(4,128)}, f32[256,128]{1,0:T(8,128)}, f32[128,128]{1,0:T(8,128)}) custom-call(s32[1]{0:T(128)S(6)} %copy.17.live_ref, f32[8,128]{1,0:T(8,128)S(1)} %get-tuple-element.28.own_scalar_ref, f32[32,8,128]{2,1,0:T(8,128)S(1)} %all-to-all-done.4.scalar_ref, f32[5,8192]{1,0:T(8,128)S(1)} %reshape.26.star_0_ref, ...), custom_call_target="tpu_custom_call" | custom-call | flops 1000000 | bytes 600000 | tf_op jit(solution)/shard_map/outputs/pallas_call | solution.py:578
  (30 shorter events, 1.2 us)
Async XLA Ops:
  9.2 7.4 %copy-start.8 = (f32[168,256]{1,0:T(8,128)S(1)}, f32[168,256]{1,0:T(8,128)}, u32[]{:S(2)}) copy-start(f32[168,256]{1,0:T(8,128)} %get-tuple-element.19) | copy-start | bytes 516100
  9.2 16.3 %all-to-all-start = ((f32[8,32,256]{2,1,0:T(8,128)}), f32[8,32,256]{2,1,0:T(8,128)S(1)}, u32[]{:S(2)}, u32[]{:S(2)}) async-start(f32[8,32,256]{2,1,0:T(8,128)} %get-tuple-element.18), calls=%async_computation | async-start | bytes 524288 | tf_op jit(solution)/shard_map/all_to_all | solution.py:544
  16.6 1.5 %collective-permute-start = (f32[168,256]{1,0:T(8,128)S(1)}, f32[168,256]{1,0:T(8,128)S(1)}, u32[]{:S(2)}, u32[]{:S(2)}) collective-permute-start(f32[168,256]{1,0:T(8,128)S(1)} %copy-done.8), channel_id=1, source_target_pairs={{0,1},{1,0},{2,3},{3,2},{4,5},{5,4},{6,7},{7,6},{8,9},{9,8},{10,11... | collective-permute-start | bytes 516104 | tf_op jit(solution)/shard_map/ppermute | solution.py:547
  18.1 6.5 %collective-permute-start.1 = (f32[168,256]{1,0:T(8,128)S(1)}, f32[168,256]{1,0:T(8,128)S(1)}, u32[]{:S(2)}, u32[]{:S(2)}) collective-permute-start(f32[168,256]{1,0:T(8,128)S(1)} %add.6.own_ref), channel_id=1, source_target_pairs={{0,2},{1,3},{2,0},{3,1},{4,6},{5,7},{6,4},{7,5},{8,10},{9,11},{10,... | collective-permute-start | bytes 516104 | tf_op jit(solution)/shard_map/ppermute | solution.py:547
  26.3 5.1 %copy-start.1 = (f32[5,128,128]{2,1,0:T(8,128)S(1)}, f32[5,128,128]{2,1,0:T(8,128)}, u32[]{:S(2)}) copy-start(f32[5,128,128]{2,1,0:T(8,128)} %star_coef_ref.5) | copy-start | bytes 983044
  26.3 5.1 %copy-start.3 = (s32[128,128]{1,0:T(8,128)S(1)}, s32[128,128]{1,0:T(8,128)}, u32[]{:S(2)}) copy-start(s32[128,128]{1,0:T(8,128)} %star_ref.5) | copy-start | bytes 196612
  26.3 14.2 %all-to-all-start.1 = ((f32[8,72,128]{2,1,0:T(8,128)}), f32[8,72,128]{2,1,0:T(8,128)S(1)}, u32[]{:S(2)}, u32[]{:S(2)}) async-start(f32[8,72,128]{2,1,0:T(8,128)} %get-tuple-element.21), calls=%async_computation.1 | async-start | bytes 589824 | tf_op jit(solution)/shard_map/all_to_all | solution.py:544
  31.4 9.0 %copy-start.2 = (f32[4,128,128]{2,1,0:T(8,128)S(1)}, f32[4,128,128]{2,1,0:T(8,128)}, u32[]{:S(2)}) copy-start(f32[4,128,128]{2,1,0:T(8,128)} %att_coef_ref.3) | copy-start | bytes 786436
  31.5 9.0 %copy-start.4 = (s32[128,128]{1,0:T(8,128)S(1)}, s32[128,128]{1,0:T(8,128)}, u32[]{:S(2)}) copy-start(s32[128,128]{1,0:T(8,128)} %knot_ref.3) | copy-start | bytes 196612
  31.5 9.0 %copy-start.5 = (f32[128,128]{1,0:T(8,128)S(1)}, f32[128,128]{1,0:T(8,128)}, u32[]{:S(2)}) copy-start(f32[128,128]{1,0:T(8,128)} %frac_ref.3) | copy-start | bytes 196612
  31.5 9.0 %copy-start.6 = (f32[128,128]{1,0:T(8,128)S(1)}, f32[128,128]{1,0:T(8,128)}, u32[]{:S(2)}) copy-start(f32[128,128]{1,0:T(8,128)} %cal_coef_ref.3) | copy-start | bytes 196612
  31.5 9.0 %copy-start.7 = (s32[128]{0:T(128)S(1)}, s32[128]{0:T(128)}, u32[]{:S(2)}) copy-start(s32[128]{0:T(128)} %param.15) | copy-start | bytes 1540
  50.1 12.2 %all-to-all-start.2 = ((f32[8,32,256]{2,1,0:T(8,128)}), f32[8,32,256]{2,1,0:T(8,128)S(1)}, u32[]{:S(2)}, u32[]{:S(2)}) async-start(f32[8,32,256]{2,1,0:T(8,128)} %get-tuple-element.22), calls=%async_computation.2 | async-start | bytes 524288 | tf_op jit(solution)/shard_map/all_to_all | solution.py:544
  53.7 1.4 %collective-permute-start.2 = (f32[168,256]{1,0:T(8,128)S(1)}, f32[168,256]{1,0:T(8,128)S(1)}, u32[]{:S(2)}, u32[]{:S(2)}) collective-permute-start(f32[168,256]{1,0:T(8,128)S(1)} %get-tuple-element.23), channel_id=1, source_target_pairs={{0,1},{1,0},{2,3},{3,2},{4,5},{5,4},{6,7},{7,6},{8,9},{9,8},{10,11... | collective-permute-start | bytes 516104 | tf_op jit(solution)/shard_map/ppermute | solution.py:547
  55.1 6.5 %collective-permute-start.3 = (f32[168,256]{1,0:T(8,128)S(1)}, f32[168,256]{1,0:T(8,128)S(1)}, u32[]{:S(2)}, u32[]{:S(2)}) collective-permute-start(f32[168,256]{1,0:T(8,128)S(1)} %add.7.own_ref), channel_id=1, source_target_pairs={{0,2},{1,3},{2,0},{3,1},{4,6},{5,7},{6,4},{7,5},{8,10},{9,11},{10,... | collective-permute-start | bytes 516104 | tf_op jit(solution)/shard_map/ppermute | solution.py:547
  63.0 14.4 %all-to-all-start.3 = ((f32[8,72,128]{2,1,0:T(8,128)}), f32[8,72,128]{2,1,0:T(8,128)S(1)}, u32[]{:S(2)}, u32[]{:S(2)}) async-start(f32[8,72,128]{2,1,0:T(8,128)} %get-tuple-element.25), calls=%async_computation.3 | async-start | bytes 589824 | tf_op jit(solution)/shard_map/all_to_all | solution.py:544
  81.5 11.9 %all-to-all-start.4 = ((f32[32,8,128]{2,1,0:T(8,128)}), f32[32,8,128]{2,1,0:T(8,128)S(1)}, u32[]{:S(2)}, u32[]{:S(2)}) async-start(f32[32,8,128]{2,1,0:T(8,128)} %get-tuple-element.29), calls=%async_computation.4 | async-start | bytes 262144 | tf_op jit(solution)/shard_map/all_to_all | solution.py:544
  86.0 7.4 %copy-start = (f32[128,128]{1,0:T(8,128)S(1)}, f32[128,128]{1,0:T(8,128)}, u32[]{:S(2)}) copy-start(f32[128,128]{1,0:T(8,128)} %value_ref.1) | copy-start | bytes 196612

commit v15 on v14

--- a/solution.py
+++ b/solution.py
@@ -327,8 +327,8 @@
         beyond.append(pltpu.roll(moved, 4, 0) if comp % 2 else moved)
     beyond = [jnp.where(row < 4, beyond[0], beyond[1]), jnp.where(row < 4, beyond[2], beyond[3])]
     knot_high, knot_low = two_parts(jnp.concatenate([table[:KNOT_ROWS]] + beyond, axis=0))
-    knot_parts_ref[:KNOT_HALF] = knot_high
-    knot_parts_ref[KNOT_HALF:] = knot_low
+    knot_parts_ref[:, :COARSE] = knot_high
+    knot_parts_ref[:, COARSE:] = knot_low
 
     blocks = jnp.concatenate([table[KNOT_ROWS:, :128], table[KNOT_ROWS:, 128:]], axis=0)
     rows = product(
@@ -341,7 +341,7 @@
     rows = pl.ds(first, WIDE_GROUP)
     coef = [att_coef_ref[comp, rows, :] for comp in range(4)]
     hot, columns = factors
-    found = product(knot_parts_ref[...], hot, ((1,), (0,)))
+    found = product(knot_parts_ref[...], jnp.concatenate([hot, hot], axis=0), ((1,), (0,)))
     width = cal_ref.shape[1]
     image_rows = []
     for tile in range(WIDE_GROUP):
@@ -349,10 +349,7 @@
         across = slice(tile * width, (tile + 1) * width)
 
         def part(begin, size):
-            return (
-                found[begin : begin + size, across]
-                + found[KNOT_HALF + begin : KNOT_HALF + begin + size, across]
-            )
+            return found[begin : begin + size, across]
 
         near, past = columns[tile]
         near = near * sum(coef[comp][here] * part(comp * FINE, FINE) for comp in range(4))
@@ -486,7 +483,7 @@
     star_shape = shaped(STAR_ROWS, COARSE)
     sent_shapes = (shaped(n_stars, TABLE_ROWS // n_stars, COARSE), shaped(STAR_ROWS + 8, COARSE))
     sums = [pltpu.VMEM((2 * KNOT_HALF, COARSE), F32), pltpu.VMEM((2 * STAR_ROWS, COARSE), F32)]
-    ready = [pltpu.VMEM((2 * KNOT_HALF, COARSE), BF16), pltpu.VMEM((tile_count, width), F32)]
+    ready = [pltpu.VMEM((KNOT_HALF, 2 * COARSE), BF16), pltpu.VMEM((tile_count, width), F32)]
 
     def first_scatter():
         observed = (obs_value, cal_coef, tile_row, obs_knot, obs_frac, att_coef, obs_star, star_coef)

time: 95.1 us -> 95.3 us (level)
  no operation moved by 1% of the time
where the time goes in v15:
time: 95.3 us; the launch traced here: 94.7 us
  Pallas kernels  32.9 us (35%)
  waiting for transfers between devices  30.8 us (32%)
  starting transfers between devices  28.4 us (30%)
  between operations  1.48 us (2%)
  local copies, waits for them, and re-layouts  1.08 us (1%)
    all_to_all x5, starting transfers between devices, swap(): return lax.all_to_all(blocks, axes, 0, 0)  25.2 us
    all_to_all x5, waiting for transfers between devices, swap(): return lax.all_to_all(blocks, axes, 0, 0)  18.2 us
    ppermute x4, waiting for transfers between devices, partner(): lax.ppermute(array, axis, [(i, i ^ distance) for i in range(lax.axis_size...  12.6 us
    pallas_call x1, Pallas kernels, middle(): pl.pallas_call(functools.partial(middle_kernel, n_stars, n_seg), out_shap...  9.77 us
    pallas_call x2, Pallas kernels, star_forward(): pl.pallas_call(star_forward_kernel, out_shape=image_shape, in_specs=in_vm...  8.5 us
    pallas_call x1, Pallas kernels, first_scatter(): pl.pallas_call(first_kernel, out_shape=sent_shapes, in_specs=in_smem(2) +...  7.92 us
    pallas_call x1, Pallas kernels, last_gather(): pl.pallas_call(functools.partial(last_kernel, n_stars, n_seg), out_shape=...  4.18 us
    ppermute x4, starting transfers between devices, partner(): lax.ppermute(array, axis, [(i, i ^ distance) for i in range(lax.axis_size...  3.24 us
  transfers between devices with their start and end apart: 9, of which 9 were waited for; matrix products, arithmetic and copies ran while one was open for 1% of the time, Pallas kernels for 9%

profile of v15, /device:TPU:0, one launch (start us, length us, event | category | flops | bytes accessed | tf_op | source)
XLA Modules:
  0.0 94.7 jit_solution(5660323869345360402)
XLA Ops:
  1.3 7.9 %first_scatter.1 = (f32[8,32,256]{2,1,0:T(8,128)}, f32[168,256]{1,0:T(8,128)}) custom-call(s32[1]{0:T(128)S(6)} %copy.17.live_ref, s32[1]{0:T(128)} %bitcast.place_ref, f32[128,128]{1,0:T(8,128)} %value_ref.1, f32[128,128]{1,0:T(8,128)} %cal_coef_ref.3, s32[1,128]{1,0:T(1,128)} %bitcast.6, s32[128,128]{1,0:T(8,128)} %knot_ref.3, f32[128,128]{1,0:T(8,128)} %frac_ref.3, ...), custom_call_target="tpu_custom_call" | custom-call | flops 3000000000 | bytes 1000000 | tf_op jit(solution)/shard_map/first_scatter/pallas_call | solution.py:491
  9.2 7.4 %all-to-all-start = ((f32[8,32,256]{2,1,0:T(8,128)}), f32[8,32,256]{2,1,0:T(8,128)S(1)}, u32[]{:S(2)}, u32[]{:S(2)}) async-start(f32[8,32,256]{2,1,0:T(8,128)} %get-tuple-element.18), calls=%async_computation | async-start | bytes 524288 | tf_op jit(solution)/shard_map/all_to_all | solution.py:541
  16.7 1.4 %collective-permute-done = f32[168,256]{1,0:T(8,128)S(1)} collective-permute-done((f32[168,256]{1,0:T(8,128)S(1)}, f32[168,256]{1,0:T(8,128)S(1)}, u32[]{:S(2)}, u32[]{:S(2)}) %collective-permute-start) | collective-permute-done | bytes 172064 | tf_op jit(solution)/shard_map/ppermute | solution.py:544
  18.1 1.6 %collective-permute-start.1 = (f32[168,256]{1,0:T(8,128)S(1)}, f32[168,256]{1,0:T(8,128)S(1)}, u32[]{:S(2)}, u32[]{:S(2)}) collective-permute-start(f32[168,256]{1,0:T(8,128)S(1)} %add.6.own_ref), channel_id=1, source_target_pairs={{0,2},{1,3},{2,0},{3,1},{4,6},{5,7},{6,4},{7,5},{8,10},{9,11},{10,... | collective-permute-start | bytes 516104 | tf_op jit(solution)/shard_map/ppermute | solution.py:544
  19.7 4.9 %collective-permute-done.1.other_ref = f32[168,256]{1,0:T(8,128)S(1)} collective-permute-done((f32[168,256]{1,0:T(8,128)S(1)}, f32[168,256]{1,0:T(8,128)S(1)}, u32[]{:S(2)}, u32[]{:S(2)}) %collective-permute-start.1) | collective-permute-done | bytes 172064 | tf_op jit(solution)/shard_map/ppermute | solution.py:544
  24.6 0.9 all-to-all-done.block_ref
  25.5 0.7 table_sum.2
  26.3 5.1 %all-to-all-start.1 = ((f32[8,72,128]{2,1,0:T(8,128)}), f32[8,72,128]{2,1,0:T(8,128)S(1)}, u32[]{:S(2)}, u32[]{:S(2)}) async-start(f32[8,72,128]{2,1,0:T(8,128)} %get-tuple-element.21), calls=%async_computation.1 | async-start | bytes 589824 | tf_op jit(solution)/shard_map/all_to_all | solution.py:541
  31.5 4.2 %star_forward.2.star_image_ref = f32[128,128]{1,0:T(8,128)S(1)} custom-call(s32[128,128]{1,0:T(8,128)S(1)} %copy-done.3, f32[5,128,128]{2,1,0:T(8,128)S(1)} %copy-done.1, f32[160,256]{1,0:T(8,128)S(1)} %get-tuple-element.20.star_x_ref.star_0_ref), custom_call_target="tpu_custom_call" | custom-call | flops 3000000000 | bytes 1000000 | tf_op jit(solution)/shard_map/star_forward/pallas_call | solution.py:529
  35.8 4.7 %all-to-all-done.1.block_ref = f32[8,72,128]{2,1,0:T(8,128)S(1)} async-done(((f32[8,72,128]{2,1,0:T(8,128)}), f32[8,72,128]{2,1,0:T(8,128)S(1)}, u32[]{:S(2)}, u32[]{:S(2)}) %all-to-all-start.1) | async-done | bytes 294944 | tf_op jit(solution)/shard_map/all_to_all | solution.py:541
  40.5 9.8 %gather_and_scatter.1 = (f32[128,128]{1,0:T(8,128)S(1)}, f32[256,256]{1,0:T(8,128)S(1)}, f32[8,32,256]{2,1,0:T(8,128)}, f32[168,256]{1,0:T(8,128)S(1)}) custom-call(s32[1]{0:T(128)S(6)} %copy.17.live_ref, s32[1]{0:T(128)} %bitcast.place_ref, s32[128,128]{1,0:T(8,128)S(1)} %copy-done.4, f32[128,128]{1,0:T(8,128)S(1)} %copy-done.5, ...), custom_call_target="tpu_custom_call" | custom-call | flops 3000000000 | bytes 1000000 | tf_op jit(solution)/shard_map/gather_and_scatter/pallas_call | solution.py:504
  50.3 3.6 %all-to-all-start.2 = ((f32[8,32,256]{2,1,0:T(8,128)}), f32[8,32,256]{2,1,0:T(8,128)S(1)}, u32[]{:S(2)}, u32[]{:S(2)}) async-start(f32[8,32,256]{2,1,0:T(8,128)} %get-tuple-element.22), calls=%async_computation.2 | async-start | bytes 524288 | tf_op jit(solution)/shard_map/all_to_all | solution.py:541
  53.9 1.4 %collective-permute-done.2 = f32[168,256]{1,0:T(8,128)S(1)} collective-permute-done((f32[168,256]{1,0:T(8,128)S(1)}, f32[168,256]{1,0:T(8,128)S(1)}, u32[]{:S(2)}, u32[]{:S(2)}) %collective-permute-start.2) | collective-permute-done | bytes 172064 | tf_op jit(solution)/shard_map/ppermute | solution.py:544
  55.3 1.6 %collective-permute-start.3 = (f32[168,256]{1,0:T(8,128)S(1)}, f32[168,256]{1,0:T(8,128)S(1)}, u32[]{:S(2)}, u32[]{:S(2)}) collective-permute-start(f32[168,256]{1,0:T(8,128)S(1)} %add.7.own_ref), channel_id=1, source_target_pairs={{0,2},{1,3},{2,0},{3,1},{4,6},{5,7},{6,4},{7,5},{8,10},{9,11},{10,... | collective-permute-start | bytes 516104 | tf_op jit(solution)/shard_map/ppermute | solution.py:544
  56.9 4.9 %collective-permute-done.3.other_ref = f32[168,256]{1,0:T(8,128)S(1)} collective-permute-done((f32[168,256]{1,0:T(8,128)S(1)}, f32[168,256]{1,0:T(8,128)S(1)}, u32[]{:S(2)}, u32[]{:S(2)}) %collective-permute-start.3) | collective-permute-done | bytes 172064 | tf_op jit(solution)/shard_map/ppermute | solution.py:544
  61.8 0.6 all-to-all-done.2.block_ref
  62.4 0.7 table_sum.3
  63.2 5.4 %all-to-all-start.3 = ((f32[8,72,128]{2,1,0:T(8,128)}), f32[8,72,128]{2,1,0:T(8,128)S(1)}, u32[]{:S(2)}, u32[]{:S(2)}) async-start(f32[8,72,128]{2,1,0:T(8,128)} %get-tuple-element.25), calls=%async_computation.3 | async-start | bytes 589824 | tf_op jit(solution)/shard_map/all_to_all | solution.py:541
  68.5 4.2 %star_forward.3.star_image_ref = f32[128,128]{1,0:T(8,128)S(1)} custom-call(s32[128,128]{1,0:T(8,128)S(1)} %copy-done.3, f32[5,128,128]{2,1,0:T(8,128)S(1)} %copy-done.1, f32[160,256]{1,0:T(8,128)S(1)} %get-tuple-element.24.star_x_ref), custom_call_target="tpu_custom_call" | custom-call | flops 3000000000 | bytes 1000000 | tf_op jit(solution)/shard_map/star_forward/pallas_call | solution.py:529
  72.8 4.8 %all-to-all-done.3.block_ref = f32[8,72,128]{2,1,0:T(8,128)S(1)} async-done(((f32[8,72,128]{2,1,0:T(8,128)}), f32[8,72,128]{2,1,0:T(8,128)S(1)}, u32[]{:S(2)}, u32[]{:S(2)}) %all-to-all-start.3) | async-done | bytes 294944 | tf_op jit(solution)/shard_map/all_to_all | solution.py:541
  77.6 4.2 %last_gather.1 = (f32[128,128]{1,0:T(8,128)S(1)}, f32[256,256]{1,0:T(8,128)S(1)}, f32[32,8,128]{2,1,0:T(8,128)}, f32[8,128]{1,0:T(8,128)S(1)}) custom-call(s32[1]{0:T(128)S(6)} %copy.17.live_ref, s32[1]{0:T(128)} %bitcast.place_ref, s32[128,128]{1,0:T(8,128)S(1)} %copy-done.4, f32[128,128]{1,0:T(8,128)S(1)} %copy-done.5, f32[4,128,128]{2,1,0:T(8,128)S(1)} %copy-done.2, ...), custom_call_target="tpu_custom_call" | custom-call | flops 3000000000 | bytes 1000000 | tf_op jit(solution)/shard_map/last_gather/pallas_call | solution.py:517
  81.8 3.7 %all-to-all-start.4 = ((f32[32,8,128]{2,1,0:T(8,128)}), f32[32,8,128]{2,1,0:T(8,128)S(1)}, u32[]{:S(2)}, u32[]{:S(2)}) async-start(f32[32,8,128]{2,1,0:T(8,128)} %get-tuple-element.29), calls=%async_computation.4 | async-start | bytes 262144 | tf_op jit(solution)/shard_map/all_to_all | solution.py:541
  86.6 7.1 %all-to-all-done.4.scalar_ref = f32[32,8,128]{2,1,0:T(8,128)S(1)} async-done(((f32[32,8,128]{2,1,0:T(8,128)}), f32[32,8,128]{2,1,0:T(8,128)S(1)}, u32[]{:S(2)}, u32[]{:S(2)}) %all-to-all-start.4) | async-done | bytes 131104 | tf_op jit(solution)/shard_map/all_to_all | solution.py:541
  93.7 1.0 %outputs.1 = (f32[5,8192]{1,0:T(8,128)}, f32[4,8192]{1,0:T(4,128)}, f32[256,128]{1,0:T(8,128)}, f32[128,128]{1,0:T(8,128)}) custom-call(s32[1]{0:T(128)S(6)} %copy.17.live_ref, f32[8,128]{1,0:T(8,128)S(1)} %get-tuple-element.28.own_scalar_ref, f32[32,8,128]{2,1,0:T(8,128)S(1)} %all-to-all-done.4.scalar_ref, f32[5,8192]{1,0:T(8,128)S(1)} %reshape.26.star_0_ref, ...), custom_call_target="tpu_custom_call" | custom-call | flops 1000000 | bytes 600000 | tf_op jit(solution)/shard_map/outputs/pallas_call | solution.py:575
  (30 shorter events, 1.2 us)
Async XLA Ops:
  9.2 7.4 %copy-start.8 = (f32[168,256]{1,0:T(8,128)S(1)}, f32[168,256]{1,0:T(8,128)}, u32[]{:S(2)}) copy-start(f32[168,256]{1,0:T(8,128)} %get-tuple-element.19) | copy-start | bytes 516100
  9.2 16.3 %all-to-all-start = ((f32[8,32,256]{2,1,0:T(8,128)}), f32[8,32,256]{2,1,0:T(8,128)S(1)}, u32[]{:S(2)}, u32[]{:S(2)}) async-start(f32[8,32,256]{2,1,0:T(8,128)} %get-tuple-element.18), calls=%async_computation | async-start | bytes 524288 | tf_op jit(solution)/shard_map/all_to_all | solution.py:541
  16.6 1.5 %collective-permute-start = (f32[168,256]{1,0:T(8,128)S(1)}, f32[168,256]{1,0:T(8,128)S(1)}, u32[]{:S(2)}, u32[]{:S(2)}) collective-permute-start(f32[168,256]{1,0:T(8,128)S(1)} %copy-done.8), channel_id=1, source_target_pairs={{0,1},{1,0},{2,3},{3,2},{4,5},{5,4},{6,7},{7,6},{8,9},{9,8},{10,11... | collective-permute-start | bytes 516104 | tf_op jit(solution)/shard_map/ppermute | solution.py:544
  18.1 6.5 %collective-permute-start.1 = (f32[168,256]{1,0:T(8,128)S(1)}, f32[168,256]{1,0:T(8,128)S(1)}, u32[]{:S(2)}, u32[]{:S(2)}) collective-permute-start(f32[168,256]{1,0:T(8,128)S(1)} %add.6.own_ref), channel_id=1, source_target_pairs={{0,2},{1,3},{2,0},{3,1},{4,6},{5,7},{6,4},{7,5},{8,10},{9,11},{10,... | collective-permute-start | bytes 516104 | tf_op jit(solution)/shard_map/ppermute | solution.py:544
  26.3 5.1 %copy-start.1 = (f32[5,128,128]{2,1,0:T(8,128)S(1)}, f32[5,128,128]{2,1,0:T(8,128)}, u32[]{:S(2)}) copy-start(f32[5,128,128]{2,1,0:T(8,128)} %star_coef_ref.5) | copy-start | bytes 983044
  26.3 5.1 %copy-start.3 = (s32[128,128]{1,0:T(8,128)S(1)}, s32[128,128]{1,0:T(8,128)}, u32[]{:S(2)}) copy-start(s32[128,128]{1,0:T(8,128)} %star_ref.5) | copy-start | bytes 196612
  26.3 14.2 %all-to-all-start.1 = ((f32[8,72,128]{2,1,0:T(8,128)}), f32[8,72,128]{2,1,0:T(8,128)S(1)}, u32[]{:S(2)}, u32[]{:S(2)}) async-start(f32[8,72,128]{2,1,0:T(8,128)} %get-tuple-element.21), calls=%async_computation.1 | async-start | bytes 589824 | tf_op jit(solution)/shard_map/all_to_all | solution.py:541
  31.4 9.0 %copy-start.2 = (f32[4,128,128]{2,1,0:T(8,128)S(1)}, f32[4,128,128]{2,1,0:T(8,128)}, u32[]{:S(2)}) copy-start(f32[4,128,128]{2,1,0:T(8,128)} %att_coef_ref.3) | copy-start | bytes 786436
  31.5 9.0 %copy-start.4 = (s32[128,128]{1,0:T(8,128)S(1)}, s32[128,128]{1,0:T(8,128)}, u32[]{:S(2)}) copy-start(s32[128,128]{1,0:T(8,128)} %knot_ref.3) | copy-start | bytes 196612
  31.5 9.0 %copy-start.5 = (f32[128,128]{1,0:T(8,128)S(1)}, f32[128,128]{1,0:T(8,128)}, u32[]{:S(2)}) copy-start(f32[128,128]{1,0:T(8,128)} %frac_ref.3) | copy-start | bytes 196612
  31.5 9.0 %copy-start.6 = (f32[128,128]{1,0:T(8,128)S(1)}, f32[128,128]{1,0:T(8,128)}, u32[]{:S(2)}) copy-start(f32[128,128]{1,0:T(8,128)} %cal_coef_ref.3) | copy-start | bytes 196612
  31.5 9.0 %copy-start.7 = (s32[128]{0:T(128)S(1)}, s32[128]{0:T(128)}, u32[]{:S(2)}) copy-start(s32[128]{0:T(128)} %param.15) | copy-start | bytes 1540
  50.3 12.1 %all-to-all-start.2 = ((f32[8,32,256]{2,1,0:T(8,128)}), f32[8,32,256]{2,1,0:T(8,128)S(1)}, u32[]{:S(2)}, u32[]{:S(2)}) async-start(f32[8,32,256]{2,1,0:T(8,128)} %get-tuple-element.22), calls=%async_computation.2 | async-start | bytes 524288 | tf_op jit(solution)/shard_map/all_to_all | solution.py:541
  53.9 1.4 %collective-permute-start.2 = (f32[168,256]{1,0:T(8,128)S(1)}, f32[168,256]{1,0:T(8,128)S(1)}, u32[]{:S(2)}, u32[]{:S(2)}) collective-permute-start(f32[168,256]{1,0:T(8,128)S(1)} %get-tuple-element.23), channel_id=1, source_target_pairs={{0,1},{1,0},{2,3},{3,2},{4,5},{5,4},{6,7},{7,6},{8,9},{9,8},{10,11... | collective-permute-start | bytes 516104 | tf_op jit(solution)/shard_map/ppermute | solution.py:544
  55.3 6.5 %collective-permute-start.3 = (f32[168,256]{1,0:T(8,128)S(1)}, f32[168,256]{1,0:T(8,128)S(1)}, u32[]{:S(2)}, u32[]{:S(2)}) collective-permute-start(f32[168,256]{1,0:T(8,128)S(1)} %add.7.own_ref), channel_id=1, source_target_pairs={{0,2},{1,3},{2,0},{3,1},{4,6},{5,7},{6,4},{7,5},{8,10},{9,11},{10,... | collective-permute-start | bytes 516104 | tf_op jit(solution)/shard_map/ppermute | solution.py:544
  63.2 14.4 %all-to-all-start.3 = ((f32[8,72,128]{2,1,0:T(8,128)}), f32[8,72,128]{2,1,0:T(8,128)S(1)}, u32[]{:S(2)}, u32[]{:S(2)}) async-start(f32[8,72,128]{2,1,0:T(8,128)} %get-tuple-element.25), calls=%async_computation.3 | async-start | bytes 589824 | tf_op jit(solution)/shard_map/all_to_all | solution.py:541
  81.8 11.9 %all-to-all-start.4 = ((f32[32,8,128]{2,1,0:T(8,128)}), f32[32,8,128]{2,1,0:T(8,128)S(1)}, u32[]{:S(2)}, u32[]{:S(2)}) async-start(f32[32,8,128]{2,1,0:T(8,128)} %get-tuple-element.29), calls=%async_computation.4 | async-start | bytes 262144 | tf_op jit(solution)/shard_map/all_to_all | solution.py:541
  86.3 7.4 %copy-start = (f32[128,128]{1,0:T(8,128)S(1)}, f32[128,128]{1,0:T(8,128)}, u32[]{:S(2)}) copy-start(f32[128,128]{1,0:T(8,128)} %value_ref.1) | copy-start | bytes 196612

commit v16 on v14

--- a/solution.py
+++ b/solution.py
@@ -424,7 +424,7 @@
     scalars = with_scalars(jnp.zeros((8, 128), F32), list(enumerate(scalars)))
     own_scalar_out[...] = scalars
     for device in range(scalar_out.shape[0]):
-        scalar_out[device] = scalars
+        scalar_out[device] = scalars[:1]
 
 
 def output_kernel(
@@ -519,7 +519,7 @@
         observed = (obs_knot, obs_frac, att_coef, cal_coef, tile_row)
         return pl.pallas_call(
             functools.partial(last_kernel, n_stars, n_seg),
-            out_shape=(image_shape, table_shape, shaped(n_stars * n_seg, 8, 128), shaped(8, 128)),
+            out_shape=(image_shape, table_shape, shaped(n_stars * n_seg, 1, 128), shaped(8, 128)),
             in_specs=in_smem(2) + in_vmem(len(observed) + len(received)),
             out_specs=tuple(in_vmem(4)),
             scratch_shapes=ready,

time: 95.1 us -> 93.8 us (0.986)
  waiting for transfers between devices: 30.8 us -> 29.6 us
    all_to_all x5, waiting for transfers between devices: 18.2 us -> 17 us  [swap(): return lax.all_to_all(blocks, axes, 0, 0)]
where the time goes in v16:
time: 93.8 us; the launch traced here: 93.2 us
  Pallas kernels  32.5 us (35%)
  waiting for transfers between devices  29.6 us (32%)
  starting transfers between devices  28.5 us (30%)
  between operations  1.48 us (2%)
  local copies, waits for them, and re-layouts  1.08 us (1%)
    all_to_all x5, starting transfers between devices, swap(): return lax.all_to_all(blocks, axes, 0, 0)  25.2 us
    all_to_all x5, waiting for transfers between devices, swap(): return lax.all_to_all(blocks, axes, 0, 0)  17 us
    ppermute x4, waiting for transfers between devices, partner(): lax.ppermute(array, axis, [(i, i ^ distance) for i in range(lax.axis_size...  12.6 us
    pallas_call x1, Pallas kernels, middle(): pl.pallas_call(functools.partial(middle_kernel, n_stars, n_seg), out_shap...  9.55 us
    pallas_call x2, Pallas kernels, star_forward(): pl.pallas_call(star_forward_kernel, out_shape=image_shape, in_specs=in_vm...  8.5 us
    pallas_call x1, Pallas kernels, first_scatter(): pl.pallas_call(first_kernel, out_shape=sent_shapes, in_specs=in_smem(2) +...  7.92 us
    pallas_call x1, Pallas kernels, last_gather(): pl.pallas_call(functools.partial(last_kernel, n_stars, n_seg), out_shape=...  4.04 us
    ppermute x4, starting transfers between devices, partner(): lax.ppermute(array, axis, [(i, i ^ distance) for i in range(lax.axis_size...  3.24 us
  transfers between devices with their start and end apart: 9, of which 9 were waited for; matrix products, arithmetic and copies ran while one was open for 1% of the time, Pallas kernels for 9%

profile of v16, /device:TPU:0, one launch (start us, length us, event | category | flops | bytes accessed | tf_op | source)
XLA Modules:
  0.0 93.2 jit_solution(5541660864851447432)
XLA Ops:
  1.3 7.9 %first_scatter.1 = (f32[8,32,256]{2,1,0:T(8,128)}, f32[168,256]{1,0:T(8,128)}) custom-call(s32[1]{0:T(128)S(6)} %copy.17.live_ref, s32[1]{0:T(128)} %bitcast.place_ref, f32[128,128]{1,0:T(8,128)} %value_ref.1, f32[128,128]{1,0:T(8,128)} %cal_coef_ref.3, s32[1,128]{1,0:T(1,128)} %bitcast.6, s32[128,128]{1,0:T(8,128)} %knot_ref.3, f32[128,128]{1,0:T(8,128)} %frac_ref.3, ...), custom_call_target="tpu_custom_call" | custom-call | flops 3000000000 | bytes 1000000 | tf_op jit(solution)/shard_map/first_scatter/pallas_call | solution.py:494
  9.2 7.4 %all-to-all-start = ((f32[8,32,256]{2,1,0:T(8,128)}), f32[8,32,256]{2,1,0:T(8,128)S(1)}, u32[]{:S(2)}, u32[]{:S(2)}) async-start(f32[8,32,256]{2,1,0:T(8,128)} %get-tuple-element.18), calls=%async_computation | async-start | bytes 524288 | tf_op jit(solution)/shard_map/all_to_all | solution.py:544
  16.7 1.4 %collective-permute-done = f32[168,256]{1,0:T(8,128)S(1)} collective-permute-done((f32[168,256]{1,0:T(8,128)S(1)}, f32[168,256]{1,0:T(8,128)S(1)}, u32[]{:S(2)}, u32[]{:S(2)}) %collective-permute-start) | collective-permute-done | bytes 172064 | tf_op jit(solution)/shard_map/ppermute | solution.py:547
  18.1 1.6 %collective-permute-start.1 = (f32[168,256]{1,0:T(8,128)S(1)}, f32[168,256]{1,0:T(8,128)S(1)}, u32[]{:S(2)}, u32[]{:S(2)}) collective-permute-start(f32[168,256]{1,0:T(8,128)S(1)} %add.6.own_ref), channel_id=1, source_target_pairs={{0,2},{1,3},{2,0},{3,1},{4,6},{5,7},{6,4},{7,5},{8,10},{9,11},{10,... | collective-permute-start | bytes 516104 | tf_op jit(solution)/shard_map/ppermute | solution.py:547
  19.7 4.9 %collective-permute-done.1.other_ref = f32[168,256]{1,0:T(8,128)S(1)} collective-permute-done((f32[168,256]{1,0:T(8,128)S(1)}, f32[168,256]{1,0:T(8,128)S(1)}, u32[]{:S(2)}, u32[]{:S(2)}) %collective-permute-start.1) | collective-permute-done | bytes 172064 | tf_op jit(solution)/shard_map/ppermute | solution.py:547
  24.6 0.9 all-to-all-done.block_ref
  25.5 0.7 table_sum.2
  26.3 5.1 %all-to-all-start.1 = ((f32[8,72,128]{2,1,0:T(8,128)}), f32[8,72,128]{2,1,0:T(8,128)S(1)}, u32[]{:S(2)}, u32[]{:S(2)}) async-start(f32[8,72,128]{2,1,0:T(8,128)} %get-tuple-element.21), calls=%async_computation.1 | async-start | bytes 589824 | tf_op jit(solution)/shard_map/all_to_all | solution.py:544
  31.5 4.2 %star_forward.2.star_image_ref = f32[128,128]{1,0:T(8,128)S(1)} custom-call(s32[128,128]{1,0:T(8,128)S(1)} %copy-done.3, f32[5,128,128]{2,1,0:T(8,128)S(1)} %copy-done.1, f32[160,256]{1,0:T(8,128)S(1)} %get-tuple-element.20.star_x_ref.star_0_ref), custom_call_target="tpu_custom_call" | custom-call | flops 3000000000 | bytes 1000000 | tf_op jit(solution)/shard_map/star_forward/pallas_call | solution.py:532
  35.8 4.7 %all-to-all-done.1.block_ref = f32[8,72,128]{2,1,0:T(8,128)S(1)} async-done(((f32[8,72,128]{2,1,0:T(8,128)}), f32[8,72,128]{2,1,0:T(8,128)S(1)}, u32[]{:S(2)}, u32[]{:S(2)}) %all-to-all-start.1) | async-done | bytes 294944 | tf_op jit(solution)/shard_map/all_to_all | solution.py:544
  40.5 9.6 %gather_and_scatter.1 = (f32[128,128]{1,0:T(8,128)S(1)}, f32[256,256]{1,0:T(8,128)S(1)}, f32[8,32,256]{2,1,0:T(8,128)}, f32[168,256]{1,0:T(8,128)S(1)}) custom-call(s32[1]{0:T(128)S(6)} %copy.17.live_ref, s32[1]{0:T(128)} %bitcast.place_ref, s32[128,128]{1,0:T(8,128)S(1)} %copy-done.4, f32[128,128]{1,0:T(8,128)S(1)} %copy-done.5, ...), custom_call_target="tpu_custom_call" | custom-call | flops 3000000000 | bytes 1000000 | tf_op jit(solution)/shard_map/gather_and_scatter/pallas_call | solution.py:507
  50.1 3.6 %all-to-all-start.2 = ((f32[8,32,256]{2,1,0:T(8,128)}), f32[8,32,256]{2,1,0:T(8,128)S(1)}, u32[]{:S(2)}, u32[]{:S(2)}) async-start(f32[8,32,256]{2,1,0:T(8,128)} %get-tuple-element.22), calls=%async_computation.2 | async-start | bytes 524288 | tf_op jit(solution)/shard_map/all_to_all | solution.py:544
  53.7 1.4 %collective-permute-done.2 = f32[168,256]{1,0:T(8,128)S(1)} collective-permute-done((f32[168,256]{1,0:T(8,128)S(1)}, f32[168,256]{1,0:T(8,128)S(1)}, u32[]{:S(2)}, u32[]{:S(2)}) %collective-permute-start.2) | collective-permute-done | bytes 172064 | tf_op jit(solution)/shard_map/ppermute | solution.py:547
  55.1 1.6 %collective-permute-start.3 = (f32[168,256]{1,0:T(8,128)S(1)}, f32[168,256]{1,0:T(8,128)S(1)}, u32[]{:S(2)}, u32[]{:S(2)}) collective-permute-start(f32[168,256]{1,0:T(8,128)S(1)} %add.7.own_ref), channel_id=1, source_target_pairs={{0,2},{1,3},{2,0},{3,1},{4,6},{5,7},{6,4},{7,5},{8,10},{9,11},{10,... | collective-permute-start | bytes 516104 | tf_op jit(solution)/shard_map/ppermute | solution.py:547
  56.7 4.9 %collective-permute-done.3.other_ref = f32[168,256]{1,0:T(8,128)S(1)} collective-permute-done((f32[168,256]{1,0:T(8,128)S(1)}, f32[168,256]{1,0:T(8,128)S(1)}, u32[]{:S(2)}, u32[]{:S(2)}) %collective-permute-start.3) | collective-permute-done | bytes 172064 | tf_op jit(solution)/shard_map/ppermute | solution.py:547
  61.6 0.6 all-to-all-done.2.block_ref
  62.2 0.7 table_sum.3
  63.0 5.4 %all-to-all-start.3 = ((f32[8,72,128]{2,1,0:T(8,128)}), f32[8,72,128]{2,1,0:T(8,128)S(1)}, u32[]{:S(2)}, u32[]{:S(2)}) async-start(f32[8,72,128]{2,1,0:T(8,128)} %get-tuple-element.25), calls=%async_computation.3 | async-start | bytes 589824 | tf_op jit(solution)/shard_map/all_to_all | solution.py:544
  68.4 4.2 %star_forward.3.star_image_ref = f32[128,128]{1,0:T(8,128)S(1)} custom-call(s32[128,128]{1,0:T(8,128)S(1)} %copy-done.3, f32[5,128,128]{2,1,0:T(8,128)S(1)} %copy-done.1, f32[160,256]{1,0:T(8,128)S(1)} %get-tuple-element.24.star_x_ref), custom_call_target="tpu_custom_call" | custom-call | flops 3000000000 | bytes 1000000 | tf_op jit(solution)/shard_map/star_forward/pallas_call | solution.py:532
  72.6 4.8 %all-to-all-done.3.block_ref = f32[8,72,128]{2,1,0:T(8,128)S(1)} async-done(((f32[8,72,128]{2,1,0:T(8,128)}), f32[8,72,128]{2,1,0:T(8,128)S(1)}, u32[]{:S(2)}, u32[]{:S(2)}) %all-to-all-start.3) | async-done | bytes 294944 | tf_op jit(solution)/shard_map/all_to_all | solution.py:544
  77.4 4.0 %last_gather.1 = (f32[128,128]{1,0:T(8,128)S(1)}, f32[256,256]{1,0:T(8,128)S(1)}, f32[32,1,128]{2,1,0:T(1,128)}, f32[8,128]{1,0:T(8,128)S(1)}) custom-call(s32[1]{0:T(128)S(6)} %copy.17.live_ref, s32[1]{0:T(128)} %bitcast.place_ref, s32[128,128]{1,0:T(8,128)S(1)} %copy-done.4, f32[128,128]{1,0:T(8,128)S(1)} %copy-done.5, f32[4,128,128]{2,1,0:T(8,128)S(1)} %copy-done.2, ...), custom_call_target="tpu_custom_call" | custom-call | flops 3000000000 | bytes 1000000 | tf_op jit(solution)/shard_map/last_gather/pallas_call | solution.py:520
  81.5 3.7 %all-to-all-start.4 = ((f32[32,1,128]{2,1,0:T(1,128)}), f32[32,1,128]{2,1,0:T(1,128)S(1)}, u32[]{:S(2)}, u32[]{:S(2)}) async-start(f32[32,1,128]{2,1,0:T(1,128)} %get-tuple-element.29), calls=%async_computation.4 | async-start | bytes 32768 | tf_op jit(solution)/shard_map/all_to_all | solution.py:544
  86.2 6.0 %all-to-all-done.4.scalar_ref = f32[32,1,128]{2,1,0:T(1,128)S(1)} async-done(((f32[32,1,128]{2,1,0:T(1,128)}), f32[32,1,128]{2,1,0:T(1,128)S(1)}, u32[]{:S(2)}, u32[]{:S(2)}) %all-to-all-start.4) | async-done | bytes 16416 | tf_op jit(solution)/shard_map/all_to_all | solution.py:544
  92.2 1.0 %outputs.1 = (f32[5,8192]{1,0:T(8,128)}, f32[4,8192]{1,0:T(4,128)}, f32[256,128]{1,0:T(8,128)}, f32[128,128]{1,0:T(8,128)}) custom-call(s32[1]{0:T(128)S(6)} %copy.17.live_ref, f32[8,128]{1,0:T(8,128)S(1)} %get-tuple-element.28.own_scalar_ref, f32[32,1,128]{2,1,0:T(1,128)S(1)} %all-to-all-done.4.scalar_ref, f32[5,8192]{1,0:T(8,128)S(1)} %reshape.26.star_0_ref, ...), custom_call_target="tpu_custom_call" | custom-call | flops 1000000 | bytes 600000 | tf_op jit(solution)/shard_map/outputs/pallas_call | solution.py:578
  (30 shorter events, 1.2 us)
Async XLA Ops:
  9.2 7.4 %copy-start.8 = (f32[168,256]{1,0:T(8,128)S(1)}, f32[168,256]{1,0:T(8,128)}, u32[]{:S(2)}) copy-start(f32[168,256]{1,0:T(8,128)} %get-tuple-element.19) | copy-start | bytes 516100
  9.2 16.3 %all-to-all-start = ((f32[8,32,256]{2,1,0:T(8,128)}), f32[8,32,256]{2,1,0:T(8,128)S(1)}, u32[]{:S(2)}, u32[]{:S(2)}) async-start(f32[8,32,256]{2,1,0:T(8,128)} %get-tuple-element.18), calls=%async_computation | async-start | bytes 524288 | tf_op jit(solution)/shard_map/all_to_all | solution.py:544
  16.6 1.5 %collective-permute-start = (f32[168,256]{1,0:T(8,128)S(1)}, f32[168,256]{1,0:T(8,128)S(1)}, u32[]{:S(2)}, u32[]{:S(2)}) collective-permute-start(f32[168,256]{1,0:T(8,128)S(1)} %copy-done.8), channel_id=1, source_target_pairs={{0,1},{1,0},{2,3},{3,2},{4,5},{5,4},{6,7},{7,6},{8,9},{9,8},{10,11... | collective-permute-start | bytes 516104 | tf_op jit(solution)/shard_map/ppermute | solution.py:547
  18.1 6.5 %collective-permute-start.1 = (f32[168,256]{1,0:T(8,128)S(1)}, f32[168,256]{1,0:T(8,128)S(1)}, u32[]{:S(2)}, u32[]{:S(2)}) collective-permute-start(f32[168,256]{1,0:T(8,128)S(1)} %add.6.own_ref), channel_id=1, source_target_pairs={{0,2},{1,3},{2,0},{3,1},{4,6},{5,7},{6,4},{7,5},{8,10},{9,11},{10,... | collective-permute-start | bytes 516104 | tf_op jit(solution)/shard_map/ppermute | solution.py:547
  26.3 5.1 %copy-start.1 = (f32[5,128,128]{2,1,0:T(8,128)S(1)}, f32[5,128,128]{2,1,0:T(8,128)}, u32[]{:S(2)}) copy-start(f32[5,128,128]{2,1,0:T(8,128)} %star_coef_ref.5) | copy-start | bytes 983044
  26.3 5.1 %copy-start.3 = (s32[128,128]{1,0:T(8,128)S(1)}, s32[128,128]{1,0:T(8,128)}, u32[]{:S(2)}) copy-start(s32[128,128]{1,0:T(8,128)} %star_ref.5) | copy-start | bytes 196612
  26.3 14.2 %all-to-all-start.1 = ((f32[8,72,128]{2,1,0:T(8,128)}), f32[8,72,128]{2,1,0:T(8,128)S(1)}, u32[]{:S(2)}, u32[]{:S(2)}) async-start(f32[8,72,128]{2,1,0:T(8,128)} %get-tuple-element.21), calls=%async_computation.1 | async-start | bytes 589824 | tf_op jit(solution)/shard_map/all_to_all | solution.py:544
  31.4 9.0 %copy-start.2 = (f32[4,128,128]{2,1,0:T(8,128)S(1)}, f32[4,128,128]{2,1,0:T(8,128)}, u32[]{:S(2)}) copy-start(f32[4,128,128]{2,1,0:T(8,128)} %att_coef_ref.3) | copy-start | bytes 786436
  31.5 9.0 %copy-start.4 = (s32[128,128]{1,0:T(8,128)S(1)}, s32[128,128]{1,0:T(8,128)}, u32[]{:S(2)}) copy-start(s32[128,128]{1,0:T(8,128)} %knot_ref.3) | copy-start | bytes 196612
  31.5 9.0 %copy-start.5 = (f32[128,128]{1,0:T(8,128)S(1)}, f32[128,128]{1,0:T(8,128)}, u32[]{:S(2)}) copy-start(f32[128,128]{1,0:T(8,128)} %frac_ref.3) | copy-start | bytes 196612
  31.5 9.0 %copy-start.6 = (f32[128,128]{1,0:T(8,128)S(1)}, f32[128,128]{1,0:T(8,128)}, u32[]{:S(2)}) copy-start(f32[128,128]{1,0:T(8,128)} %cal_coef_ref.3) | copy-start | bytes 196612
  31.5 9.0 %copy-start.7 = (s32[128]{0:T(128)S(1)}, s32[128]{0:T(128)}, u32[]{:S(2)}) copy-start(s32[128]{0:T(128)} %param.15) | copy-start | bytes 1540
  50.1 12.2 %all-to-all-start.2 = ((f32[8,32,256]{2,1,0:T(8,128)}), f32[8,32,256]{2,1,0:T(8,128)S(1)}, u32[]{:S(2)}, u32[]{:S(2)}) async-start(f32[8,32,256]{2,1,0:T(8,128)} %get-tuple-element.22), calls=%async_computation.2 | async-start | bytes 524288 | tf_op jit(solution)/shard_map/all_to_all | solution.py:544
  53.7 1.4 %collective-permute-start.2 = (f32[168,256]{1,0:T(8,128)S(1)}, f32[168,256]{1,0:T(8,128)S(1)}, u32[]{:S(2)}, u32[]{:S(2)}) collective-permute-start(f32[168,256]{1,0:T(8,128)S(1)} %get-tuple-element.23), channel_id=1, source_target_pairs={{0,1},{1,0},{2,3},{3,2},{4,5},{5,4},{6,7},{7,6},{8,9},{9,8},{10,11... | collective-permute-start | bytes 516104 | tf_op jit(solution)/shard_map/ppermute | solution.py:547
  55.1 6.5 %collective-permute-start.3 = (f32[168,256]{1,0:T(8,128)S(1)}, f32[168,256]{1,0:T(8,128)S(1)}, u32[]{:S(2)}, u32[]{:S(2)}) collective-permute-start(f32[168,256]{1,0:T(8,128)S(1)} %add.7.own_ref), channel_id=1, source_target_pairs={{0,2},{1,3},{2,0},{3,1},{4,6},{5,7},{6,4},{7,5},{8,10},{9,11},{10,... | collective-permute-start | bytes 516104 | tf_op jit(solution)/shard_map/ppermute | solution.py:547
  63.0 14.4 %all-to-all-start.3 = ((f32[8,72,128]{2,1,0:T(8,128)}), f32[8,72,128]{2,1,0:T(8,128)S(1)}, u32[]{:S(2)}, u32[]{:S(2)}) async-start(f32[8,72,128]{2,1,0:T(8,128)} %get-tuple-element.25), calls=%async_computation.3 | async-start | bytes 589824 | tf_op jit(solution)/shard_map/all_to_all | solution.py:544
  81.5 10.8 %all-to-all-start.4 = ((f32[32,1,128]{2,1,0:T(1,128)}), f32[32,1,128]{2,1,0:T(1,128)S(1)}, u32[]{:S(2)}, u32[]{:S(2)}) async-start(f32[32,1,128]{2,1,0:T(1,128)} %get-tuple-element.29), calls=%async_computation.4 | async-start | bytes 32768 | tf_op jit(solution)/shard_map/all_to_all | solution.py:544
  86.0 6.3 %copy-start = (f32[128,128]{1,0:T(8,128)S(1)}, f32[128,128]{1,0:T(8,128)}, u32[]{:S(2)}) copy-start(f32[128,128]{1,0:T(8,128)} %value_ref.1) | copy-start | bytes 196612

commit v17 on v16

--- a/solution.py
+++ b/solution.py
@@ -101,27 +101,27 @@
         out_ref[where // block, where % block : where % block + 8, :] = rows[offset : offset + 8]
 
 
-def knot_factors(first, knot_ref, frac_ref):
-    rows = pl.ds(first, WIDE_GROUP)
+def knot_factors(first, size, knot_ref, frac_ref):
+    rows = pl.ds(first, size)
     knot = knot_ref[rows, :]
     coarse, fine = knot >> 5, knot & (FINE - 1)
     weights = spline_weights(frac_ref[rows, :])
-    hot = [one_hot(coarse[tile : tile + 1], COARSE) for tile in range(WIDE_GROUP)]
-    columns = [near_and_past(weights, fine, tile) for tile in range(WIDE_GROUP)]
+    hot = [one_hot(coarse[tile : tile + 1], COARSE) for tile in range(size)]
+    columns = [near_and_past(weights, fine, tile) for tile in range(size)]
     return jnp.concatenate(hot, axis=1), columns
 
 
 def scatter(first, factors, values, observed, knot_acc, star_acc):
     att_coef_ref, star_ref, star_coef_ref = observed
-    rows = pl.ds(first, WIDE_GROUP)
     knot_hot, columns = factors
+    rows = pl.ds(first, len(columns))
     star = star_ref[rows, :]
     star_coarse, star_fine = star & (COARSE - 1), star >> 8
     terms = [att_coef_ref[comp, rows, :] * values for comp in range(4)]
     parts = [two_parts(star_coef_ref[comp, rows, :] * values) for comp in range(5)]
     parts = [pair[half].astype(F32) for half in range(2) for pair in parts]
     knot_left, star_left, star_right = [], [], []
-    for tile in range(WIDE_GROUP):
+    for tile in range(len(columns)):
         here = slice(tile, tile + 1)
         near, past = columns[tile]
         spread = jnp.concatenate(
@@ -217,7 +217,7 @@
         first = pl.multiple_of(group * WIDE_GROUP, WIDE_GROUP)
         values = value_ref[pl.ds(first, WIDE_GROUP), :]
         values = values * live_mask(live_ref, first, values.shape)
-        scatter(first, knot_factors(first, knot_ref, frac_ref), values, observed, knot_acc, star_acc)
+        scatter(first, knot_factors(first, WIDE_GROUP, knot_ref, frac_ref), values, observed, knot_acc, star_acc)
 
     scatter_end(place_ref, [], knot_acc, star_acc, table_out, star_out)
 
@@ -296,7 +296,7 @@
         edges = edges + block_ref[block, -8:, :]
 
     def slot(which):
-        return pltpu.roll(edges, 128 - SLOT * jnp.clip(which, 0, n_seg - 1), 1)
+        return pltpu.roll(edges, (128 - SLOT * jnp.clip(which, 0, n_seg - 1)) & 127, 1)
 
     before, own, after = slot(segment - 1), slot(segment), slot(segment + 1)
     before = jnp.where(segment > 0, before, 0.0)
@@ -338,13 +338,13 @@
 
 
 def gather(first, live_ref, factors, att_coef_ref, knot_parts_ref, cal_ref):
-    rows = pl.ds(first, WIDE_GROUP)
+    hot, columns = factors
+    rows = pl.ds(first, len(columns))
     coef = [att_coef_ref[comp, rows, :] for comp in range(4)]
-    hot, columns = factors
     found = product(knot_parts_ref[...], hot, ((1,), (0,)))
     width = cal_ref.shape[1]
     image_rows = []
-    for tile in range(WIDE_GROUP):
+    for tile in range(len(columns)):
         here = slice(tile, tile + 1)
         across = slice(tile * width, (tile + 1) * width)
 
@@ -378,18 +378,12 @@
     gather_ready(table, ahead, cal_coef_ref, tile_cal_ref, star_image_ref, knot_parts_ref, cal_ref)
     knot_acc[...] = jnp.zeros_like(knot_acc)
     star_acc[...] = jnp.zeros_like(star_acc)
-    def one_group(group, total):
-        first = pl.multiple_of(group * WIDE_GROUP, WIDE_GROUP)
-        factors = knot_factors(first, knot_ref, frac_ref)
-        image = gather(first, live_ref, factors, att_coef_ref, knot_parts_ref, cal_ref)
-        image_ref[pl.ds(first, WIDE_GROUP), :] = image
-        scatter(first, factors, image, (att_coef_ref, star_ref, star_coef_ref), knot_acc, star_acc)
-        return total + image * image
-
-    zero = jnp.zeros((WIDE_GROUP, knot_ref.shape[1]), F32)
-    total = lax.fori_loop(0, knot_ref.shape[0] // WIDE_GROUP, one_group, zero)
-    scatter_calibration(image_ref[...] * cal_coef_ref[...], tile_cal_ref, scatter_out)
-    scalars = [(0, norm), (1, jnp.sum(total, keepdims=True))]
+    factors = knot_factors(0, knot_ref.shape[0], knot_ref, frac_ref)
+    image = gather(0, live_ref, factors, att_coef_ref, knot_parts_ref, cal_ref)
+    image_ref[...] = image
+    scatter(0, factors, image, (att_coef_ref, star_ref, star_coef_ref), knot_acc, star_acc)
+    scatter_calibration(image * cal_coef_ref[...], tile_cal_ref, scatter_out)
+    scalars = [(0, norm), (1, squares(image))]
     scatter_end(place_ref, scalars, knot_acc, star_acc, scatter_out, star_out)
 
 
@@ -408,19 +402,13 @@
     )
     gather_ready(table, ahead, cal_coef_ref, tile_cal_ref, star_image_ref, knot_parts_ref, cal_ref)
 
-    def one_group(group, sums):
-        first = pl.multiple_of(group * WIDE_GROUP, WIDE_GROUP)
-        rows = pl.ds(first, WIDE_GROUP)
-        image_0 = image_0_ref[rows, :]
-        factors = knot_factors(first, knot_ref, frac_ref)
-        image = gather(first, live_ref, factors, att_coef_ref, knot_parts_ref, cal_ref)
-        image = image_0 - step * image
-        image_ref[rows, :] = image
-        return sums[0] + image * image, sums[1] + image * image_0
-
-    zero = jnp.zeros((WIDE_GROUP, knot_ref.shape[1]), F32)
-    sums = lax.fori_loop(0, knot_ref.shape[0] // WIDE_GROUP, one_group, (zero, zero))
-    scalars = [norm] + [jnp.sum(part, keepdims=True) for part in sums] + [norm_0, square_0]
+    factors = knot_factors(0, knot_ref.shape[0], knot_ref, frac_ref)
+    image_0 = image_0_ref[...]
+    image = gather(0, live_ref, factors, att_coef_ref, knot_parts_ref, cal_ref)
+    image = image_0 - step * image
+    image_ref[...] = image
+    cross = jnp.sum(image * image_0, keepdims=True)
+    scalars = [norm, squares(image), cross, norm_0, square_0]
     scalars = with_scalars(jnp.zeros((8, 128), F32), list(enumerate(scalars)))
     own_scalar_out[...] = scalars
     for device in range(scalar_out.shape[0]):

time: 93.8 us -> 93.1 us (level)
  no operation moved by 1% of the time
where the time goes in v17:
time: 93.1 us; the launch traced here: 92.5 us
  Pallas kernels  31.8 us (34%)
  waiting for transfers between devices  29.6 us (32%)
  starting transfers between devices  28.5 us (31%)
  between operations  1.48 us (2%)
  local copies, waits for them, and re-layouts  1.08 us (1%)
    all_to_all x5, starting transfers between devices, swap(): return lax.all_to_all(blocks, axes, 0, 0)  25.2 us
    all_to_all x5, waiting for transfers between devices, swap(): return lax.all_to_all(blocks, axes, 0, 0)  17 us
    ppermute x4, waiting for transfers between devices, partner(): lax.ppermute(array, axis, [(i, i ^ distance) for i in range(lax.axis_size...  12.6 us
    pallas_call x1, Pallas kernels, middle(): pl.pallas_call(functools.partial(middle_kernel, n_stars, n_seg), out_shap...  9.05 us
    pallas_call x2, Pallas kernels, star_forward(): pl.pallas_call(star_forward_kernel, out_shape=image_shape, in_specs=in_vm...  8.5 us
    pallas_call x1, Pallas kernels, first_scatter(): pl.pallas_call(first_kernel, out_shape=sent_shapes, in_specs=in_smem(2) +...  7.92 us
    pallas_call x1, Pallas kernels, last_gather(): pl.pallas_call(functools.partial(last_kernel, n_stars, n_seg), out_shape=...  3.76 us
    ppermute x4, starting transfers between devices, partner(): lax.ppermute(array, axis, [(i, i ^ distance) for i in range(lax.axis_size...  3.23 us
  transfers between devices with their start and end apart: 9, of which 9 were waited for; matrix products, arithmetic and copies ran while one was open for 1% of the time, Pallas kernels for 9%

profile of v17, /device:TPU:0, one launch (start us, length us, event | category | flops | bytes accessed | tf_op | source)
XLA Modules:
  0.0 92.5 jit_solution(2791161853176784297)
XLA Ops:
  1.3 7.9 %first_scatter.1 = (f32[8,32,256]{2,1,0:T(8,128)}, f32[168,256]{1,0:T(8,128)}) custom-call(s32[1]{0:T(128)S(6)} %copy.17.live_ref, s32[1]{0:T(128)} %bitcast.place_ref, f32[128,128]{1,0:T(8,128)} %value_ref.1, f32[128,128]{1,0:T(8,128)} %cal_coef_ref.3, s32[1,128]{1,0:T(1,128)} %bitcast.6, s32[128,128]{1,0:T(8,128)} %knot_ref.3, f32[128,128]{1,0:T(8,128)} %frac_ref.3, ...), custom_call_target="tpu_custom_call" | custom-call | flops 3000000000 | bytes 1000000 | tf_op jit(solution)/shard_map/first_scatter/pallas_call | solution.py:482
  9.2 7.4 %all-to-all-start = ((f32[8,32,256]{2,1,0:T(8,128)}), f32[8,32,256]{2,1,0:T(8,128)S(1)}, u32[]{:S(2)}, u32[]{:S(2)}) async-start(f32[8,32,256]{2,1,0:T(8,128)} %get-tuple-element.18), calls=%async_computation | async-start | bytes 524288 | tf_op jit(solution)/shard_map/all_to_all | solution.py:532
  16.7 1.4 %collective-permute-done = f32[168,256]{1,0:T(8,128)S(1)} collective-permute-done((f32[168,256]{1,0:T(8,128)S(1)}, f32[168,256]{1,0:T(8,128)S(1)}, u32[]{:S(2)}, u32[]{:S(2)}) %collective-permute-start) | collective-permute-done | bytes 172064 | tf_op jit(solution)/shard_map/ppermute | solution.py:535
  18.1 1.6 %collective-permute-start.1 = (f32[168,256]{1,0:T(8,128)S(1)}, f32[168,256]{1,0:T(8,128)S(1)}, u32[]{:S(2)}, u32[]{:S(2)}) collective-permute-start(f32[168,256]{1,0:T(8,128)S(1)} %add.6.own_ref), channel_id=1, source_target_pairs={{0,2},{1,3},{2,0},{3,1},{4,6},{5,7},{6,4},{7,5},{8,10},{9,11},{10,... | collective-permute-start | bytes 516104 | tf_op jit(solution)/shard_map/ppermute | solution.py:535
  19.7 4.9 %collective-permute-done.1.other_ref = f32[168,256]{1,0:T(8,128)S(1)} collective-permute-done((f32[168,256]{1,0:T(8,128)S(1)}, f32[168,256]{1,0:T(8,128)S(1)}, u32[]{:S(2)}, u32[]{:S(2)}) %collective-permute-start.1) | collective-permute-done | bytes 172064 | tf_op jit(solution)/shard_map/ppermute | solution.py:535
  24.6 0.9 all-to-all-done.block_ref
  25.5 0.7 table_sum.2
  26.3 5.1 %all-to-all-start.1 = ((f32[8,72,128]{2,1,0:T(8,128)}), f32[8,72,128]{2,1,0:T(8,128)S(1)}, u32[]{:S(2)}, u32[]{:S(2)}) async-start(f32[8,72,128]{2,1,0:T(8,128)} %get-tuple-element.21), calls=%async_computation.1 | async-start | bytes 589824 | tf_op jit(solution)/shard_map/all_to_all | solution.py:532
  31.5 4.2 %star_forward.2.star_image_ref = f32[128,128]{1,0:T(8,128)S(1)} custom-call(s32[128,128]{1,0:T(8,128)S(1)} %copy-done.3, f32[5,128,128]{2,1,0:T(8,128)S(1)} %copy-done.1, f32[160,256]{1,0:T(8,128)S(1)} %get-tuple-element.20.star_x_ref.star_0_ref), custom_call_target="tpu_custom_call" | custom-call | flops 3000000000 | bytes 1000000 | tf_op jit(solution)/shard_map/star_forward/pallas_call | solution.py:520
  35.8 4.7 %all-to-all-done.1.block_ref = f32[8,72,128]{2,1,0:T(8,128)S(1)} async-done(((f32[8,72,128]{2,1,0:T(8,128)}), f32[8,72,128]{2,1,0:T(8,128)S(1)}, u32[]{:S(2)}, u32[]{:S(2)}) %all-to-all-start.1) | async-done | bytes 294944 | tf_op jit(solution)/shard_map/all_to_all | solution.py:532
  40.5 9.0 %gather_and_scatter.1 = (f32[128,128]{1,0:T(8,128)S(1)}, f32[256,256]{1,0:T(8,128)S(1)}, f32[8,32,256]{2,1,0:T(8,128)}, f32[168,256]{1,0:T(8,128)S(1)}) custom-call(s32[1]{0:T(128)S(6)} %copy.17.live_ref, s32[1]{0:T(128)} %bitcast.place_ref, s32[128,128]{1,0:T(8,128)S(1)} %copy-done.4, f32[128,128]{1,0:T(8,128)S(1)} %copy-done.5, ...), custom_call_target="tpu_custom_call" | custom-call | flops 3000000000 | bytes 1000000 | tf_op jit(solution)/shard_map/gather_and_scatter/pallas_call | solution.py:495
  49.6 3.6 %all-to-all-start.2 = ((f32[8,32,256]{2,1,0:T(8,128)}), f32[8,32,256]{2,1,0:T(8,128)S(1)}, u32[]{:S(2)}, u32[]{:S(2)}) async-start(f32[8,32,256]{2,1,0:T(8,128)} %get-tuple-element.22), calls=%async_computation.2 | async-start | bytes 524288 | tf_op jit(solution)/shard_map/all_to_all | solution.py:532
  53.2 1.4 %collective-permute-done.2 = f32[168,256]{1,0:T(8,128)S(1)} collective-permute-done((f32[168,256]{1,0:T(8,128)S(1)}, f32[168,256]{1,0:T(8,128)S(1)}, u32[]{:S(2)}, u32[]{:S(2)}) %collective-permute-start.2) | collective-permute-done | bytes 172064 | tf_op jit(solution)/shard_map/ppermute | solution.py:535
  54.6 1.6 %collective-permute-start.3 = (f32[168,256]{1,0:T(8,128)S(1)}, f32[168,256]{1,0:T(8,128)S(1)}, u32[]{:S(2)}, u32[]{:S(2)}) collective-permute-start(f32[168,256]{1,0:T(8,128)S(1)} %add.7.own_ref), channel_id=1, source_target_pairs={{0,2},{1,3},{2,0},{3,1},{4,6},{5,7},{6,4},{7,5},{8,10},{9,11},{10,... | collective-permute-start | bytes 516104 | tf_op jit(solution)/shard_map/ppermute | solution.py:535
  56.2 4.9 %collective-permute-done.3.other_ref = f32[168,256]{1,0:T(8,128)S(1)} collective-permute-done((f32[168,256]{1,0:T(8,128)S(1)}, f32[168,256]{1,0:T(8,128)S(1)}, u32[]{:S(2)}, u32[]{:S(2)}) %collective-permute-start.3) | collective-permute-done | bytes 172064 | tf_op jit(solution)/shard_map/ppermute | solution.py:535
  61.1 0.6 all-to-all-done.2.block_ref
  61.7 0.7 table_sum.3
  62.5 5.4 %all-to-all-start.3 = ((f32[8,72,128]{2,1,0:T(8,128)}), f32[8,72,128]{2,1,0:T(8,128)S(1)}, u32[]{:S(2)}, u32[]{:S(2)}) async-start(f32[8,72,128]{2,1,0:T(8,128)} %get-tuple-element.25), calls=%async_computation.3 | async-start | bytes 589824 | tf_op jit(solution)/shard_map/all_to_all | solution.py:532
  67.8 4.2 %star_forward.3.star_image_ref = f32[128,128]{1,0:T(8,128)S(1)} custom-call(s32[128,128]{1,0:T(8,128)S(1)} %copy-done.3, f32[5,128,128]{2,1,0:T(8,128)S(1)} %copy-done.1, f32[160,256]{1,0:T(8,128)S(1)} %get-tuple-element.24.star_x_ref), custom_call_target="tpu_custom_call" | custom-call | flops 3000000000 | bytes 1000000 | tf_op jit(solution)/shard_map/star_forward/pallas_call | solution.py:520
  72.1 4.8 %all-to-all-done.3.block_ref = f32[8,72,128]{2,1,0:T(8,128)S(1)} async-done(((f32[8,72,128]{2,1,0:T(8,128)}), f32[8,72,128]{2,1,0:T(8,128)S(1)}, u32[]{:S(2)}, u32[]{:S(2)}) %all-to-all-start.3) | async-done | bytes 294944 | tf_op jit(solution)/shard_map/all_to_all | solution.py:532
  76.9 3.8 %last_gather.1 = (f32[128,128]{1,0:T(8,128)S(1)}, f32[256,256]{1,0:T(8,128)S(1)}, f32[32,1,128]{2,1,0:T(1,128)}, f32[8,128]{1,0:T(8,128)S(1)}) custom-call(s32[1]{0:T(128)S(6)} %copy.17.live_ref, s32[1]{0:T(128)} %bitcast.place_ref, s32[128,128]{1,0:T(8,128)S(1)} %copy-done.4, f32[128,128]{1,0:T(8,128)S(1)} %copy-done.5, f32[4,128,128]{2,1,0:T(8,128)S(1)} %copy-done.2, ...), custom_call_target="tpu_custom_call" | custom-call | flops 3000000000 | bytes 1000000 | tf_op jit(solution)/shard_map/last_gather/pallas_call | solution.py:508
  80.7 3.7 %all-to-all-start.4 = ((f32[32,1,128]{2,1,0:T(1,128)}), f32[32,1,128]{2,1,0:T(1,128)S(1)}, u32[]{:S(2)}, u32[]{:S(2)}) async-start(f32[32,1,128]{2,1,0:T(1,128)} %get-tuple-element.29), calls=%async_computation.4 | async-start | bytes 32768 | tf_op jit(solution)/shard_map/all_to_all | solution.py:532
  85.4 6.0 %all-to-all-done.4.scalar_ref = f32[32,1,128]{2,1,0:T(1,128)S(1)} async-done(((f32[32,1,128]{2,1,0:T(1,128)}), f32[32,1,128]{2,1,0:T(1,128)S(1)}, u32[]{:S(2)}, u32[]{:S(2)}) %all-to-all-start.4) | async-done | bytes 16416 | tf_op jit(solution)/shard_map/all_to_all | solution.py:532
  91.4 1.0 %outputs.1 = (f32[5,8192]{1,0:T(8,128)}, f32[4,8192]{1,0:T(4,128)}, f32[256,128]{1,0:T(8,128)}, f32[128,128]{1,0:T(8,128)}) custom-call(s32[1]{0:T(128)S(6)} %copy.17.live_ref, f32[8,128]{1,0:T(8,128)S(1)} %get-tuple-element.28.own_scalar_ref, f32[32,1,128]{2,1,0:T(1,128)S(1)} %all-to-all-done.4.scalar_ref, f32[5,8192]{1,0:T(8,128)S(1)} %reshape.26.star_0_ref, ...), custom_call_target="tpu_custom_call" | custom-call | flops 1000000 | bytes 600000 | tf_op jit(solution)/shard_map/outputs/pallas_call | solution.py:566
  (30 shorter events, 1.2 us)
Async XLA Ops:
  9.2 7.4 %copy-start.8 = (f32[168,256]{1,0:T(8,128)S(1)}, f32[168,256]{1,0:T(8,128)}, u32[]{:S(2)}) copy-start(f32[168,256]{1,0:T(8,128)} %get-tuple-element.19) | copy-start | bytes 516100
  9.2 16.3 %all-to-all-start = ((f32[8,32,256]{2,1,0:T(8,128)}), f32[8,32,256]{2,1,0:T(8,128)S(1)}, u32[]{:S(2)}, u32[]{:S(2)}) async-start(f32[8,32,256]{2,1,0:T(8,128)} %get-tuple-element.18), calls=%async_computation | async-start | bytes 524288 | tf_op jit(solution)/shard_map/all_to_all | solution.py:532
  16.6 1.5 %collective-permute-start = (f32[168,256]{1,0:T(8,128)S(1)}, f32[168,256]{1,0:T(8,128)S(1)}, u32[]{:S(2)}, u32[]{:S(2)}) collective-permute-start(f32[168,256]{1,0:T(8,128)S(1)} %copy-done.8), channel_id=1, source_target_pairs={{0,1},{1,0},{2,3},{3,2},{4,5},{5,4},{6,7},{7,6},{8,9},{9,8},{10,11... | collective-permute-start | bytes 516104 | tf_op jit(solution)/shard_map/ppermute | solution.py:535
  18.1 6.5 %collective-permute-start.1 = (f32[168,256]{1,0:T(8,128)S(1)}, f32[168,256]{1,0:T(8,128)S(1)}, u32[]{:S(2)}, u32[]{:S(2)}) collective-permute-start(f32[168,256]{1,0:T(8,128)S(1)} %add.6.own_ref), channel_id=1, source_target_pairs={{0,2},{1,3},{2,0},{3,1},{4,6},{5,7},{6,4},{7,5},{8,10},{9,11},{10,... | collective-permute-start | bytes 516104 | tf_op jit(solution)/shard_map/ppermute | solution.py:535
  26.3 5.2 %copy-start.1 = (f32[5,128,128]{2,1,0:T(8,128)S(1)}, f32[5,128,128]{2,1,0:T(8,128)}, u32[]{:S(2)}) copy-start(f32[5,128,128]{2,1,0:T(8,128)} %star_coef_ref.5) | copy-start | bytes 983044
  26.3 5.2 %copy-start.3 = (s32[128,128]{1,0:T(8,128)S(1)}, s32[128,128]{1,0:T(8,128)}, u32[]{:S(2)}) copy-start(s32[128,128]{1,0:T(8,128)} %star_ref.5) | copy-start | bytes 196612
  26.3 14.2 %all-to-all-start.1 = ((f32[8,72,128]{2,1,0:T(8,128)}), f32[8,72,128]{2,1,0:T(8,128)S(1)}, u32[]{:S(2)}, u32[]{:S(2)}) async-start(f32[8,72,128]{2,1,0:T(8,128)} %get-tuple-element.21), calls=%async_computation.1 | async-start | bytes 589824 | tf_op jit(solution)/shard_map/all_to_all | solution.py:532
  31.4 9.0 %copy-start.2 = (f32[4,128,128]{2,1,0:T(8,128)S(1)}, f32[4,128,128]{2,1,0:T(8,128)}, u32[]{:S(2)}) copy-start(f32[4,128,128]{2,1,0:T(8,128)} %att_coef_ref.3) | copy-start | bytes 786436
  31.5 9.0 %copy-start.4 = (s32[128,128]{1,0:T(8,128)S(1)}, s32[128,128]{1,0:T(8,128)}, u32[]{:S(2)}) copy-start(s32[128,128]{1,0:T(8,128)} %knot_ref.3) | copy-start | bytes 196612
  31.5 9.0 %copy-start.5 = (f32[128,128]{1,0:T(8,128)S(1)}, f32[128,128]{1,0:T(8,128)}, u32[]{:S(2)}) copy-start(f32[128,128]{1,0:T(8,128)} %frac_ref.3) | copy-start | bytes 196612
  31.5 9.0 %copy-start.6 = (f32[128,128]{1,0:T(8,128)S(1)}, f32[128,128]{1,0:T(8,128)}, u32[]{:S(2)}) copy-start(f32[128,128]{1,0:T(8,128)} %cal_coef_ref.3) | copy-start | bytes 196612
  31.5 9.0 %copy-start.7 = (s32[128]{0:T(128)S(1)}, s32[128]{0:T(128)}, u32[]{:S(2)}) copy-start(s32[128]{0:T(128)} %param.15) | copy-start | bytes 1540
  49.6 12.1 %all-to-all-start.2 = ((f32[8,32,256]{2,1,0:T(8,128)}), f32[8,32,256]{2,1,0:T(8,128)S(1)}, u32[]{:S(2)}, u32[]{:S(2)}) async-start(f32[8,32,256]{2,1,0:T(8,128)} %get-tuple-element.22), calls=%async_computation.2 | async-start | bytes 524288 | tf_op jit(solution)/shard_map/all_to_all | solution.py:532
  53.2 1.4 %collective-permute-start.2 = (f32[168,256]{1,0:T(8,128)S(1)}, f32[168,256]{1,0:T(8,128)S(1)}, u32[]{:S(2)}, u32[]{:S(2)}) collective-permute-start(f32[168,256]{1,0:T(8,128)S(1)} %get-tuple-element.23), channel_id=1, source_target_pairs={{0,1},{1,0},{2,3},{3,2},{4,5},{5,4},{6,7},{7,6},{8,9},{9,8},{10,11... | collective-permute-start | bytes 516104 | tf_op jit(solution)/shard_map/ppermute | solution.py:535
  54.6 6.5 %collective-permute-start.3 = (f32[168,256]{1,0:T(8,128)S(1)}, f32[168,256]{1,0:T(8,128)S(1)}, u32[]{:S(2)}, u32[]{:S(2)}) collective-permute-start(f32[168,256]{1,0:T(8,128)S(1)} %add.7.own_ref), channel_id=1, source_target_pairs={{0,2},{1,3},{2,0},{3,1},{4,6},{5,7},{6,4},{7,5},{8,10},{9,11},{10,... | collective-permute-start | bytes 516104 | tf_op jit(solution)/shard_map/ppermute | solution.py:535
  62.5 14.4 %all-to-all-start.3 = ((f32[8,72,128]{2,1,0:T(8,128)}), f32[8,72,128]{2,1,0:T(8,128)S(1)}, u32[]{:S(2)}, u32[]{:S(2)}) async-start(f32[8,72,128]{2,1,0:T(8,128)} %get-tuple-element.25), calls=%async_computation.3 | async-start | bytes 589824 | tf_op jit(solution)/shard_map/all_to_all | solution.py:532
  80.7 10.8 %all-to-all-start.4 = ((f32[32,1,128]{2,1,0:T(1,128)}), f32[32,1,128]{2,1,0:T(1,128)S(1)}, u32[]{:S(2)}, u32[]{:S(2)}) async-start(f32[32,1,128]{2,1,0:T(1,128)} %get-tuple-element.29), calls=%async_computation.4 | async-start | bytes 32768 | tf_op jit(solution)/shard_map/all_to_all | solution.py:532
  85.2 6.3 %copy-start = (f32[128,128]{1,0:T(8,128)S(1)}, f32[128,128]{1,0:T(8,128)}, u32[]{:S(2)}) copy-start(f32[128,128]{1,0:T(8,128)} %value_ref.1) | copy-start | bytes 196612

commit v18 on v17

--- a/solution.py
+++ b/solution.py
@@ -528,8 +528,14 @@
             name="star_forward",
         )(obs_star, star_coef, star)
 
-    def swap(blocks, axes):
-        return lax.all_to_all(blocks, axes, 0, 0)
+    def swap(blocks, groups=None):
+        return lax.all_to_all(blocks, ("stars", "seg"), 0, 0, axis_index_groups=groups)
+
+    def star_groups():
+        forward = list(range(n_stars))
+        turned = forward[n_stars // 2 :] + forward[: n_stars // 2]
+        orders = (forward, forward[::-1], turned, turned[::-1])
+        return [[star * n_seg + seg for star in orders[seg % 4]] for seg in range(n_seg)]
 
     def partner(array, axis, distance):
         return lax.ppermute(array, axis, [(i, i ^ distance) for i in range(lax.axis_size(axis))])
@@ -546,8 +552,8 @@
             compiler_params=PARAMS,
             cost_estimate=SMALL_COST,
             name="table_sum",
-        )(swap(table, "stars"), star, partner(star, "seg", distances[-1]))
-        return star_forward(star), star, swap(blocks, "stars")
+        )(swap(table, star_groups()), star, partner(star, "seg", distances[-1]))
+        return star_forward(star), star, swap(blocks, star_groups())
 
     first = reduced(*first_scatter())
     star_0 = first[1]
@@ -572,7 +578,7 @@
         cost_estimate=SMALL_COST,
         name="outputs",
     )(
-        live_tiles, own_scalars, swap(scalars, ("stars", "seg")), star_order(star_0), star_order(star_h),
+        live_tiles, own_scalars, swap(scalars), star_order(star_0), star_order(star_h),
         att_order(table_0), att_order(table_h), table_0, table_h, obs_value, image_0, image_1,
     )
 

time: 93.1 us -> 93.1 us (level)
    ppermute x4, waiting for transfers between devices: 12.6 us -> 14.4 us  [partner(): lax.ppermute(array, axis, [(i, i ^ distance) for i in range(lax.axis_size...]
    all_to_all x5, waiting for transfers between devices: 17 us -> 15.4 us  [swap(): lax.all_to_all(blocks, ('stars', 'seg'), 0, 0, axis_index_groups=groups)]
  transfers between devices with their start and end apart: 9 -> 9, of which waited for: 9 -> 7; matrix products, arithmetic and copies ran while one was open for 1% -> 1% of each run, Pallas kernels for 9% -> 9%
where the time goes in v18:
time: 93.1 us; the launch traced here: 92.5 us
  Pallas kernels  31.7 us (34%)
  waiting for transfers between devices  29.9 us (32%)
  starting transfers between devices  28.3 us (30%)
  between operations  1.47 us (2%)
  local copies, waits for them, and re-layouts  1.08 us (1%)
    all_to_all x5, starting transfers between devices, swap(): lax.all_to_all(blocks, ('stars', 'seg'), 0, 0, axis_index_groups=groups)  25.1 us
    all_to_all x5, waiting for transfers between devices, swap(): lax.all_to_all(blocks, ('stars', 'seg'), 0, 0, axis_index_groups=groups)  15.4 us
    ppermute x4, waiting for transfers between devices, partner(): lax.ppermute(array, axis, [(i, i ^ distance) for i in range(lax.axis_size...  14.4 us
    pallas_call x1, Pallas kernels, middle(): pl.pallas_call(functools.partial(middle_kernel, n_stars, n_seg), out_shap...  9.03 us
    pallas_call x2, Pallas kernels, star_forward(): pl.pallas_call(star_forward_kernel, out_shape=image_shape, in_specs=in_vm...  8.5 us
    pallas_call x1, Pallas kernels, first_scatter(): pl.pallas_call(first_kernel, out_shape=sent_shapes, in_specs=in_smem(2) +...  7.92 us
    pallas_call x1, Pallas kernels, last_gather(): pl.pallas_call(functools.partial(last_kernel, n_stars, n_seg), out_shape=...  3.76 us
    ppermute x4, starting transfers between devices, partner(): lax.ppermute(array, axis, [(i, i ^ distance) for i in range(lax.axis_size...  3.22 us
  transfers between devices with their start and end apart: 9, of which 7 were waited for; matrix products, arithmetic and copies ran while one was open for 1% of the time, Pallas kernels for 9%

profile of v18, /device:TPU:0, one launch (start us, length us, event | category | flops | bytes accessed | tf_op | source)
XLA Modules:
  0.0 92.5 jit_solution(12606828106331427470)
XLA Ops:
  1.3 7.9 %first_scatter.1 = (f32[8,32,256]{2,1,0:T(8,128)}, f32[168,256]{1,0:T(8,128)}) custom-call(s32[1]{0:T(128)S(6)} %copy.17.live_ref, s32[1]{0:T(128)} %bitcast.place_ref, f32[128,128]{1,0:T(8,128)} %value_ref.1, f32[128,128]{1,0:T(8,128)} %cal_coef_ref.3, s32[1,128]{1,0:T(1,128)} %bitcast.6, s32[128,128]{1,0:T(8,128)} %knot_ref.3, f32[128,128]{1,0:T(8,128)} %frac_ref.3, ...), custom_call_target="tpu_custom_call" | custom-call | flops 3000000000 | bytes 1000000 | tf_op jit(solution)/shard_map/first_scatter/pallas_call | solution.py:482
  9.2 7.4 %all-to-all-start = ((f32[8,32,256]{2,1,0:T(8,128)}), f32[8,32,256]{2,1,0:T(8,128)S(1)}, u32[]{:S(2)}, u32[]{:S(2)}) async-start(f32[8,32,256]{2,1,0:T(8,128)} %get-tuple-element.18), calls=%async_computation | async-start | bytes 524288 | tf_op jit(solution)/shard_map/all_to_all | solution.py:532
  16.6 1.6 %collective-permute-start = (f32[168,256]{1,0:T(8,128)S(1)}, f32[168,256]{1,0:T(8,128)S(1)}, u32[]{:S(2)}, u32[]{:S(2)}) collective-permute-start(f32[168,256]{1,0:T(8,128)S(1)} %copy-done.8), channel_id=1, source_target_pairs={{0,1},{1,0},{2,3},{3,2},{4,5},{5,4},{6,7},{7,6},{8,9},{9,8},{10,11... | collective-permute-start | bytes 516104 | tf_op jit(solution)/shard_map/ppermute | solution.py:541
  18.2 1.0 %collective-permute-done = f32[168,256]{1,0:T(8,128)S(1)} collective-permute-done((f32[168,256]{1,0:T(8,128)S(1)}, f32[168,256]{1,0:T(8,128)S(1)}, u32[]{:S(2)}, u32[]{:S(2)}) %collective-permute-start) | collective-permute-done | bytes 172064 | tf_op jit(solution)/shard_map/ppermute | solution.py:541
  19.3 0.9 collective-permute-start.1
  20.2 5.8 %collective-permute-done.1.other_ref = f32[168,256]{1,0:T(8,128)S(1)} collective-permute-done((f32[168,256]{1,0:T(8,128)S(1)}, f32[168,256]{1,0:T(8,128)S(1)}, u32[]{:S(2)}, u32[]{:S(2)}) %collective-permute-start.1) | collective-permute-done | bytes 172064 | tf_op jit(solution)/shard_map/ppermute | solution.py:541
  26.0 0.7 table_sum.2
  26.8 4.6 %all-to-all-start.1 = ((f32[8,72,128]{2,1,0:T(8,128)}), f32[8,72,128]{2,1,0:T(8,128)S(1)}, u32[]{:S(2)}, u32[]{:S(2)}) async-start(f32[8,72,128]{2,1,0:T(8,128)} %get-tuple-element.21), calls=%async_computation.1 | async-start | bytes 589824 | tf_op jit(solution)/shard_map/all_to_all | solution.py:532
  31.5 4.2 %star_forward.2.star_image_ref = f32[128,128]{1,0:T(8,128)S(1)} custom-call(s32[128,128]{1,0:T(8,128)S(1)} %copy-done.3, f32[5,128,128]{2,1,0:T(8,128)S(1)} %copy-done.1, f32[160,256]{1,0:T(8,128)S(1)} %get-tuple-element.20.star_x_ref.star_0_ref), custom_call_target="tpu_custom_call" | custom-call | flops 3000000000 | bytes 1000000 | tf_op jit(solution)/shard_map/star_forward/pallas_call | solution.py:520
  35.8 4.7 %all-to-all-done.1.block_ref = f32[8,72,128]{2,1,0:T(8,128)S(1)} async-done(((f32[8,72,128]{2,1,0:T(8,128)}), f32[8,72,128]{2,1,0:T(8,128)S(1)}, u32[]{:S(2)}, u32[]{:S(2)}) %all-to-all-start.1) | async-done | bytes 294944 | tf_op jit(solution)/shard_map/all_to_all | solution.py:532
  40.5 9.0 %gather_and_scatter.1 = (f32[128,128]{1,0:T(8,128)S(1)}, f32[256,256]{1,0:T(8,128)S(1)}, f32[8,32,256]{2,1,0:T(8,128)}, f32[168,256]{1,0:T(8,128)S(1)}) custom-call(s32[1]{0:T(128)S(6)} %copy.17.live_ref, s32[1]{0:T(128)} %bitcast.place_ref, s32[128,128]{1,0:T(8,128)S(1)} %copy-done.4, f32[128,128]{1,0:T(8,128)S(1)} %copy-done.5, ...), custom_call_target="tpu_custom_call" | custom-call | flops 3000000000 | bytes 1000000 | tf_op jit(solution)/shard_map/gather_and_scatter/pallas_call | solution.py:495
  49.5 4.2 %all-to-all-start.2 = ((f32[8,32,256]{2,1,0:T(8,128)}), f32[8,32,256]{2,1,0:T(8,128)S(1)}, u32[]{:S(2)}, u32[]{:S(2)}) async-start(f32[8,32,256]{2,1,0:T(8,128)} %get-tuple-element.22), calls=%async_computation.2 | async-start | bytes 524288 | tf_op jit(solution)/shard_map/all_to_all | solution.py:532
  53.7 0.5 collective-permute-start.2
  54.2 1.0 %collective-permute-done.2 = f32[168,256]{1,0:T(8,128)S(1)} collective-permute-done((f32[168,256]{1,0:T(8,128)S(1)}, f32[168,256]{1,0:T(8,128)S(1)}, u32[]{:S(2)}, u32[]{:S(2)}) %collective-permute-start.2) | collective-permute-done | bytes 172064 | tf_op jit(solution)/shard_map/ppermute | solution.py:541
  55.5 6.5 %collective-permute-done.3.other_ref = f32[168,256]{1,0:T(8,128)S(1)} collective-permute-done((f32[168,256]{1,0:T(8,128)S(1)}, f32[168,256]{1,0:T(8,128)S(1)}, u32[]{:S(2)}, u32[]{:S(2)}) %collective-permute-start.3) | collective-permute-done | bytes 172064 | tf_op jit(solution)/shard_map/ppermute | solution.py:541
  62.0 0.7 table_sum.3
  62.7 5.6 %all-to-all-start.3 = ((f32[8,72,128]{2,1,0:T(8,128)}), f32[8,72,128]{2,1,0:T(8,128)S(1)}, u32[]{:S(2)}, u32[]{:S(2)}) async-start(f32[8,72,128]{2,1,0:T(8,128)} %get-tuple-element.25), calls=%async_computation.3 | async-start | bytes 589824 | tf_op jit(solution)/shard_map/all_to_all | solution.py:532
  68.4 4.2 %star_forward.3.star_image_ref = f32[128,128]{1,0:T(8,128)S(1)} custom-call(s32[128,128]{1,0:T(8,128)S(1)} %copy-done.3, f32[5,128,128]{2,1,0:T(8,128)S(1)} %copy-done.1, f32[160,256]{1,0:T(8,128)S(1)} %get-tuple-element.24.star_x_ref), custom_call_target="tpu_custom_call" | custom-call | flops 3000000000 | bytes 1000000 | tf_op jit(solution)/shard_map/star_forward/pallas_call | solution.py:520
  72.6 4.8 %all-to-all-done.3.block_ref = f32[8,72,128]{2,1,0:T(8,128)S(1)} async-done(((f32[8,72,128]{2,1,0:T(8,128)}), f32[8,72,128]{2,1,0:T(8,128)S(1)}, u32[]{:S(2)}, u32[]{:S(2)}) %all-to-all-start.3) | async-done | bytes 294944 | tf_op jit(solution)/shard_map/all_to_all | solution.py:532
  77.4 3.8 %last_gather.1 = (f32[128,128]{1,0:T(8,128)S(1)}, f32[256,256]{1,0:T(8,128)S(1)}, f32[32,1,128]{2,1,0:T(1,128)}, f32[8,128]{1,0:T(8,128)S(1)}) custom-call(s32[1]{0:T(128)S(6)} %copy.17.live_ref, s32[1]{0:T(128)} %bitcast.place_ref, s32[128,128]{1,0:T(8,128)S(1)} %copy-done.4, f32[128,128]{1,0:T(8,128)S(1)} %copy-done.5, f32[4,128,128]{2,1,0:T(8,128)S(1)} %copy-done.2, ...), custom_call_target="tpu_custom_call" | custom-call | flops 3000000000 | bytes 1000000 | tf_op jit(solution)/shard_map/last_gather/pallas_call | solution.py:508
  81.1 3.3 %all-to-all-start.4 = ((f32[32,1,128]{2,1,0:T(1,128)}), f32[32,1,128]{2,1,0:T(1,128)S(1)}, u32[]{:S(2)}, u32[]{:S(2)}) async-start(f32[32,1,128]{2,1,0:T(1,128)} %get-tuple-element.29), calls=%async_computation.4 | async-start | bytes 32768 | tf_op jit(solution)/shard_map/all_to_all | solution.py:532
  84.7 0.3 reshape.29.att_0_ref
  85.5 6.0 %all-to-all-done.4.scalar_ref = f32[32,1,128]{2,1,0:T(1,128)S(1)} async-done(((f32[32,1,128]{2,1,0:T(1,128)}), f32[32,1,128]{2,1,0:T(1,128)S(1)}, u32[]{:S(2)}, u32[]{:S(2)}) %all-to-all-start.4) | async-done | bytes 16416 | tf_op jit(solution)/shard_map/all_to_all | solution.py:532
  91.5 1.0 %outputs.1 = (f32[5,8192]{1,0:T(8,128)}, f32[4,8192]{1,0:T(4,128)}, f32[256,128]{1,0:T(8,128)}, f32[128,128]{1,0:T(8,128)}) custom-call(s32[1]{0:T(128)S(6)} %copy.17.live_ref, f32[8,128]{1,0:T(8,128)S(1)} %get-tuple-element.28.own_scalar_ref, f32[32,1,128]{2,1,0:T(1,128)S(1)} %all-to-all-done.4.scalar_ref, f32[5,8192]{1,0:T(8,128)S(1)} %reshape.26.star_0_ref, ...), custom_call_target="tpu_custom_call" | custom-call | flops 1000000 | bytes 600000 | tf_op jit(solution)/shard_map/outputs/pallas_call | solution.py:572
  (30 shorter events, 1.1 us)
Async XLA Ops:
  9.2 7.4 %copy-start.8 = (f32[168,256]{1,0:T(8,128)S(1)}, f32[168,256]{1,0:T(8,128)}, u32[]{:S(2)}) copy-start(f32[168,256]{1,0:T(8,128)} %get-tuple-element.19) | copy-start | bytes 516100
  9.2 16.8 %all-to-all-start = ((f32[8,32,256]{2,1,0:T(8,128)}), f32[8,32,256]{2,1,0:T(8,128)S(1)}, u32[]{:S(2)}, u32[]{:S(2)}) async-start(f32[8,32,256]{2,1,0:T(8,128)} %get-tuple-element.18), calls=%async_computation | async-start | bytes 524288 | tf_op jit(solution)/shard_map/all_to_all | solution.py:532
  16.6 2.7 %collective-permute-start = (f32[168,256]{1,0:T(8,128)S(1)}, f32[168,256]{1,0:T(8,128)S(1)}, u32[]{:S(2)}, u32[]{:S(2)}) collective-permute-start(f32[168,256]{1,0:T(8,128)S(1)} %copy-done.8), channel_id=1, source_target_pairs={{0,1},{1,0},{2,3},{3,2},{4,5},{5,4},{6,7},{7,6},{8,9},{9,8},{10,11... | collective-permute-start | bytes 516104 | tf_op jit(solution)/shard_map/ppermute | solution.py:541
  19.3 6.7 %collective-permute-start.1 = (f32[168,256]{1,0:T(8,128)S(1)}, f32[168,256]{1,0:T(8,128)S(1)}, u32[]{:S(2)}, u32[]{:S(2)}) collective-permute-start(f32[168,256]{1,0:T(8,128)S(1)} %add.6.own_ref), channel_id=1, source_target_pairs={{0,2},{1,3},{2,0},{3,1},{4,6},{5,7},{6,4},{7,5},{8,10},{9,11},{10,... | collective-permute-start | bytes 516104 | tf_op jit(solution)/shard_map/ppermute | solution.py:541
  26.8 4.7 %copy-start.1 = (f32[5,128,128]{2,1,0:T(8,128)S(1)}, f32[5,128,128]{2,1,0:T(8,128)}, u32[]{:S(2)}) copy-start(f32[5,128,128]{2,1,0:T(8,128)} %star_coef_ref.5) | copy-start | bytes 983044
  26.8 4.7 %copy-start.3 = (s32[128,128]{1,0:T(8,128)S(1)}, s32[128,128]{1,0:T(8,128)}, u32[]{:S(2)}) copy-start(s32[128,128]{1,0:T(8,128)} %star_ref.5) | copy-start | bytes 196612
  26.8 13.7 %all-to-all-start.1 = ((f32[8,72,128]{2,1,0:T(8,128)}), f32[8,72,128]{2,1,0:T(8,128)S(1)}, u32[]{:S(2)}, u32[]{:S(2)}) async-start(f32[8,72,128]{2,1,0:T(8,128)} %get-tuple-element.21), calls=%async_computation.1 | async-start | bytes 589824 | tf_op jit(solution)/shard_map/all_to_all | solution.py:532
  31.4 9.0 %copy-start.2 = (f32[4,128,128]{2,1,0:T(8,128)S(1)}, f32[4,128,128]{2,1,0:T(8,128)}, u32[]{:S(2)}) copy-start(f32[4,128,128]{2,1,0:T(8,128)} %att_coef_ref.3) | copy-start | bytes 786436
  31.5 9.0 %copy-start.4 = (s32[128,128]{1,0:T(8,128)S(1)}, s32[128,128]{1,0:T(8,128)}, u32[]{:S(2)}) copy-start(s32[128,128]{1,0:T(8,128)} %knot_ref.3) | copy-start | bytes 196612
  31.5 9.0 %copy-start.5 = (f32[128,128]{1,0:T(8,128)S(1)}, f32[128,128]{1,0:T(8,128)}, u32[]{:S(2)}) copy-start(f32[128,128]{1,0:T(8,128)} %frac_ref.3) | copy-start | bytes 196612
  31.5 9.0 %copy-start.6 = (f32[128,128]{1,0:T(8,128)S(1)}, f32[128,128]{1,0:T(8,128)}, u32[]{:S(2)}) copy-start(f32[128,128]{1,0:T(8,128)} %cal_coef_ref.3) | copy-start | bytes 196612
  31.5 9.0 %copy-start.7 = (s32[128]{0:T(128)S(1)}, s32[128]{0:T(128)}, u32[]{:S(2)}) copy-start(s32[128]{0:T(128)} %param.15) | copy-start | bytes 1540
  49.5 12.5 %all-to-all-start.2 = ((f32[8,32,256]{2,1,0:T(8,128)}), f32[8,32,256]{2,1,0:T(8,128)S(1)}, u32[]{:S(2)}, u32[]{:S(2)}) async-start(f32[8,32,256]{2,1,0:T(8,128)} %get-tuple-element.22), calls=%async_computation.2 | async-start | bytes 524288 | tf_op jit(solution)/shard_map/all_to_all | solution.py:532
  53.7 1.6 %collective-permute-start.2 = (f32[168,256]{1,0:T(8,128)S(1)}, f32[168,256]{1,0:T(8,128)S(1)}, u32[]{:S(2)}, u32[]{:S(2)}) collective-permute-start(f32[168,256]{1,0:T(8,128)S(1)} %get-tuple-element.23), channel_id=1, source_target_pairs={{0,1},{1,0},{2,3},{3,2},{4,5},{5,4},{6,7},{7,6},{8,9},{9,8},{10,11... | collective-permute-start | bytes 516104 | tf_op jit(solution)/shard_map/ppermute | solution.py:541
  55.3 6.7 %collective-permute-start.3 = (f32[168,256]{1,0:T(8,128)S(1)}, f32[168,256]{1,0:T(8,128)S(1)}, u32[]{:S(2)}, u32[]{:S(2)}) collective-permute-start(f32[168,256]{1,0:T(8,128)S(1)} %add.7.own_ref), channel_id=1, source_target_pairs={{0,2},{1,3},{2,0},{3,1},{4,6},{5,7},{6,4},{7,5},{8,10},{9,11},{10,... | collective-permute-start | bytes 516104 | tf_op jit(solution)/shard_map/ppermute | solution.py:541
  62.7 14.6 %all-to-all-start.3 = ((f32[8,72,128]{2,1,0:T(8,128)}), f32[8,72,128]{2,1,0:T(8,128)S(1)}, u32[]{:S(2)}, u32[]{:S(2)}) async-start(f32[8,72,128]{2,1,0:T(8,128)} %get-tuple-element.25), calls=%async_computation.3 | async-start | bytes 589824 | tf_op jit(solution)/shard_map/all_to_all | solution.py:532
  81.1 10.3 %all-to-all-start.4 = ((f32[32,1,128]{2,1,0:T(1,128)}), f32[32,1,128]{2,1,0:T(1,128)S(1)}, u32[]{:S(2)}, u32[]{:S(2)}) async-start(f32[32,1,128]{2,1,0:T(1,128)} %get-tuple-element.29), calls=%async_computation.4 | async-start | bytes 32768 | tf_op jit(solution)/shard_map/all_to_all | solution.py:532
  85.2 6.3 %copy-start = (f32[128,128]{1,0:T(8,128)S(1)}, f32[128,128]{1,0:T(8,128)}, u32[]{:S(2)}) copy-start(f32[128,128]{1,0:T(8,128)} %value_ref.1) | copy-start | bytes 196612

commit v19 on v18

--- a/solution.py
+++ b/solution.py
@@ -95,10 +95,11 @@
 
 
 def store_rows(out_ref, begin, rows):
-    block = out_ref.shape[1]
+    size = (out_ref.shape[1] - 8) // 2
     for offset in range(0, rows.shape[0], 8):
-        where = begin + offset
-        out_ref[where // block, where % block : where % block + 8, :] = rows[offset : offset + 8]
+        block, place = divmod(begin + offset, size)
+        out_ref[block, place : place + 8, :] = rows[offset : offset + 8, :128]
+        out_ref[block, size + place : size + place + 8, :] = rows[offset : offset + 8, 128:]
 
 
 def knot_factors(first, size, knot_ref, frac_ref):
@@ -177,8 +178,9 @@
         edges = jnp.where((lane == 2 * comp) & (row < 3), tail, edges)
         edges = jnp.where((lane == 2 * comp + 1) & (row < 3), head, edges)
     edges = with_scalars(pltpu.roll(edges, SLOT * place_ref[0], 1), scalars)
-    star_out[:STAR_ROWS] = star_acc[:STAR_ROWS] + star_acc[STAR_ROWS:]
-    star_out[STAR_ROWS:] = jnp.concatenate([edges, jnp.zeros_like(edges)], axis=1)
+    for device in range(table_out.shape[0]):
+        table_out[device, -8:, :] = edges
+    star_out[...] = star_acc[:STAR_ROWS] + star_acc[STAR_ROWS:]
 
 
 def first_kernel(live_ref, place_ref, *refs):
@@ -222,15 +224,14 @@
     scatter_end(place_ref, [], knot_acc, star_acc, table_out, star_out)
 
 
-def sum_kernel(block_ref, own_ref, other_ref, out_ref, star_out):
+def sum_kernel(block_ref, own_ref, other_ref, out_ref, star_out, edge_out):
     total = block_ref[0]
     for device in range(1, block_ref.shape[0]):
         total = total + block_ref[device]
-    star = own_ref[...] + other_ref[...]
-    star_out[...] = star[:STAR_ROWS]
-    total = jnp.concatenate([total[:, :128], total[:, 128:], star[STAR_ROWS:, :128]], axis=0)
+    star_out[...] = own_ref[...] + other_ref[...]
     for device in range(block_ref.shape[0]):
-        out_ref[device] = total
+        out_ref[device] = total[:-8]
+    edge_out[...] = total[-8:]
 
 
 def picked(array, which):
@@ -287,13 +288,10 @@
         image_ref[rows, :] = jnp.concatenate(image_rows, axis=0)
 
 
-def received_table(n_stars, n_seg, place_ref, block_ref):
+def received_table(n_stars, n_seg, place_ref, block_ref, edges):
     segment = place_ref[0]
     lane = lax.broadcasted_iota(jnp.int32, (8, 128), 1)
     row = lax.broadcasted_iota(jnp.int32, (8, 128), 0)
-    edges = block_ref[0, -8:, :]
-    for block in range(1, n_stars):
-        edges = edges + block_ref[block, -8:, :]
 
     def slot(which):
         return pltpu.roll(edges, (128 - SLOT * jnp.clip(which, 0, n_seg - 1)) & 127, 1)
@@ -313,7 +311,7 @@
         top = table[comp * FINE : comp * FINE + 8]
         pieces.append(top + jnp.concatenate([shifted, jnp.zeros_like(shifted)], axis=1))
         pieces.append(table[comp * FINE + 8 : (comp + 1) * FINE])
-    return jnp.concatenate(pieces + [table[KNOT_ROWS:]], axis=0), ahead, edges
+    return jnp.concatenate(pieces + [table[KNOT_ROWS:]], axis=0), ahead
 
 
 def gather_ready(table, ahead, cal_coef_ref, tile_cal_ref, star_image_ref, knot_parts_ref, cal_ref):
@@ -369,10 +367,11 @@
 
 def middle_kernel(
     n_stars, n_seg, live_ref, place_ref, knot_ref, frac_ref, att_coef_ref, star_ref, star_coef_ref,
-    cal_coef_ref, tile_cal_ref, star_image_ref, star_x_ref, block_ref, image_ref, table_out, scatter_out,
+    cal_coef_ref, tile_cal_ref, star_image_ref, star_x_ref, block_ref, edge_ref, other_edge_ref, image_ref, table_out, scatter_out,
     star_out, knot_parts_ref, cal_ref, knot_acc, star_acc,
 ):
-    table, ahead, _ = received_table(n_stars, n_seg, place_ref, block_ref)
+    edges = edge_ref[...] + other_edge_ref[...]
+    table, ahead = received_table(n_stars, n_seg, place_ref, block_ref, edges)
     table_out[...] = table
     norm = squares(star_x_ref[...]) / n_seg + squares(table) / n_stars
     gather_ready(table, ahead, cal_coef_ref, tile_cal_ref, star_image_ref, knot_parts_ref, cal_ref)
@@ -389,10 +388,11 @@
 
 def last_kernel(
     n_stars, n_seg, live_ref, place_ref, knot_ref, frac_ref, att_coef_ref, cal_coef_ref, tile_cal_ref,
-    star_image_ref, star_x_ref, block_ref, star_0_ref, table_0_ref, image_0_ref, image_ref, table_out,
+    star_image_ref, star_x_ref, block_ref, edge_ref, other_edge_ref, star_0_ref, table_0_ref, image_0_ref, image_ref, table_out,
     scalar_out, own_scalar_out, knot_parts_ref, cal_ref,
 ):
-    table, ahead, edges = received_table(n_stars, n_seg, place_ref, block_ref)
+    edges = edge_ref[...] + other_edge_ref[...]
+    table, ahead = received_table(n_stars, n_seg, place_ref, block_ref, edges)
     table_out[...] = table
     norm_0, square_0 = first_step(edges)
     step = norm_0 / square_0
@@ -472,7 +472,7 @@
     image_shape = shaped(tile_count, width)
     table_shape = shaped(TABLE_ROWS, COARSE)
     star_shape = shaped(STAR_ROWS, COARSE)
-    sent_shapes = (shaped(n_stars, TABLE_ROWS // n_stars, COARSE), shaped(STAR_ROWS + 8, COARSE))
+    sent_shapes = (shaped(n_stars, 2 * TABLE_ROWS // n_stars + 8, 128), star_shape)
     sums = [pltpu.VMEM((2 * KNOT_HALF, COARSE), F32), pltpu.VMEM((2 * STAR_ROWS, COARSE), F32)]
     ready = [pltpu.VMEM((2 * KNOT_HALF, COARSE), BF16), pltpu.VMEM((tile_count, width), F32)]
 
@@ -544,16 +544,19 @@
         distances = [1 << bit for bit in range(n_seg.bit_length() - 1)]
         for distance in distances[:-1]:
             star = star + partner(star, "seg", distance)
-        blocks, star = pl.pallas_call(
+        blocks, star, edge = pl.pallas_call(
             sum_kernel,
-            out_shape=(shaped(n_stars, 2 * TABLE_ROWS // n_stars + 8, 128), star_shape),
+            out_shape=(shaped(n_stars, 2 * TABLE_ROWS // n_stars, 128), star_shape, shaped(8, 128)),
             in_specs=in_vmem(3),
-            out_specs=tuple(in_vmem(2)),
+            out_specs=tuple(in_vmem(3)),
             compiler_params=PARAMS,
             cost_estimate=SMALL_COST,
             name="table_sum",
         )(swap(table, star_groups()), star, partner(star, "seg", distances[-1]))
-        return star_forward(star), star, swap(blocks, star_groups())
+        for distance in distances[:-1]:
+            edge = edge + partner(edge, "seg", distance)
+        gathered = swap(blocks, star_groups())
+        return star_forward(star), star, gathered, edge, partner(edge, "seg", distances[-1])
 
     first = reduced(*first_scatter())
     star_0 = first[1]

time: 93.1 us -> 91.8 us (0.986)
  waiting for transfers between devices: 29.9 us -> 25.1 us
  starting transfers between devices: 28.3 us -> 31.7 us
    all_to_all x5, waiting for transfers between devices: 15.4 us -> 10.3 us  [swap(): lax.all_to_all(blocks, ('stars', 'seg'), 0, 0, axis_index_groups=groups)]
    ppermute x4 -> x8, starting transfers between devices: 3.22 us -> 7.22 us  [partner(): lax.ppermute(array, axis, [(i, i ^ distance) for i in range(lax.axis_size...]
    ppermute x4 -> x8, waiting for transfers between devices: 14.4 us -> 14.9 us  [partner(): lax.ppermute(array, axis, [(i, i ^ distance) for i in range(lax.axis_size...]
  transfers between devices with their start and end apart: 9 -> 13, of which waited for: 7 -> 11; matrix products, arithmetic and copies ran while one was open for 1% -> 1% of each run, Pallas kernels for 9% -> 9%
where the time goes in v19:
time: 91.8 us; the launch traced here: 91.2 us
  Pallas kernels  31.7 us (35%)
  starting transfers between devices  31.7 us (35%)
  waiting for transfers between devices  25.1 us (27%)
  between operations  1.47 us (2%)
  local copies, waits for them, and re-layouts  1.08 us (1%)
    all_to_all x5, starting transfers between devices, swap(): lax.all_to_all(blocks, ('stars', 'seg'), 0, 0, axis_index_groups=groups)  24.5 us
    ppermute x8, waiting for transfers between devices, partner(): lax.ppermute(array, axis, [(i, i ^ distance) for i in range(lax.axis_size...  14.9 us
    all_to_all x5, waiting for transfers between devices, swap(): lax.all_to_all(blocks, ('stars', 'seg'), 0, 0, axis_index_groups=groups)  10.3 us
    pallas_call x1, Pallas kernels, middle(): pl.pallas_call(functools.partial(middle_kernel, n_stars, n_seg), out_shap...  9.03 us
    pallas_call x2, Pallas kernels, star_forward(): pl.pallas_call(star_forward_kernel, out_shape=image_shape, in_specs=in_vm...  8.5 us
    pallas_call x1, Pallas kernels, first_scatter(): pl.pallas_call(first_kernel, out_shape=sent_shapes, in_specs=in_smem(2) +...  7.95 us
    ppermute x8, starting transfers between devices, partner(): lax.ppermute(array, axis, [(i, i ^ distance) for i in range(lax.axis_size...  7.22 us
    pallas_call x1, Pallas kernels, last_gather(): pl.pallas_call(functools.partial(last_kernel, n_stars, n_seg), out_shape=...  3.76 us
  transfers between devices with their start and end apart: 13, of which 11 were waited for; matrix products, arithmetic and copies ran while one was open for 1% of the time, Pallas kernels for 9%

profile of v19, /device:TPU:0, one launch (start us, length us, event | category | flops | bytes accessed | tf_op | source)
XLA Modules:
  0.0 91.2 jit_solution(5367477782663700923)
XLA Ops:
  1.3 7.9 %first_scatter.1 = (f32[8,72,128]{2,1,0:T(8,128)}, f32[160,256]{1,0:T(8,128)}) custom-call(s32[1]{0:T(128)S(6)} %copy.17.live_ref, s32[1]{0:T(128)} %bitcast.place_ref, f32[128,128]{1,0:T(8,128)} %value_ref.1, f32[128,128]{1,0:T(8,128)} %cal_coef_ref.3, s32[1,128]{1,0:T(1,128)} %bitcast.6, s32[128,128]{1,0:T(8,128)} %knot_ref.3, f32[128,128]{1,0:T(8,128)} %frac_ref.3, ...), custom_call_target="tpu_custom_call" | custom-call | flops 3000000000 | bytes 1000000 | tf_op jit(solution)/shard_map/first_scatter/pallas_call | solution.py:482
  9.2 7.4 %all-to-all-start = ((f32[8,72,128]{2,1,0:T(8,128)}), f32[8,72,128]{2,1,0:T(8,128)S(1)}, u32[]{:S(2)}, u32[]{:S(2)}) async-start(f32[8,72,128]{2,1,0:T(8,128)} %get-tuple-element.20), calls=%async_computation | async-start | bytes 589824 | tf_op jit(solution)/shard_map/all_to_all | solution.py:532
  16.6 1.6 %collective-permute-start = (f32[160,256]{1,0:T(8,128)S(1)}, f32[160,256]{1,0:T(8,128)S(1)}, u32[]{:S(2)}, u32[]{:S(2)}) collective-permute-start(f32[160,256]{1,0:T(8,128)S(1)} %copy-done.8), channel_id=1, source_target_pairs={{0,1},{1,0},{2,3},{3,2},{4,5},{5,4},{6,7},{7,6},{8,9},{9,8},{10,11... | collective-permute-start | bytes 491528 | tf_op jit(solution)/shard_map/ppermute | solution.py:541
  18.3 1.0 %collective-permute-done = f32[160,256]{1,0:T(8,128)S(1)} collective-permute-done((f32[160,256]{1,0:T(8,128)S(1)}, f32[160,256]{1,0:T(8,128)S(1)}, u32[]{:S(2)}, u32[]{:S(2)}) %collective-permute-start) | collective-permute-done | bytes 163872 | tf_op jit(solution)/shard_map/ppermute | solution.py:541
  19.3 0.9 collective-permute-start.1
  20.2 5.7 %collective-permute-done.1.other_ref = f32[160,256]{1,0:T(8,128)S(1)} collective-permute-done((f32[160,256]{1,0:T(8,128)S(1)}, f32[160,256]{1,0:T(8,128)S(1)}, u32[]{:S(2)}, u32[]{:S(2)}) %collective-permute-start.1) | collective-permute-done | bytes 163872 | tf_op jit(solution)/shard_map/ppermute | solution.py:541
  26.9 4.3 %all-to-all-start.1 = ((f32[8,64,128]{2,1,0:T(8,128)}), f32[8,64,128]{2,1,0:T(8,128)S(1)}, u32[]{:S(2)}, u32[]{:S(2)}) async-start(f32[8,64,128]{2,1,0:T(8,128)} %get-tuple-element.23), calls=%async_computation.1 | async-start | bytes 524288 | tf_op jit(solution)/shard_map/all_to_all | solution.py:532
  31.3 1.1 %collective-permute-start.2 = (f32[8,128]{1,0:T(8,128)S(1)}, f32[8,128]{1,0:T(8,128)S(1)}, u32[]{:S(2)}, u32[]{:S(2)}) collective-permute-start(f32[8,128]{1,0:T(8,128)S(1)} %get-tuple-element.24), channel_id=1, source_target_pairs={{0,1},{1,0},{2,3},{3,2},{4,5},{5,4},{6,7},{7,6},{8,9},{9,8},{10,11... | collective-permute-start | bytes 12296 | tf_op jit(solution)/shard_map/ppermute | solution.py:541
  33.7 4.2 %star_forward.2.star_image_ref = f32[128,128]{1,0:T(8,128)S(1)} custom-call(s32[128,128]{1,0:T(8,128)S(1)} %copy-done.3, f32[5,128,128]{2,1,0:T(8,128)S(1)} %copy-done.1, f32[160,256]{1,0:T(8,128)S(1)} %get-tuple-element.22.star_x_ref.star_0_ref), custom_call_target="tpu_custom_call" | custom-call | flops 3000000000 | bytes 1000000 | tf_op jit(solution)/shard_map/star_forward/pallas_call | solution.py:520
  37.9 1.6 %all-to-all-done.1.block_ref = f32[8,64,128]{2,1,0:T(8,128)S(1)} async-done(((f32[8,64,128]{2,1,0:T(8,128)}), f32[8,64,128]{2,1,0:T(8,128)S(1)}, u32[]{:S(2)}, u32[]{:S(2)}) %all-to-all-start.1) | async-done | bytes 262176 | tf_op jit(solution)/shard_map/all_to_all | solution.py:532
  39.6 9.0 %gather_and_scatter.1 = (f32[128,128]{1,0:T(8,128)S(1)}, f32[256,256]{1,0:T(8,128)S(1)}, f32[8,72,128]{2,1,0:T(8,128)}, f32[160,256]{1,0:T(8,128)S(1)}) custom-call(s32[1]{0:T(128)S(6)} %copy.17.live_ref, s32[1]{0:T(128)} %bitcast.place_ref, s32[128,128]{1,0:T(8,128)S(1)} %copy-done.4, f32[128,128]{1,0:T(8,128)S(1)} %copy-done.5, ...), custom_call_target="tpu_custom_call" | custom-call | flops 3000000000 | bytes 1000000 | tf_op jit(solution)/shard_map/gather_and_scatter/pallas_call | solution.py:495
  48.6 4.2 %all-to-all-start.2 = ((f32[8,72,128]{2,1,0:T(8,128)}), f32[8,72,128]{2,1,0:T(8,128)S(1)}, u32[]{:S(2)}, u32[]{:S(2)}) async-start(f32[8,72,128]{2,1,0:T(8,128)} %get-tuple-element.25), calls=%async_computation.2 | async-start | bytes 589824 | tf_op jit(solution)/shard_map/all_to_all | solution.py:532
  52.9 1.0 %collective-permute-start.4 = (f32[160,256]{1,0:T(8,128)S(1)}, f32[160,256]{1,0:T(8,128)S(1)}, u32[]{:S(2)}, u32[]{:S(2)}) collective-permute-start(f32[160,256]{1,0:T(8,128)S(1)} %get-tuple-element.26), channel_id=1, source_target_pairs={{0,1},{1,0},{2,3},{3,2},{4,5},{5,4},{6,7},{7,6},{8,9},{9,8},{10,11... | collective-permute-start | bytes 491528 | tf_op jit(solution)/shard_map/ppermute | solution.py:541
  53.8 1.0 %collective-permute-done.4 = f32[160,256]{1,0:T(8,128)S(1)} collective-permute-done((f32[160,256]{1,0:T(8,128)S(1)}, f32[160,256]{1,0:T(8,128)S(1)}, u32[]{:S(2)}, u32[]{:S(2)}) %collective-permute-start.4) | collective-permute-done | bytes 163872 | tf_op jit(solution)/shard_map/ppermute | solution.py:541
  54.9 1.0 %collective-permute-start.5 = (f32[160,256]{1,0:T(8,128)S(1)}, f32[160,256]{1,0:T(8,128)S(1)}, u32[]{:S(2)}, u32[]{:S(2)}) collective-permute-start(f32[160,256]{1,0:T(8,128)S(1)} %add.14.own_ref), channel_id=1, source_target_pairs={{0,2},{1,3},{2,0},{3,1},{4,6},{5,7},{6,4},{7,5},{8,10},{9,11},{10,... | collective-permute-start | bytes 491528 | tf_op jit(solution)/shard_map/ppermute | solution.py:541
  55.9 5.5 %collective-permute-done.5.other_ref = f32[160,256]{1,0:T(8,128)S(1)} collective-permute-done((f32[160,256]{1,0:T(8,128)S(1)}, f32[160,256]{1,0:T(8,128)S(1)}, u32[]{:S(2)}, u32[]{:S(2)}) %collective-permute-start.5) | collective-permute-done | bytes 163872 | tf_op jit(solution)/shard_map/ppermute | solution.py:541
  62.5 4.8 %all-to-all-start.3 = ((f32[8,64,128]{2,1,0:T(8,128)}), f32[8,64,128]{2,1,0:T(8,128)S(1)}, u32[]{:S(2)}, u32[]{:S(2)}) async-start(f32[8,64,128]{2,1,0:T(8,128)} %get-tuple-element.28), calls=%async_computation.3 | async-start | bytes 524288 | tf_op jit(solution)/shard_map/all_to_all | solution.py:532
  67.3 1.1 %collective-permute-start.6 = (f32[8,128]{1,0:T(8,128)S(1)}, f32[8,128]{1,0:T(8,128)S(1)}, u32[]{:S(2)}, u32[]{:S(2)}) collective-permute-start(f32[8,128]{1,0:T(8,128)S(1)} %get-tuple-element.29), channel_id=1, source_target_pairs={{0,1},{1,0},{2,3},{3,2},{4,5},{5,4},{6,7},{7,6},{8,9},{9,8},{10,11... | collective-permute-start | bytes 12296 | tf_op jit(solution)/shard_map/ppermute | solution.py:541
  69.3 4.2 %star_forward.3.star_image_ref = f32[128,128]{1,0:T(8,128)S(1)} custom-call(s32[128,128]{1,0:T(8,128)S(1)} %copy-done.3, f32[5,128,128]{2,1,0:T(8,128)S(1)} %copy-done.1, f32[160,256]{1,0:T(8,128)S(1)} %get-tuple-element.27.star_x_ref), custom_call_target="tpu_custom_call" | custom-call | flops 3000000000 | bytes 1000000 | tf_op jit(solution)/shard_map/star_forward/pallas_call | solution.py:520
  73.6 2.0 %all-to-all-done.3.block_ref = f32[8,64,128]{2,1,0:T(8,128)S(1)} async-done(((f32[8,64,128]{2,1,0:T(8,128)}), f32[8,64,128]{2,1,0:T(8,128)S(1)}, u32[]{:S(2)}, u32[]{:S(2)}) %all-to-all-start.3) | async-done | bytes 262176 | tf_op jit(solution)/shard_map/all_to_all | solution.py:532
  75.6 3.8 %last_gather.1 = (f32[128,128]{1,0:T(8,128)S(1)}, f32[256,256]{1,0:T(8,128)S(1)}, f32[32,1,128]{2,1,0:T(1,128)}, f32[8,128]{1,0:T(8,128)S(1)}) custom-call(s32[1]{0:T(128)S(6)} %copy.17.live_ref, s32[1]{0:T(128)} %bitcast.place_ref, s32[128,128]{1,0:T(8,128)S(1)} %copy-done.4, f32[128,128]{1,0:T(8,128)S(1)} %copy-done.5, f32[4,128,128]{2,1,0:T(8,128)S(1)} %copy-done.2, ...), custom_call_target="tpu_custom_call" | custom-call | flops 3000000000 | bytes 1000000 | tf_op jit(solution)/shard_map/last_gather/pallas_call | solution.py:508
  79.4 3.7 %all-to-all-start.4 = ((f32[32,1,128]{2,1,0:T(1,128)}), f32[32,1,128]{2,1,0:T(1,128)S(1)}, u32[]{:S(2)}, u32[]{:S(2)}) async-start(f32[32,1,128]{2,1,0:T(1,128)} %get-tuple-element.33), calls=%async_computation.4 | async-start | bytes 32768 | tf_op jit(solution)/shard_map/all_to_all | solution.py:532
  84.2 6.0 %all-to-all-done.4.scalar_ref = f32[32,1,128]{2,1,0:T(1,128)S(1)} async-done(((f32[32,1,128]{2,1,0:T(1,128)}), f32[32,1,128]{2,1,0:T(1,128)S(1)}, u32[]{:S(2)}, u32[]{:S(2)}) %all-to-all-start.4) | async-done | bytes 16416 | tf_op jit(solution)/shard_map/all_to_all | solution.py:532
  90.2 1.0 %outputs.1 = (f32[5,8192]{1,0:T(8,128)}, f32[4,8192]{1,0:T(4,128)}, f32[256,128]{1,0:T(8,128)}, f32[128,128]{1,0:T(8,128)}) custom-call(s32[1]{0:T(128)S(6)} %copy.17.live_ref, f32[8,128]{1,0:T(8,128)S(1)} %get-tuple-element.32.own_scalar_ref, f32[32,1,128]{2,1,0:T(1,128)S(1)} %all-to-all-done.4.scalar_ref, f32[5,8192]{1,0:T(8,128)S(1)} %reshape.26.star_0_ref, ...), custom_call_target="tpu_custom_call" | custom-call | flops 1000000 | bytes 600000 | tf_op jit(solution)/shard_map/outputs/pallas_call | solution.py:575
  (40 shorter events, 5.4 us)
Async XLA Ops:
  9.2 7.4 %copy-start.8 = (f32[160,256]{1,0:T(8,128)S(1)}, f32[160,256]{1,0:T(8,128)}, u32[]{:S(2)}) copy-start(f32[160,256]{1,0:T(8,128)} %get-tuple-element.21) | copy-start | bytes 491524
  9.2 16.9 %all-to-all-start = ((f32[8,72,128]{2,1,0:T(8,128)}), f32[8,72,128]{2,1,0:T(8,128)S(1)}, u32[]{:S(2)}, u32[]{:S(2)}) async-start(f32[8,72,128]{2,1,0:T(8,128)} %get-tuple-element.20), calls=%async_computation | async-start | bytes 589824 | tf_op jit(solution)/shard_map/all_to_all | solution.py:532
  16.6 2.7 %collective-permute-start = (f32[160,256]{1,0:T(8,128)S(1)}, f32[160,256]{1,0:T(8,128)S(1)}, u32[]{:S(2)}, u32[]{:S(2)}) collective-permute-start(f32[160,256]{1,0:T(8,128)S(1)} %copy-done.8), channel_id=1, source_target_pairs={{0,1},{1,0},{2,3},{3,2},{4,5},{5,4},{6,7},{7,6},{8,9},{9,8},{10,11... | collective-permute-start | bytes 491528 | tf_op jit(solution)/shard_map/ppermute | solution.py:541
  19.3 6.5 %collective-permute-start.1 = (f32[160,256]{1,0:T(8,128)S(1)}, f32[160,256]{1,0:T(8,128)S(1)}, u32[]{:S(2)}, u32[]{:S(2)}) collective-permute-start(f32[160,256]{1,0:T(8,128)S(1)} %add.12.own_ref), channel_id=1, source_target_pairs={{0,2},{1,3},{2,0},{3,1},{4,6},{5,7},{6,4},{7,5},{8,10},{9,11},{10,... | collective-permute-start | bytes 491528 | tf_op jit(solution)/shard_map/ppermute | solution.py:541
  26.9 6.7 %copy-start.1 = (f32[5,128,128]{2,1,0:T(8,128)S(1)}, f32[5,128,128]{2,1,0:T(8,128)}, u32[]{:S(2)}) copy-start(f32[5,128,128]{2,1,0:T(8,128)} %star_coef_ref.5) | copy-start | bytes 983044
  26.9 6.7 %copy-start.3 = (s32[128,128]{1,0:T(8,128)S(1)}, s32[128,128]{1,0:T(8,128)}, u32[]{:S(2)}) copy-start(s32[128,128]{1,0:T(8,128)} %star_ref.5) | copy-start | bytes 196612
  26.9 12.6 %all-to-all-start.1 = ((f32[8,64,128]{2,1,0:T(8,128)}), f32[8,64,128]{2,1,0:T(8,128)S(1)}, u32[]{:S(2)}, u32[]{:S(2)}) async-start(f32[8,64,128]{2,1,0:T(8,128)} %get-tuple-element.23), calls=%async_computation.1 | async-start | bytes 524288 | tf_op jit(solution)/shard_map/all_to_all | solution.py:532
  31.3 1.9 %collective-permute-start.2 = (f32[8,128]{1,0:T(8,128)S(1)}, f32[8,128]{1,0:T(8,128)S(1)}, u32[]{:S(2)}, u32[]{:S(2)}) collective-permute-start(f32[8,128]{1,0:T(8,128)S(1)} %get-tuple-element.24), channel_id=1, source_target_pairs={{0,1},{1,0},{2,3},{3,2},{4,5},{5,4},{6,7},{7,6},{8,9},{9,8},{10,11... | collective-permute-start | bytes 12296 | tf_op jit(solution)/shard_map/ppermute | solution.py:541
  33.2 4.7 %collective-permute-start.3 = (f32[8,128]{1,0:T(8,128)S(1)}, f32[8,128]{1,0:T(8,128)S(1)}, u32[]{:S(2)}, u32[]{:S(2)}) collective-permute-start(f32[8,128]{1,0:T(8,128)S(1)} %add.13.edge_ref), channel_id=1, source_target_pairs={{0,2},{1,3},{2,0},{3,1},{4,6},{5,7},{6,4},{7,5},{8,10},{9,11},{10,... | collective-permute-start | bytes 12296 | tf_op jit(solution)/shard_map/ppermute | solution.py:541
  33.6 6.0 %copy-start.2 = (f32[4,128,128]{2,1,0:T(8,128)S(1)}, f32[4,128,128]{2,1,0:T(8,128)}, u32[]{:S(2)}) copy-start(f32[4,128,128]{2,1,0:T(8,128)} %att_coef_ref.3) | copy-start | bytes 786436
  33.6 6.0 %copy-start.4 = (s32[128,128]{1,0:T(8,128)S(1)}, s32[128,128]{1,0:T(8,128)}, u32[]{:S(2)}) copy-start(s32[128,128]{1,0:T(8,128)} %knot_ref.3) | copy-start | bytes 196612
  33.6 6.0 %copy-start.5 = (f32[128,128]{1,0:T(8,128)S(1)}, f32[128,128]{1,0:T(8,128)}, u32[]{:S(2)}) copy-start(f32[128,128]{1,0:T(8,128)} %frac_ref.3) | copy-start | bytes 196612
  33.6 6.0 %copy-start.6 = (f32[128,128]{1,0:T(8,128)S(1)}, f32[128,128]{1,0:T(8,128)}, u32[]{:S(2)}) copy-start(f32[128,128]{1,0:T(8,128)} %cal_coef_ref.3) | copy-start | bytes 196612
  33.6 6.0 %copy-start.7 = (s32[128]{0:T(128)S(1)}, s32[128]{0:T(128)}, u32[]{:S(2)}) copy-start(s32[128]{0:T(128)} %param.15) | copy-start | bytes 1540
  48.6 13.1 %all-to-all-start.2 = ((f32[8,72,128]{2,1,0:T(8,128)}), f32[8,72,128]{2,1,0:T(8,128)S(1)}, u32[]{:S(2)}, u32[]{:S(2)}) async-start(f32[8,72,128]{2,1,0:T(8,128)} %get-tuple-element.25), calls=%async_computation.2 | async-start | bytes 589824 | tf_op jit(solution)/shard_map/all_to_all | solution.py:532
  52.9 2.0 %collective-permute-start.4 = (f32[160,256]{1,0:T(8,128)S(1)}, f32[160,256]{1,0:T(8,128)S(1)}, u32[]{:S(2)}, u32[]{:S(2)}) collective-permute-start(f32[160,256]{1,0:T(8,128)S(1)} %get-tuple-element.26), channel_id=1, source_target_pairs={{0,1},{1,0},{2,3},{3,2},{4,5},{5,4},{6,7},{7,6},{8,9},{9,8},{10,11... | collective-permute-start | bytes 491528 | tf_op jit(solution)/shard_map/ppermute | solution.py:541
  54.9 6.5 %collective-permute-start.5 = (f32[160,256]{1,0:T(8,128)S(1)}, f32[160,256]{1,0:T(8,128)S(1)}, u32[]{:S(2)}, u32[]{:S(2)}) collective-permute-start(f32[160,256]{1,0:T(8,128)S(1)} %add.14.own_ref), channel_id=1, source_target_pairs={{0,2},{1,3},{2,0},{3,1},{4,6},{5,7},{6,4},{7,5},{8,10},{9,11},{10,... | collective-permute-start | bytes 491528 | tf_op jit(solution)/shard_map/ppermute | solution.py:541
  62.5 13.2 %all-to-all-start.3 = ((f32[8,64,128]{2,1,0:T(8,128)}), f32[8,64,128]{2,1,0:T(8,128)S(1)}, u32[]{:S(2)}, u32[]{:S(2)}) async-start(f32[8,64,128]{2,1,0:T(8,128)} %get-tuple-element.28), calls=%async_computation.3 | async-start | bytes 524288 | tf_op jit(solution)/shard_map/all_to_all | solution.py:532
  67.3 1.9 %collective-permute-start.6 = (f32[8,128]{1,0:T(8,128)S(1)}, f32[8,128]{1,0:T(8,128)S(1)}, u32[]{:S(2)}, u32[]{:S(2)}) collective-permute-start(f32[8,128]{1,0:T(8,128)S(1)} %get-tuple-element.29), channel_id=1, source_target_pairs={{0,1},{1,0},{2,3},{3,2},{4,5},{5,4},{6,7},{7,6},{8,9},{9,8},{10,11... | collective-permute-start | bytes 12296 | tf_op jit(solution)/shard_map/ppermute | solution.py:541
  69.3 4.3 %collective-permute-start.7 = (f32[8,128]{1,0:T(8,128)S(1)}, f32[8,128]{1,0:T(8,128)S(1)}, u32[]{:S(2)}, u32[]{:S(2)}) collective-permute-start(f32[8,128]{1,0:T(8,128)S(1)} %add.15.edge_ref), channel_id=1, source_target_pairs={{0,2},{1,3},{2,0},{3,1},{4,6},{5,7},{6,4},{7,5},{8,10},{9,11},{10,... | collective-permute-start | bytes 12296 | tf_op jit(solution)/shard_map/ppermute | solution.py:541
  79.4 10.8 %all-to-all-start.4 = ((f32[32,1,128]{2,1,0:T(1,128)}), f32[32,1,128]{2,1,0:T(1,128)S(1)}, u32[]{:S(2)}, u32[]{:S(2)}) async-start(f32[32,1,128]{2,1,0:T(1,128)} %get-tuple-element.33), calls=%async_computation.4 | async-start | bytes 32768 | tf_op jit(solution)/shard_map/all_to_all | solution.py:532
  83.9 6.3 %copy-start = (f32[128,128]{1,0:T(8,128)S(1)}, f32[128,128]{1,0:T(8,128)}, u32[]{:S(2)}) copy-start(f32[128,128]{1,0:T(8,128)} %value_ref.1) | copy-start | bytes 196612

commit v20 on v19

--- a/solution.py
+++ b/solution.py
@@ -12,7 +12,7 @@
 CALB_DEV = 256
 FINE = 32
 COARSE = 256
-GROUP = 16
+GROUP = 64
 WIDE_GROUP = 64
 SLOT = 8
 STAR_ROWS = 5 * FINE

time: 91.8 us -> 91.4 us (level)
  waiting for transfers between devices: 25.1 us -> 28.2 us
  Pallas kernels: 31.7 us -> 29.5 us
  starting transfers between devices: 31.7 us -> 30.5 us
    pallas_call x2, Pallas kernels: 8.5 us -> 6.3 us  [star_forward(): pl.pallas_call(star_forward_kernel, out_shape=image_shape, in_specs=in_vm...]
    all_to_all x5, waiting for transfers between devices: 10.3 us -> 12.1 us  [swap(): lax.all_to_all(blocks, ('stars', 'seg'), 0, 0, axis_index_groups=groups)]
    ppermute x8, waiting for transfers between devices: 14.9 us -> 16.1 us  [partner(): lax.ppermute(array, axis, [(i, i ^ distance) for i in range(lax.axis_size...]
    ppermute x8, starting transfers between devices: 7.22 us -> 6.11 us  [partner(): lax.ppermute(array, axis, [(i, i ^ distance) for i in range(lax.axis_size...]
  transfers between devices with their start and end apart: 13 -> 13, of which waited for: 11 -> 12; matrix products, arithmetic and copies ran while one was open for 1% -> 1% of each run, Pallas kernels for 9% -> 7%
where the time goes in v20:
time: 91.4 us; the launch traced here: 90.8 us
  starting transfers between devices  30.5 us (33%)
  Pallas kernels  29.5 us (32%)
  waiting for transfers between devices  28.2 us (31%)
  between operations  1.46 us (2%)
  local copies, waits for them, and re-layouts  1.08 us (1%)
    all_to_all x5, starting transfers between devices, swap(): lax.all_to_all(blocks, ('stars', 'seg'), 0, 0, axis_index_groups=groups)  24.4 us
    ppermute x8, waiting for transfers between devices, partner(): lax.ppermute(array, axis, [(i, i ^ distance) for i in range(lax.axis_size...  16.1 us
    all_to_all x5, waiting for transfers between devices, swap(): lax.all_to_all(blocks, ('stars', 'seg'), 0, 0, axis_index_groups=groups)  12.1 us
    pallas_call x1, Pallas kernels, middle(): pl.pallas_call(functools.partial(middle_kernel, n_stars, n_seg), out_shap...  9.03 us
    pallas_call x1, Pallas kernels, first_scatter(): pl.pallas_call(first_kernel, out_shape=sent_shapes, in_specs=in_smem(2) +...  7.95 us
    pallas_call x2, Pallas kernels, star_forward(): pl.pallas_call(star_forward_kernel, out_shape=image_shape, in_specs=in_vm...  6.3 us
    ppermute x8, starting transfers between devices, partner(): lax.ppermute(array, axis, [(i, i ^ distance) for i in range(lax.axis_size...  6.11 us
    pallas_call x1, Pallas kernels, last_gather(): pl.pallas_call(functools.partial(last_kernel, n_stars, n_seg), out_shape=...  3.76 us
  transfers between devices with their start and end apart: 13, of which 12 were waited for; matrix products, arithmetic and copies ran while one was open for 1% of the time, Pallas kernels for 7%

profile of v20, /device:TPU:0, one launch (start us, length us, event | category | flops | bytes accessed | tf_op | source)
XLA Modules:
  0.0 90.8 jit_solution(18081263090082360842)
XLA Ops:
  1.3 7.9 %first_scatter.1 = (f32[8,72,128]{2,1,0:T(8,128)}, f32[160,256]{1,0:T(8,128)}) custom-call(s32[1]{0:T(128)S(6)} %copy.17.live_ref, s32[1]{0:T(128)} %bitcast.place_ref, f32[128,128]{1,0:T(8,128)} %value_ref.1, f32[128,128]{1,0:T(8,128)} %cal_coef_ref.3, s32[1,128]{1,0:T(1,128)} %bitcast.6, s32[128,128]{1,0:T(8,128)} %knot_ref.3, f32[128,128]{1,0:T(8,128)} %frac_ref.3, ...), custom_call_target="tpu_custom_call" | custom-call | flops 3000000000 | bytes 1000000 | tf_op jit(solution)/shard_map/first_scatter/pallas_call | solution.py:482
  9.2 7.4 %all-to-all-start = ((f32[8,72,128]{2,1,0:T(8,128)}), f32[8,72,128]{2,1,0:T(8,128)S(1)}, u32[]{:S(2)}, u32[]{:S(2)}) async-start(f32[8,72,128]{2,1,0:T(8,128)} %get-tuple-element.20), calls=%async_computation | async-start | bytes 589824 | tf_op jit(solution)/shard_map/all_to_all | solution.py:532
  16.6 1.6 %collective-permute-start = (f32[160,256]{1,0:T(8,128)S(1)}, f32[160,256]{1,0:T(8,128)S(1)}, u32[]{:S(2)}, u32[]{:S(2)}) collective-permute-start(f32[160,256]{1,0:T(8,128)S(1)} %copy-done.8), channel_id=1, source_target_pairs={{0,1},{1,0},{2,3},{3,2},{4,5},{5,4},{6,7},{7,6},{8,9},{9,8},{10,11... | collective-permute-start | bytes 491528 | tf_op jit(solution)/shard_map/ppermute | solution.py:541
  18.3 1.0 %collective-permute-done = f32[160,256]{1,0:T(8,128)S(1)} collective-permute-done((f32[160,256]{1,0:T(8,128)S(1)}, f32[160,256]{1,0:T(8,128)S(1)}, u32[]{:S(2)}, u32[]{:S(2)}) %collective-permute-start) | collective-permute-done | bytes 163872 | tf_op jit(solution)/shard_map/ppermute | solution.py:541
  19.3 0.9 collective-permute-start.1
  20.2 5.7 %collective-permute-done.1.other_ref = f32[160,256]{1,0:T(8,128)S(1)} collective-permute-done((f32[160,256]{1,0:T(8,128)S(1)}, f32[160,256]{1,0:T(8,128)S(1)}, u32[]{:S(2)}, u32[]{:S(2)}) %collective-permute-start.1) | collective-permute-done | bytes 163872 | tf_op jit(solution)/shard_map/ppermute | solution.py:541
  26.9 4.3 %all-to-all-start.1 = ((f32[8,64,128]{2,1,0:T(8,128)}), f32[8,64,128]{2,1,0:T(8,128)S(1)}, u32[]{:S(2)}, u32[]{:S(2)}) async-start(f32[8,64,128]{2,1,0:T(8,128)} %get-tuple-element.23), calls=%async_computation.1 | async-start | bytes 524288 | tf_op jit(solution)/shard_map/all_to_all | solution.py:532
  31.3 1.1 %collective-permute-start.2 = (f32[8,128]{1,0:T(8,128)S(1)}, f32[8,128]{1,0:T(8,128)S(1)}, u32[]{:S(2)}, u32[]{:S(2)}) collective-permute-start(f32[8,128]{1,0:T(8,128)S(1)} %get-tuple-element.24), channel_id=1, source_target_pairs={{0,1},{1,0},{2,3},{3,2},{4,5},{5,4},{6,7},{7,6},{8,9},{9,8},{10,11... | collective-permute-start | bytes 12296 | tf_op jit(solution)/shard_map/ppermute | solution.py:541
  32.4 0.8 collective-permute-done.2
  33.7 3.2 %star_forward.2.star_image_ref = f32[128,128]{1,0:T(8,128)S(1)} custom-call(s32[128,128]{1,0:T(8,128)S(1)} %copy-done.3, f32[5,128,128]{2,1,0:T(8,128)S(1)} %copy-done.1, f32[160,256]{1,0:T(8,128)S(1)} %get-tuple-element.22.star_x_ref.star_0_ref), custom_call_target="tpu_custom_call" | custom-call | flops 3000000000 | bytes 1000000 | tf_op jit(solution)/shard_map/star_forward/pallas_call | solution.py:520
  36.8 2.7 %all-to-all-done.1.block_ref = f32[8,64,128]{2,1,0:T(8,128)S(1)} async-done(((f32[8,64,128]{2,1,0:T(8,128)}), f32[8,64,128]{2,1,0:T(8,128)S(1)}, u32[]{:S(2)}, u32[]{:S(2)}) %all-to-all-start.1) | async-done | bytes 262176 | tf_op jit(solution)/shard_map/all_to_all | solution.py:532
  39.6 9.0 %gather_and_scatter.1 = (f32[128,128]{1,0:T(8,128)S(1)}, f32[256,256]{1,0:T(8,128)S(1)}, f32[8,72,128]{2,1,0:T(8,128)}, f32[160,256]{1,0:T(8,128)S(1)}) custom-call(s32[1]{0:T(128)S(6)} %copy.17.live_ref, s32[1]{0:T(128)} %bitcast.place_ref, s32[128,128]{1,0:T(8,128)S(1)} %copy-done.4, f32[128,128]{1,0:T(8,128)S(1)} %copy-done.5, ...), custom_call_target="tpu_custom_call" | custom-call | flops 3000000000 | bytes 1000000 | tf_op jit(solution)/shard_map/gather_and_scatter/pallas_call | solution.py:495
  48.6 4.2 %all-to-all-start.2 = ((f32[8,72,128]{2,1,0:T(8,128)}), f32[8,72,128]{2,1,0:T(8,128)S(1)}, u32[]{:S(2)}, u32[]{:S(2)}) async-start(f32[8,72,128]{2,1,0:T(8,128)} %get-tuple-element.25), calls=%async_computation.2 | async-start | bytes 589824 | tf_op jit(solution)/shard_map/all_to_all | solution.py:532
  53.6 1.0 %collective-permute-done.4 = f32[160,256]{1,0:T(8,128)S(1)} collective-permute-done((f32[160,256]{1,0:T(8,128)S(1)}, f32[160,256]{1,0:T(8,128)S(1)}, u32[]{:S(2)}, u32[]{:S(2)}) %collective-permute-start.4) | collective-permute-done | bytes 163872 | tf_op jit(solution)/shard_map/ppermute | solution.py:541
  54.8 6.3 %collective-permute-done.5.other_ref = f32[160,256]{1,0:T(8,128)S(1)} collective-permute-done((f32[160,256]{1,0:T(8,128)S(1)}, f32[160,256]{1,0:T(8,128)S(1)}, u32[]{:S(2)}, u32[]{:S(2)}) %collective-permute-start.5) | collective-permute-done | bytes 163872 | tf_op jit(solution)/shard_map/ppermute | solution.py:541
  62.2 5.1 %all-to-all-start.3 = ((f32[8,64,128]{2,1,0:T(8,128)}), f32[8,64,128]{2,1,0:T(8,128)S(1)}, u32[]{:S(2)}, u32[]{:S(2)}) async-start(f32[8,64,128]{2,1,0:T(8,128)} %get-tuple-element.28), calls=%async_computation.3 | async-start | bytes 524288 | tf_op jit(solution)/shard_map/all_to_all | solution.py:532
  67.3 1.1 %collective-permute-start.6 = (f32[8,128]{1,0:T(8,128)S(1)}, f32[8,128]{1,0:T(8,128)S(1)}, u32[]{:S(2)}, u32[]{:S(2)}) collective-permute-start(f32[8,128]{1,0:T(8,128)S(1)} %get-tuple-element.29), channel_id=1, source_target_pairs={{0,1},{1,0},{2,3},{3,2},{4,5},{5,4},{6,7},{7,6},{8,9},{9,8},{10,11... | collective-permute-start | bytes 12296 | tf_op jit(solution)/shard_map/ppermute | solution.py:541
  68.4 0.8 collective-permute-done.6
  69.3 3.1 %star_forward.3.star_image_ref = f32[128,128]{1,0:T(8,128)S(1)} custom-call(s32[128,128]{1,0:T(8,128)S(1)} %copy-done.3, f32[5,128,128]{2,1,0:T(8,128)S(1)} %copy-done.1, f32[160,256]{1,0:T(8,128)S(1)} %get-tuple-element.27.star_x_ref), custom_call_target="tpu_custom_call" | custom-call | flops 3000000000 | bytes 1000000 | tf_op jit(solution)/shard_map/star_forward/pallas_call | solution.py:520
  72.9 2.8 %all-to-all-done.3.block_ref = f32[8,64,128]{2,1,0:T(8,128)S(1)} async-done(((f32[8,64,128]{2,1,0:T(8,128)}), f32[8,64,128]{2,1,0:T(8,128)S(1)}, u32[]{:S(2)}, u32[]{:S(2)}) %all-to-all-start.3) | async-done | bytes 262176 | tf_op jit(solution)/shard_map/all_to_all | solution.py:532
  75.6 3.8 %last_gather.1 = (f32[128,128]{1,0:T(8,128)S(1)}, f32[256,256]{1,0:T(8,128)S(1)}, f32[32,1,128]{2,1,0:T(1,128)}, f32[8,128]{1,0:T(8,128)S(1)}) custom-call(s32[1]{0:T(128)S(6)} %copy.17.live_ref, s32[1]{0:T(128)} %bitcast.place_ref, s32[128,128]{1,0:T(8,128)S(1)} %copy-done.4, f32[128,128]{1,0:T(8,128)S(1)} %copy-done.5, f32[4,128,128]{2,1,0:T(8,128)S(1)} %copy-done.2, ...), custom_call_target="tpu_custom_call" | custom-call | flops 3000000000 | bytes 1000000 | tf_op jit(solution)/shard_map/last_gather/pallas_call | solution.py:508
  79.4 3.3 %all-to-all-start.4 = ((f32[32,1,128]{2,1,0:T(1,128)}), f32[32,1,128]{2,1,0:T(1,128)S(1)}, u32[]{:S(2)}, u32[]{:S(2)}) async-start(f32[32,1,128]{2,1,0:T(1,128)} %get-tuple-element.33), calls=%async_computation.4 | async-start | bytes 32768 | tf_op jit(solution)/shard_map/all_to_all | solution.py:532
  83.8 6.0 %all-to-all-done.4.scalar_ref = f32[32,1,128]{2,1,0:T(1,128)S(1)} async-done(((f32[32,1,128]{2,1,0:T(1,128)}), f32[32,1,128]{2,1,0:T(1,128)S(1)}, u32[]{:S(2)}, u32[]{:S(2)}) %all-to-all-start.4) | async-done | bytes 16416 | tf_op jit(solution)/shard_map/all_to_all | solution.py:532
  89.8 1.0 %outputs.1 = (f32[5,8192]{1,0:T(8,128)}, f32[4,8192]{1,0:T(4,128)}, f32[256,128]{1,0:T(8,128)}, f32[128,128]{1,0:T(8,128)}) custom-call(s32[1]{0:T(128)S(6)} %copy.17.live_ref, f32[8,128]{1,0:T(8,128)S(1)} %get-tuple-element.32.own_scalar_ref, f32[32,1,128]{2,1,0:T(1,128)S(1)} %all-to-all-done.4.scalar_ref, f32[5,8192]{1,0:T(8,128)S(1)} %reshape.26.star_0_ref, ...), custom_call_target="tpu_custom_call" | custom-call | flops 1000000 | bytes 600000 | tf_op jit(solution)/shard_map/outputs/pallas_call | solution.py:575
  (40 shorter events, 5.0 us)
Async XLA Ops:
  9.2 7.4 %copy-start.8 = (f32[160,256]{1,0:T(8,128)S(1)}, f32[160,256]{1,0:T(8,128)}, u32[]{:S(2)}) copy-start(f32[160,256]{1,0:T(8,128)} %get-tuple-element.21) | copy-start | bytes 491524
  9.2 16.9 %all-to-all-start = ((f32[8,72,128]{2,1,0:T(8,128)}), f32[8,72,128]{2,1,0:T(8,128)S(1)}, u32[]{:S(2)}, u32[]{:S(2)}) async-start(f32[8,72,128]{2,1,0:T(8,128)} %get-tuple-element.20), calls=%async_computation | async-start | bytes 589824 | tf_op jit(solution)/shard_map/all_to_all | solution.py:532
  16.6 2.7 %collective-permute-start = (f32[160,256]{1,0:T(8,128)S(1)}, f32[160,256]{1,0:T(8,128)S(1)}, u32[]{:S(2)}, u32[]{:S(2)}) collective-permute-start(f32[160,256]{1,0:T(8,128)S(1)} %copy-done.8), channel_id=1, source_target_pairs={{0,1},{1,0},{2,3},{3,2},{4,5},{5,4},{6,7},{7,6},{8,9},{9,8},{10,11... | collective-permute-start | bytes 491528 | tf_op jit(solution)/shard_map/ppermute | solution.py:541
  19.3 6.5 %collective-permute-start.1 = (f32[160,256]{1,0:T(8,128)S(1)}, f32[160,256]{1,0:T(8,128)S(1)}, u32[]{:S(2)}, u32[]{:S(2)}) collective-permute-start(f32[160,256]{1,0:T(8,128)S(1)} %add.12.own_ref), channel_id=1, source_target_pairs={{0,2},{1,3},{2,0},{3,1},{4,6},{5,7},{6,4},{7,5},{8,10},{9,11},{10,... | collective-permute-start | bytes 491528 | tf_op jit(solution)/shard_map/ppermute | solution.py:541
  26.9 6.7 %copy-start.1 = (f32[5,128,128]{2,1,0:T(8,128)S(1)}, f32[5,128,128]{2,1,0:T(8,128)}, u32[]{:S(2)}) copy-start(f32[5,128,128]{2,1,0:T(8,128)} %star_coef_ref.5) | copy-start | bytes 983044
  26.9 6.7 %copy-start.3 = (s32[128,128]{1,0:T(8,128)S(1)}, s32[128,128]{1,0:T(8,128)}, u32[]{:S(2)}) copy-start(s32[128,128]{1,0:T(8,128)} %star_ref.5) | copy-start | bytes 196612
  26.9 12.6 %all-to-all-start.1 = ((f32[8,64,128]{2,1,0:T(8,128)}), f32[8,64,128]{2,1,0:T(8,128)S(1)}, u32[]{:S(2)}, u32[]{:S(2)}) async-start(f32[8,64,128]{2,1,0:T(8,128)} %get-tuple-element.23), calls=%async_computation.1 | async-start | bytes 524288 | tf_op jit(solution)/shard_map/all_to_all | solution.py:532
  31.3 1.9 %collective-permute-start.2 = (f32[8,128]{1,0:T(8,128)S(1)}, f32[8,128]{1,0:T(8,128)S(1)}, u32[]{:S(2)}, u32[]{:S(2)}) collective-permute-start(f32[8,128]{1,0:T(8,128)S(1)} %get-tuple-element.24), channel_id=1, source_target_pairs={{0,1},{1,0},{2,3},{3,2},{4,5},{5,4},{6,7},{7,6},{8,9},{9,8},{10,11... | collective-permute-start | bytes 12296 | tf_op jit(solution)/shard_map/ppermute | solution.py:541
  33.2 3.6 %collective-permute-start.3 = (f32[8,128]{1,0:T(8,128)S(1)}, f32[8,128]{1,0:T(8,128)S(1)}, u32[]{:S(2)}, u32[]{:S(2)}) collective-permute-start(f32[8,128]{1,0:T(8,128)S(1)} %add.13.edge_ref), channel_id=1, source_target_pairs={{0,2},{1,3},{2,0},{3,1},{4,6},{5,7},{6,4},{7,5},{8,10},{9,11},{10,... | collective-permute-start | bytes 12296 | tf_op jit(solution)/shard_map/ppermute | solution.py:541
  33.6 6.0 %copy-start.2 = (f32[4,128,128]{2,1,0:T(8,128)S(1)}, f32[4,128,128]{2,1,0:T(8,128)}, u32[]{:S(2)}) copy-start(f32[4,128,128]{2,1,0:T(8,128)} %att_coef_ref.3) | copy-start | bytes 786436
  33.6 6.0 %copy-start.4 = (s32[128,128]{1,0:T(8,128)S(1)}, s32[128,128]{1,0:T(8,128)}, u32[]{:S(2)}) copy-start(s32[128,128]{1,0:T(8,128)} %knot_ref.3) | copy-start | bytes 196612
  33.6 6.0 %copy-start.5 = (f32[128,128]{1,0:T(8,128)S(1)}, f32[128,128]{1,0:T(8,128)}, u32[]{:S(2)}) copy-start(f32[128,128]{1,0:T(8,128)} %frac_ref.3) | copy-start | bytes 196612
  33.6 6.0 %copy-start.6 = (f32[128,128]{1,0:T(8,128)S(1)}, f32[128,128]{1,0:T(8,128)}, u32[]{:S(2)}) copy-start(f32[128,128]{1,0:T(8,128)} %cal_coef_ref.3) | copy-start | bytes 196612
  33.6 6.0 %copy-start.7 = (s32[128]{0:T(128)S(1)}, s32[128]{0:T(128)}, u32[]{:S(2)}) copy-start(s32[128]{0:T(128)} %param.15) | copy-start | bytes 1540
  48.6 12.8 %all-to-all-start.2 = ((f32[8,72,128]{2,1,0:T(8,128)}), f32[8,72,128]{2,1,0:T(8,128)S(1)}, u32[]{:S(2)}, u32[]{:S(2)}) async-start(f32[8,72,128]{2,1,0:T(8,128)} %get-tuple-element.25), calls=%async_computation.2 | async-start | bytes 589824 | tf_op jit(solution)/shard_map/all_to_all | solution.py:532
  52.9 1.7 %collective-permute-start.4 = (f32[160,256]{1,0:T(8,128)S(1)}, f32[160,256]{1,0:T(8,128)S(1)}, u32[]{:S(2)}, u32[]{:S(2)}) collective-permute-start(f32[160,256]{1,0:T(8,128)S(1)} %get-tuple-element.26), channel_id=1, source_target_pairs={{0,1},{1,0},{2,3},{3,2},{4,5},{5,4},{6,7},{7,6},{8,9},{9,8},{10,11... | collective-permute-start | bytes 491528 | tf_op jit(solution)/shard_map/ppermute | solution.py:541
  54.6 6.5 %collective-permute-start.5 = (f32[160,256]{1,0:T(8,128)S(1)}, f32[160,256]{1,0:T(8,128)S(1)}, u32[]{:S(2)}, u32[]{:S(2)}) collective-permute-start(f32[160,256]{1,0:T(8,128)S(1)} %add.14.own_ref), channel_id=1, source_target_pairs={{0,2},{1,3},{2,0},{3,1},{4,6},{5,7},{6,4},{7,5},{8,10},{9,11},{10,... | collective-permute-start | bytes 491528 | tf_op jit(solution)/shard_map/ppermute | solution.py:541
  62.2 13.4 %all-to-all-start.3 = ((f32[8,64,128]{2,1,0:T(8,128)}), f32[8,64,128]{2,1,0:T(8,128)S(1)}, u32[]{:S(2)}, u32[]{:S(2)}) async-start(f32[8,64,128]{2,1,0:T(8,128)} %get-tuple-element.28), calls=%async_computation.3 | async-start | bytes 524288 | tf_op jit(solution)/shard_map/all_to_all | solution.py:532
  67.3 1.9 %collective-permute-start.6 = (f32[8,128]{1,0:T(8,128)S(1)}, f32[8,128]{1,0:T(8,128)S(1)}, u32[]{:S(2)}, u32[]{:S(2)}) collective-permute-start(f32[8,128]{1,0:T(8,128)S(1)} %get-tuple-element.29), channel_id=1, source_target_pairs={{0,1},{1,0},{2,3},{3,2},{4,5},{5,4},{6,7},{7,6},{8,9},{9,8},{10,11... | collective-permute-start | bytes 12296 | tf_op jit(solution)/shard_map/ppermute | solution.py:541
  69.3 3.6 %collective-permute-start.7 = (f32[8,128]{1,0:T(8,128)S(1)}, f32[8,128]{1,0:T(8,128)S(1)}, u32[]{:S(2)}, u32[]{:S(2)}) collective-permute-start(f32[8,128]{1,0:T(8,128)S(1)} %add.15.edge_ref), channel_id=1, source_target_pairs={{0,2},{1,3},{2,0},{3,1},{4,6},{5,7},{6,4},{7,5},{8,10},{9,11},{10,... | collective-permute-start | bytes 12296 | tf_op jit(solution)/shard_map/ppermute | solution.py:541
  79.4 10.4 %all-to-all-start.4 = ((f32[32,1,128]{2,1,0:T(1,128)}), f32[32,1,128]{2,1,0:T(1,128)S(1)}, u32[]{:S(2)}, u32[]{:S(2)}) async-start(f32[32,1,128]{2,1,0:T(1,128)} %get-tuple-element.33), calls=%async_computation.4 | async-start | bytes 32768 | tf_op jit(solution)/shard_map/all_to_all | solution.py:532
  83.5 6.3 %copy-start = (f32[128,128]{1,0:T(8,128)S(1)}, f32[128,128]{1,0:T(8,128)}, u32[]{:S(2)}) copy-start(f32[128,128]{1,0:T(8,128)} %value_ref.1) | copy-start | bytes 196612
